TPU v7x, 32 devices: a whole 2x2x4 slice. The times are simulated.
32 devices in a mesh: solver: 16 (over z, y, core), analysis: 2 (over x).
Axes of the slice: x: 2, y: 2, z: 4, core: 2. Of those that a mesh axis runs over, the one named last changes fastest.
Arguments:
- windows: float32 [2, 5, 128, 8, 512], P(None, None, 'solver', 'analysis'), may hold values from -2.3 to 3.7, as said below
- pod_basis: bfloat16 [64, 5, 128, 8, 512], P(None, None, ('solver', 'analysis')), may hold values from -1.9 to 3.4
Outputs:
- next_windows: float32 [2, 5, 128, 8, 512], P(None, None, 'solver', 'analysis')
- coefficients: float32 [2, 64], replicated
- new_modes: float32 [2, 5, 128, 8, 512], P(None, None, ('solver', 'analysis'))
- r_factor: float32 [2, 2], replicated
Inputs may be any that keep to these rules, and one draw needn't show every extreme that they name: `windows`: field 0 (density) lies between 0.4 and 1.6 everywhere.
All inputs are finite; a program needn't handle non-finite values.
Results may differ from a plain program's by a relative error of at most 0.00185.
The roundings to bfloat16 on the way count: a program that leaves them out, or rounds other values in their place, can miss the bound.
Values may be sent and summed in bfloat16 or wider, within the bound.
No kernel may reach another device: no remote copies, remote signals or barrier semaphores. Data moves between devices by JAX's collectives and lax.ppermute only.
A program may use at most 128 MiB of HBM per device.

v0:
```python
import jax
import jax.numpy as jnp
from jax import lax
from jax.sharding import PartitionSpec as P

HEAT_RATIO = 1.4
SECTION_STEP = 0.25
CENTRAL_WEIGHTS = (0.8, -0.2, 4.0 / 105.0, -1.0 / 280.0)


def padded(cells, sides, width, closed):
    for axis, dim in sides:
        count = lax.axis_size(axis)
        ends = count if closed else count - 1
        head = lax.slice_in_dim(cells, 0, width, axis=dim)
        tail = lax.slice_in_dim(cells, cells.shape[dim] - width, cells.shape[dim], axis=dim)
        cells = jnp.concatenate(
            [
                lax.ppermute(tail, axis, [(i, (i + 1) % count) for i in range(ends)]),
                cells,
                lax.ppermute(head, axis, [((i + 1) % count, i) for i in range(ends)]),
            ],
            axis=dim,
        )
    return cells


def flux_parts(fields_in):
    density = fields_in[:, 0]
    moment_x = fields_in[:, 1]
    moment_y = fields_in[:, 2]
    moment_z = fields_in[:, 3]
    energy = fields_in[:, 4]
    speed_x = moment_x / density
    speed_y = moment_y / density
    speed_z = moment_z / density
    pressure = (HEAT_RATIO - 1.0) * (
        energy - 0.5 * (moment_x * speed_x + moment_y * speed_y + moment_z * speed_z)
    )
    enthalpy = energy + pressure
    flux_x = jnp.stack(
        [
            moment_x,
            moment_x * speed_x + pressure,
            moment_y * speed_x,
            moment_z * speed_x,
            enthalpy * speed_x,
        ],
        axis=1,
    )
    flux_y = jnp.stack(
        [
            moment_y,
            moment_x * speed_y,
            moment_y * speed_y + pressure,
            moment_z * speed_y,
            enthalpy * speed_y,
        ],
        axis=1,
    )
    flux_z = jnp.stack(
        [
            moment_z,
            moment_x * speed_z,
            moment_y * speed_z,
            moment_z * speed_z + pressure,
            enthalpy * speed_z,
        ],
        axis=1,
    )
    return (flux_x, flux_y, flux_z)


def centered(extended, dimension, length):
    summed = None
    for offset, weight in enumerate(CENTRAL_WEIGHTS, start=1):
        forward_cells = lax.slice_in_dim(extended, 4 + offset, 4 + offset + length, axis=dimension)
        behind_cells = lax.slice_in_dim(extended, 4 - offset, 4 - offset + length, axis=dimension)
        term = weight * (forward_cells - behind_cells)
        summed = term if summed is None else summed + term
    return summed


def spanwise(flux_z):
    summed = None
    for offset, weight in enumerate(CENTRAL_WEIGHTS, start=1):
        term = weight * (jnp.roll(flux_z, -offset, axis=4) - jnp.roll(flux_z, offset, axis=4))
        summed = term if summed is None else summed + term
    return summed


def tendency(wide_x, wide_y, flux_z, cells_x, cells_y):
    return -(centered(wide_x, 2, cells_x) + centered(wide_y, 3, cells_y) + spanwise(flux_z))


def cholesky_lower(matrix):
    highest = lax.Precision.HIGHEST
    order = matrix.shape[0]
    index = jnp.arange(order, dtype=jnp.int32)

    def column_step(column, lower):
        picker = (index == column).astype(matrix.dtype)
        row_now = jnp.dot(picker, lower, precision=highest)
        left = jnp.dot(matrix, picker, precision=highest) - jnp.dot(
            lower, row_now, precision=highest
        )
        pivot = jnp.sqrt(jnp.dot(left, picker, precision=highest))
        fresh = jnp.where(index >= column, left / pivot, jnp.zeros_like(left))
        return lower + fresh[:, None] * picker[None, :]

    return lax.fori_loop(0, order, column_step, jnp.zeros_like(matrix))


def solve_modes(basis_gram, projected):
    highest = lax.Precision.HIGHEST
    lower = cholesky_lower(basis_gram)
    order = lower.shape[0]
    index = jnp.arange(order, dtype=jnp.int32)

    def forward_step(row, solution):
        picker = (index == row).astype(lower.dtype)
        row_now = jnp.dot(picker, lower, precision=highest)
        pivot = jnp.dot(row_now, picker, precision=highest)
        value = (
            jnp.dot(picker, projected, precision=highest)
            - jnp.dot(row_now, solution, precision=highest)
        ) / pivot
        return solution + picker[:, None] * value[None, :]

    halfway = lax.fori_loop(0, order, forward_step, jnp.zeros_like(projected))

    def backward_step(count, solution):
        row = order - 1 - count
        picker = (index == row).astype(lower.dtype)
        column_now = jnp.dot(lower, picker, precision=highest)
        pivot = jnp.dot(column_now, picker, precision=highest)
        value = (
            jnp.dot(picker, halfway, precision=highest)
            - jnp.dot(column_now, solution, precision=highest)
        ) / pivot
        return solution + picker[:, None] * value[None, :]

    return lax.fori_loop(0, order, backward_step, jnp.zeros_like(projected))


def small_factor(gram_small):
    first = jnp.sqrt(gram_small[0, 0])
    below = gram_small[1, 0] / first
    second = jnp.sqrt(gram_small[1, 1] - below * below)
    return (first, below, second)


def upper_factor(first, below, second, scaling):
    zero = jnp.zeros_like(first)
    return jnp.stack([jnp.stack([first, below]), jnp.stack([zero, second])]) / scaling


def residual_rows(flat_snap, flat_basis, solved):
    upper_part = solved.astype(jnp.bfloat16)
    lower_part = (solved - upper_part.astype(jnp.float32)).astype(jnp.bfloat16)
    contract = (((0,), (0,)), ((), ()))
    fitted = lax.dot_general(upper_part, flat_basis, contract, preferred_element_type=jnp.float32)
    fitted = fitted + lax.dot_general(
        lower_part, flat_basis, contract, preferred_element_type=jnp.float32
    )
    return flat_snap.astype(jnp.float32) - fitted


def row_products(residuals):
    return jnp.sum(residuals[:, None, :] * residuals[None, :, :], axis=2)


def body(windows, pod_basis):
    cells_x = windows.shape[2]
    cells_y = windows.shape[3]
    flux_x, flux_y, flux_z = flux_parts(windows)
    wide_x = padded(flux_x, (("solver", 2),), 4, True)
    wide_y = padded(flux_y, (("analysis", 3),), 4, False)
    next_windows = windows + SECTION_STEP * tendency(wide_x, wide_y, flux_z, cells_x, cells_y)
    snapshots = next_windows.astype(jnp.bfloat16)
    relaid = lax.all_to_all(snapshots, "analysis", split_axis=2, concat_axis=3, tiled=True)
    window_count = relaid.shape[0]
    modes_count = pod_basis.shape[0]
    flat_basis = pod_basis.reshape(modes_count, -1)
    flat_snap = relaid.reshape(window_count, -1)
    contract = (((1,), (1,)), ((), ()))
    basis_gram = lax.dot_general(
        flat_basis, flat_basis, contract, preferred_element_type=jnp.float32
    )
    projected = lax.dot_general(flat_basis, flat_snap, contract, preferred_element_type=jnp.float32)
    basis_gram, projected = lax.psum((basis_gram, projected), ("solver", "analysis"))
    solved = solve_modes(basis_gram, projected)
    residuals = residual_rows(flat_snap, flat_basis, solved)
    local_gram = row_products(residuals)
    gram_small = lax.psum(local_gram, ("solver", "analysis"))
    rows_total = (
        pod_basis.shape[1] * cells_x * lax.axis_size("solver") * relaid.shape[3] * relaid.shape[4]
    )
    scaling = jnp.sqrt(jnp.float32(rows_total))
    first, below, second = small_factor(gram_small)
    row_zero = residuals[0] / first
    row_one = (residuals[1] - below * row_zero) / second
    new_modes = jnp.stack([row_zero, row_one], axis=0) * scaling
    return (
        next_windows,
        solved.T,
        new_modes.reshape(relaid.shape),
        upper_factor(first, below, second, scaling),
    )


def solution(mesh):
    in_specs = (
        P(None, None, "solver", "analysis", None),
        P(None, None, ("solver", "analysis"), None, None),
    )
    out_specs = (
        P(None, None, "solver", "analysis", None),
        P(),
        P(None, None, ("solver", "analysis"), None, None),
        P(),
    )
    return jax.shard_map(body, mesh=mesh, in_specs=in_specs, out_specs=out_specs, check_vma=False)
```

profile of v0, /device:TPU:0, one launch (start us, length us, event | category | flops | bytes accessed | tf_op | source)
XLA Modules:
  0.0 534.8 jit_solution(8771649962195939120)
XLA Ops:
  1.6 1.4 add_dynamic-update-slice_fusion.2
  3.0 1.0 multiply_dynamic-update-slice_fusion.8
  5.0 1.1 multiply_dynamic-update-slice_fusion.7
  6.1 1.1 multiply_dynamic-update-slice_fusion.5
  7.1 1.1 multiply_dynamic-update-slice_fusion.6
  10.2 4.9 collective-permute-start.3
  15.1 1.3 collective-permute-start.2
  16.4 3.8 collective-permute-start
  22.5 2.3 collective-permute-done
  24.8 4.6 collective-permute-done.1
  29.4 3.8 collective-permute-done.2
  33.2 5.7 %fusion.94 = (bf16[2,5,8,4,512]{4,3,1,0,2:T(4,128)(2,1)}, f32[2,5,8,4,512]{4,3,1,0,2:T(4,128)S(1)}) fusion(f32[2,5,8,4,508]{4,3,1,0,2:T(4,128)S(1)} %get-tuple-element.409, f32[2,5,8,4,4]{4,3,1,0,2:T(4,128)S(1)} %get-tuple-element.411, f32[2,5,8,4,4]{4,3,1,0,2:T(4,128)S(1)} %get-tuple-element.410, f32[2,5,8,4,508]{4,3,1,0,2:T(4,128)S(1)} %get-tuple-element.408, ...), kind=kLoop, calls=%fused_computation.170 | loop fusion | flops 9994240 | bytes 10158080 | tf_op jit(solution)/shard_map/convert_element_type | solution.py:180
  38.9 4.0 all-to-all-start
  42.9 28.8 %fusion.47 = f32[64,64]{1,0:T(8,128)S(1)} fusion(bf16[64,5,4,8,512]{4,3,2,1,0:T(8,128)(2,1)} %param.9), kind=kOutput, calls=%fused_computation.78 | convolution fusion | flops 671088640 | bytes 10502144 | tf_op jit(solution)/shard_map/dot_general | solution.py:187
  71.7 14.6 %copy.36 = bf16[8,8,160,512]{3,1,2,0:T(8,128)(2,1)} copy(bf16[8,8,160,512]{3,2,1,0:T(8,128)(2,1)} %bitcast.141) | data formatting | bytes 20971520
  86.6 5.5 %convolution_bitcast_fusion.7 = f32[64,2]{0,1:T(2,128)S(1)} fusion(bf16[2,81920]{1,0:T(2,128)(2,1)S(1)} %reshape.43, bf16[64,81920]{1,0:T(8,128)(2,1)} %bitcast.138), kind=kOutput, calls=%fused_computation.79 | convolution fusion | flops 20971520 | bytes 10813952 | tf_op jit(solution)/shard_map/dot_general | solution.py:190
  92.1 41.6 %all-reduce = (f32[64,2]{0,1:T(2,128)S(1)}, f32[64,64]{1,0:T(8,128)S(1)}) all-reduce(f32[64,2]{0,1:T(2,128)S(1)} %convolution_bitcast_fusion.7, f32[64,64]{1,0:T(8,128)S(1)} %fusion.47), channel_id=1, replica_groups=mesh['solver'=16,'analysis'=2] {'solver','analysis'}, use_global_device_ids=true, to_apply=%region_3.4 | all-reduce | flops 4224 | bytes 33792 | tf_op jit(solution)/shard_map/psum | solution.py:191
  133.7 119.8 %while.45 = (s32[]{:T(128)}, f32[64,64]{1,0:T(8,128)S(1)}, f32[64,64]{1,0:T(8,128)S(1)}, s32[]{:T(128)}, s32[]{:T(128)}) while((s32[]{:T(128)}, f32[64,64]{1,0:T(8,128)S(1)}, f32[64,64]{1,0:T(8,128)S(1)}, s32[]{:T(128)}, s32[]{:T(128)}) %tuple.128), condition=%wide.region_2.3_spmd.clone.clone, body=%wide.region_1.2_spmd.clone.clone.sunk | while | flops 168642 | bytes 84597 | solution.py:111
  253.6 110.8 %while.43 = (s32[]{:T(128)}, f32[64,2]{0,1:T(2,128)S(1)}, f32[64,2]{0,1:T(2,128)S(1)}, f32[64,64]{1,0:T(8,128)S(1)}, s32[]{:T(128)}, /*index=5*/s32[]{:T(128)}) while((s32[]{:T(128)}, f32[64,2]{0,1:T(2,128)S(1)}, f32[64,2]{0,1:T(2,128)S(1)}, f32[64,64]{1,0:T(8,128)S(1)}, s32[]{:T(128)}, /*index=5*/s32[]{:T(128)}) %tuple.131), condition=%wide.region_5.6_spmd.clone, body=%wide.region_4.5_spmd.clone.sunk | while | flops 53190 | bytes 19596 | solution.py:130
  364.4 112.0 %while.44 = (s32[]{:T(128)}, f32[64,2]{0,1:T(2,128)S(1)}, f32[64,2]{0,1:T(2,128)S(1)}, f32[64,64]{1,0:T(8,128)S(1)}, s32[]{:T(128)}, /*index=5*/s32[]{:T(128)}, s32[]{:T(128)}) while((s32[]{:T(128)}, f32[64,2]{0,1:T(2,128)S(1)}, f32[64,2]{0,1:T(2,128)S(1)}, f32[64,64]{1,0:T(8,128)S(1)}, s32[]{:T(128)}, /*index=5*/s32[]{:T(128)}, ...), condition=%wide.region_7.8_spmd.clone, body=%wide.region_6.7_spmd.clone.sunk | while | flops 53191 | bytes 19616 | solution.py:143
  476.4 5.5 %fusion.92 = f32[2,81920]{1,0:T(2,128)S(1)} fusion(bf16[64,81920]{1,0:T(8,128)(2,1)} %bitcast.139, f32[64,2]{0,1:T(2,128)S(1)} %get-tuple-element.276), kind=kOutput, calls=%fused_computation.168 | convolution fusion | flops 20971648 | bytes 11141632 | tf_op jit(solution)/shard_map/dot_general | solution.py:162
  481.9 5.5 %fusion.44 = f32[2,81920]{1,0:T(2,128)S(1)} fusion(f32[2,81920]{1,0:T(2,128)S(1)} %fusion.92, bf16[64,81920]{1,0:T(8,128)(2,1)} %bitcast.140, bf16[2,81920]{1,0:T(2,128)(2,1)S(1)} %reshape.43, f32[64,2]{0,1:T(2,128)S(1)} %get-tuple-element.276), kind=kOutput, calls=%fused_computation.60 | convolution fusion | flops 21463552 | bytes 12124672 | tf_op jit(solution)/shard_map/dot_general | solution.py:163
  489.1 40.0 %psum.23 = f32[2,2]{1,0:T(2,128)S(1)} all-reduce(f32[2,2]{1,0:T(2,128)S(1)} %multiply_reduce_fusion), channel_id=1, replica_groups=mesh['solver'=16,'analysis'=2] {'solver','analysis'}, use_global_device_ids=true, to_apply=%region_9.10 | all-reduce | flops 4 | bytes 32 | tf_op jit(solution)/shard_map/psum | solution.py:195
  531.6 1.2 fusion.90
  (1057 shorter events, 307.3 us)
Async XLA Ops:
  0.6 32.6 %copy-start = (f32[2,5,8,4,512]{4,3,2,1,0:T(4,128)S(1)}, f32[2,5,8,4,512]{4,3,2,1,0:T(4,128)}, u32[]{:S(2)}) copy-start(f32[2,5,8,4,512]{4,3,2,1,0:T(4,128)} %param.8) | copy-start | bytes 1966084
  10.2 19.2 %collective-permute-start.3 = (f32[2,5,8,4,512]{4,3,1,0,2:T(4,128)S(1)}, f32[2,5,8,4,512]{4,3,1,0,2:T(4,128)S(1)}, u32[]{:S(2)}, u32[]{:S(2)}) collective-permute-start(f32[2,5,8,4,512]{4,3,1,0,2:T(4,128)S(1)} %multiply_dynamic-update-slice_fusion.3), channel_id=1, source_target_pairs={{0,1},{2,3},{4,5},{6,7},{8,9},{10,11},{12,13},{14,15},{16,17},{18,... | collective-permute-start | bytes 1966088 | tf_op jit(solution)/shard_map/ppermute | solution.py:19
  15.1 18.1 %collective-permute-start.2 = (f32[2,5,8,4,512]{4,3,1,0,2:T(4,128)S(1)}, f32[2,5,8,4,512]{4,3,1,0,2:T(4,128)S(1)}, u32[]{:S(2)}, u32[]{:S(2)}) collective-permute-start(f32[2,5,8,4,512]{4,3,1,0,2:T(4,128)S(1)} %multiply_dynamic-update-slice_fusion.3), channel_id=1, source_target_pairs={{1,0},{3,2},{5,4},{7,6},{9,8},{11,10},{13,12},{15,14},{17,16},{19,... | collective-permute-start | bytes 1966088 | tf_op jit(solution)/shard_map/ppermute | solution.py:21
  16.4 8.4 %collective-permute-start = (f32[2,5,4,4,512]{4,3,1,0,2:T(4,128)S(1)}, f32[2,5,4,4,512]{4,3,1,0,2:T(4,128)S(1)}, u32[]{:S(2)}, u32[]{:S(2)}) collective-permute-start(f32[2,5,4,4,512]{4,3,1,0,2:T(4,128)S(1)} %get-tuple-element.387), channel_id=1, source_target_pairs={{2,0},{4,2},{6,4},{8,6},{10,8},{12,10},{14,12},{16,14},{18,16},{20... | collective-permute-start | bytes 983048 | tf_op jit(solution)/shard_map/ppermute | solution.py:21
  20.2 9.2 %collective-permute-start.1 = (f32[2,5,4,4,512]{4,3,1,0,2:T(4,128)S(1)}, f32[2,5,4,4,512]{4,3,1,0,2:T(4,128)S(1)}, u32[]{:S(2)}, u32[]{:S(2)}) collective-permute-start(f32[2,5,4,4,512]{4,3,1,0,2:T(4,128)S(1)} %get-tuple-element.388), channel_id=1, source_target_pairs={{0,2},{2,4},{4,6},{6,8},{8,10},{10,12},{12,14},{14,16},{16,18},{18... | collective-permute-start | bytes 983048 | tf_op jit(solution)/shard_map/ppermute | solution.py:19
  38.9 47.4 %all-to-all-start = ((bf16[2,5,8,4,512]{4,3,1,0,2:T(4,128)(2,1)}), bf16[2,5,8,4,512]{4,3,1,0,2:T(4,128)(2,1)S(1)}, u32[]{:S(2)}, u32[]{:S(2)}) async-start(bf16[2,5,8,4,512]{4,3,1,0,2:T(4,128)(2,1)} %get-tuple-element.371), calls=%async_computation | async-start | bytes 655360 | tf_op jit(solution)/shard_map/all_to_all | solution.py:181
  476.4 10.9 %copy-start.1 = (f32[64,2]{0,1:T(2,128)}, f32[64,2]{0,1:T(2,128)S(1)}, u32[]{:S(2)}) copy-start(f32[64,2]{0,1:T(2,128)S(1)} %get-tuple-element.276) | copy-start | bytes 1540
where the time goes:
time: 544 us; the launch traced here: 535 us
  matrix products  326 us (60%)
  blocking collectives  81.6 us (15%)
  loops' own time  45.8 us (8%)
  other arithmetic  34.2 us (6%)
  local copies, waits for them, and re-layouts  19.7 us (4%)
  starting transfers between devices  13.9 us (3%)
  waiting for transfers between devices  10.7 us (2%)
    dot_general x64, matrix products, column_step(): jnp.dot(lower, row_now, precision=highest)  50.8 us
    dot_general x64, matrix products, backward_step(): jnp.dot(picker, halfway, precision=highest)  49.4 us
    dot_general x64, matrix products, forward_step(): jnp.dot(picker, projected, precision=highest)  49.4 us
    dot_general x64, matrix products, backward_step(): column_now = jnp.dot(lower, picker, precision=highest)  49.2 us
    dot_general x64, matrix products, forward_step(): row_now = jnp.dot(picker, lower, precision=highest)  48 us
    another operation x1, loops' own time, cholesky_lower(): return lax.fori_loop(0, order, column_step, jnp.zeros_like(matrix))  45.5 us
    psum x1, blocking collectives, body(): lax.psum((basis_gram, projected), ('solver', 'analysis'))  41.6 us
    psum x1, blocking collectives, body(): gram_small = lax.psum(local_gram, ('solver', 'analysis'))  40 us
  transfers between devices with their start and end apart: 5, of which 3 were waited for; matrix products, arithmetic and copies ran while one was open for 9% of the time, Pallas kernels for 0%

commit v1 on v0

v1 whole, which is shorter than its diff:
```python
import functools

import jax
import jax.numpy as jnp
from jax import lax
from jax.experimental import pallas as pl
from jax.experimental.pallas import tpu as pltpu
from jax.sharding import PartitionSpec as P

PRESSURE_FACTOR = 1.4 - 1.0
SECTION_STEP = 0.25
CENTRAL_WEIGHTS = (0.8, -0.2, 4.0 / 105.0, -1.0 / 280.0)
REACH = 4
LANES = 128
HIGHEST = lax.Precision.HIGHEST
NT = (((1,), (1,)), ((), ()))


def weight(k):
    if k == 0 or abs(k) > REACH:
        return 0.0
    value = -SECTION_STEP * CENTRAL_WEIGHTS[abs(k) - 1]
    return value if k > 0 else -value


def row_weights(shape, values):
    rows = lax.broadcasted_iota(jnp.int32, shape, len(shape) - 2)
    made = jnp.full(shape, values[0], jnp.float32)
    for i, value in enumerate(values[1:], start=1):
        made = jnp.where(rows == i, jnp.float32(value), made)
    return made


def primitives(windows_ref, w, x):
    density, mx, my, mz, energy = (windows_ref[w, f, x] for f in range(5))
    inverse = 1.0 / density
    ux, uy, uz = mx * inverse, my * inverse, mz * inverse
    pressure = PRESSURE_FACTOR * (energy - 0.5 * (mx * ux + my * uy + mz * uz))
    return (mx, my, mz), (ux, uy, uz), pressure, energy + pressure


def flux(parts, direction):
    moments, speeds, pressure, enthalpy = parts
    speed = speeds[direction]
    made = [moments[direction]]
    for axis in range(3):
        term = moments[axis] * speed
        made.append(term + pressure if axis == direction else term)
    made.append(enthalpy * speed)
    return made


def face_kernel(two_sided, where_ref, windows_ref, left_ref, right_ref, *rest):
    windows, _, planes, layers, cells = windows_ref.shape
    wall_refs, scratch = rest[:-1], rest[-1]
    tile = (layers, cells)
    up = [
        row_weights(tile, [weight(j - layers - i) for i in range(layers)]) for j in range(layers)
    ]
    down = [
        row_weights(tile, [weight(layers + j - i) for i in range(layers)]) for j in range(layers)
    ]
    if two_sided:
        tables = (up, down)
    else:
        first = where_ref[0] == 0
        tables = ([jnp.where(first, u, d) for u, d in zip(up, down)],)
    for w in range(windows):
        for x in range(planes):
            parts = primitives(windows_ref, w, x)
            for f, value in enumerate(flux(parts, 0)):
                scratch[f, x] = value
            for f, value in enumerate(flux(parts, 1)):
                for ref, table in zip(wall_refs, tables):
                    total = None
                    for j in range(layers):
                        term = table[j] * value[j : j + 1, :]
                        total = term if total is None else total + term
                    ref[w, f, x] = total
        for f in range(5):
            for i in range(REACH):
                total = None
                for j in range(planes):
                    c = weight(j - planes - i)
                    if c:
                        term = c * scratch[f, j]
                        total = term if total is None else total + term
                left_ref[w, f, i] = total
                total = None
                for j in range(planes):
                    c = weight(j + REACH - i)
                    if c:
                        term = c * scratch[f, j]
                        total = term if total is None else total + term
                right_ref[w, f, i] = total


def inner_kernel(windows_ref, part_ref, scratch):
    windows, _, planes, layers, cells = windows_ref.shape
    tile = (layers, cells)
    wall = [
        row_weights(tile, [weight(j - i) for i in range(layers)]) for j in range(layers)
    ]
    for w in range(windows):
        for x in range(planes):
            parts = primitives(windows_ref, w, x)
            for f, value in enumerate(flux(parts, 0)):
                scratch[f, x] = value
            flux_y, flux_z = flux(parts, 1), flux(parts, 2)
            for f in range(5):
                total = windows_ref[w, f, x]
                for j in range(layers):
                    total = total + wall[j] * flux_y[f][j : j + 1, :]
                for k in range(1, REACH + 1):
                    total = total + weight(k) * (
                        pltpu.roll(flux_z[f], cells - k, 1) - pltpu.roll(flux_z[f], k, 1)
                    )
                part_ref[w, f, x] = total
        for f in range(5):
            for x in range(planes):
                total = part_ref[w, f, x]
                for k in range(-REACH, REACH + 1):
                    if k and 0 <= x + k < planes:
                        total = total + weight(k) * scratch[f, x + k]
                part_ref[w, f, x] = total


def join_kernel(walls, paired, where_ref, part_ref, left_ref, right_ref, *rest):
    wall_refs, next_ref = rest[:walls], rest[walls]
    windows, _, planes, layers, cells = part_ref.shape
    for w in range(windows):
        for f in range(5):
            for x in range(planes):
                total = part_ref[w, f, x]
                for ref in wall_refs:
                    total = total + ref[w, f, x]
                if x < REACH:
                    total = total + left_ref[w, f, x]
                if x >= planes - REACH:
                    total = total + right_ref[w, f, x - planes + REACH]
                next_ref[w, f, x] = total
            if paired:
                half = planes // 2
                low = jnp.concatenate([next_ref[w, f, x] for x in range(half)], axis=0)
                high = jnp.concatenate([next_ref[w, f, x] for x in range(half, planes)], axis=0)
                first = where_ref[0] == 0
                rest[walls + 1][w, f] = jnp.where(first, low, high).astype(jnp.bfloat16)
                rest[walls + 2][w, f] = jnp.where(first, high, low).astype(jnp.bfloat16)


def same_layer(shape):
    rows = lax.broadcasted_iota(jnp.int32, shape, 0)
    columns = lax.broadcasted_iota(jnp.int32, shape, 1)
    return lax.rem(rows, 8) == lax.rem(columns, 8)


def modes_of(basis_ref, t):
    modes, _, layers, cells = basis_ref.shape
    return basis_ref[:, t].reshape(modes * layers, cells)


def gram_kernel(basis_ref, gram_ref, total):
    step = pl.program_id(0)

    @pl.when(step == 0)
    def _():
        total[...] = jnp.zeros_like(total)

    for t in range(basis_ref.shape[1]):
        rows = modes_of(basis_ref, t)
        total[...] += lax.dot_general(rows, rows, NT, preferred_element_type=jnp.float32)

    @pl.when(step == pl.num_programs(0) - 1)
    def _():
        wide = total.shape[0]
        modes = wide // 8
        kept = jnp.where(same_layer(total.shape), total[...], 0.0)
        rows = jnp.sum(kept.reshape(modes, 8, wide), axis=1)
        picks = (
            lax.broadcasted_iota(jnp.int32, (wide, modes), 0) // 8
            == lax.broadcasted_iota(jnp.int32, (wide, modes), 1)
        ).astype(jnp.float32)
        gram_ref[...] = jnp.dot(
            rows, picks, precision=HIGHEST, preferred_element_type=jnp.float32
        )


def project_kernel(paired, where_ref, *rest):
    step = pl.program_id(0)
    if paired:
        own_ref, got_ref, basis_ref, sums_ref, snaps_ref, total, small, square = rest
        steps = basis_ref.shape[1]
        first = where_ref[0] == 0
        for w in range(own_ref.shape[0]):
            own = own_ref[w, 0].astype(jnp.float32)
            got = got_ref[w, 0].astype(jnp.float32)
            low = jnp.where(first, own, got)
            high = jnp.where(first, got, own)
            for t in range(steps):
                snaps_ref[t, pl.ds(8 * w, 8)] = jnp.concatenate(
                    [low[4 * t : 4 * t + 4], high[4 * t : 4 * t + 4]], axis=0
                ).astype(jnp.bfloat16)
    else:
        snaps_ref, basis_ref, sums_ref, total, small, square = rest
        steps = basis_ref.shape[1]

    @pl.when(step == 0)
    def _():
        total[...] = jnp.zeros_like(total)
        small[...] = jnp.zeros_like(small)

    for t in range(steps):
        snaps = snaps_ref[t]
        total[...] += lax.dot_general(
            modes_of(basis_ref, t), snaps, NT, preferred_element_type=jnp.float32
        )
        small[...] += lax.dot_general(snaps, snaps, NT, preferred_element_type=jnp.float32)

    @pl.when(step == pl.num_programs(0) - 1)
    def _():
        modes = total.shape[0] // 8
        columns = total.shape[1]
        kept = jnp.where(same_layer(total.shape), total[...], 0.0)
        square[...] = jnp.zeros_like(square)
        square[0:modes, 0:columns] = jnp.sum(kept.reshape(modes, 8, columns), axis=1)
        kept = jnp.where(same_layer(small.shape), small[...], 0.0)
        square[modes : modes + 1, 0:columns] = jnp.sum(kept[0:8], axis=0, keepdims=True)
        square[modes + 1 : modes + 2, 0:columns] = jnp.sum(kept[8:16], axis=0, keepdims=True)
        turned = square[...].T
        sums_ref[...] = jnp.zeros_like(sums_ref)
        sums_ref[0:1, :] = jnp.sum(turned[0:8], axis=0, keepdims=True)
        sums_ref[1:2, :] = jnp.sum(turned[8:16], axis=0, keepdims=True)


def inverse_kernel(gram_ref, inverse_ref):
    modes = gram_ref.shape[0]
    shape = (modes, 2 * modes)
    rows = lax.broadcasted_iota(jnp.int32, shape, 0)
    columns = lax.broadcasted_iota(jnp.int32, shape, 1)
    eye = (rows[:, :modes] == columns[:, :modes]).astype(jnp.float32)
    whole = jnp.concatenate([gram_ref[...], eye], axis=1)
    for k in range(modes):
        row = whole[k : k + 1, :] / whole[k : k + 1, k : k + 1]
        whole = jnp.where(rows == k, row, whole - whole[:, k : k + 1] * row)
    inverse_ref[...] = whole[:, modes:]


def finish_kernel(
    rows_total, sums_ref, gram_ref, inverse_ref, snaps_ref, basis_ref,
    modes_ref, solved_ref, factor_ref, fit, scales,
):
    step = pl.program_id(0)
    modes = gram_ref.shape[0]

    @pl.when(step == 0)
    def _():
        exact = functools.partial(
            jnp.dot, precision=HIGHEST, preferred_element_type=jnp.float32
        )
        projected = sums_ref[:, 0:modes]
        gram, inverse = gram_ref[...], inverse_ref[...]
        solved = exact(projected, inverse)
        solved = solved + exact(projected - exact(solved, gram), inverse)
        left = projected - exact(solved, gram)

        def inner(p, i, q, j):
            return jnp.sum(p[i : i + 1] * q[j : j + 1], axis=1, keepdims=True)

        def entry(i, j):
            square = sums_ref[i : i + 1, modes + j : modes + j + 1]
            return square - inner(projected, i, solved, j) - inner(solved, i, left, j)

        first = jnp.sqrt(entry(0, 0))
        below = entry(1, 0) / first
        second = jnp.sqrt(entry(1, 1) - below * below)
        scaling = jnp.sqrt(jnp.float32(rows_total))
        w00 = scaling / first
        w11 = scaling / second
        w01 = -(below / first) * w11
        solved_ref[...] = solved[0:2]
        factor_ref[0:1, 0:1] = first / scaling
        factor_ref[0:1, 1:2] = below / scaling
        factor_ref[1:2, 0:1] = jnp.zeros_like(first)
        factor_ref[1:2, 1:2] = second / scaling
        wide = fit.shape[1]
        spread = (
            lax.broadcasted_iota(jnp.int32, (modes, wide), 1) // 8
            == lax.broadcasted_iota(jnp.int32, (modes, wide), 0)
        ).astype(jnp.float32)
        scaled = jnp.concatenate(
            [solved[0:1] * w00, solved[1:2] * w11 + solved[0:1] * w01, solved[2:8]], axis=0
        )
        lines = exact(scaled, spread)
        full = jnp.concatenate(
            [jnp.broadcast_to(lines[0:1], (8, wide)), jnp.broadcast_to(lines[1:2], (8, wide))],
            axis=0,
        )
        full = jnp.where(same_layer(full.shape), full, 0.0)
        upper = full.astype(jnp.bfloat16)
        fit[0:16] = upper
        fit[16:32] = (full - upper.astype(jnp.float32)).astype(jnp.bfloat16)
        scales[0] = jnp.broadcast_to(w00, scales.shape[1:])
        scales[1] = jnp.broadcast_to(w11, scales.shape[1:])
        scales[2] = jnp.broadcast_to(w01, scales.shape[1:])

    for t in range(basis_ref.shape[1]):
        fitted = jnp.dot(fit[...], modes_of(basis_ref, t), preferred_element_type=jnp.float32)
        fitted = fitted[0:16] + fitted[16:32]
        snaps = snaps_ref[t].astype(jnp.float32)
        modes_ref[0, t] = snaps[0:8] * scales[0] - fitted[0:8]
        modes_ref[1, t] = snaps[8:16] * scales[1] + snaps[0:8] * scales[2] - fitted[8:16]


def params(mib):
    return pltpu.CompilerParams(vmem_limit_bytes=mib * 1024 * 1024)


def cost(flops, moved):
    return pl.CostEstimate(flops=flops, bytes_accessed=moved, transcendentals=0)


WHOLE = pl.BlockSpec(memory_space=pltpu.VMEM)
SCALAR = pl.BlockSpec(memory_space=pltpu.SMEM)


def summed(value, axes):
    for axis in axes:
        count = lax.axis_size(axis)
        if count & (count - 1):
            value = lax.psum(value, axis)
            continue
        bit = 1
        while bit < count:
            value = value + lax.ppermute(value, axis, [(i, i ^ bit) for i in range(count)])
            bit *= 2
    return value


def body(windows, pod_basis):
    f32, bf16 = jnp.float32, jnp.bfloat16
    shape = jax.ShapeDtypeStruct
    count, fields, planes, layers, cells = windows.shape
    ring, walls = lax.axis_size("solver"), lax.axis_size("analysis")
    paired = walls == 2 and planes == 8 and layers == 4
    place = lax.axis_index("analysis").astype(jnp.int32).reshape(1)
    modes, _, pod_planes, pod_layers, _ = pod_basis.shape
    tiles = fields * pod_planes * (pod_layers // 8)
    per_step = tiles // fields
    basis = pod_basis.reshape(modes, tiles, 8, cells)
    basis_spec = pl.BlockSpec((modes, per_step, 8, cells), lambda i: (0, i, 0, 0))
    wide = modes * 8
    basis_bytes = basis.size * 2

    sides = 1 if walls == 2 else 2
    faces = pl.pallas_call(
        functools.partial(face_kernel, sides == 2),
        out_shape=[shape((count, fields, REACH, layers, cells), f32)] * 2
        + [shape(windows.shape, f32)] * sides,
        in_specs=[SCALAR, WHOLE],
        out_specs=[WHOLE] * (2 + sides),
        scratch_shapes=[pltpu.VMEM((fields, planes, layers, cells), f32)],
        compiler_params=params(16),
        cost_estimate=cost(10_000_000, 10 * windows.size),
        name="faces",
    )(place, windows)
    to_right = [(i, (i + 1) % ring) for i in range(ring)]
    to_left = [((i + 1) % ring, i) for i in range(ring)]
    upward = [(i, i + 1) for i in range(walls - 1)]
    downward = [(i + 1, i) for i in range(walls - 1)]
    if sides == 1:
        wall_terms = [lax.ppermute(faces[2], "analysis", upward + downward)]
    else:
        wall_terms = [
            lax.ppermute(faces[2], "analysis", upward),
            lax.ppermute(faces[3], "analysis", downward),
        ]
    from_left = lax.ppermute(faces[0], "solver", to_right)
    from_right = lax.ppermute(faces[1], "solver", to_left)

    inner = pl.pallas_call(
        inner_kernel,
        out_shape=shape(windows.shape, f32),
        in_specs=[WHOLE],
        out_specs=WHOLE,
        scratch_shapes=[pltpu.VMEM((fields, planes, layers, cells), f32)],
        compiler_params=params(16),
        cost_estimate=cost(30_000_000, 8 * windows.size),
        name="inner",
    )(windows)

    gram = pl.pallas_call(
        gram_kernel,
        grid=(fields,),
        out_shape=shape((modes, modes), f32),
        in_specs=[basis_spec],
        out_specs=pl.BlockSpec((modes, modes), lambda i: (0, 0)),
        scratch_shapes=[pltpu.VMEM((wide, wide), f32)],
        compiler_params=params(32),
        cost_estimate=cost(2 * wide * wide * cells * tiles, basis_bytes),
        name="gram",
    )(basis)
    gram = summed(gram, ("analysis", "solver"))
    inverse = pl.pallas_call(
        inverse_kernel,
        out_shape=shape((modes, modes), f32),
        in_specs=[WHOLE],
        out_specs=WHOLE,
        compiler_params=params(16),
        cost_estimate=cost(20_000_000, 8 * modes * modes),
        name="inverse",
    )(gram)

    half_shape = (count, fields, planes * layers // 2, cells)
    joined = pl.pallas_call(
        functools.partial(join_kernel, sides, paired),
        out_shape=[shape(windows.shape, f32)] + ([shape(half_shape, bf16)] * 2 if paired else []),
        in_specs=[SCALAR] + [WHOLE] * (3 + sides),
        out_specs=[WHOLE] * (3 if paired else 1),
        compiler_params=params(16),
        cost_estimate=cost(1_000_000, 16 * windows.size),
        name="join",
    )(place, inner, from_left, from_right, *wall_terms)
    next_windows = joined[0]

    sums_shape = shape((8, LANES), f32)
    sums_spec = pl.BlockSpec((8, LANES), lambda i: (0, 0))
    snaps_shape = shape((tiles, 2 * 8, cells), bf16)
    snaps_spec = pl.BlockSpec((per_step, 2 * 8, cells), lambda i: (i, 0, 0))
    scratch = [
        pltpu.VMEM((wide, 2 * 8), f32),
        pltpu.VMEM((2 * 8, 2 * 8), f32),
        pltpu.VMEM((LANES, LANES), f32),
    ]
    project_cost = cost(2 * wide * 16 * cells * tiles, basis_bytes)
    if paired:
        own, given = joined[1], joined[2]
        got = lax.ppermute(given, "analysis", [(0, 1), (1, 0)])
        half_spec = pl.BlockSpec(
            (count, 1, planes * layers // 2, cells), lambda i: (0, i, 0, 0)
        )
        sums, snaps = pl.pallas_call(
            functools.partial(project_kernel, True),
            grid=(fields,),
            out_shape=[sums_shape, snaps_shape],
            in_specs=[SCALAR, half_spec, half_spec, basis_spec],
            out_specs=[sums_spec, snaps_spec],
            scratch_shapes=scratch,
            compiler_params=params(32),
            cost_estimate=project_cost,
            name="project",
        )(place, own, got, basis)
    else:
        relaid = lax.all_to_all(
            next_windows.astype(bf16), "analysis", split_axis=2, concat_axis=3, tiled=True
        )
        snaps = relaid.reshape(count, tiles, 8, cells).transpose(1, 0, 2, 3)
        snaps = snaps.reshape(tiles, count * 8, cells)
        sums = pl.pallas_call(
            functools.partial(project_kernel, False),
            grid=(fields,),
            out_shape=sums_shape,
            in_specs=[SCALAR, snaps_spec, basis_spec],
            out_specs=sums_spec,
            scratch_shapes=scratch,
            compiler_params=params(32),
            cost_estimate=project_cost,
            name="project",
        )(place, snaps, basis)
    sums = summed(sums, ("analysis", "solver"))

    rows_total = ring * walls * tiles * 8 * cells
    new_modes, solved, factor = pl.pallas_call(
        functools.partial(finish_kernel, rows_total),
        grid=(fields,),
        out_shape=[
            shape((count, tiles, 8, cells), f32),
            shape((count, modes), f32),
            shape((count, count), f32),
        ],
        in_specs=[
            sums_spec,
            pl.BlockSpec((modes, modes), lambda i: (0, 0)),
            pl.BlockSpec((modes, modes), lambda i: (0, 0)),
            snaps_spec,
            basis_spec,
        ],
        out_specs=[
            pl.BlockSpec((count, per_step, 8, cells), lambda i: (0, i, 0, 0)),
            pl.BlockSpec((count, modes), lambda i: (0, 0)),
            pl.BlockSpec((count, count), lambda i: (0, 0)),
        ],
        scratch_shapes=[pltpu.VMEM((32, wide), bf16), pltpu.VMEM((3, 8, cells), f32)],
        compiler_params=params(32),
        cost_estimate=cost(2 * wide * 32 * cells * tiles, basis_bytes + 8 * windows.size),
        name="finish",
    )(sums, gram, inverse, snaps, basis)
    new_modes = new_modes.reshape(count, fields, pod_planes, pod_layers, cells)
    return next_windows, solved, new_modes, factor


def solution(mesh):
    in_specs = (
        P(None, None, "solver", "analysis", None),
        P(None, None, ("solver", "analysis"), None, None),
    )
    out_specs = (
        P(None, None, "solver", "analysis", None),
        P(),
        P(None, None, ("solver", "analysis"), None, None),
        P(),
    )
    return jax.shard_map(body, mesh=mesh, in_specs=in_specs, out_specs=out_specs, check_vma=False)
```

time: 544 us -> 75.5 us (0.14); the launches traced: 535 us -> 75.3 us
  matrix products: 326 us -> 0 us
  blocking collectives: 81.6 us -> 0 us
  loops' own time: 45.8 us -> 0 us
  other arithmetic: 34.2 us -> 0.04 us
  Pallas kernels: 0 us -> 27.4 us
  local copies, waits for them, and re-layouts: 19.7 us -> 5.08 us
  waiting for transfers between devices: 10.7 us -> 21.6 us
  starting transfers between devices: 13.9 us -> 20.4 us
    dot_general x580 -> x0, matrix products: 326 us -> none  [the longest x64 50.8 us: column_step(): jnp.dot(lower, row_now, precision=highest)]
    psum x2 -> x0, blocking collectives: 81.6 us -> none  [the longest x1 41.6 us: body(): lax.psum((basis_gram, projected), ('solver', 'analysis'))]
    another operation x3 -> x0, loops' own time: 45.8 us -> none  [the longest x1 45.5 us: cholesky_lower(): return lax.fori_loop(0, order, column_step, jnp.zeros_like(matrix))]
    pallas_call x0 -> x7, Pallas kernels: none -> 27.4 us  [the longest x1 7.88 us: body(): pl.pallas_call(gram_kernel, grid=(fields,), out_shape=shape((modes, modes...]
    add x192 -> x10, other arithmetic: 15.3 us -> 0.04 us  [summed(): value + lax.ppermute(value, axis, [(i, i ^ bit) for i in range(count)])]
    unnamed x8 -> x6, local copies, waits for them, and re-layouts: 16.5 us -> 5.08 us
    ppermute x4 -> x14, waiting for transfers between devices: 10.7 us -> 21.6 us  [the longest x10 14.1 us: summed(): lax.ppermute(value, axis, [(i, i ^ bit) for i in range(count)])]
    ppermute x4 -> x14, starting transfers between devices: 9.95 us -> 20.4 us  [the longest x10 11.3 us: summed(): lax.ppermute(value, axis, [(i, i ^ bit) for i in range(count)])]
  transfers between devices with their start and end apart: 5 -> 14, of which waited for: 3 -> 9; matrix products, arithmetic and copies ran while one was open for 9% -> 0% of each run, Pallas kernels for 0% -> 28%
where the time goes in v1:
time: 75.5 us; the launch traced here: 75.3 us
  Pallas kernels  27.4 us (36%)
  waiting for transfers between devices  21.6 us (29%)
  starting transfers between devices  20.4 us (27%)
  local copies, waits for them, and re-layouts  5.08 us (7%)
    ppermute x10, waiting for transfers between devices, summed(): lax.ppermute(value, axis, [(i, i ^ bit) for i in range(count)])  14.1 us
    ppermute x10, starting transfers between devices, summed(): lax.ppermute(value, axis, [(i, i ^ bit) for i in range(count)])  11.3 us
    pallas_call x1, Pallas kernels, body(): pl.pallas_call(gram_kernel, grid=(fields,), out_shape=shape((modes, modes...  7.88 us
    pallas_call x1, Pallas kernels, body(): pl.pallas_call(inverse_kernel, out_shape=shape((modes, modes), f32), in_s...  5.56 us
    ppermute x1, waiting for transfers between devices, body(): wall_terms = [lax.ppermute(faces[2], 'analysis', upward + downward)]  5.43 us
    unnamed x6, local copies, waits for them, and re-layouts  5.08 us
    pallas_call x1, Pallas kernels, body(): pl.pallas_call(functools.partial(finish_kernel, rows_total), grid=(fields...  4.9 us
    pallas_call x1, Pallas kernels, body(): pl.pallas_call(functools.partial(project_kernel, True), grid=(fields,), o...  4.56 us
  transfers between devices with their start and end apart: 14, of which 9 were waited for; matrix products, arithmetic and copies ran while one was open for 0% of the time, Pallas kernels for 28%

profile of v1, /device:TPU:0, one launch (start us, length us, event | category | flops | bytes accessed | tf_op | source)
XLA Modules:
  0.0 75.3 jit_solution(17816392075923959680)
XLA Ops:
  0.6 1.1 %copy-done.2 = f32[2,5,8,4,512]{4,3,2,1,0:T(4,128)S(1)} copy-done((f32[2,5,8,4,512]{4,3,2,1,0:T(4,128)S(1)}, f32[2,5,8,4,512]{4,3,2,1,0:T(4,128)}, u32[]{:S(2)}) %copy-start.2) | copy-done | bytes 655384
  2.5 3.0 %collective-permute-start.2 = (f32[2,5,8,4,512]{4,3,2,1,0:T(4,128)S(1)}, f32[2,5,8,4,512]{4,3,2,1,0:T(4,128)S(1)}, u32[]{:S(2)}, u32[]{:S(2)}) collective-permute-start(f32[2,5,8,4,512]{4,3,2,1,0:T(4,128)S(1)} %get-tuple-element.17), channel_id=1, source_target_pairs={{0,1},{1,0},{2,3},{3,2},{4,5},{5,4},{6,7},{7,6},{8,9},{9,8},{10,11... | collective-permute-start | bytes 1966088 | tf_op jit(solution)/shard_map/ppermute | solution.py:371
  5.5 4.4 %collective-permute-start.1 = (f32[2,5,4,4,512]{4,3,2,1,0:T(4,128)S(1)}, f32[2,5,4,4,512]{4,3,2,1,0:T(4,128)S(1)}, u32[]{:S(2)}, u32[]{:S(2)}) collective-permute-start(f32[2,5,4,4,512]{4,3,2,1,0:T(4,128)S(1)} %get-tuple-element.16), channel_id=1, source_target_pairs={{2,0},{4,2},{6,4},{8,6},{10,8},{12,10},{14,12},{16,14},{18,16},{20... | collective-permute-start | bytes 983048 | tf_op jit(solution)/shard_map/ppermute | solution.py:378
  10.0 2.8 %inner.1.part_ref = f32[2,5,8,4,512]{4,3,2,1,0:T(4,128)S(1)} custom-call(f32[2,5,8,4,512]{4,3,2,1,0:T(4,128)S(1)} %copy-done.2), custom_call_target="tpu_custom_call" | custom-call | flops 30000000 | bytes 1310720 | tf_op jit(solution)/shard_map/inner/pallas_call | solution.py:380
  12.7 2.1 %collective-permute-done.left_ref = f32[2,5,4,4,512]{4,3,2,1,0:T(4,128)S(1)} collective-permute-done((f32[2,5,4,4,512]{4,3,2,1,0:T(4,128)S(1)}, f32[2,5,4,4,512]{4,3,2,1,0:T(4,128)S(1)}, u32[]{:S(2)}, u32[]{:S(2)}) %collective-permute-start) | collective-permute-done | bytes 327712 | tf_op jit(solution)/shard_map/ppermute | solution.py:377
  14.8 5.4 %collective-permute-done.2.rest_0_ = f32[2,5,8,4,512]{4,3,2,1,0:T(4,128)S(1)} collective-permute-done((f32[2,5,8,4,512]{4,3,2,1,0:T(4,128)S(1)}, f32[2,5,8,4,512]{4,3,2,1,0:T(4,128)S(1)}, u32[]{:S(2)}, u32[]{:S(2)}) %collective-permute-start.2) | collective-permute-done | bytes 655392 | tf_op jit(solution)/shard_map/ppermute | solution.py:371
  20.3 1.0 %join.1 = (f32[2,5,8,4,512]{4,3,2,1,0:T(4,128)}, bf16[2,5,16,512]{3,2,1,0:T(8,128)(2,1)S(1)}, bf16[2,5,16,512]{3,2,1,0:T(8,128)(2,1)S(1)}) custom-call(s32[1]{0:T(128)} %bitcast.where_ref, f32[2,5,8,4,512]{4,3,2,1,0:T(4,128)S(1)} %inner.1.part_ref, f32[2,5,4,4,512]{4,3,2,1,0:T(4,128)S(1)} %collective-permute-done.left_ref, ...), custom_call_target="tpu_custom_call" | custom-call | flops 1000000 | bytes 2621440 | tf_op jit(solution)/shard_map/join/pallas_call | solution.py:414
  21.2 1.7 %collective-permute-start.3 = (bf16[2,5,16,512]{3,2,1,0:T(8,128)(2,1)S(1)}, bf16[2,5,16,512]{3,2,1,0:T(8,128)(2,1)S(1)}, u32[]{:S(2)}, u32[]{:S(2)}) collective-permute-start(bf16[2,5,16,512]{3,2,1,0:T(8,128)(2,1)S(1)} %get-tuple-element.20), channel_id=1, source_target_pairs={{0,1},{1,0},{2,3},{3,2},{4,5},{5,4},{6,7},{7,6},{8,9},{9,8},{10,11... | collective-permute-start | bytes 491528 | tf_op jit(solution)/shard_map/ppermute | solution.py:437
  23.0 4.0 %copy-done = bf16[64,5,4,8,512]{4,3,2,1,0:T(8,128)(2,1)S(1)} copy-done((bf16[64,5,4,8,512]{4,3,2,1,0:T(8,128)(2,1)S(1)}, bf16[64,5,4,8,512]{4,3,2,1,0:T(8,128)(2,1)}, u32[]{:S(2)}) %copy-start) | copy-done | bytes 10485784
  27.0 7.9 %gram.1 = f32[64,64]{1,0:T(8,128)S(1)} custom-call(bf16[64,20,8,512]{3,2,1,0:T(8,128)(2,1)S(1)} %bitcast.3), custom_call_target="tpu_custom_call" | custom-call | flops 5368709120 | bytes 10485760 | tf_op jit(solution)/shard_map/gram/pallas_call | solution.py:391
  35.2 3.6 %collective-permute-done.9 = f32[64,64]{1,0:T(8,128)S(1)} collective-permute-done((f32[64,64]{1,0:T(8,128)S(1)}, f32[64,64]{1,0:T(8,128)S(1)}, u32[]{:S(2)}, u32[]{:S(2)}) %collective-permute-start.9) | collective-permute-done | bytes 16416 | tf_op jit(solution)/shard_map/ppermute | solution.py:334
  38.9 1.2 %collective-permute-done.10 = f32[64,64]{1,0:T(8,128)S(1)} collective-permute-done((f32[64,64]{1,0:T(8,128)S(1)}, f32[64,64]{1,0:T(8,128)S(1)}, u32[]{:S(2)}, u32[]{:S(2)}) %collective-permute-start.10) | collective-permute-done | bytes 16416 | tf_op jit(solution)/shard_map/ppermute | solution.py:334
  40.1 1.5 %collective-permute-start.11 = (f32[64,64]{1,0:T(8,128)S(1)}, f32[64,64]{1,0:T(8,128)S(1)}, u32[]{:S(2)}, u32[]{:S(2)}) collective-permute-start(f32[64,64]{1,0:T(8,128)S(1)} %add.36), channel_id=1, source_target_pairs={{0,4},{2,6},{4,0},{6,2},{8,12},{10,14},{12,8},{14,10},{16,20},{18,... | collective-permute-start | bytes 49160 | tf_op jit(solution)/shard_map/ppermute | solution.py:334
  41.6 2.4 %collective-permute-done.11 = f32[64,64]{1,0:T(8,128)S(1)} collective-permute-done((f32[64,64]{1,0:T(8,128)S(1)}, f32[64,64]{1,0:T(8,128)S(1)}, u32[]{:S(2)}, u32[]{:S(2)}) %collective-permute-start.11) | collective-permute-done | bytes 16416 | tf_op jit(solution)/shard_map/ppermute | solution.py:334
  44.0 1.6 %collective-permute-start.12 = (f32[64,64]{1,0:T(8,128)S(1)}, f32[64,64]{1,0:T(8,128)S(1)}, u32[]{:S(2)}, u32[]{:S(2)}) collective-permute-start(f32[64,64]{1,0:T(8,128)S(1)} %add.37), channel_id=1, source_target_pairs={{0,8},{2,10},{4,12},{6,14},{8,0},{10,2},{12,4},{14,6},{16,24},{18,... | collective-permute-start | bytes 49160 | tf_op jit(solution)/shard_map/ppermute | solution.py:334
  45.6 4.6 %project.1 = (f32[8,128]{1,0:T(8,128)S(1)}, bf16[20,16,512]{2,1,0:T(8,128)(2,1)S(1)}) custom-call(s32[1]{0:T(128)} %bitcast.where_ref, bf16[2,5,16,512]{3,2,1,0:T(8,128)(2,1)S(1)} %get-tuple-element.19.rest_0_, bf16[2,5,16,512]{3,2,1,0:T(8,128)(2,1)S(1)} %collective-permute-done.3.rest_1_, bf16[64,20,8,512]{3,2,1,0:T(8,128)(2,1)S(1)} %bitcast.4), custom_call_target="tpu_custom_call" | custom-call | flops 167772160 | bytes 10485760 | tf_op jit(solution)/shard_map/project/pallas_call | solution.py:441
  50.7 2.6 %collective-permute-start.13 = (f32[64,64]{1,0:T(8,128)S(1)}, f32[64,64]{1,0:T(8,128)S(1)}, u32[]{:S(2)}, u32[]{:S(2)}) collective-permute-start(f32[64,64]{1,0:T(8,128)S(1)} %add.38), channel_id=1, source_target_pairs={{0,16},{2,18},{4,20},{6,22},{8,24},{10,26},{12,28},{14,30},{16,0},... | collective-permute-start | bytes 49160 | tf_op jit(solution)/shard_map/ppermute | solution.py:334
  53.8 1.2 %collective-permute-done.5 = f32[8,128]{1,0:T(8,128)S(1)} collective-permute-done((f32[8,128]{1,0:T(8,128)S(1)}, f32[8,128]{1,0:T(8,128)S(1)}, u32[]{:S(2)}, u32[]{:S(2)}) %collective-permute-start.5) | collective-permute-done | bytes 4128 | tf_op jit(solution)/shard_map/ppermute | solution.py:334
  55.0 1.5 %collective-permute-start.6 = (f32[8,128]{1,0:T(8,128)S(1)}, f32[8,128]{1,0:T(8,128)S(1)}, u32[]{:S(2)}, u32[]{:S(2)}) collective-permute-start(f32[8,128]{1,0:T(8,128)S(1)} %add.31), channel_id=1, source_target_pairs={{0,4},{2,6},{4,0},{6,2},{8,12},{10,14},{12,8},{14,10},{16,20},{18,... | collective-permute-start | bytes 12296 | tf_op jit(solution)/shard_map/ppermute | solution.py:334
  56.5 2.1 %collective-permute-done.6 = f32[8,128]{1,0:T(8,128)S(1)} collective-permute-done((f32[8,128]{1,0:T(8,128)S(1)}, f32[8,128]{1,0:T(8,128)S(1)}, u32[]{:S(2)}, u32[]{:S(2)}) %collective-permute-start.6) | collective-permute-done | bytes 4128 | tf_op jit(solution)/shard_map/ppermute | solution.py:334
  59.0 3.2 %collective-permute-done.7 = f32[8,128]{1,0:T(8,128)S(1)} collective-permute-done((f32[8,128]{1,0:T(8,128)S(1)}, f32[8,128]{1,0:T(8,128)S(1)}, u32[]{:S(2)}, u32[]{:S(2)}) %collective-permute-start.7) | collective-permute-done | bytes 4128 | tf_op jit(solution)/shard_map/ppermute | solution.py:334
  62.2 2.6 %collective-permute-start.8 = (f32[8,128]{1,0:T(8,128)S(1)}, f32[8,128]{1,0:T(8,128)S(1)}, u32[]{:S(2)}, u32[]{:S(2)}) collective-permute-start(f32[8,128]{1,0:T(8,128)S(1)} %add.33), channel_id=1, source_target_pairs={{0,16},{2,18},{4,20},{6,22},{8,24},{10,26},{12,28},{14,30},{16,0},... | collective-permute-start | bytes 12296 | tf_op jit(solution)/shard_map/ppermute | solution.py:334
  64.8 5.6 %inverse.1.inverse_ref = f32[64,64]{1,0:T(8,128)S(1)} custom-call(f32[64,64]{1,0:T(8,128)S(1)} %add.39.gram_ref), custom_call_target="tpu_custom_call" | custom-call | flops 20000000 | bytes 32768 | tf_op jit(solution)/shard_map/inverse/pallas_call | solution.py:403
  70.4 4.9 %finish.1 = (f32[2,20,8,512]{3,2,1,0:T(8,128)}, f32[2,64]{1,0:T(2,128)}, f32[2,2]{1,0:T(2,128)}) custom-call(f32[8,128]{1,0:T(8,128)S(1)} %add.34.sums_ref, f32[64,64]{1,0:T(8,128)S(1)} %add.39.gram_ref, f32[64,64]{1,0:T(8,128)S(1)} %inverse.1.inverse_ref, bf16[20,16,512]{2,1,0:T(8,128)(2,1)S(1)} %get-tuple-element.22.snaps_ref, ...), custom_call_target="tpu_custom_call" | custom-call | flops 335544320 | bytes 11796480 | tf_op jit(solution)/shard_map/finish/pallas_call | solution.py:472
  (27 shorter events, 2.7 us)
Async XLA Ops:
  0.6 1.1 %copy-start.2 = (f32[2,5,8,4,512]{4,3,2,1,0:T(4,128)S(1)}, f32[2,5,8,4,512]{4,3,2,1,0:T(4,128)}, u32[]{:S(2)}) copy-start(f32[2,5,8,4,512]{4,3,2,1,0:T(4,128)} %windows_ref.3) | copy-start | bytes 1966084
  2.5 17.7 %collective-permute-start.2 = (f32[2,5,8,4,512]{4,3,2,1,0:T(4,128)S(1)}, f32[2,5,8,4,512]{4,3,2,1,0:T(4,128)S(1)}, u32[]{:S(2)}, u32[]{:S(2)}) collective-permute-start(f32[2,5,8,4,512]{4,3,2,1,0:T(4,128)S(1)} %get-tuple-element.17), channel_id=1, source_target_pairs={{0,1},{1,0},{2,3},{3,2},{4,5},{5,4},{6,7},{7,6},{8,9},{9,8},{10,11... | collective-permute-start | bytes 1966088 | tf_op jit(solution)/shard_map/ppermute | solution.py:371
  5.5 9.3 %collective-permute-start = (f32[2,5,4,4,512]{4,3,2,1,0:T(4,128)S(1)}, f32[2,5,4,4,512]{4,3,2,1,0:T(4,128)S(1)}, u32[]{:S(2)}, u32[]{:S(2)}) collective-permute-start(f32[2,5,4,4,512]{4,3,2,1,0:T(4,128)S(1)} %get-tuple-element.15), channel_id=1, source_target_pairs={{0,2},{2,4},{4,6},{6,8},{8,10},{10,12},{12,14},{14,16},{16,18},{18... | collective-permute-start | bytes 983048 | tf_op jit(solution)/shard_map/ppermute | solution.py:377
  5.5 9.3 %collective-permute-start.1 = (f32[2,5,4,4,512]{4,3,2,1,0:T(4,128)S(1)}, f32[2,5,4,4,512]{4,3,2,1,0:T(4,128)S(1)}, u32[]{:S(2)}, u32[]{:S(2)}) collective-permute-start(f32[2,5,4,4,512]{4,3,2,1,0:T(4,128)S(1)} %get-tuple-element.16), channel_id=1, source_target_pairs={{2,0},{4,2},{6,4},{8,6},{10,8},{12,10},{14,12},{16,14},{18,16},{20... | collective-permute-start | bytes 983048 | tf_op jit(solution)/shard_map/ppermute | solution.py:378
  21.2 24.3 %collective-permute-start.3 = (bf16[2,5,16,512]{3,2,1,0:T(8,128)(2,1)S(1)}, bf16[2,5,16,512]{3,2,1,0:T(8,128)(2,1)S(1)}, u32[]{:S(2)}, u32[]{:S(2)}) collective-permute-start(bf16[2,5,16,512]{3,2,1,0:T(8,128)(2,1)S(1)} %get-tuple-element.20), channel_id=1, source_target_pairs={{0,1},{1,0},{2,3},{3,2},{4,5},{5,4},{6,7},{7,6},{8,9},{9,8},{10,11... | collective-permute-start | bytes 491528 | tf_op jit(solution)/shard_map/ppermute | solution.py:437
  23.0 4.0 %copy-start = (bf16[64,5,4,8,512]{4,3,2,1,0:T(8,128)(2,1)S(1)}, bf16[64,5,4,8,512]{4,3,2,1,0:T(8,128)(2,1)}, u32[]{:S(2)}) copy-start(bf16[64,5,4,8,512]{4,3,2,1,0:T(8,128)(2,1)} %param.3) | copy-start | bytes 31457284
  27.0 18.6 %copy-start.1 = (bf16[64,5,4,8,512]{4,3,2,1,0:T(8,128)(2,1)S(1)}, bf16[64,5,4,8,512]{4,3,2,1,0:T(8,128)(2,1)}, u32[]{:S(2)}) copy-start(bf16[64,5,4,8,512]{4,3,2,1,0:T(8,128)(2,1)} %param.3) | copy-start | bytes 31457284
  34.9 4.0 %collective-permute-start.9 = (f32[64,64]{1,0:T(8,128)S(1)}, f32[64,64]{1,0:T(8,128)S(1)}, u32[]{:S(2)}, u32[]{:S(2)}) collective-permute-start(f32[64,64]{1,0:T(8,128)S(1)} %gram.1), channel_id=1, source_target_pairs={{0,1},{1,0},{2,3},{3,2},{4,5},{5,4},{6,7},{7,6},{8,9},{9,8},{10,11... | collective-permute-start | bytes 49160 | tf_op jit(solution)/shard_map/ppermute | solution.py:334
  38.8 1.2 %collective-permute-start.10 = (f32[64,64]{1,0:T(8,128)S(1)}, f32[64,64]{1,0:T(8,128)S(1)}, u32[]{:S(2)}, u32[]{:S(2)}) collective-permute-start(f32[64,64]{1,0:T(8,128)S(1)} %add.35), channel_id=1, source_target_pairs={{0,2},{2,0},{4,6},{6,4},{8,10},{10,8},{12,14},{14,12},{16,18},{18,... | collective-permute-start | bytes 49160 | tf_op jit(solution)/shard_map/ppermute | solution.py:334
  40.1 3.9 %collective-permute-start.11 = (f32[64,64]{1,0:T(8,128)S(1)}, f32[64,64]{1,0:T(8,128)S(1)}, u32[]{:S(2)}, u32[]{:S(2)}) collective-permute-start(f32[64,64]{1,0:T(8,128)S(1)} %add.36), channel_id=1, source_target_pairs={{0,4},{2,6},{4,0},{6,2},{8,12},{10,14},{12,8},{14,10},{16,20},{18,... | collective-permute-start | bytes 49160 | tf_op jit(solution)/shard_map/ppermute | solution.py:334
  44.0 6.7 %collective-permute-start.12 = (f32[64,64]{1,0:T(8,128)S(1)}, f32[64,64]{1,0:T(8,128)S(1)}, u32[]{:S(2)}, u32[]{:S(2)}) collective-permute-start(f32[64,64]{1,0:T(8,128)S(1)} %add.37), channel_id=1, source_target_pairs={{0,8},{2,10},{4,12},{6,14},{8,0},{10,2},{12,4},{14,6},{16,24},{18,... | collective-permute-start | bytes 49160 | tf_op jit(solution)/shard_map/ppermute | solution.py:334
  50.1 3.7 %collective-permute-start.4 = (f32[8,128]{1,0:T(8,128)S(1)}, f32[8,128]{1,0:T(8,128)S(1)}, u32[]{:S(2)}, u32[]{:S(2)}) collective-permute-start(f32[8,128]{1,0:T(8,128)S(1)} %get-tuple-element.21), channel_id=1, source_target_pairs={{0,1},{1,0},{2,3},{3,2},{4,5},{5,4},{6,7},{7,6},{8,9},{9,8},{10,11... | collective-permute-start | bytes 12296 | tf_op jit(solution)/shard_map/ppermute | solution.py:334
  50.7 14.1 %collective-permute-start.13 = (f32[64,64]{1,0:T(8,128)S(1)}, f32[64,64]{1,0:T(8,128)S(1)}, u32[]{:S(2)}, u32[]{:S(2)}) collective-permute-start(f32[64,64]{1,0:T(8,128)S(1)} %add.38), channel_id=1, source_target_pairs={{0,16},{2,18},{4,20},{6,22},{8,24},{10,26},{12,28},{14,30},{16,0},... | collective-permute-start | bytes 49160 | tf_op jit(solution)/shard_map/ppermute | solution.py:334
  53.8 1.2 %collective-permute-start.5 = (f32[8,128]{1,0:T(8,128)S(1)}, f32[8,128]{1,0:T(8,128)S(1)}, u32[]{:S(2)}, u32[]{:S(2)}) collective-permute-start(f32[8,128]{1,0:T(8,128)S(1)} %add.30), channel_id=1, source_target_pairs={{0,2},{2,0},{4,6},{6,4},{8,10},{10,8},{12,14},{14,12},{16,18},{18,... | collective-permute-start | bytes 12296 | tf_op jit(solution)/shard_map/ppermute | solution.py:334
  55.0 3.6 %collective-permute-start.6 = (f32[8,128]{1,0:T(8,128)S(1)}, f32[8,128]{1,0:T(8,128)S(1)}, u32[]{:S(2)}, u32[]{:S(2)}) collective-permute-start(f32[8,128]{1,0:T(8,128)S(1)} %add.31), channel_id=1, source_target_pairs={{0,4},{2,6},{4,0},{6,2},{8,12},{10,14},{12,8},{14,10},{16,20},{18,... | collective-permute-start | bytes 12296 | tf_op jit(solution)/shard_map/ppermute | solution.py:334
  58.6 3.6 %collective-permute-start.7 = (f32[8,128]{1,0:T(8,128)S(1)}, f32[8,128]{1,0:T(8,128)S(1)}, u32[]{:S(2)}, u32[]{:S(2)}) collective-permute-start(f32[8,128]{1,0:T(8,128)S(1)} %add.32), channel_id=1, source_target_pairs={{0,8},{2,10},{4,12},{6,14},{8,0},{10,2},{12,4},{14,6},{16,24},{18,... | collective-permute-start | bytes 12296 | tf_op jit(solution)/shard_map/ppermute | solution.py:334
  62.2 8.2 %collective-permute-start.8 = (f32[8,128]{1,0:T(8,128)S(1)}, f32[8,128]{1,0:T(8,128)S(1)}, u32[]{:S(2)}, u32[]{:S(2)}) collective-permute-start(f32[8,128]{1,0:T(8,128)S(1)} %add.33), channel_id=1, source_target_pairs={{0,16},{2,18},{4,20},{6,22},{8,24},{10,26},{12,28},{14,30},{16,0},... | collective-permute-start | bytes 12296 | tf_op jit(solution)/shard_map/ppermute | solution.py:334

commit v2 on v1

v2 whole, which is shorter than its diff:
```python
import functools

import jax
import jax.numpy as jnp
from jax import lax
from jax.experimental import pallas as pl
from jax.experimental.pallas import tpu as pltpu
from jax.sharding import PartitionSpec as P

PRESSURE_FACTOR = 1.4 - 1.0
SECTION_STEP = 0.25
CENTRAL_WEIGHTS = (0.8, -0.2, 4.0 / 105.0, -1.0 / 280.0)
REACH = 4
LANES = 128
HIGHEST = lax.Precision.HIGHEST
NT = (((1,), (1,)), ((), ()))


def weight(k):
    if k == 0 or abs(k) > REACH:
        return 0.0
    value = -SECTION_STEP * CENTRAL_WEIGHTS[abs(k) - 1]
    return value if k > 0 else -value


def row_weights(shape, values):
    rows = lax.broadcasted_iota(jnp.int32, shape, len(shape) - 2)
    made = jnp.full(shape, values[0], jnp.float32)
    for i, value in enumerate(values[1:], start=1):
        made = jnp.where(rows == i, jnp.float32(value), made)
    return made


def primitives(windows_ref, w, x):
    density, mx, my, mz, energy = (windows_ref[w, f, x] for f in range(5))
    inverse = 1.0 / density
    ux, uy, uz = mx * inverse, my * inverse, mz * inverse
    pressure = PRESSURE_FACTOR * (energy - 0.5 * (mx * ux + my * uy + mz * uz))
    return (mx, my, mz), (ux, uy, uz), pressure, energy + pressure


def flux(parts, direction):
    moments, speeds, pressure, enthalpy = parts
    speed = speeds[direction]
    made = [moments[direction]]
    for axis in range(3):
        term = moments[axis] * speed
        made.append(term + pressure if axis == direction else term)
    made.append(enthalpy * speed)
    return made


def face_kernel(two_sided, where_ref, source_ref, windows_ref, left_ref, right_ref, *rest):
    windows, _, planes, layers, cells = windows_ref.shape
    wall_refs, scratch, sems = rest[:-2], rest[-2], rest[-1]
    copies = [
        pltpu.make_async_copy(source_ref.at[w], windows_ref.at[w], sems.at[w])
        for w in range(windows)
    ]
    for copy in copies:
        copy.start()
    tile = (layers, cells)
    up = [
        row_weights(tile, [weight(j - layers - i) for i in range(layers)]) for j in range(layers)
    ]
    down = [
        row_weights(tile, [weight(layers + j - i) for i in range(layers)]) for j in range(layers)
    ]
    if two_sided:
        tables = (up, down)
    else:
        first = where_ref[0] == 0
        tables = ([jnp.where(first, u, d) for u, d in zip(up, down)],)
    for w in range(windows):
        copies[w].wait()
        for x in range(planes):
            parts = primitives(windows_ref, w, x)
            for f, value in enumerate(flux(parts, 0)):
                scratch[f, x] = value
            for f, value in enumerate(flux(parts, 1)):
                for ref, table in zip(wall_refs, tables):
                    total = None
                    for j in range(layers):
                        term = table[j] * value[j : j + 1, :]
                        total = term if total is None else total + term
                    ref[w, f, x] = total
        for f in range(5):
            for i in range(REACH):
                total = None
                for j in range(planes):
                    c = weight(j - planes - i)
                    if c:
                        term = c * scratch[f, j]
                        total = term if total is None else total + term
                left_ref[w, f, i] = total
                total = None
                for j in range(planes):
                    c = weight(j + REACH - i)
                    if c:
                        term = c * scratch[f, j]
                        total = term if total is None else total + term
                right_ref[w, f, i] = total


def inner_part(windows_ref, part_ref, scratch):
    windows, _, planes, layers, cells = windows_ref.shape
    tile = (layers, cells)
    wall = [
        row_weights(tile, [weight(j - i) for i in range(layers)]) for j in range(layers)
    ]
    for w in range(windows):
        for x in range(planes):
            parts = primitives(windows_ref, w, x)
            for f, value in enumerate(flux(parts, 0)):
                scratch[f, x] = value
            flux_y, flux_z = flux(parts, 1), flux(parts, 2)
            for f in range(5):
                total = windows_ref[w, f, x]
                for j in range(layers):
                    total = total + wall[j] * flux_y[f][j : j + 1, :]
                for k in range(1, REACH + 1):
                    total = total + weight(k) * (
                        pltpu.roll(flux_z[f], cells - k, 1) - pltpu.roll(flux_z[f], k, 1)
                    )
                part_ref[w, f, x] = total
        for f in range(5):
            for x in range(planes):
                total = part_ref[w, f, x]
                for k in range(-REACH, REACH + 1):
                    if k and 0 <= x + k < planes:
                        total = total + weight(k) * scratch[f, x + k]
                part_ref[w, f, x] = total


def inner_gram_kernel(windows_ref, basis_ref, part_ref, gram_ref, kept_ref, scratch, total, sems):
    chunks = sems.shape[0]
    modes, tiles, _, cells = kept_ref.shape
    per_chunk = tiles // chunks
    wide = modes * 8
    half = wide // 2
    copies = []
    for c in range(chunks):
        span = pl.ds(c * per_chunk, per_chunk)
        copies.append(
            pltpu.make_async_copy(basis_ref.at[:, span], kept_ref.at[:, span], sems.at[c])
        )
        copies[c].start()
    inner_part(windows_ref, part_ref, scratch)
    for c in range(chunks):
        copies[c].wait()
        right = jnp.zeros((wide, half), jnp.float32) if c == 0 else total[:, half:]
        left = jnp.zeros((half, half), jnp.float32) if c == 0 else total[0:half, 0:half]
        for t in range(c * per_chunk, (c + 1) * per_chunk):
            rows = modes_of(kept_ref, t)
            right = right + lax.dot_general(
                rows, rows[half:], NT, preferred_element_type=jnp.float32
            )
            left = left + lax.dot_general(
                rows[:half], rows[:half], NT, preferred_element_type=jnp.float32
            )
        total[:, half:] = right
        total[0:half, 0:half] = left
    total[half:, 0:half] = total[0:half, half:].T
    kept = jnp.where(same_layer(total.shape), total[...], 0.0)
    rows = jnp.sum(kept.reshape(modes, 8, wide), axis=1)
    lanes = gram_ref.shape[1]
    picks = (
        lax.broadcasted_iota(jnp.int32, (wide, lanes), 0) // 8
        == lax.broadcasted_iota(jnp.int32, (wide, lanes), 1)
    ).astype(jnp.float32)
    gram_ref[...] = jnp.dot(rows, picks, precision=HIGHEST, preferred_element_type=jnp.float32)


def join_kernel(walls, paired, where_ref, part_ref, left_ref, right_ref, *rest):
    wall_refs, next_ref = rest[:walls], rest[walls]
    windows, _, planes, layers, cells = part_ref.shape
    for w in range(windows):
        for f in range(5):
            for x in range(planes):
                total = part_ref[w, f, x]
                for ref in wall_refs:
                    total = total + ref[w, f, x]
                if x < REACH:
                    total = total + left_ref[w, f, x]
                if x >= planes - REACH:
                    total = total + right_ref[w, f, x - planes + REACH]
                next_ref[w, f, x] = total
            if paired:
                half = planes // 2
                low = jnp.concatenate([next_ref[w, f, x] for x in range(half)], axis=0)
                high = jnp.concatenate([next_ref[w, f, x] for x in range(half, planes)], axis=0)
                first = where_ref[0] == 0
                rest[walls + 1][w, f] = jnp.where(first, low, high).astype(jnp.bfloat16)
                rest[walls + 2][w, f] = jnp.where(first, high, low).astype(jnp.bfloat16)


def same_layer(shape):
    rows = lax.broadcasted_iota(jnp.int32, shape, 0)
    columns = lax.broadcasted_iota(jnp.int32, shape, 1)
    return lax.rem(rows, 8) == lax.rem(columns, 8)


def modes_of(basis_ref, t):
    modes, _, layers, cells = basis_ref.shape
    return basis_ref[:, t].reshape(modes * layers, cells)


def project_kernel(paired, where_ref, *rest):
    if paired:
        own_ref, got_ref, basis_ref, sums_ref, snaps_ref, square = rest
        first = where_ref[0] == 0
        for w in range(own_ref.shape[0]):
            for f in range(own_ref.shape[1]):
                own = own_ref[w, f].astype(jnp.float32)
                got = got_ref[w, f].astype(jnp.float32)
                low = jnp.where(first, own, got)
                high = jnp.where(first, got, own)
                for t in range(4):
                    snaps_ref[4 * f + t, pl.ds(8 * w, 8)] = jnp.concatenate(
                        [low[4 * t : 4 * t + 4], high[4 * t : 4 * t + 4]], axis=0
                    ).astype(jnp.bfloat16)
    else:
        snaps_ref, basis_ref, sums_ref, square = rest
    modes, tiles = basis_ref.shape[:2]
    columns = snaps_ref.shape[1]
    total = jnp.zeros((modes * 8, columns), jnp.float32)
    small = jnp.zeros((columns, columns), jnp.float32)
    for t in range(tiles):
        snaps = snaps_ref[t]
        total = total + lax.dot_general(
            modes_of(basis_ref, t), snaps, NT, preferred_element_type=jnp.float32
        )
        small = small + lax.dot_general(snaps, snaps, NT, preferred_element_type=jnp.float32)
    kept = jnp.where(same_layer(total.shape), total, 0.0)
    square[...] = jnp.zeros_like(square)
    square[0:modes, 0:columns] = jnp.sum(kept.reshape(modes, 8, columns), axis=1)
    kept = jnp.where(same_layer(small.shape), small, 0.0)
    square[modes : modes + 1, 0:columns] = jnp.sum(kept[0:8], axis=0, keepdims=True)
    square[modes + 1 : modes + 2, 0:columns] = jnp.sum(kept[8:16], axis=0, keepdims=True)
    turned = square[...].T
    sums = jnp.concatenate(
        [
            jnp.sum(turned[0:8], axis=0, keepdims=True),
            jnp.sum(turned[8:16], axis=0, keepdims=True),
        ],
        axis=0,
    )
    for device in range(sums_ref.shape[0]):
        sums_ref[device] = sums


def inverse_kernel(gram_ref, inverse_ref):
    modes = gram_ref.shape[0]
    shape = (modes, 2 * modes)
    rows = lax.broadcasted_iota(jnp.int32, shape, 0)
    columns = lax.broadcasted_iota(jnp.int32, shape, 1)
    eye = (rows[:, :modes] == columns[:, :modes]).astype(jnp.float32)
    whole = jnp.concatenate([gram_ref[:, :modes], eye], axis=1)
    for k in range(modes):
        row = whole[k : k + 1, :] / whole[k : k + 1, k : k + 1]
        whole = jnp.where(rows == k, row, whole - whole[:, k : k + 1] * row)
    inverse_ref[...] = whole[:, modes:]


def finish_kernel(
    rows_total, sums_ref, gram_ref, inverse_ref, snaps_ref, basis_ref,
    modes_ref, solved_ref, factor_ref, made, sems,
):
    modes, tiles, _, cells = basis_ref.shape
    wide = modes * 8
    exact = functools.partial(jnp.dot, precision=HIGHEST, preferred_element_type=jnp.float32)
    sums = jnp.sum(sums_ref[...], axis=0)
    sums = jnp.concatenate([sums, jnp.zeros((6, sums.shape[1]), jnp.float32)], axis=0)
    projected = sums[:, 0:modes]
    gram, inverse = gram_ref[:, :modes], inverse_ref[...]
    solved = exact(projected, inverse)
    solved = solved + exact(projected - exact(solved, gram), inverse)
    left = projected - exact(solved, gram)

    def inner(p, i, q, j):
        return jnp.sum(p[i : i + 1] * q[j : j + 1], axis=1, keepdims=True)

    def entry(i, j):
        square = sums[i : i + 1, modes + j : modes + j + 1]
        return square - inner(projected, i, solved, j) - inner(solved, i, left, j)

    first = jnp.sqrt(entry(0, 0))
    below = entry(1, 0) / first
    second = jnp.sqrt(entry(1, 1) - below * below)
    scaling = jnp.sqrt(jnp.float32(rows_total))
    w00 = scaling / first
    w11 = scaling / second
    w01 = -(below / first) * w11
    solved_ref[...] = solved[0:2]
    factor_ref[0:1, 0:1] = first / scaling
    factor_ref[0:1, 1:2] = below / scaling
    factor_ref[1:2, 0:1] = jnp.zeros_like(first)
    factor_ref[1:2, 1:2] = second / scaling
    spread = (
        lax.broadcasted_iota(jnp.int32, (modes, wide), 1) // 8
        == lax.broadcasted_iota(jnp.int32, (modes, wide), 0)
    ).astype(jnp.float32)
    scaled = jnp.concatenate(
        [solved[0:1] * w00, solved[1:2] * w11 + solved[0:1] * w01, solved[2:8]], axis=0
    )
    lines = exact(scaled, spread)
    full = jnp.concatenate(
        [jnp.broadcast_to(lines[0:1], (8, wide)), jnp.broadcast_to(lines[1:2], (8, wide))],
        axis=0,
    )
    full = jnp.where(same_layer(full.shape), full, 0.0)
    upper = full.astype(jnp.bfloat16)
    fit = jnp.concatenate([upper, (full - upper.astype(jnp.float32)).astype(jnp.bfloat16)], axis=0)

    chunks = sems.shape[0]
    per_chunk = tiles // chunks
    copies = []
    for c in range(chunks):
        for t in range(c * per_chunk, (c + 1) * per_chunk):
            fitted = jnp.dot(fit, modes_of(basis_ref, t), preferred_element_type=jnp.float32)
            fitted = fitted[0:16] + fitted[16:32]
            snaps = snaps_ref[t].astype(jnp.float32)
            made[0, t] = snaps[0:8] * w00 - fitted[0:8]
            made[1, t] = snaps[8:16] * w11 + snaps[0:8] * w01 - fitted[8:16]
        span = pl.ds(c * per_chunk, per_chunk)
        copies.append(
            pltpu.make_async_copy(made.at[:, span], modes_ref.at[:, span], sems.at[c])
        )
        copies[c].start()
    for copy in copies:
        copy.wait()


def params(mib):
    return pltpu.CompilerParams(vmem_limit_bytes=mib * 1024 * 1024)


def cost(flops, moved):
    return pl.CostEstimate(flops=flops, bytes_accessed=moved, transcendentals=0)


WHOLE = pl.BlockSpec(memory_space=pltpu.VMEM)
FAR = pl.BlockSpec(memory_space=pltpu.HBM)
SCALAR = pl.BlockSpec(memory_space=pltpu.SMEM)


BOTH = ("solver", "analysis")


def everywhere(value):
    count = lax.axis_size("solver") * lax.axis_size("analysis")
    return lax.all_to_all(
        jnp.broadcast_to(value[None], (count,) + value.shape), BOTH, 0, 0, tiled=True
    )


def summed_rows(value):
    count = lax.axis_size("solver") * lax.axis_size("analysis")
    rows, columns = value.shape
    if rows % count:
        return jnp.sum(everywhere(value), axis=0)
    shares = lax.all_to_all(
        value.reshape(count, rows // count, columns), BOTH, 0, 0, tiled=True
    )
    return everywhere(jnp.sum(shares, axis=0)).reshape(rows, columns)


def body(windows, pod_basis):
    f32, bf16 = jnp.float32, jnp.bfloat16
    shape = jax.ShapeDtypeStruct
    count, fields, planes, layers, cells = windows.shape
    ring, walls = lax.axis_size("solver"), lax.axis_size("analysis")
    paired = walls == 2 and planes == 8 and layers == 4
    place = lax.axis_index("analysis").astype(jnp.int32).reshape(1)
    modes, _, pod_planes, pod_layers, _ = pod_basis.shape
    tiles = fields * pod_planes * (pod_layers // 8)
    basis = pod_basis.reshape(modes, tiles, 8, cells)
    wide = modes * 8
    basis_bytes = basis.size * 2

    sides = 1 if walls == 2 else 2
    kept, *faces = pl.pallas_call(
        functools.partial(face_kernel, sides == 2),
        out_shape=[shape(windows.shape, f32)]
        + [shape((count, fields, REACH, layers, cells), f32)] * 2
        + [shape(windows.shape, f32)] * sides,
        in_specs=[SCALAR, FAR],
        out_specs=[WHOLE] * (3 + sides),
        scratch_shapes=[
            pltpu.VMEM((fields, planes, layers, cells), f32),
            pltpu.SemaphoreType.DMA((count,)),
        ],
        compiler_params=params(16),
        cost_estimate=cost(10_000_000, 10 * windows.size),
        name="faces",
    )(place, windows)
    to_right = [(i, (i + 1) % ring) for i in range(ring)]
    to_left = [((i + 1) % ring, i) for i in range(ring)]
    upward = [(i, i + 1) for i in range(walls - 1)]
    downward = [(i + 1, i) for i in range(walls - 1)]
    if sides == 1:
        wall_terms = [lax.ppermute(faces[2], "analysis", upward + downward)]
    else:
        wall_terms = [
            lax.ppermute(faces[2], "analysis", upward),
            lax.ppermute(faces[3], "analysis", downward),
        ]
    from_left = lax.ppermute(faces[0], "solver", to_right)
    from_right = lax.ppermute(faces[1], "solver", to_left)

    inner, gram, basis = pl.pallas_call(
        inner_gram_kernel,
        out_shape=[shape(windows.shape, f32), shape((modes, LANES), f32), shape(basis.shape, bf16)],
        in_specs=[WHOLE, FAR],
        out_specs=[WHOLE] * 3,
        scratch_shapes=[
            pltpu.VMEM((fields, planes, layers, cells), f32),
            pltpu.VMEM((wide, wide), f32),
            pltpu.SemaphoreType.DMA((fields,)),
        ],
        compiler_params=params(40),
        cost_estimate=cost(2 * wide * wide * cells * tiles, 2 * basis_bytes),
        name="inner_gram",
    )(kept, basis)
    gram = summed_rows(gram)
    inverse = pl.pallas_call(
        inverse_kernel,
        out_shape=shape((modes, modes), f32),
        in_specs=[WHOLE],
        out_specs=WHOLE,
        compiler_params=params(16),
        cost_estimate=cost(20_000_000, 8 * modes * modes),
        name="inverse",
    )(gram)

    half_shape = (count, fields, planes * layers // 2, cells)
    joined = pl.pallas_call(
        functools.partial(join_kernel, sides, paired),
        out_shape=[shape(windows.shape, f32)] + ([shape(half_shape, bf16)] * 2 if paired else []),
        in_specs=[SCALAR] + [WHOLE] * (3 + sides),
        out_specs=[WHOLE] * (3 if paired else 1),
        compiler_params=params(16),
        cost_estimate=cost(1_000_000, 16 * windows.size),
        name="join",
    )(place, inner, from_left, from_right, *wall_terms)
    next_windows = joined[0]

    sums_shape = shape((ring * walls, 2, LANES), f32)
    snaps_shape = shape((tiles, 2 * 8, cells), bf16)
    scratch = [pltpu.VMEM((LANES, LANES), f32)]
    project_cost = cost(2 * wide * 16 * cells * tiles, basis_bytes)
    if paired:
        own, given = joined[1], joined[2]
        got = lax.ppermute(given, "analysis", [(0, 1), (1, 0)])
        sums, snaps = pl.pallas_call(
            functools.partial(project_kernel, True),
            out_shape=[sums_shape, snaps_shape],
            in_specs=[SCALAR] + [WHOLE] * 3,
            out_specs=[WHOLE] * 2,
            scratch_shapes=scratch,
            compiler_params=params(16),
            cost_estimate=project_cost,
            name="project",
        )(place, own, got, basis)
    else:
        relaid = lax.all_to_all(
            next_windows.astype(bf16), "analysis", split_axis=2, concat_axis=3, tiled=True
        )
        snaps = relaid.reshape(count, tiles, 8, cells).transpose(1, 0, 2, 3)
        snaps = snaps.reshape(tiles, count * 8, cells)
        sums = pl.pallas_call(
            functools.partial(project_kernel, False),
            out_shape=sums_shape,
            in_specs=[SCALAR] + [WHOLE] * 2,
            out_specs=WHOLE,
            scratch_shapes=scratch,
            compiler_params=params(16),
            cost_estimate=project_cost,
            name="project",
        )(place, snaps, basis)
    sums = lax.all_to_all(sums, BOTH, 0, 0, tiled=True)

    rows_total = ring * walls * tiles * 8 * cells
    new_modes, solved, factor = pl.pallas_call(
        functools.partial(finish_kernel, rows_total),
        out_shape=[
            shape((count, tiles, 8, cells), f32),
            shape((count, modes), f32),
            shape((count, count), f32),
        ],
        in_specs=[WHOLE] * 5,
        out_specs=[FAR, WHOLE, WHOLE],
        scratch_shapes=[
            pltpu.VMEM((count, tiles, 8, cells), f32),
            pltpu.SemaphoreType.DMA((fields,)),
        ],
        compiler_params=params(16),
        cost_estimate=cost(2 * wide * 32 * cells * tiles, basis_bytes + 8 * windows.size),
        name="finish",
    )(sums, gram, inverse, snaps, basis)
    new_modes = new_modes.reshape(count, fields, pod_planes, pod_layers, cells)
    return next_windows, solved, new_modes, factor


def solution(mesh):
    in_specs = (
        P(None, None, "solver", "analysis", None),
        P(None, None, ("solver", "analysis"), None, None),
    )
    out_specs = (
        P(None, None, "solver", "analysis", None),
        P(),
        P(None, None, ("solver", "analysis"), None, None),
        P(),
    )
    return jax.shard_map(body, mesh=mesh, in_specs=in_specs, out_specs=out_specs, check_vma=False)
```

time: 75.5 us -> 69.8 us (0.925)
  waiting for transfers between devices: 21.6 us -> 1.62 us
  blocking collectives: 0 us -> 10.8 us
  local copies, waits for them, and re-layouts: 5.08 us -> 13.6 us
  starting transfers between devices: 20.4 us -> 16 us
  Pallas kernels: 27.4 us -> 26.5 us
    ppermute x10 -> x0, waiting for transfers between devices: 14.1 us -> none  [summed(): lax.ppermute(value, axis, [(i, i ^ bit) for i in range(count)])]
    ppermute x10 -> x0, starting transfers between devices: 11.3 us -> none  [summed(): lax.ppermute(value, axis, [(i, i ^ bit) for i in range(count)])]
    all_to_all x0 -> x1, blocking collectives: none -> 10.8 us  [summed_rows(): lax.all_to_all(value.reshape(count, rows // count, columns), BOTH, 0, 0,...]
    all_to_all x0 -> x2, starting transfers between devices: none -> 8.51 us  [the longest x1 6.01 us: body(): sums = lax.all_to_all(sums, BOTH, 0, 0, tiled=True)]
    unnamed x6 -> x8, local copies, waits for them, and re-layouts: 5.08 us -> 13 us
    ppermute x1, waiting for transfers between devices: 5.43 us -> 0.01 us  [body(): wall_terms = [lax.ppermute(faces[2], 'analysis', upward + downward)]]
    ppermute x1, waiting for transfers between devices: 2.09 us -> 0.01 us  [body(): from_left = lax.ppermute(faces[0], 'solver', to_right)]
    ppermute x1, starting transfers between devices: 1.74 us -> 0.07 us  [body(): got = lax.ppermute(given, 'analysis', [(0, 1), (1, 0)])]
  transfers between devices with their start and end apart: 14 -> 6, of which waited for: 9 -> 1; matrix products, arithmetic and copies ran while one was open for 0% -> 1% of each run, Pallas kernels for 28% -> 29%
where the time goes in v2:
time: 69.8 us; the launch traced here: 69.5 us
  Pallas kernels  26.5 us (38%)
  starting transfers between devices  16 us (23%)
  local copies, waits for them, and re-layouts  13.6 us (19%)
  blocking collectives  10.8 us (15%)
  waiting for transfers between devices  1.62 us (2%)
  between operations  0.87 us (1%)
    unnamed x8, local copies, waits for them, and re-layouts  13 us
    pallas_call x1, Pallas kernels, body(): pl.pallas_call(inner_gram_kernel, out_shape=[shape(windows.shape, f32), s...  11.1 us
    all_to_all x1, blocking collectives, summed_rows(): lax.all_to_all(value.reshape(count, rows // count, columns), BOTH, 0, 0,...  10.8 us
    all_to_all x1, starting transfers between devices, body(): sums = lax.all_to_all(sums, BOTH, 0, 0, tiled=True)  6.01 us
    pallas_call x1, Pallas kernels, body(): pl.pallas_call(inverse_kernel, out_shape=shape((modes, modes), f32), in_s...  5.56 us
    ppermute x1, starting transfers between devices, body(): from_right = lax.ppermute(faces[1], 'solver', to_left)  4.44 us
    pallas_call x1, Pallas kernels, body(): pl.pallas_call(functools.partial(finish_kernel, rows_total), out_shape=[s...  4.2 us
    pallas_call x1, Pallas kernels, body(): pl.pallas_call(functools.partial(project_kernel, True), out_shape=[sums_s...  3.71 us
  transfers between devices with their start and end apart: 6, of which 1 were waited for; matrix products, arithmetic and copies ran while one was open for 1% of the time, Pallas kernels for 29%

profile of v2, /device:TPU:0, one launch (start us, length us, event | category | flops | bytes accessed | tf_op | source)
XLA Modules:
  0.0 69.5 jit_solution(9958113492899929097)
XLA Ops:
  0.6 1.1 %copy-done.3 = f32[2,5,8,4,512]{4,3,2,1,0:T(4,128)S(1)} copy-done((f32[2,5,8,4,512]{4,3,2,1,0:T(4,128)S(1)}, f32[2,5,8,4,512]{4,3,2,1,0:T(4,128)}, u32[]{:S(2)}) %copy-start.3) | copy-done | bytes 655384
  1.7 1.0 %faces.1 = (f32[2,5,8,4,512]{4,3,2,1,0:T(4,128)S(1)}, f32[2,5,4,4,512]{4,3,2,1,0:T(4,128)S(1)}, f32[2,5,4,4,512]{4,3,2,1,0:T(4,128)S(1)}, f32[2,5,8,4,512]{4,3,2,1,0:T(4,128)S(1)}) custom-call(s32[1]{0:T(128)} %bitcast.where_ref, f32[2,5,8,4,512]{4,3,2,1,0:T(4,128)S(1)} %copy-done.3), custom_call_target="tpu_custom_call" | custom-call | flops 10000000 | bytes 1638400 | tf_op jit(solution)/shard_map/faces/pallas_call | solution.py:382
  2.8 3.0 %collective-permute-start.2 = (f32[2,5,8,4,512]{4,3,2,1,0:T(4,128)S(1)}, f32[2,5,8,4,512]{4,3,2,1,0:T(4,128)S(1)}, u32[]{:S(2)}, u32[]{:S(2)}) collective-permute-start(f32[2,5,8,4,512]{4,3,2,1,0:T(4,128)S(1)} %get-tuple-element.23), channel_id=1, source_target_pairs={{0,1},{1,0},{2,3},{3,2},{4,5},{5,4},{6,7},{7,6},{8,9},{9,8},{10,11... | collective-permute-start | bytes 1966088 | tf_op jit(solution)/shard_map/ppermute | solution.py:402
  5.8 0.0 collective-permute-start
  5.8 4.4 %collective-permute-start.1 = (f32[2,5,4,4,512]{4,3,2,1,0:T(4,128)S(1)}, f32[2,5,4,4,512]{4,3,2,1,0:T(4,128)S(1)}, u32[]{:S(2)}, u32[]{:S(2)}) collective-permute-start(f32[2,5,4,4,512]{4,3,2,1,0:T(4,128)S(1)} %get-tuple-element.22), channel_id=1, source_target_pairs={{2,0},{4,2},{6,4},{8,6},{10,8},{12,10},{14,12},{16,14},{18,16},{20... | collective-permute-start | bytes 983048 | tf_op jit(solution)/shard_map/ppermute | solution.py:409
  10.2 11.1 %inner_gram.1 = (f32[2,5,8,4,512]{4,3,2,1,0:T(4,128)S(1)}, f32[64,128]{1,0:T(8,128)S(1)}, bf16[64,20,8,512]{3,2,1,0:T(8,128)(2,1)S(1)}) custom-call(f32[2,5,8,4,512]{4,3,2,1,0:T(4,128)S(1)} %get-tuple-element.19.windows_ref, bf16[64,20,8,512]{3,2,1,0:T(8,128)(2,1)} %bitcast.8), custom_call_target="tpu_custom_call" | custom-call | flops 5368709120 | bytes 20971520 | tf_op jit(solution)/shard_map/inner_gram/pallas_call | solution.py:411
  21.3 4.0 %copy-done = bf16[64,20,8,512]{3,2,1,0:T(8,128)(2,1)} copy-done((bf16[64,20,8,512]{3,2,1,0:T(8,128)(2,1)}, bf16[64,20,8,512]{3,2,1,0:T(8,128)(2,1)S(1)}, u32[]{:S(2)}) %copy-start) | copy-done | bytes 10485784
  25.3 0.0 collective-permute-done.left_ref
  25.3 0.0 collective-permute-done.1.right_ref
  25.3 0.0 collective-permute-done.2.rest_0_
  25.3 1.0 %join.1 = (f32[2,5,8,4,512]{4,3,2,1,0:T(4,128)}, bf16[2,5,16,512]{3,2,1,0:T(8,128)(2,1)S(1)}, bf16[2,5,16,512]{3,2,1,0:T(8,128)(2,1)S(1)}) custom-call(s32[1]{0:T(128)} %bitcast.where_ref, f32[2,5,8,4,512]{4,3,2,1,0:T(4,128)S(1)} %get-tuple-element.20.part_ref, f32[2,5,4,4,512]{4,3,2,1,0:T(4,128)S(1)} %collective-permute-done.left_ref, ...), custom_call_target="tpu_custom_call" | custom-call | flops 1000000 | bytes 2621440 | tf_op jit(solution)/shard_map/join/pallas_call | solution.py:437
  26.3 0.1 collective-permute-start.3
  26.3 10.8 %all_to_all.15 = f32[32,2,128]{2,1,0:T(2,128)S(1)} all-to-all(f32[32,2,128]{2,1,0:T(2,128)S(1)} %bitcast.7), channel_id=1, replica_groups=mesh['solver'=16,'analysis'=2] {'solver','analysis'}, dimensions={0} | all-to-all | bytes 65536 | tf_op jit(solution)/shard_map/all_to_all | solution.py:362
  37.2 0.6 broadcast_in_dim.2
  37.8 2.5 %all-to-all-start.2 = ((f32[32,2,128]{2,1,0:T(2,128)}), f32[32,2,128]{2,1,0:T(2,128)S(1)}, u32[]{:S(2)}, u32[]{:S(2)}) async-start(f32[32,2,128]{2,1,0:T(2,128)} %broadcast_in_dim.2), calls=%async_computation.2 | async-start | bytes 65536 | tf_op jit(solution)/shard_map/all_to_all | solution.py:352
  40.3 0.0 collective-permute-done.3.rest_1_
  40.3 4.0 %copy-done.1 = bf16[64,20,8,512]{3,2,1,0:T(8,128)(2,1)S(1)} copy-done((bf16[64,20,8,512]{3,2,1,0:T(8,128)(2,1)S(1)}, bf16[64,20,8,512]{3,2,1,0:T(8,128)(2,1)}, u32[]{:S(2)}) %copy-start.1) | copy-done | bytes 10485784
  44.3 3.7 %project.1 = (f32[32,2,128]{2,1,0:T(2,128)}, bf16[20,16,512]{2,1,0:T(8,128)(2,1)S(1)}) custom-call(s32[1]{0:T(128)} %bitcast.where_ref, bf16[2,5,16,512]{3,2,1,0:T(8,128)(2,1)S(1)} %get-tuple-element.25.rest_0_, bf16[2,5,16,512]{3,2,1,0:T(8,128)(2,1)S(1)} %collective-permute-done.3.rest_1_, bf16[64,20,8,512]{3,2,1,0:T(8,128)(2,1)S(1)} %copy-done.1), custom_call_target="tpu_custom_call" | custom-call | flops 167772160 | bytes 10485760 | tf_op jit(solution)/shard_map/project/pallas_call | solution.py:455
  48.0 0.0 all-to-all-done.2
  48.0 6.0 %all-to-all-start = ((f32[32,2,128]{2,1,0:T(2,128)}), f32[32,2,128]{2,1,0:T(2,128)S(1)}, u32[]{:S(2)}, u32[]{:S(2)}) async-start(f32[32,2,128]{2,1,0:T(2,128)} %get-tuple-element.28), calls=%async_computation | async-start | bytes 65536 | tf_op jit(solution)/shard_map/all_to_all | solution.py:481
  54.0 5.6 %inverse.1.inverse_ref = f32[64,64]{1,0:T(8,128)S(1)} custom-call(f32[64,128]{1,0:T(8,128)S(1)} %bitcast.5), custom_call_target="tpu_custom_call" | custom-call | flops 20000000 | bytes 32768 | tf_op jit(solution)/shard_map/inverse/pallas_call | solution.py:426
  59.6 1.6 %all-to-all-done.sums_ref = f32[32,2,128]{2,1,0:T(2,128)S(1)} async-done(((f32[32,2,128]{2,1,0:T(2,128)}), f32[32,2,128]{2,1,0:T(2,128)S(1)}, u32[]{:S(2)}, u32[]{:S(2)}) %all-to-all-start) | async-done | bytes 32800 | tf_op jit(solution)/shard_map/all_to_all | solution.py:481
  61.2 4.0 %copy-done.2 = bf16[64,20,8,512]{3,2,1,0:T(8,128)(2,1)S(1)} copy-done((bf16[64,20,8,512]{3,2,1,0:T(8,128)(2,1)S(1)}, bf16[64,20,8,512]{3,2,1,0:T(8,128)(2,1)}, u32[]{:S(2)}) %copy-start.2) | copy-done | bytes 10485784
  65.2 4.2 %finish.1 = (f32[2,20,8,512]{3,2,1,0:T(8,128)}, f32[2,64]{1,0:T(2,128)}, f32[2,2]{1,0:T(2,128)}) custom-call(f32[32,2,128]{2,1,0:T(2,128)S(1)} %all-to-all-done.sums_ref, f32[64,128]{1,0:T(8,128)S(1)} %bitcast.6, f32[64,64]{1,0:T(8,128)S(1)} %inverse.1.inverse_ref, bf16[20,16,512]{2,1,0:T(8,128)(2,1)S(1)} %get-tuple-element.30.snaps_ref, ...), custom_call_target="tpu_custom_call" | custom-call | flops 335544320 | bytes 11796480 | tf_op jit(solution)/shard_map/finish/pallas_call | solution.py:484
  (5 shorter events, 0.1 us)
Async XLA Ops:
  0.6 1.1 %copy-start.3 = (f32[2,5,8,4,512]{4,3,2,1,0:T(4,128)S(1)}, f32[2,5,8,4,512]{4,3,2,1,0:T(4,128)}, u32[]{:S(2)}) copy-start(f32[2,5,8,4,512]{4,3,2,1,0:T(4,128)} %source_ref.1) | copy-start | bytes 1966084
  2.8 22.5 %collective-permute-start.2 = (f32[2,5,8,4,512]{4,3,2,1,0:T(4,128)S(1)}, f32[2,5,8,4,512]{4,3,2,1,0:T(4,128)S(1)}, u32[]{:S(2)}, u32[]{:S(2)}) collective-permute-start(f32[2,5,8,4,512]{4,3,2,1,0:T(4,128)S(1)} %get-tuple-element.23), channel_id=1, source_target_pairs={{0,1},{1,0},{2,3},{3,2},{4,5},{5,4},{6,7},{7,6},{8,9},{9,8},{10,11... | collective-permute-start | bytes 1966088 | tf_op jit(solution)/shard_map/ppermute | solution.py:402
  5.8 19.5 %collective-permute-start = (f32[2,5,4,4,512]{4,3,2,1,0:T(4,128)S(1)}, f32[2,5,4,4,512]{4,3,2,1,0:T(4,128)S(1)}, u32[]{:S(2)}, u32[]{:S(2)}) collective-permute-start(f32[2,5,4,4,512]{4,3,2,1,0:T(4,128)S(1)} %get-tuple-element.21), channel_id=1, source_target_pairs={{0,2},{2,4},{4,6},{6,8},{8,10},{10,12},{12,14},{14,16},{16,18},{18... | collective-permute-start | bytes 983048 | tf_op jit(solution)/shard_map/ppermute | solution.py:408
  5.8 19.5 %collective-permute-start.1 = (f32[2,5,4,4,512]{4,3,2,1,0:T(4,128)S(1)}, f32[2,5,4,4,512]{4,3,2,1,0:T(4,128)S(1)}, u32[]{:S(2)}, u32[]{:S(2)}) collective-permute-start(f32[2,5,4,4,512]{4,3,2,1,0:T(4,128)S(1)} %get-tuple-element.22), channel_id=1, source_target_pairs={{2,0},{4,2},{6,4},{8,6},{10,8},{12,10},{14,12},{16,14},{18,16},{20... | collective-permute-start | bytes 983048 | tf_op jit(solution)/shard_map/ppermute | solution.py:409
  21.3 4.0 %copy-start = (bf16[64,20,8,512]{3,2,1,0:T(8,128)(2,1)}, bf16[64,20,8,512]{3,2,1,0:T(8,128)(2,1)S(1)}, u32[]{:S(2)}) copy-start(bf16[64,20,8,512]{3,2,1,0:T(8,128)(2,1)S(1)} %get-tuple-element.27.rest_2_.basis_ref) | copy-start | bytes 31457284
  26.3 14.0 %collective-permute-start.3 = (bf16[2,5,16,512]{3,2,1,0:T(8,128)(2,1)S(1)}, bf16[2,5,16,512]{3,2,1,0:T(8,128)(2,1)S(1)}, u32[]{:S(2)}, u32[]{:S(2)}) collective-permute-start(bf16[2,5,16,512]{3,2,1,0:T(8,128)(2,1)S(1)} %get-tuple-element.26), channel_id=1, source_target_pairs={{0,1},{1,0},{2,3},{3,2},{4,5},{5,4},{6,7},{7,6},{8,9},{9,8},{10,11... | collective-permute-start | bytes 491528 | tf_op jit(solution)/shard_map/ppermute | solution.py:454
  37.8 10.2 %all-to-all-start.2 = ((f32[32,2,128]{2,1,0:T(2,128)}), f32[32,2,128]{2,1,0:T(2,128)S(1)}, u32[]{:S(2)}, u32[]{:S(2)}) async-start(f32[32,2,128]{2,1,0:T(2,128)} %broadcast_in_dim.2), calls=%async_computation.2 | async-start | bytes 65536 | tf_op jit(solution)/shard_map/all_to_all | solution.py:352
  40.3 4.0 %copy-start.1 = (bf16[64,20,8,512]{3,2,1,0:T(8,128)(2,1)S(1)}, bf16[64,20,8,512]{3,2,1,0:T(8,128)(2,1)}, u32[]{:S(2)}) copy-start(bf16[64,20,8,512]{3,2,1,0:T(8,128)(2,1)} %copy-done) | copy-start | bytes 31457284
  48.0 13.2 %all-to-all-start = ((f32[32,2,128]{2,1,0:T(2,128)}), f32[32,2,128]{2,1,0:T(2,128)S(1)}, u32[]{:S(2)}, u32[]{:S(2)}) async-start(f32[32,2,128]{2,1,0:T(2,128)} %get-tuple-element.28), calls=%async_computation | async-start | bytes 65536 | tf_op jit(solution)/shard_map/all_to_all | solution.py:481
  61.2 4.0 %copy-start.2 = (bf16[64,20,8,512]{3,2,1,0:T(8,128)(2,1)S(1)}, bf16[64,20,8,512]{3,2,1,0:T(8,128)(2,1)}, u32[]{:S(2)}) copy-start(bf16[64,20,8,512]{3,2,1,0:T(8,128)(2,1)} %copy-done) | copy-start | bytes 31457284

commit v3 on v2

--- a/solution.py
+++ b/solution.py
@@ -146,23 +146,27 @@
         )
         copies[c].start()
     inner_part(windows_ref, part_ref, scratch)
+    right = jnp.zeros((wide, half), jnp.float32)
+    left = jnp.zeros((half, half), jnp.float32)
     for c in range(chunks):
         copies[c].wait()
-        right = jnp.zeros((wide, half), jnp.float32) if c == 0 else total[:, half:]
-        left = jnp.zeros((half, half), jnp.float32) if c == 0 else total[0:half, 0:half]
-        for t in range(c * per_chunk, (c + 1) * per_chunk):
-            rows = modes_of(kept_ref, t)
-            right = right + lax.dot_general(
-                rows, rows[half:], NT, preferred_element_type=jnp.float32
-            )
-            left = left + lax.dot_general(
-                rows[:half], rows[:half], NT, preferred_element_type=jnp.float32
-            )
-        total[:, half:] = right
-        total[0:half, 0:half] = left
-    total[half:, 0:half] = total[0:half, half:].T
-    kept = jnp.where(same_layer(total.shape), total[...], 0.0)
-    rows = jnp.sum(kept.reshape(modes, 8, wide), axis=1)
+        rows = jnp.concatenate(
+            [modes_of(kept_ref, t) for t in range(c * per_chunk, (c + 1) * per_chunk)], axis=1
+        )
+        right = right + lax.dot_general(
+            rows, rows[half:], NT, preferred_element_type=jnp.float32
+        )
+        left = left + lax.dot_general(
+            rows[:half], rows[:half], NT, preferred_element_type=jnp.float32
+        )
+    tiles_left = half // LANES
+    turned = right[0:half].T
+    for tile in range(tiles_left):
+        span = slice(tile * LANES, (tile + 1) * LANES)
+        total[tile, 0:half] = left[:, span]
+        total[tile, half:] = turned[:, span]
+        total[tiles_left + tile] = right[:, span]
+    rows = folded(total, modes)
     lanes = gram_ref.shape[1]
     picks = (
         lax.broadcasted_iota(jnp.int32, (wide, lanes), 0) // 8
@@ -200,6 +204,17 @@
     return lax.rem(rows, 8) == lax.rem(columns, 8)
 
 
+def folded(total, modes):
+    kept = lax.rem(lax.broadcasted_iota(jnp.int32, (modes, LANES), 1), 8)
+    made = []
+    for tile in range(total.shape[0]):
+        rows = jnp.zeros((modes, LANES), jnp.float32)
+        for y in range(8):
+            rows = jnp.where(kept == y, total[tile, pl.ds(y, modes, 8), :], rows)
+        made.append(rows)
+    return made[0] if len(made) == 1 else jnp.concatenate(made, axis=1)
+
+
 def modes_of(basis_ref, t):
     modes, _, layers, cells = basis_ref.shape
     return basis_ref[:, t].reshape(modes * layers, cells)
@@ -207,7 +222,7 @@
 
 def project_kernel(paired, where_ref, *rest):
     if paired:
-        own_ref, got_ref, basis_ref, sums_ref, snaps_ref, square = rest
+        own_ref, got_ref, basis_ref, sums_ref, snaps_ref, square, wide_sums = rest
         first = where_ref[0] == 0
         for w in range(own_ref.shape[0]):
             for f in range(own_ref.shape[1]):
@@ -220,7 +235,7 @@
                         [low[4 * t : 4 * t + 4], high[4 * t : 4 * t + 4]], axis=0
                     ).astype(jnp.bfloat16)
     else:
-        snaps_ref, basis_ref, sums_ref, square = rest
+        snaps_ref, basis_ref, sums_ref, square, wide_sums = rest
     modes, tiles = basis_ref.shape[:2]
     columns = snaps_ref.shape[1]
     total = jnp.zeros((modes * 8, columns), jnp.float32)
@@ -231,13 +246,14 @@
             modes_of(basis_ref, t), snaps, NT, preferred_element_type=jnp.float32
         )
         small = small + lax.dot_general(snaps, snaps, NT, preferred_element_type=jnp.float32)
-    kept = jnp.where(same_layer(total.shape), total, 0.0)
+    wide_sums[0, :, 0:columns] = total
     square[...] = jnp.zeros_like(square)
-    square[0:modes, 0:columns] = jnp.sum(kept.reshape(modes, 8, columns), axis=1)
+    square[0:modes, :] = folded(wide_sums, modes)
     kept = jnp.where(same_layer(small.shape), small, 0.0)
     square[modes : modes + 1, 0:columns] = jnp.sum(kept[0:8], axis=0, keepdims=True)
     square[modes + 1 : modes + 2, 0:columns] = jnp.sum(kept[8:16], axis=0, keepdims=True)
-    turned = square[...].T
+    lanes = lax.broadcasted_iota(jnp.int32, square.shape, 1)
+    turned = jnp.where(lanes < columns, square[...], 0.0).T
     sums = jnp.concatenate(
         [
             jnp.sum(turned[0:8], axis=0, keepdims=True),
@@ -245,21 +261,35 @@
         ],
         axis=0,
     )
-    for device in range(sums_ref.shape[0]):
-        sums_ref[device] = sums
-
-
-def inverse_kernel(gram_ref, inverse_ref):
+    sums_ref[...] = jnp.concatenate([sums, jnp.zeros((6, sums.shape[1]), jnp.float32)], axis=0)
+
+
+def eliminate(whole, start, stop):
+    rows = lax.broadcasted_iota(jnp.int32, whole.shape, 0)
+    for k in range(start, stop, 2):
+        first, second = whole[k : k + 1, :], whole[k + 1 : k + 2, :]
+        a, b = first[:, k : k + 1], first[:, k + 1 : k + 2]
+        c, d = second[:, k : k + 1], second[:, k + 1 : k + 2]
+        inverse = 1.0 / (a * d - b * c)
+        upper = (d * first - b * second) * inverse
+        lower = (a * second - c * first) * inverse
+        rest = whole - whole[:, k : k + 1] * upper - whole[:, k + 1 : k + 2] * lower
+        whole = jnp.where(rows == k, upper, jnp.where(rows == k + 1, lower, rest))
+    return whole
+
+
+def half_inverse_kernel(gram_ref, half_ref):
     modes = gram_ref.shape[0]
-    shape = (modes, 2 * modes)
-    rows = lax.broadcasted_iota(jnp.int32, shape, 0)
-    columns = lax.broadcasted_iota(jnp.int32, shape, 1)
-    eye = (rows[:, :modes] == columns[:, :modes]).astype(jnp.float32)
+    rows = lax.broadcasted_iota(jnp.int32, (modes, modes), 0)
+    columns = lax.broadcasted_iota(jnp.int32, (modes, modes), 1)
+    eye = (rows == columns).astype(jnp.float32)
     whole = jnp.concatenate([gram_ref[:, :modes], eye], axis=1)
-    for k in range(modes):
-        row = whole[k : k + 1, :] / whole[k : k + 1, k : k + 1]
-        whole = jnp.where(rows == k, row, whole - whole[:, k : k + 1] * row)
-    inverse_ref[...] = whole[:, modes:]
+    half_ref[...] = eliminate(whole, 0, modes // 2)
+
+
+def inverse_kernel(half_ref, inverse_ref):
+    modes = half_ref.shape[0]
+    inverse_ref[...] = eliminate(half_ref[...], modes // 2, modes)[:, modes:]
 
 
 def finish_kernel(
@@ -269,8 +299,7 @@
     modes, tiles, _, cells = basis_ref.shape
     wide = modes * 8
     exact = functools.partial(jnp.dot, precision=HIGHEST, preferred_element_type=jnp.float32)
-    sums = jnp.sum(sums_ref[...], axis=0)
-    sums = jnp.concatenate([sums, jnp.zeros((6, sums.shape[1]), jnp.float32)], axis=0)
+    sums = sums_ref[...]
     projected = sums[:, 0:modes]
     gram, inverse = gram_ref[:, :modes], inverse_ref[...]
     solved = exact(projected, inverse)
@@ -340,29 +369,22 @@
 
 
 WHOLE = pl.BlockSpec(memory_space=pltpu.VMEM)
+AXES = ("analysis", "solver")
 FAR = pl.BlockSpec(memory_space=pltpu.HBM)
 SCALAR = pl.BlockSpec(memory_space=pltpu.SMEM)
 
 
-BOTH = ("solver", "analysis")
-
-
-def everywhere(value):
-    count = lax.axis_size("solver") * lax.axis_size("analysis")
-    return lax.all_to_all(
-        jnp.broadcast_to(value[None], (count,) + value.shape), BOTH, 0, 0, tiled=True
-    )
-
-
-def summed_rows(value):
-    count = lax.axis_size("solver") * lax.axis_size("analysis")
-    rows, columns = value.shape
-    if rows % count:
-        return jnp.sum(everywhere(value), axis=0)
-    shares = lax.all_to_all(
-        value.reshape(count, rows // count, columns), BOTH, 0, 0, tiled=True
-    )
-    return everywhere(jnp.sum(shares, axis=0)).reshape(rows, columns)
+def summed(value, axes):
+    for axis in axes:
+        count = lax.axis_size(axis)
+        if count & (count - 1):
+            value = lax.psum(value, axis)
+            continue
+        bit = 1
+        while bit < count:
+            value = value + lax.ppermute(value, axis, [(i, i ^ bit) for i in range(count)])
+            bit *= 2
+    return value
 
 
 def body(windows, pod_basis):
@@ -415,23 +437,32 @@
         out_specs=[WHOLE] * 3,
         scratch_shapes=[
             pltpu.VMEM((fields, planes, layers, cells), f32),
-            pltpu.VMEM((wide, wide), f32),
+            pltpu.VMEM((wide // LANES, wide, LANES), f32),
             pltpu.SemaphoreType.DMA((fields,)),
         ],
         compiler_params=params(40),
         cost_estimate=cost(2 * wide * wide * cells * tiles, 2 * basis_bytes),
         name="inner_gram",
     )(kept, basis)
-    gram = summed_rows(gram)
+    gram = summed(gram, AXES)
+    half_inverse = pl.pallas_call(
+        half_inverse_kernel,
+        out_shape=shape((modes, 2 * modes), f32),
+        in_specs=[WHOLE],
+        out_specs=WHOLE,
+        compiler_params=params(16),
+        cost_estimate=cost(10_000_000, 8 * modes * modes),
+        name="half_inverse",
+    )(gram)
     inverse = pl.pallas_call(
         inverse_kernel,
         out_shape=shape((modes, modes), f32),
         in_specs=[WHOLE],
         out_specs=WHOLE,
         compiler_params=params(16),
-        cost_estimate=cost(20_000_000, 8 * modes * modes),
+        cost_estimate=cost(10_000_000, 8 * modes * modes),
         name="inverse",
-    )(gram)
+    )(half_inverse)
 
     half_shape = (count, fields, planes * layers // 2, cells)
     joined = pl.pallas_call(
@@ -445,9 +476,9 @@
     )(place, inner, from_left, from_right, *wall_terms)
     next_windows = joined[0]
 
-    sums_shape = shape((ring * walls, 2, LANES), f32)
+    sums_shape = shape((8, LANES), f32)
     snaps_shape = shape((tiles, 2 * 8, cells), bf16)
-    scratch = [pltpu.VMEM((LANES, LANES), f32)]
+    scratch = [pltpu.VMEM((LANES, LANES), f32), pltpu.VMEM((1, wide, LANES), f32)]
     project_cost = cost(2 * wide * 16 * cells * tiles, basis_bytes)
     if paired:
         own, given = joined[1], joined[2]
@@ -478,7 +509,7 @@
             cost_estimate=project_cost,
             name="project",
         )(place, snaps, basis)
-    sums = lax.all_to_all(sums, BOTH, 0, 0, tiled=True)
+    sums = summed(sums, AXES)
 
     rows_total = ring * walls * tiles * 8 * cells
     new_modes, solved, factor = pl.pallas_call(

time: 69.8 us -> 67.1 us (0.961)
  waiting for transfers between devices: 1.62 us -> 18.5 us
  local copies, waits for them, and re-layouts: 13.6 us -> 1.08 us
  blocking collectives: 10.8 us -> 0 us
  starting transfers between devices: 16 us -> 18.6 us
  Pallas kernels: 26.5 us -> 28 us
    ppermute x0 -> x10, waiting for transfers between devices: none -> 18.5 us  [summed(): lax.ppermute(value, axis, [(i, i ^ bit) for i in range(count)])]
    unnamed x8 -> x2, local copies, waits for them, and re-layouts: 13 us -> 1.08 us
    all_to_all x1 -> x0, blocking collectives: 10.8 us -> none  [summed_rows(): lax.all_to_all(value.reshape(count, rows // count, columns), BOTH, 0, 0,...]
    ppermute x0 -> x10, starting transfers between devices: none -> 10.5 us  [summed(): lax.ppermute(value, axis, [(i, i ^ bit) for i in range(count)])]
    all_to_all x2 -> x0, starting transfers between devices: 8.51 us -> none  [the longest x1 6.01 us: body(): sums = lax.all_to_all(sums, BOTH, 0, 0, tiled=True)]
    pallas_call x0 -> x1, Pallas kernels: none -> 3.71 us  [body(): pl.pallas_call(half_inverse_kernel, out_shape=shape((modes, 2 * modes), f...]
    pallas_call x1, Pallas kernels: 5.56 us -> 3.65 us  [body(): pl.pallas_call(inverse_kernel, out_shape=shape((modes, modes), f32), in_s...]
    all_to_all x2 -> x0, waiting for transfers between devices: 1.61 us -> none  [the longest x1 1.61 us: body(): sums = lax.all_to_all(sums, BOTH, 0, 0, tiled=True)]
  transfers between devices with their start and end apart: 6 -> 14, of which waited for: 1 -> 8; matrix products, arithmetic and copies ran while one was open for 1% -> 0% of each run, Pallas kernels for 29% -> 33%
where the time goes in v3:
time: 67.1 us; the launch traced here: 66.9 us
  Pallas kernels  28 us (42%)
  starting transfers between devices  18.6 us (28%)
  waiting for transfers between devices  18.5 us (28%)
  local copies, waits for them, and re-layouts  1.08 us (2%)
  between operations  0.73 us (1%)
    ppermute x10, waiting for transfers between devices, summed(): lax.ppermute(value, axis, [(i, i ^ bit) for i in range(count)])  18.5 us
    pallas_call x1, Pallas kernels, body(): pl.pallas_call(inner_gram_kernel, out_shape=[shape(windows.shape, f32), s...  11.4 us
    ppermute x10, starting transfers between devices, summed(): lax.ppermute(value, axis, [(i, i ^ bit) for i in range(count)])  10.5 us
    ppermute x1, starting transfers between devices, body(): from_right = lax.ppermute(faces[1], 'solver', to_left)  4.44 us
    pallas_call x1, Pallas kernels, body(): pl.pallas_call(functools.partial(finish_kernel, rows_total), out_shape=[s...  4.17 us
    pallas_call x1, Pallas kernels, body(): pl.pallas_call(half_inverse_kernel, out_shape=shape((modes, 2 * modes), f...  3.71 us
    pallas_call x1, Pallas kernels, body(): pl.pallas_call(inverse_kernel, out_shape=shape((modes, modes), f32), in_s...  3.65 us
    pallas_call x1, Pallas kernels, body(): pl.pallas_call(functools.partial(project_kernel, True), out_shape=[sums_s...  3.08 us
  transfers between devices with their start and end apart: 14, of which 8 were waited for; matrix products, arithmetic and copies ran while one was open for 0% of the time, Pallas kernels for 33%

profile of v3, /device:TPU:0, one launch (start us, length us, event | category | flops | bytes accessed | tf_op | source)
XLA Modules:
  0.0 66.9 jit_solution(1349986555629884863)
XLA Ops:
  0.6 1.1 %copy-done = f32[2,5,8,4,512]{4,3,2,1,0:T(4,128)S(1)} copy-done((f32[2,5,8,4,512]{4,3,2,1,0:T(4,128)S(1)}, f32[2,5,8,4,512]{4,3,2,1,0:T(4,128)}, u32[]{:S(2)}) %copy-start) | copy-done | bytes 655384
  1.7 1.0 %faces.1 = (f32[2,5,8,4,512]{4,3,2,1,0:T(4,128)S(1)}, f32[2,5,4,4,512]{4,3,2,1,0:T(4,128)S(1)}, f32[2,5,4,4,512]{4,3,2,1,0:T(4,128)S(1)}, f32[2,5,8,4,512]{4,3,2,1,0:T(4,128)S(1)}) custom-call(s32[1]{0:T(128)} %bitcast.where_ref, f32[2,5,8,4,512]{4,3,2,1,0:T(4,128)S(1)} %copy-done), custom_call_target="tpu_custom_call" | custom-call | flops 10000000 | bytes 1638400 | tf_op jit(solution)/shard_map/faces/pallas_call | solution.py:404
  2.8 3.0 %collective-permute-start.2 = (f32[2,5,8,4,512]{4,3,2,1,0:T(4,128)S(1)}, f32[2,5,8,4,512]{4,3,2,1,0:T(4,128)S(1)}, u32[]{:S(2)}, u32[]{:S(2)}) collective-permute-start(f32[2,5,8,4,512]{4,3,2,1,0:T(4,128)S(1)} %get-tuple-element.23), channel_id=1, source_target_pairs={{0,1},{1,0},{2,3},{3,2},{4,5},{5,4},{6,7},{7,6},{8,9},{9,8},{10,11... | collective-permute-start | bytes 1966088 | tf_op jit(solution)/shard_map/ppermute | solution.py:424
  5.8 4.4 %collective-permute-start.1 = (f32[2,5,4,4,512]{4,3,2,1,0:T(4,128)S(1)}, f32[2,5,4,4,512]{4,3,2,1,0:T(4,128)S(1)}, u32[]{:S(2)}, u32[]{:S(2)}) collective-permute-start(f32[2,5,4,4,512]{4,3,2,1,0:T(4,128)S(1)} %get-tuple-element.22), channel_id=1, source_target_pairs={{2,0},{4,2},{6,4},{8,6},{10,8},{12,10},{14,12},{16,14},{18,16},{20... | collective-permute-start | bytes 983048 | tf_op jit(solution)/shard_map/ppermute | solution.py:431
  10.2 11.4 %inner_gram.1 = (f32[2,5,8,4,512]{4,3,2,1,0:T(4,128)S(1)}, f32[64,128]{1,0:T(8,128)S(1)}, bf16[64,20,8,512]{3,2,1,0:T(8,128)(2,1)S(1)}) custom-call(f32[2,5,8,4,512]{4,3,2,1,0:T(4,128)S(1)} %get-tuple-element.19.windows_ref, bf16[64,20,8,512]{3,2,1,0:T(8,128)(2,1)} %bitcast.3), custom_call_target="tpu_custom_call" | custom-call | flops 5368709120 | bytes 20971520 | tf_op jit(solution)/shard_map/inner_gram/pallas_call | solution.py:433
  21.6 1.0 %join.1 = (f32[2,5,8,4,512]{4,3,2,1,0:T(4,128)}, bf16[2,5,16,512]{3,2,1,0:T(8,128)(2,1)S(1)}, bf16[2,5,16,512]{3,2,1,0:T(8,128)(2,1)S(1)}) custom-call(s32[1]{0:T(128)} %bitcast.where_ref, f32[2,5,8,4,512]{4,3,2,1,0:T(4,128)S(1)} %get-tuple-element.20.part_ref, f32[2,5,4,4,512]{4,3,2,1,0:T(4,128)S(1)} %collective-permute-done.left_ref, ...), custom_call_target="tpu_custom_call" | custom-call | flops 1000000 | bytes 2621440 | tf_op jit(solution)/shard_map/join/pallas_call | solution.py:468
  23.2 1.4 %collective-permute-start.9 = (f32[64,128]{1,0:T(8,128)S(1)}, f32[64,128]{1,0:T(8,128)S(1)}, u32[]{:S(2)}, u32[]{:S(2)}) collective-permute-start(f32[64,128]{1,0:T(8,128)S(1)} %get-tuple-element.29), channel_id=1, source_target_pairs={{0,1},{1,0},{2,3},{3,2},{4,5},{5,4},{6,7},{7,6},{8,9},{9,8},{10,11... | collective-permute-start | bytes 98312 | tf_op jit(solution)/shard_map/ppermute | solution.py:385
  24.6 3.6 %collective-permute-done.9 = f32[64,128]{1,0:T(8,128)S(1)} collective-permute-done((f32[64,128]{1,0:T(8,128)S(1)}, f32[64,128]{1,0:T(8,128)S(1)}, u32[]{:S(2)}, u32[]{:S(2)}) %collective-permute-start.9) | collective-permute-done | bytes 32800 | tf_op jit(solution)/shard_map/ppermute | solution.py:385
  28.3 1.2 %collective-permute-done.10 = f32[64,128]{1,0:T(8,128)S(1)} collective-permute-done((f32[64,128]{1,0:T(8,128)S(1)}, f32[64,128]{1,0:T(8,128)S(1)}, u32[]{:S(2)}, u32[]{:S(2)}) %collective-permute-start.10) | collective-permute-done | bytes 32800 | tf_op jit(solution)/shard_map/ppermute | solution.py:385
  30.2 3.2 %collective-permute-done.11 = f32[64,128]{1,0:T(8,128)S(1)} collective-permute-done((f32[64,128]{1,0:T(8,128)S(1)}, f32[64,128]{1,0:T(8,128)S(1)}, u32[]{:S(2)}, u32[]{:S(2)}) %collective-permute-start.11) | collective-permute-done | bytes 32800 | tf_op jit(solution)/shard_map/ppermute | solution.py:385
  34.2 3.1 %collective-permute-done.12 = f32[64,128]{1,0:T(8,128)S(1)} collective-permute-done((f32[64,128]{1,0:T(8,128)S(1)}, f32[64,128]{1,0:T(8,128)S(1)}, u32[]{:S(2)}, u32[]{:S(2)}) %collective-permute-start.12) | collective-permute-done | bytes 32800 | tf_op jit(solution)/shard_map/ppermute | solution.py:385
  37.3 1.8 %collective-permute-start.13 = (f32[64,128]{1,0:T(8,128)S(1)}, f32[64,128]{1,0:T(8,128)S(1)}, u32[]{:S(2)}, u32[]{:S(2)}) collective-permute-start(f32[64,128]{1,0:T(8,128)S(1)} %add.38), channel_id=1, source_target_pairs={{0,16},{2,18},{4,20},{6,22},{8,24},{10,26},{12,28},{14,30},{16,0},... | collective-permute-start | bytes 98312 | tf_op jit(solution)/shard_map/ppermute | solution.py:385
  39.1 3.1 %project.1 = (f32[8,128]{1,0:T(8,128)S(1)}, bf16[20,16,512]{2,1,0:T(8,128)(2,1)S(1)}) custom-call(s32[1]{0:T(128)} %bitcast.where_ref, bf16[2,5,16,512]{3,2,1,0:T(8,128)(2,1)S(1)} %get-tuple-element.25.rest_0_, bf16[2,5,16,512]{3,2,1,0:T(8,128)(2,1)S(1)} %collective-permute-done.3.rest_1_, bf16[64,20,8,512]{3,2,1,0:T(8,128)(2,1)S(1)} %get-tuple-element.27.rest_2_.basis_ref), custom_call_target="tpu_custom_call" | custom-call | flops 167772160 | bytes 10485760 | tf_op jit(solution)/shard_map/project/pallas_call | solution.py:486
  42.2 1.5 %collective-permute-start.4 = (f32[8,128]{1,0:T(8,128)S(1)}, f32[8,128]{1,0:T(8,128)S(1)}, u32[]{:S(2)}, u32[]{:S(2)}) collective-permute-start(f32[8,128]{1,0:T(8,128)S(1)} %get-tuple-element.28), channel_id=1, source_target_pairs={{0,1},{1,0},{2,3},{3,2},{4,5},{5,4},{6,7},{7,6},{8,9},{9,8},{10,11... | collective-permute-start | bytes 12296 | tf_op jit(solution)/shard_map/ppermute | solution.py:385
  43.8 2.1 %collective-permute-done.4 = f32[8,128]{1,0:T(8,128)S(1)} collective-permute-done((f32[8,128]{1,0:T(8,128)S(1)}, f32[8,128]{1,0:T(8,128)S(1)}, u32[]{:S(2)}, u32[]{:S(2)}) %collective-permute-start.4) | collective-permute-done | bytes 4128 | tf_op jit(solution)/shard_map/ppermute | solution.py:385
  45.9 1.2 %collective-permute-done.5 = f32[8,128]{1,0:T(8,128)S(1)} collective-permute-done((f32[8,128]{1,0:T(8,128)S(1)}, f32[8,128]{1,0:T(8,128)S(1)}, u32[]{:S(2)}, u32[]{:S(2)}) %collective-permute-start.5) | collective-permute-done | bytes 4128 | tf_op jit(solution)/shard_map/ppermute | solution.py:385
  47.0 1.5 %collective-permute-start.6 = (f32[8,128]{1,0:T(8,128)S(1)}, f32[8,128]{1,0:T(8,128)S(1)}, u32[]{:S(2)}, u32[]{:S(2)}) collective-permute-start(f32[8,128]{1,0:T(8,128)S(1)} %add.31), channel_id=1, source_target_pairs={{0,4},{2,6},{4,0},{6,2},{8,12},{10,14},{12,8},{14,10},{16,20},{18,... | collective-permute-start | bytes 12296 | tf_op jit(solution)/shard_map/ppermute | solution.py:385
  48.6 2.1 %collective-permute-done.6 = f32[8,128]{1,0:T(8,128)S(1)} collective-permute-done((f32[8,128]{1,0:T(8,128)S(1)}, f32[8,128]{1,0:T(8,128)S(1)}, u32[]{:S(2)}, u32[]{:S(2)}) %collective-permute-start.6) | collective-permute-done | bytes 4128 | tf_op jit(solution)/shard_map/ppermute | solution.py:385
  50.7 1.6 %collective-permute-start.7 = (f32[8,128]{1,0:T(8,128)S(1)}, f32[8,128]{1,0:T(8,128)S(1)}, u32[]{:S(2)}, u32[]{:S(2)}) collective-permute-start(f32[8,128]{1,0:T(8,128)S(1)} %add.32), channel_id=1, source_target_pairs={{0,8},{2,10},{4,12},{6,14},{8,0},{10,2},{12,4},{14,6},{16,24},{18,... | collective-permute-start | bytes 12296 | tf_op jit(solution)/shard_map/ppermute | solution.py:385
  52.2 2.0 %collective-permute-done.7 = f32[8,128]{1,0:T(8,128)S(1)} collective-permute-done((f32[8,128]{1,0:T(8,128)S(1)}, f32[8,128]{1,0:T(8,128)S(1)}, u32[]{:S(2)}, u32[]{:S(2)}) %collective-permute-start.7) | collective-permute-done | bytes 4128 | tf_op jit(solution)/shard_map/ppermute | solution.py:385
  54.3 1.1 %collective-permute-start.8 = (f32[8,128]{1,0:T(8,128)S(1)}, f32[8,128]{1,0:T(8,128)S(1)}, u32[]{:S(2)}, u32[]{:S(2)}) collective-permute-start(f32[8,128]{1,0:T(8,128)S(1)} %add.33), channel_id=1, source_target_pairs={{0,16},{2,18},{4,20},{6,22},{8,24},{10,26},{12,28},{14,30},{16,0},... | collective-permute-start | bytes 12296 | tf_op jit(solution)/shard_map/ppermute | solution.py:385
  55.4 3.7 %half_inverse.1.half_ref = f32[64,128]{1,0:T(8,128)S(1)} custom-call(f32[64,128]{1,0:T(8,128)S(1)} %add.39.gram_ref), custom_call_target="tpu_custom_call" | custom-call | flops 10000000 | bytes 32768 | tf_op jit(solution)/shard_map/half_inverse/pallas_call | solution.py:448
  59.1 3.6 %inverse.1.inverse_ref = f32[64,64]{1,0:T(8,128)S(1)} custom-call(f32[64,128]{1,0:T(8,128)S(1)} %half_inverse.1.half_ref), custom_call_target="tpu_custom_call" | custom-call | flops 10000000 | bytes 32768 | tf_op jit(solution)/shard_map/inverse/pallas_call | solution.py:457
  62.8 4.2 %finish.1 = (f32[2,20,8,512]{3,2,1,0:T(8,128)}, f32[2,64]{1,0:T(2,128)}, f32[2,2]{1,0:T(2,128)}) custom-call(f32[8,128]{1,0:T(8,128)S(1)} %add.34.sums_ref, f32[64,128]{1,0:T(8,128)S(1)} %add.39.gram_ref, f32[64,64]{1,0:T(8,128)S(1)} %inverse.1.inverse_ref, bf16[20,16,512]{2,1,0:T(8,128)(2,1)S(1)} %get-tuple-element.30.snaps_ref, ...), custom_call_target="tpu_custom_call" | custom-call | flops 335544320 | bytes 11796480 | tf_op jit(solution)/shard_map/finish/pallas_call | solution.py:515
  (23 shorter events, 2.3 us)
Async XLA Ops:
  0.6 1.1 %copy-start = (f32[2,5,8,4,512]{4,3,2,1,0:T(4,128)S(1)}, f32[2,5,8,4,512]{4,3,2,1,0:T(4,128)}, u32[]{:S(2)}) copy-start(f32[2,5,8,4,512]{4,3,2,1,0:T(4,128)} %source_ref.1) | copy-start | bytes 1966084
  2.8 18.8 %collective-permute-start.2 = (f32[2,5,8,4,512]{4,3,2,1,0:T(4,128)S(1)}, f32[2,5,8,4,512]{4,3,2,1,0:T(4,128)S(1)}, u32[]{:S(2)}, u32[]{:S(2)}) collective-permute-start(f32[2,5,8,4,512]{4,3,2,1,0:T(4,128)S(1)} %get-tuple-element.23), channel_id=1, source_target_pairs={{0,1},{1,0},{2,3},{3,2},{4,5},{5,4},{6,7},{7,6},{8,9},{9,8},{10,11... | collective-permute-start | bytes 1966088 | tf_op jit(solution)/shard_map/ppermute | solution.py:424
  5.8 15.8 %collective-permute-start = (f32[2,5,4,4,512]{4,3,2,1,0:T(4,128)S(1)}, f32[2,5,4,4,512]{4,3,2,1,0:T(4,128)S(1)}, u32[]{:S(2)}, u32[]{:S(2)}) collective-permute-start(f32[2,5,4,4,512]{4,3,2,1,0:T(4,128)S(1)} %get-tuple-element.21), channel_id=1, source_target_pairs={{0,2},{2,4},{4,6},{6,8},{8,10},{10,12},{12,14},{14,16},{16,18},{18... | collective-permute-start | bytes 983048 | tf_op jit(solution)/shard_map/ppermute | solution.py:430
  5.8 15.8 %collective-permute-start.1 = (f32[2,5,4,4,512]{4,3,2,1,0:T(4,128)S(1)}, f32[2,5,4,4,512]{4,3,2,1,0:T(4,128)S(1)}, u32[]{:S(2)}, u32[]{:S(2)}) collective-permute-start(f32[2,5,4,4,512]{4,3,2,1,0:T(4,128)S(1)} %get-tuple-element.22), channel_id=1, source_target_pairs={{2,0},{4,2},{6,4},{8,6},{10,8},{12,10},{14,12},{16,14},{18,16},{20... | collective-permute-start | bytes 983048 | tf_op jit(solution)/shard_map/ppermute | solution.py:431
  22.6 16.6 %collective-permute-start.3 = (bf16[2,5,16,512]{3,2,1,0:T(8,128)(2,1)S(1)}, bf16[2,5,16,512]{3,2,1,0:T(8,128)(2,1)S(1)}, u32[]{:S(2)}, u32[]{:S(2)}) collective-permute-start(bf16[2,5,16,512]{3,2,1,0:T(8,128)(2,1)S(1)} %get-tuple-element.26), channel_id=1, source_target_pairs={{0,1},{1,0},{2,3},{3,2},{4,5},{5,4},{6,7},{7,6},{8,9},{9,8},{10,11... | collective-permute-start | bytes 491528 | tf_op jit(solution)/shard_map/ppermute | solution.py:485
  23.2 5.0 %collective-permute-start.9 = (f32[64,128]{1,0:T(8,128)S(1)}, f32[64,128]{1,0:T(8,128)S(1)}, u32[]{:S(2)}, u32[]{:S(2)}) collective-permute-start(f32[64,128]{1,0:T(8,128)S(1)} %get-tuple-element.29), channel_id=1, source_target_pairs={{0,1},{1,0},{2,3},{3,2},{4,5},{5,4},{6,7},{7,6},{8,9},{9,8},{10,11... | collective-permute-start | bytes 98312 | tf_op jit(solution)/shard_map/ppermute | solution.py:385
  28.3 1.2 %collective-permute-start.10 = (f32[64,128]{1,0:T(8,128)S(1)}, f32[64,128]{1,0:T(8,128)S(1)}, u32[]{:S(2)}, u32[]{:S(2)}) collective-permute-start(f32[64,128]{1,0:T(8,128)S(1)} %add.35), channel_id=1, source_target_pairs={{0,2},{2,0},{4,6},{6,4},{8,10},{10,8},{12,14},{14,12},{16,18},{18,... | collective-permute-start | bytes 98312 | tf_op jit(solution)/shard_map/ppermute | solution.py:385
  29.5 3.9 %collective-permute-start.11 = (f32[64,128]{1,0:T(8,128)S(1)}, f32[64,128]{1,0:T(8,128)S(1)}, u32[]{:S(2)}, u32[]{:S(2)}) collective-permute-start(f32[64,128]{1,0:T(8,128)S(1)} %add.36), channel_id=1, source_target_pairs={{0,4},{2,6},{4,0},{6,2},{8,12},{10,14},{12,8},{14,10},{16,20},{18,... | collective-permute-start | bytes 98312 | tf_op jit(solution)/shard_map/ppermute | solution.py:385
  33.4 3.9 %collective-permute-start.12 = (f32[64,128]{1,0:T(8,128)S(1)}, f32[64,128]{1,0:T(8,128)S(1)}, u32[]{:S(2)}, u32[]{:S(2)}) collective-permute-start(f32[64,128]{1,0:T(8,128)S(1)} %add.37), channel_id=1, source_target_pairs={{0,8},{2,10},{4,12},{6,14},{8,0},{10,2},{12,4},{14,6},{16,24},{18,... | collective-permute-start | bytes 98312 | tf_op jit(solution)/shard_map/ppermute | solution.py:385
  37.3 18.1 %collective-permute-start.13 = (f32[64,128]{1,0:T(8,128)S(1)}, f32[64,128]{1,0:T(8,128)S(1)}, u32[]{:S(2)}, u32[]{:S(2)}) collective-permute-start(f32[64,128]{1,0:T(8,128)S(1)} %add.38), channel_id=1, source_target_pairs={{0,16},{2,18},{4,20},{6,22},{8,24},{10,26},{12,28},{14,30},{16,0},... | collective-permute-start | bytes 98312 | tf_op jit(solution)/shard_map/ppermute | solution.py:385
  42.2 3.6 %collective-permute-start.4 = (f32[8,128]{1,0:T(8,128)S(1)}, f32[8,128]{1,0:T(8,128)S(1)}, u32[]{:S(2)}, u32[]{:S(2)}) collective-permute-start(f32[8,128]{1,0:T(8,128)S(1)} %get-tuple-element.28), channel_id=1, source_target_pairs={{0,1},{1,0},{2,3},{3,2},{4,5},{5,4},{6,7},{7,6},{8,9},{9,8},{10,11... | collective-permute-start | bytes 12296 | tf_op jit(solution)/shard_map/ppermute | solution.py:385
  45.9 1.2 %collective-permute-start.5 = (f32[8,128]{1,0:T(8,128)S(1)}, f32[8,128]{1,0:T(8,128)S(1)}, u32[]{:S(2)}, u32[]{:S(2)}) collective-permute-start(f32[8,128]{1,0:T(8,128)S(1)} %add.30), channel_id=1, source_target_pairs={{0,2},{2,0},{4,6},{6,4},{8,10},{10,8},{12,14},{14,12},{16,18},{18,... | collective-permute-start | bytes 12296 | tf_op jit(solution)/shard_map/ppermute | solution.py:385
  47.0 3.6 %collective-permute-start.6 = (f32[8,128]{1,0:T(8,128)S(1)}, f32[8,128]{1,0:T(8,128)S(1)}, u32[]{:S(2)}, u32[]{:S(2)}) collective-permute-start(f32[8,128]{1,0:T(8,128)S(1)} %add.31), channel_id=1, source_target_pairs={{0,4},{2,6},{4,0},{6,2},{8,12},{10,14},{12,8},{14,10},{16,20},{18,... | collective-permute-start | bytes 12296 | tf_op jit(solution)/shard_map/ppermute | solution.py:385
  50.7 3.6 %collective-permute-start.7 = (f32[8,128]{1,0:T(8,128)S(1)}, f32[8,128]{1,0:T(8,128)S(1)}, u32[]{:S(2)}, u32[]{:S(2)}) collective-permute-start(f32[8,128]{1,0:T(8,128)S(1)} %add.32), channel_id=1, source_target_pairs={{0,8},{2,10},{4,12},{6,14},{8,0},{10,2},{12,4},{14,6},{16,24},{18,... | collective-permute-start | bytes 12296 | tf_op jit(solution)/shard_map/ppermute | solution.py:385
  54.3 8.5 %collective-permute-start.8 = (f32[8,128]{1,0:T(8,128)S(1)}, f32[8,128]{1,0:T(8,128)S(1)}, u32[]{:S(2)}, u32[]{:S(2)}) collective-permute-start(f32[8,128]{1,0:T(8,128)S(1)} %add.33), channel_id=1, source_target_pairs={{0,16},{2,18},{4,20},{6,22},{8,24},{10,26},{12,28},{14,30},{16,0},... | collective-permute-start | bytes 12296 | tf_op jit(solution)/shard_map/ppermute | solution.py:385

commit v4 on v3

--- a/solution.py
+++ b/solution.py
@@ -220,7 +220,7 @@
     return basis_ref[:, t].reshape(modes * layers, cells)
 
 
-def project_kernel(paired, where_ref, *rest):
+def project_kernel(paired, where_ref, gram_ref, far_ref, *rest):
     if paired:
         own_ref, got_ref, basis_ref, sums_ref, snaps_ref, square, wide_sums = rest
         first = where_ref[0] == 0
@@ -261,47 +261,46 @@
         ],
         axis=0,
     )
-    sums_ref[...] = jnp.concatenate([sums, jnp.zeros((6, sums.shape[1]), jnp.float32)], axis=0)
-
-
-def eliminate(whole, start, stop):
-    rows = lax.broadcasted_iota(jnp.int32, whole.shape, 0)
-    for k in range(start, stop, 2):
-        first, second = whole[k : k + 1, :], whole[k + 1 : k + 2, :]
-        a, b = first[:, k : k + 1], first[:, k + 1 : k + 2]
-        c, d = second[:, k : k + 1], second[:, k + 1 : k + 2]
-        inverse = 1.0 / (a * d - b * c)
-        upper = (d * first - b * second) * inverse
-        lower = (a * second - c * first) * inverse
-        rest = whole - whole[:, k : k + 1] * upper - whole[:, k + 1 : k + 2] * lower
-        whole = jnp.where(rows == k, upper, jnp.where(rows == k + 1, lower, rest))
-    return whole
-
-
-def half_inverse_kernel(gram_ref, half_ref):
-    modes = gram_ref.shape[0]
-    rows = lax.broadcasted_iota(jnp.int32, (modes, modes), 0)
-    columns = lax.broadcasted_iota(jnp.int32, (modes, modes), 1)
-    eye = (rows == columns).astype(jnp.float32)
-    whole = jnp.concatenate([gram_ref[:, :modes], eye], axis=1)
-    half_ref[...] = eliminate(whole, 0, modes // 2)
-
-
-def inverse_kernel(half_ref, inverse_ref):
-    modes = half_ref.shape[0]
-    inverse_ref[...] = eliminate(half_ref[...], modes // 2, modes)[:, modes:]
+    sums_ref[0:modes] = gram_ref[...] + far_ref[...]
+    sums_ref[modes : modes + 8] = jnp.concatenate(
+        [sums, jnp.zeros((6, sums.shape[1]), jnp.float32)], axis=0
+    )
+
+
+def inverse_kernel(sums_ref, inverse_ref, plain, scaled):
+    modes = inverse_ref.shape[0]
+    rows = lax.broadcasted_iota(jnp.int32, (8, 2 * modes), 0)
+    lanes = lax.broadcasted_iota(jnp.int32, (8, 2 * modes), 1)
+    tiles = []
+    for tile in range(modes // 8):
+        eye = (lanes == rows + (modes + 8 * tile)).astype(jnp.float32)
+        tiles.append(jnp.where(lanes < modes, sums_ref[8 * tile : 8 * tile + 8, :], eye))
+    for k in range(modes):
+        home, line = divmod(k, 8)
+        row = tiles[home][line : line + 1, :]
+        ready = row / row[:, k : k + 1]
+        plain[k : k + 1, :] = row
+        scaled[k : k + 1, :] = ready
+        for tile in range(home, modes // 8):
+            column = tiles[tile][:, k : k + 1]
+            if tile == home:
+                column = jnp.where(rows[:, 0:1] > line, column, 0.0)
+            tiles[tile] = tiles[tile] - column * ready
+    inverse_ref[...] = lax.dot_general(
+        plain[:, modes:], scaled[:, modes:], (((0,), (0,)), ((), ())),
+        precision=HIGHEST, preferred_element_type=jnp.float32,
+    )
 
 
 def finish_kernel(
-    rows_total, sums_ref, gram_ref, inverse_ref, snaps_ref, basis_ref,
+    rows_total, projected_ref, sums_ref, inverse_ref, snaps_ref, basis_ref,
     modes_ref, solved_ref, factor_ref, made, sems,
 ):
     modes, tiles, _, cells = basis_ref.shape
     wide = modes * 8
     exact = functools.partial(jnp.dot, precision=HIGHEST, preferred_element_type=jnp.float32)
-    sums = sums_ref[...]
-    projected = sums[:, 0:modes]
-    gram, inverse = gram_ref[:, :modes], inverse_ref[...]
+    projected = projected_ref[modes : modes + 8, 0:modes]
+    gram, inverse = sums_ref[0:modes, 0:modes], inverse_ref[...]
     solved = exact(projected, inverse)
     solved = solved + exact(projected - exact(solved, gram), inverse)
     left = projected - exact(solved, gram)
@@ -310,7 +309,7 @@
         return jnp.sum(p[i : i + 1] * q[j : j + 1], axis=1, keepdims=True)
 
     def entry(i, j):
-        square = sums[i : i + 1, modes + j : modes + j + 1]
+        square = projected_ref[modes + i : modes + i + 1, modes + j : modes + j + 1]
         return square - inner(projected, i, solved, j) - inner(solved, i, left, j)
 
     first = jnp.sqrt(entry(0, 0))
@@ -369,22 +368,20 @@
 
 
 WHOLE = pl.BlockSpec(memory_space=pltpu.VMEM)
-AXES = ("analysis", "solver")
 FAR = pl.BlockSpec(memory_space=pltpu.HBM)
 SCALAR = pl.BlockSpec(memory_space=pltpu.SMEM)
 
 
-def summed(value, axes):
-    for axis in axes:
-        count = lax.axis_size(axis)
-        if count & (count - 1):
-            value = lax.psum(value, axis)
-            continue
-        bit = 1
-        while bit < count:
-            value = value + lax.ppermute(value, axis, [(i, i ^ bit) for i in range(count)])
-            bit *= 2
-    return value
+def swap_added(value, axis, bit):
+    count = lax.axis_size(axis)
+    return value + lax.ppermute(value, axis, [(i, i ^ bit) for i in range(count)])
+
+
+def bits(count):
+    made = [1 << k for k in range(count.bit_length() - 1)]
+    if count != 1 << len(made):
+        raise ValueError("axis size")
+    return made
 
 
 def body(windows, pod_basis):
@@ -444,26 +441,8 @@
         cost_estimate=cost(2 * wide * wide * cells * tiles, 2 * basis_bytes),
         name="inner_gram",
     )(kept, basis)
-    gram = summed(gram, AXES)
-    half_inverse = pl.pallas_call(
-        half_inverse_kernel,
-        out_shape=shape((modes, 2 * modes), f32),
-        in_specs=[WHOLE],
-        out_specs=WHOLE,
-        compiler_params=params(16),
-        cost_estimate=cost(10_000_000, 8 * modes * modes),
-        name="half_inverse",
-    )(gram)
-    inverse = pl.pallas_call(
-        inverse_kernel,
-        out_shape=shape((modes, modes), f32),
-        in_specs=[WHOLE],
-        out_specs=WHOLE,
-        compiler_params=params(16),
-        cost_estimate=cost(10_000_000, 8 * modes * modes),
-        name="inverse",
-    )(half_inverse)
-
+    *near, far = bits(ring)
+    gram_far = lax.ppermute(gram, "solver", [(i, i ^ far) for i in range(ring)])
     half_shape = (count, fields, planes * layers // 2, cells)
     joined = pl.pallas_call(
         functools.partial(join_kernel, sides, paired),
@@ -476,7 +455,7 @@
     )(place, inner, from_left, from_right, *wall_terms)
     next_windows = joined[0]
 
-    sums_shape = shape((8, LANES), f32)
+    sums_shape = shape((modes + 8, LANES), f32)
     snaps_shape = shape((tiles, 2 * 8, cells), bf16)
     scratch = [pltpu.VMEM((LANES, LANES), f32), pltpu.VMEM((1, wide, LANES), f32)]
     project_cost = cost(2 * wide * 16 * cells * tiles, basis_bytes)
@@ -486,13 +465,13 @@
         sums, snaps = pl.pallas_call(
             functools.partial(project_kernel, True),
             out_shape=[sums_shape, snaps_shape],
-            in_specs=[SCALAR] + [WHOLE] * 3,
+            in_specs=[SCALAR] + [WHOLE] * 5,
             out_specs=[WHOLE] * 2,
             scratch_shapes=scratch,
             compiler_params=params(16),
             cost_estimate=project_cost,
             name="project",
-        )(place, own, got, basis)
+        )(place, gram, gram_far, own, got, basis)
     else:
         relaid = lax.all_to_all(
             next_windows.astype(bf16), "analysis", split_axis=2, concat_axis=3, tiled=True
@@ -502,14 +481,28 @@
         sums = pl.pallas_call(
             functools.partial(project_kernel, False),
             out_shape=sums_shape,
-            in_specs=[SCALAR] + [WHOLE] * 2,
+            in_specs=[SCALAR] + [WHOLE] * 4,
             out_specs=WHOLE,
             scratch_shapes=scratch,
             compiler_params=params(16),
             cost_estimate=project_cost,
             name="project",
-        )(place, snaps, basis)
-    sums = summed(sums, AXES)
+        )(place, gram, gram_far, snaps, basis)
+    for bit in bits(walls):
+        sums = swap_added(sums, "analysis", bit)
+    for bit in near:
+        sums = swap_added(sums, "solver", bit)
+    inverse = pl.pallas_call(
+        inverse_kernel,
+        out_shape=shape((modes, modes), f32),
+        in_specs=[WHOLE],
+        out_specs=WHOLE,
+        scratch_shapes=[pltpu.VMEM((modes, 2 * modes), f32)] * 2,
+        compiler_params=params(16),
+        cost_estimate=cost(20_000_000, 8 * modes * modes),
+        name="inverse",
+    )(sums)
+    projected = swap_added(sums, "solver", far)
 
     rows_total = ring * walls * tiles * 8 * cells
     new_modes, solved, factor = pl.pallas_call(
@@ -528,7 +521,7 @@
         compiler_params=params(16),
         cost_estimate=cost(2 * wide * 32 * cells * tiles, basis_bytes + 8 * windows.size),
         name="finish",
-    )(sums, gram, inverse, snaps, basis)
+    )(projected, sums, inverse, snaps, basis)
     new_modes = new_modes.reshape(count, fields, pod_planes, pod_layers, cells)
     return next_windows, solved, new_modes, factor
 

time: 67.1 us -> 56.8 us (0.85)
  waiting for transfers between devices: 18.5 us -> 10.5 us
  Pallas kernels: 28 us -> 26.1 us
    ppermute x10 -> x6, waiting for transfers between devices: 18.5 us -> 10.5 us  [the longest x5 8.23 us: swap_added(): lax.ppermute(value, axis, [(i, i ^ bit) for i in range(count)])]
    pallas_call x1 -> x0, Pallas kernels: 3.71 us -> none  [body(): pl.pallas_call(half_inverse_kernel, out_shape=shape((modes, 2 * modes), f...]
    pallas_call x1, Pallas kernels: 3.65 us -> 5.51 us  [body(): pl.pallas_call(inverse_kernel, out_shape=shape((modes, modes), f32), in_s...]
    ppermute x10 -> x6, starting transfers between devices: 10.5 us -> 10.1 us  [the longest x5 7.5 us: swap_added(): lax.ppermute(value, axis, [(i, i ^ bit) for i in range(count)])]
  transfers between devices with their start and end apart: 14 -> 10, of which waited for: 8 -> 5; matrix products, arithmetic and copies ran while one was open for 0% -> 0% of each run, Pallas kernels for 33% -> 30%
where the time goes in v4:
time: 56.8 us; the launch traced here: 56.6 us
  Pallas kernels  26.1 us (46%)
  starting transfers between devices  18.2 us (32%)
  waiting for transfers between devices  10.5 us (18%)
  local copies, waits for them, and re-layouts  1.08 us (2%)
  between operations  0.73 us (1%)
    pallas_call x1, Pallas kernels, body(): pl.pallas_call(inner_gram_kernel, out_shape=[shape(windows.shape, f32), s...  11.4 us
    ppermute x5, waiting for transfers between devices, swap_added(): lax.ppermute(value, axis, [(i, i ^ bit) for i in range(count)])  8.23 us
    ppermute x5, starting transfers between devices, swap_added(): lax.ppermute(value, axis, [(i, i ^ bit) for i in range(count)])  7.5 us
    pallas_call x1, Pallas kernels, body(): pl.pallas_call(inverse_kernel, out_shape=shape((modes, modes), f32), in_s...  5.51 us
    ppermute x1, starting transfers between devices, body(): from_right = lax.ppermute(faces[1], 'solver', to_left)  4.44 us
    pallas_call x1, Pallas kernels, body(): pl.pallas_call(functools.partial(finish_kernel, rows_total), out_shape=[s...  4.18 us
    pallas_call x1, Pallas kernels, body(): pl.pallas_call(functools.partial(project_kernel, True), out_shape=[sums_s...  3.08 us
    ppermute x1, starting transfers between devices, body(): wall_terms = [lax.ppermute(faces[2], 'analysis', upward + downward)]  3 us
  transfers between devices with their start and end apart: 10, of which 5 were waited for; matrix products, arithmetic and copies ran while one was open for 0% of the time, Pallas kernels for 30%

profile of v4, /device:TPU:0, one launch (start us, length us, event | category | flops | bytes accessed | tf_op | source)
XLA Modules:
  0.0 56.6 jit_solution(8119617386673557582)
XLA Ops:
  0.6 1.1 %copy-done = f32[2,5,8,4,512]{4,3,2,1,0:T(4,128)S(1)} copy-done((f32[2,5,8,4,512]{4,3,2,1,0:T(4,128)S(1)}, f32[2,5,8,4,512]{4,3,2,1,0:T(4,128)}, u32[]{:S(2)}) %copy-start) | copy-done | bytes 655384
  1.7 1.0 %faces.1 = (f32[2,5,8,4,512]{4,3,2,1,0:T(4,128)S(1)}, f32[2,5,4,4,512]{4,3,2,1,0:T(4,128)S(1)}, f32[2,5,4,4,512]{4,3,2,1,0:T(4,128)S(1)}, f32[2,5,8,4,512]{4,3,2,1,0:T(4,128)S(1)}) custom-call(s32[1]{0:T(128)} %bitcast.where_ref, f32[2,5,8,4,512]{4,3,2,1,0:T(4,128)S(1)} %copy-done), custom_call_target="tpu_custom_call" | custom-call | flops 10000000 | bytes 1638400 | tf_op jit(solution)/shard_map/faces/pallas_call | solution.py:401
  2.8 3.0 %collective-permute-start.2 = (f32[2,5,8,4,512]{4,3,2,1,0:T(4,128)S(1)}, f32[2,5,8,4,512]{4,3,2,1,0:T(4,128)S(1)}, u32[]{:S(2)}, u32[]{:S(2)}) collective-permute-start(f32[2,5,8,4,512]{4,3,2,1,0:T(4,128)S(1)} %get-tuple-element.23), channel_id=1, source_target_pairs={{0,1},{1,0},{2,3},{3,2},{4,5},{5,4},{6,7},{7,6},{8,9},{9,8},{10,11... | collective-permute-start | bytes 1966088 | tf_op jit(solution)/shard_map/ppermute | solution.py:421
  5.8 0.0 collective-permute-start
  5.8 4.4 %collective-permute-start.1 = (f32[2,5,4,4,512]{4,3,2,1,0:T(4,128)S(1)}, f32[2,5,4,4,512]{4,3,2,1,0:T(4,128)S(1)}, u32[]{:S(2)}, u32[]{:S(2)}) collective-permute-start(f32[2,5,4,4,512]{4,3,2,1,0:T(4,128)S(1)} %get-tuple-element.22), channel_id=1, source_target_pairs={{2,0},{4,2},{6,4},{8,6},{10,8},{12,10},{14,12},{16,14},{18,16},{20... | collective-permute-start | bytes 983048 | tf_op jit(solution)/shard_map/ppermute | solution.py:428
  10.2 11.4 %inner_gram.1 = (f32[2,5,8,4,512]{4,3,2,1,0:T(4,128)S(1)}, f32[64,128]{1,0:T(8,128)S(1)}, bf16[64,20,8,512]{3,2,1,0:T(8,128)(2,1)S(1)}) custom-call(f32[2,5,8,4,512]{4,3,2,1,0:T(4,128)S(1)} %get-tuple-element.19.windows_ref, bf16[64,20,8,512]{3,2,1,0:T(8,128)(2,1)} %bitcast.3), custom_call_target="tpu_custom_call" | custom-call | flops 5368709120 | bytes 20971520 | tf_op jit(solution)/shard_map/inner_gram/pallas_call | solution.py:430
  21.6 0.0 collective-permute-done.1.right_ref
  21.6 0.0 collective-permute-done.2.rest_0_
  21.6 1.0 %join.1 = (f32[2,5,8,4,512]{4,3,2,1,0:T(4,128)}, bf16[2,5,16,512]{3,2,1,0:T(8,128)(2,1)S(1)}, bf16[2,5,16,512]{3,2,1,0:T(8,128)(2,1)S(1)}) custom-call(s32[1]{0:T(128)} %bitcast.where_ref, f32[2,5,8,4,512]{4,3,2,1,0:T(4,128)S(1)} %get-tuple-element.20.part_ref, f32[2,5,4,4,512]{4,3,2,1,0:T(4,128)S(1)} %collective-permute-done.left_ref, ...), custom_call_target="tpu_custom_call" | custom-call | flops 1000000 | bytes 2621440 | tf_op jit(solution)/shard_map/join/pallas_call | solution.py:447
  22.6 0.6 %collective-permute-start.4 = (bf16[2,5,16,512]{3,2,1,0:T(8,128)(2,1)S(1)}, bf16[2,5,16,512]{3,2,1,0:T(8,128)(2,1)S(1)}, u32[]{:S(2)}, u32[]{:S(2)}) collective-permute-start(bf16[2,5,16,512]{3,2,1,0:T(8,128)(2,1)S(1)} %get-tuple-element.27), channel_id=1, source_target_pairs={{0,1},{1,0},{2,3},{3,2},{4,5},{5,4},{6,7},{7,6},{8,9},{9,8},{10,11... | collective-permute-start | bytes 491528 | tf_op jit(solution)/shard_map/ppermute | solution.py:464
  23.2 2.6 %collective-permute-start.3 = (f32[64,128]{1,0:T(8,128)S(1)}, f32[64,128]{1,0:T(8,128)S(1)}, u32[]{:S(2)}, u32[]{:S(2)}) collective-permute-start(f32[64,128]{1,0:T(8,128)S(1)} %get-tuple-element.25.gram_ref), channel_id=1, source_target_pairs={{0,16},{2,18},{4,20},{6,22},{8,24},{10,26},{12,28},{14,30},{16,0},... | collective-permute-start | bytes 98312 | tf_op jit(solution)/shard_map/ppermute | solution.py:445
  25.8 2.2 %collective-permute-done.3.far_ref = f32[64,128]{1,0:T(8,128)S(1)} collective-permute-done((f32[64,128]{1,0:T(8,128)S(1)}, f32[64,128]{1,0:T(8,128)S(1)}, u32[]{:S(2)}, u32[]{:S(2)}) %collective-permute-start.3) | collective-permute-done | bytes 32800 | tf_op jit(solution)/shard_map/ppermute | solution.py:445
  28.0 3.1 %project.1 = (f32[72,128]{1,0:T(8,128)S(1)}, bf16[20,16,512]{2,1,0:T(8,128)(2,1)S(1)}) custom-call(s32[1]{0:T(128)} %bitcast.where_ref, f32[64,128]{1,0:T(8,128)S(1)} %get-tuple-element.25.gram_ref, f32[64,128]{1,0:T(8,128)S(1)} %collective-permute-done.3.far_ref, bf16[2,5,16,512]{3,2,1,0:T(8,128)(2,1)S(1)} %get-tuple-element.26.rest_0_, ...), custom_call_target="tpu_custom_call" | custom-call | flops 167772160 | bytes 10485760 | tf_op jit(solution)/shard_map/project/pallas_call | solution.py:465
  31.1 1.8 %collective-permute-start.5 = (f32[72,128]{1,0:T(8,128)S(1)}, f32[72,128]{1,0:T(8,128)S(1)}, u32[]{:S(2)}, u32[]{:S(2)}) collective-permute-start(f32[72,128]{1,0:T(8,128)S(1)} %get-tuple-element.29), channel_id=1, source_target_pairs={{0,1},{1,0},{2,3},{3,2},{4,5},{5,4},{6,7},{7,6},{8,9},{9,8},{10,11... | collective-permute-start | bytes 110600 | tf_op jit(solution)/shard_map/ppermute | solution.py:377
  32.9 2.2 %collective-permute-done.5 = f32[72,128]{1,0:T(8,128)S(1)} collective-permute-done((f32[72,128]{1,0:T(8,128)S(1)}, f32[72,128]{1,0:T(8,128)S(1)}, u32[]{:S(2)}, u32[]{:S(2)}) %collective-permute-start.5) | collective-permute-done | bytes 36896 | tf_op jit(solution)/shard_map/ppermute | solution.py:377
  35.1 1.2 %collective-permute-done.6 = f32[72,128]{1,0:T(8,128)S(1)} collective-permute-done((f32[72,128]{1,0:T(8,128)S(1)}, f32[72,128]{1,0:T(8,128)S(1)}, u32[]{:S(2)}, u32[]{:S(2)}) %collective-permute-start.6) | collective-permute-done | bytes 36896 | tf_op jit(solution)/shard_map/ppermute | solution.py:377
  36.3 1.5 %collective-permute-start.7 = (f32[72,128]{1,0:T(8,128)S(1)}, f32[72,128]{1,0:T(8,128)S(1)}, u32[]{:S(2)}, u32[]{:S(2)}) collective-permute-start(f32[72,128]{1,0:T(8,128)S(1)} %add.16), channel_id=1, source_target_pairs={{0,4},{2,6},{4,0},{6,2},{8,12},{10,14},{12,8},{14,10},{16,20},{18,... | collective-permute-start | bytes 110600 | tf_op jit(solution)/shard_map/ppermute | solution.py:377
  37.9 2.4 %collective-permute-done.7 = f32[72,128]{1,0:T(8,128)S(1)} collective-permute-done((f32[72,128]{1,0:T(8,128)S(1)}, f32[72,128]{1,0:T(8,128)S(1)}, u32[]{:S(2)}, u32[]{:S(2)}) %collective-permute-start.7) | collective-permute-done | bytes 36896 | tf_op jit(solution)/shard_map/ppermute | solution.py:377
  40.3 1.6 %collective-permute-start.8 = (f32[72,128]{1,0:T(8,128)S(1)}, f32[72,128]{1,0:T(8,128)S(1)}, u32[]{:S(2)}, u32[]{:S(2)}) collective-permute-start(f32[72,128]{1,0:T(8,128)S(1)} %add.17), channel_id=1, source_target_pairs={{0,8},{2,10},{4,12},{6,14},{8,0},{10,2},{12,4},{14,6},{16,24},{18,... | collective-permute-start | bytes 110600 | tf_op jit(solution)/shard_map/ppermute | solution.py:377
  41.9 2.4 %collective-permute-done.8 = f32[72,128]{1,0:T(8,128)S(1)} collective-permute-done((f32[72,128]{1,0:T(8,128)S(1)}, f32[72,128]{1,0:T(8,128)S(1)}, u32[]{:S(2)}, u32[]{:S(2)}) %collective-permute-start.8) | collective-permute-done | bytes 36896 | tf_op jit(solution)/shard_map/ppermute | solution.py:377
  44.3 2.6 %collective-permute-start.9 = (f32[72,128]{1,0:T(8,128)S(1)}, f32[72,128]{1,0:T(8,128)S(1)}, u32[]{:S(2)}, u32[]{:S(2)}) collective-permute-start(f32[72,128]{1,0:T(8,128)S(1)} %add.18.sums_ref), channel_id=1, source_target_pairs={{0,16},{2,18},{4,20},{6,22},{8,24},{10,26},{12,28},{14,30},{16,0},... | collective-permute-start | bytes 110600 | tf_op jit(solution)/shard_map/ppermute | solution.py:377
  46.9 5.5 %inverse.1.inverse_ref = f32[64,64]{1,0:T(8,128)S(1)} custom-call(f32[72,128]{1,0:T(8,128)S(1)} %add.18.sums_ref), custom_call_target="tpu_custom_call" | custom-call | flops 20000000 | bytes 32768 | tf_op jit(solution)/shard_map/inverse/pallas_call | solution.py:495
  52.4 0.0 collective-permute-done.9
  52.4 4.2 %finish.1 = (f32[2,20,8,512]{3,2,1,0:T(8,128)}, f32[2,64]{1,0:T(2,128)}, f32[2,2]{1,0:T(2,128)}) custom-call(f32[72,128]{1,0:T(8,128)S(1)} %add.19.projected_ref, f32[72,128]{1,0:T(8,128)S(1)} %add.18.sums_ref, f32[64,64]{1,0:T(8,128)S(1)} %inverse.1.inverse_ref, bf16[20,16,512]{2,1,0:T(8,128)(2,1)S(1)} %get-tuple-element.30.snaps_ref, ...), custom_call_target="tpu_custom_call" | custom-call | flops 335544320 | bytes 11796480 | tf_op jit(solution)/shard_map/finish/pallas_call | solution.py:508
  (9 shorter events, 0.0 us)
Async XLA Ops:
  0.6 1.1 %copy-start = (f32[2,5,8,4,512]{4,3,2,1,0:T(4,128)S(1)}, f32[2,5,8,4,512]{4,3,2,1,0:T(4,128)}, u32[]{:S(2)}) copy-start(f32[2,5,8,4,512]{4,3,2,1,0:T(4,128)} %source_ref.1) | copy-start | bytes 1966084
  2.8 18.8 %collective-permute-start.2 = (f32[2,5,8,4,512]{4,3,2,1,0:T(4,128)S(1)}, f32[2,5,8,4,512]{4,3,2,1,0:T(4,128)S(1)}, u32[]{:S(2)}, u32[]{:S(2)}) collective-permute-start(f32[2,5,8,4,512]{4,3,2,1,0:T(4,128)S(1)} %get-tuple-element.23), channel_id=1, source_target_pairs={{0,1},{1,0},{2,3},{3,2},{4,5},{5,4},{6,7},{7,6},{8,9},{9,8},{10,11... | collective-permute-start | bytes 1966088 | tf_op jit(solution)/shard_map/ppermute | solution.py:421
  5.8 15.8 %collective-permute-start = (f32[2,5,4,4,512]{4,3,2,1,0:T(4,128)S(1)}, f32[2,5,4,4,512]{4,3,2,1,0:T(4,128)S(1)}, u32[]{:S(2)}, u32[]{:S(2)}) collective-permute-start(f32[2,5,4,4,512]{4,3,2,1,0:T(4,128)S(1)} %get-tuple-element.21), channel_id=1, source_target_pairs={{0,2},{2,4},{4,6},{6,8},{8,10},{10,12},{12,14},{14,16},{16,18},{18... | collective-permute-start | bytes 983048 | tf_op jit(solution)/shard_map/ppermute | solution.py:427
  5.8 15.8 %collective-permute-start.1 = (f32[2,5,4,4,512]{4,3,2,1,0:T(4,128)S(1)}, f32[2,5,4,4,512]{4,3,2,1,0:T(4,128)S(1)}, u32[]{:S(2)}, u32[]{:S(2)}) collective-permute-start(f32[2,5,4,4,512]{4,3,2,1,0:T(4,128)S(1)} %get-tuple-element.22), channel_id=1, source_target_pairs={{2,0},{4,2},{6,4},{8,6},{10,8},{12,10},{14,12},{16,14},{18,16},{20... | collective-permute-start | bytes 983048 | tf_op jit(solution)/shard_map/ppermute | solution.py:428
  22.6 5.4 %collective-permute-start.4 = (bf16[2,5,16,512]{3,2,1,0:T(8,128)(2,1)S(1)}, bf16[2,5,16,512]{3,2,1,0:T(8,128)(2,1)S(1)}, u32[]{:S(2)}, u32[]{:S(2)}) collective-permute-start(bf16[2,5,16,512]{3,2,1,0:T(8,128)(2,1)S(1)} %get-tuple-element.27), channel_id=1, source_target_pairs={{0,1},{1,0},{2,3},{3,2},{4,5},{5,4},{6,7},{7,6},{8,9},{9,8},{10,11... | collective-permute-start | bytes 491528 | tf_op jit(solution)/shard_map/ppermute | solution.py:464
  23.2 4.8 %collective-permute-start.3 = (f32[64,128]{1,0:T(8,128)S(1)}, f32[64,128]{1,0:T(8,128)S(1)}, u32[]{:S(2)}, u32[]{:S(2)}) collective-permute-start(f32[64,128]{1,0:T(8,128)S(1)} %get-tuple-element.25.gram_ref), channel_id=1, source_target_pairs={{0,16},{2,18},{4,20},{6,22},{8,24},{10,26},{12,28},{14,30},{16,0},... | collective-permute-start | bytes 98312 | tf_op jit(solution)/shard_map/ppermute | solution.py:445
  31.1 4.0 %collective-permute-start.5 = (f32[72,128]{1,0:T(8,128)S(1)}, f32[72,128]{1,0:T(8,128)S(1)}, u32[]{:S(2)}, u32[]{:S(2)}) collective-permute-start(f32[72,128]{1,0:T(8,128)S(1)} %get-tuple-element.29), channel_id=1, source_target_pairs={{0,1},{1,0},{2,3},{3,2},{4,5},{5,4},{6,7},{7,6},{8,9},{9,8},{10,11... | collective-permute-start | bytes 110600 | tf_op jit(solution)/shard_map/ppermute | solution.py:377
  35.1 1.2 %collective-permute-start.6 = (f32[72,128]{1,0:T(8,128)S(1)}, f32[72,128]{1,0:T(8,128)S(1)}, u32[]{:S(2)}, u32[]{:S(2)}) collective-permute-start(f32[72,128]{1,0:T(8,128)S(1)} %add.15), channel_id=1, source_target_pairs={{0,2},{2,0},{4,6},{6,4},{8,10},{10,8},{12,14},{14,12},{16,18},{18,... | collective-permute-start | bytes 110600 | tf_op jit(solution)/shard_map/ppermute | solution.py:377
  36.3 4.0 %collective-permute-start.7 = (f32[72,128]{1,0:T(8,128)S(1)}, f32[72,128]{1,0:T(8,128)S(1)}, u32[]{:S(2)}, u32[]{:S(2)}) collective-permute-start(f32[72,128]{1,0:T(8,128)S(1)} %add.16), channel_id=1, source_target_pairs={{0,4},{2,6},{4,0},{6,2},{8,12},{10,14},{12,8},{14,10},{16,20},{18,... | collective-permute-start | bytes 110600 | tf_op jit(solution)/shard_map/ppermute | solution.py:377
  40.3 4.0 %collective-permute-start.8 = (f32[72,128]{1,0:T(8,128)S(1)}, f32[72,128]{1,0:T(8,128)S(1)}, u32[]{:S(2)}, u32[]{:S(2)}) collective-permute-start(f32[72,128]{1,0:T(8,128)S(1)} %add.17), channel_id=1, source_target_pairs={{0,8},{2,10},{4,12},{6,14},{8,0},{10,2},{12,4},{14,6},{16,24},{18,... | collective-permute-start | bytes 110600 | tf_op jit(solution)/shard_map/ppermute | solution.py:377
  44.3 8.1 %collective-permute-start.9 = (f32[72,128]{1,0:T(8,128)S(1)}, f32[72,128]{1,0:T(8,128)S(1)}, u32[]{:S(2)}, u32[]{:S(2)}) collective-permute-start(f32[72,128]{1,0:T(8,128)S(1)} %add.18.sums_ref), channel_id=1, source_target_pairs={{0,16},{2,18},{4,20},{6,22},{8,24},{10,26},{12,28},{14,30},{16,0},... | collective-permute-start | bytes 110600 | tf_op jit(solution)/shard_map/ppermute | solution.py:377

commit v5 on v4

--- a/solution.py
+++ b/solution.py
@@ -102,6 +102,73 @@
                 right_ref[w, f, i] = total
 
 
+def paired_face_kernel(
+    where_ref, source_ref, windows_ref, left_ref, right_ref, near_ref, later_ref,
+    scratch, lows, sems,
+):
+    windows, _, planes, layers, cells = windows_ref.shape
+    copies = [
+        pltpu.make_async_copy(source_ref.at[w], windows_ref.at[w], sems.at[w])
+        for w in range(windows)
+    ]
+    for copy in copies:
+        copy.start()
+    tile = (layers, cells)
+    first = where_ref[0] == 0
+    table = [
+        jnp.where(
+            first,
+            row_weights(tile, [weight(j - layers - i) for i in range(layers)]),
+            row_weights(tile, [weight(layers + j - i) for i in range(layers)]),
+        )
+        for j in range(layers)
+    ]
+    half = planes // 2
+    for w in range(windows):
+        copies[w].wait()
+        for group, group_ref in enumerate((near_ref, later_ref)):
+            base = half * (1 - where_ref[0] if group else where_ref[0])
+            upper = [[] for _ in range(5)]
+            lower = [[] for _ in range(5)]
+            for x in range(half):
+                parts = primitives(windows_ref, w, base + x)
+                for f, value in enumerate(flux(parts, 0)):
+                    scratch[f, base + x] = value
+                for f, value in enumerate(flux(parts, 1)):
+                    total = None
+                    for j in range(layers):
+                        term = table[j] * value[j : j + 1, :]
+                        total = term if total is None else total + term
+                    high = total.astype(jnp.bfloat16).astype(jnp.float32)
+                    rest = total - high
+                    upper[f].append(high)
+                    lower[f].append(jnp.where(first, rest[0:2], rest[2:4]))
+            for f in range(5):
+                group_ref[f, 16 * w : 16 * w + 16] = jnp.concatenate(upper[f], axis=0).astype(
+                    jnp.bfloat16
+                )
+                lows[group, f, 8 * w : 8 * w + 8] = jnp.concatenate(lower[f], axis=0)
+        for f in range(5):
+            for i in range(REACH):
+                total = None
+                for j in range(planes):
+                    c = weight(j - planes - i)
+                    if c:
+                        term = c * scratch[f, j]
+                        total = term if total is None else total + term
+                left_ref[w, f, i] = total
+                total = None
+                for j in range(planes):
+                    c = weight(j + REACH - i)
+                    if c:
+                        term = c * scratch[f, j]
+                        total = term if total is None else total + term
+                right_ref[w, f, i] = total
+    for group, group_ref in enumerate((near_ref, later_ref)):
+        for f in range(5):
+            group_ref[f, 32:48] = lows[group, f].astype(jnp.bfloat16)
+
+
 def inner_part(windows_ref, part_ref, scratch):
     windows, _, planes, layers, cells = windows_ref.shape
     tile = (layers, cells)
@@ -132,12 +199,26 @@
                 part_ref[w, f, x] = total
 
 
-def inner_gram_kernel(windows_ref, basis_ref, part_ref, gram_ref, kept_ref, scratch, total, sems):
+def gram_blocks(basis_ref, chunks, per_chunk, right, left):
+    half = left.shape[0]
+    for c in chunks:
+        rows = jnp.concatenate(
+            [modes_of(basis_ref, t) for t in range(c * per_chunk, (c + 1) * per_chunk)], axis=1
+        )
+        right = right + lax.dot_general(
+            rows, rows[half:], NT, preferred_element_type=jnp.float32
+        )
+        left = left + lax.dot_general(
+            rows[:half], rows[:half], NT, preferred_element_type=jnp.float32
+        )
+    return right, left
+
+
+def inner_gram_kernel(
+    early, windows_ref, basis_ref, part_ref, right_ref, left_ref, kept_ref, scratch, sems
+):
     chunks = sems.shape[0]
-    modes, tiles, _, cells = kept_ref.shape
-    per_chunk = tiles // chunks
-    wide = modes * 8
-    half = wide // 2
+    per_chunk = kept_ref.shape[1] // chunks
     copies = []
     for c in range(chunks):
         span = pl.ds(c * per_chunk, per_chunk)
@@ -146,19 +227,22 @@
         )
         copies[c].start()
     inner_part(windows_ref, part_ref, scratch)
-    right = jnp.zeros((wide, half), jnp.float32)
-    left = jnp.zeros((half, half), jnp.float32)
+    right, left = jnp.zeros(right_ref.shape, jnp.float32), jnp.zeros(left_ref.shape, jnp.float32)
     for c in range(chunks):
         copies[c].wait()
-        rows = jnp.concatenate(
-            [modes_of(kept_ref, t) for t in range(c * per_chunk, (c + 1) * per_chunk)], axis=1
-        )
-        right = right + lax.dot_general(
-            rows, rows[half:], NT, preferred_element_type=jnp.float32
-        )
-        left = left + lax.dot_general(
-            rows[:half], rows[:half], NT, preferred_element_type=jnp.float32
-        )
+        if c < early:
+            right, left = gram_blocks(kept_ref, [c], per_chunk, right, left)
+    right_ref[...] = right
+    left_ref[...] = left
+
+
+def gram_kernel(early, chunks, _, right_ref, left_ref, basis_ref, gram_ref, total):
+    modes, tiles = basis_ref.shape[:2]
+    wide = modes * 8
+    half = wide // 2
+    right, left = gram_blocks(
+        basis_ref, range(early, chunks), tiles // chunks, right_ref[...], left_ref[...]
+    )
     tiles_left = half // LANES
     turned = right[0:half].T
     for tile in range(tiles_left):
@@ -175,7 +259,7 @@
     gram_ref[...] = jnp.dot(rows, picks, precision=HIGHEST, preferred_element_type=jnp.float32)
 
 
-def join_kernel(walls, paired, where_ref, part_ref, left_ref, right_ref, *rest):
+def join_kernel(walls, part_ref, left_ref, right_ref, *rest):
     wall_refs, next_ref = rest[:walls], rest[walls]
     windows, _, planes, layers, cells = part_ref.shape
     for w in range(windows):
@@ -189,13 +273,40 @@
                 if x >= planes - REACH:
                     total = total + right_ref[w, f, x - planes + REACH]
                 next_ref[w, f, x] = total
-            if paired:
-                half = planes // 2
-                low = jnp.concatenate([next_ref[w, f, x] for x in range(half)], axis=0)
-                high = jnp.concatenate([next_ref[w, f, x] for x in range(half, planes)], axis=0)
-                first = where_ref[0] == 0
-                rest[walls + 1][w, f] = jnp.where(first, low, high).astype(jnp.bfloat16)
-                rest[walls + 2][w, f] = jnp.where(first, high, low).astype(jnp.bfloat16)
+
+
+def paired_join_kernel(
+    own, where_ref, _, part_ref, left_ref, right_ref, group_ref, *rest
+):
+    next_ref, snaps_ref, made, sem = rest[-4:]
+    windows, _, planes, layers, cells = part_ref.shape
+    half = planes // 2
+    first = where_ref[0] == 0
+    base = half * (where_ref[0] if own else 1 - where_ref[0])
+    ahead = base == 0
+    zero = jnp.zeros((2, cells), jnp.float32)
+    for w in range(windows):
+        for f in range(5):
+            upper = group_ref[f, 16 * w : 16 * w + 16].astype(jnp.float32)
+            lower = group_ref[f, 32:48].astype(jnp.float32)[8 * w : 8 * w + 8]
+            done = []
+            for x in range(half):
+                rest_now = lower[2 * x : 2 * x + 2]
+                total = part_ref[w, f, base + x] + (
+                    upper[layers * x : layers * x + layers]
+                    + jnp.where(
+                        first,
+                        jnp.concatenate([zero, rest_now], axis=0),
+                        jnp.concatenate([rest_now, zero], axis=0),
+                    )
+                )
+                total = total + jnp.where(ahead, left_ref[w, f, x], right_ref[w, f, x])
+                made[w, f, x] = total
+                done.append(total)
+            snaps_ref[w, f] = jnp.concatenate(done, axis=0).astype(jnp.bfloat16)
+    copy = pltpu.make_async_copy(made, next_ref.at[:, :, pl.ds(base, half)], sem)
+    copy.start()
+    copy.wait()
 
 
 def same_layer(shape):
@@ -220,7 +331,7 @@
     return basis_ref[:, t].reshape(modes * layers, cells)
 
 
-def project_kernel(paired, where_ref, gram_ref, far_ref, *rest):
+def project_kernel(paired, where_ref, *rest):
     if paired:
         own_ref, got_ref, basis_ref, sums_ref, snaps_ref, square, wide_sums = rest
         first = where_ref[0] == 0
@@ -261,10 +372,15 @@
         ],
         axis=0,
     )
-    sums_ref[0:modes] = gram_ref[...] + far_ref[...]
-    sums_ref[modes : modes + 8] = jnp.concatenate(
+    sums_ref[...] = jnp.concatenate(
         [sums, jnp.zeros((6, sums.shape[1]), jnp.float32)], axis=0
     )
+
+
+def merge_kernel(gram_ref, far_ref, sums_ref, merged_ref):
+    modes = gram_ref.shape[0]
+    merged_ref[0:modes] = gram_ref[...] + far_ref[...]
+    merged_ref[modes:] = sums_ref[...]
 
 
 def inverse_kernel(sums_ref, inverse_ref, plain, scaled):
@@ -275,17 +391,31 @@
     for tile in range(modes // 8):
         eye = (lanes == rows + (modes + 8 * tile)).astype(jnp.float32)
         tiles.append(jnp.where(lanes < modes, sums_ref[8 * tile : 8 * tile + 8, :], eye))
-    for k in range(modes):
-        home, line = divmod(k, 8)
-        row = tiles[home][line : line + 1, :]
-        ready = row / row[:, k : k + 1]
-        plain[k : k + 1, :] = row
-        scaled[k : k + 1, :] = ready
-        for tile in range(home, modes // 8):
-            column = tiles[tile][:, k : k + 1]
-            if tile == home:
-                column = jnp.where(rows[:, 0:1] > line, column, 0.0)
-            tiles[tile] = tiles[tile] - column * ready
+    count = modes // 8
+    for home in range(count):
+        columns = [
+            [
+                jnp.broadcast_to(
+                    tiles[tile][:, 8 * home + j : 8 * home + j + 1], (8, 2 * modes)
+                )
+                for tile in range(home, count)
+            ]
+            for j in range(8)
+        ]
+        for j in range(8):
+            k = 8 * home + j
+            inverse = 1.0 / columns[j][0]
+            inverse = inverse[j : j + 1, :]
+            row = tiles[home][j : j + 1, :]
+            ready = row * inverse
+            plain[k : k + 1, :] = row
+            scaled[k : k + 1, :] = ready
+            factors = [jnp.where(rows > j, columns[j][0], 0.0)] + columns[j][1:]
+            for later in range(j + 1, 8):
+                share = columns[j][0][later : later + 1, :] * inverse
+                columns[later] = [c - f * share for c, f in zip(columns[later], factors)]
+            for tile in range(home, count):
+                tiles[tile] = tiles[tile] - factors[tile - home] * ready
     inverse_ref[...] = lax.dot_general(
         plain[:, modes:], scaled[:, modes:], (((0,), (0,)), ((), ())),
         precision=HIGHEST, preferred_element_type=jnp.float32,
@@ -369,6 +499,7 @@
 
 WHOLE = pl.BlockSpec(memory_space=pltpu.VMEM)
 FAR = pl.BlockSpec(memory_space=pltpu.HBM)
+LOOSE = pl.BlockSpec(memory_space=pl.ANY)
 SCALAR = pl.BlockSpec(memory_space=pltpu.SMEM)
 
 
@@ -397,81 +528,136 @@
     wide = modes * 8
     basis_bytes = basis.size * 2
 
-    sides = 1 if walls == 2 else 2
-    kept, *faces = pl.pallas_call(
-        functools.partial(face_kernel, sides == 2),
-        out_shape=[shape(windows.shape, f32)]
-        + [shape((count, fields, REACH, layers, cells), f32)] * 2
-        + [shape(windows.shape, f32)] * sides,
-        in_specs=[SCALAR, FAR],
-        out_specs=[WHOLE] * (3 + sides),
+    to_right = [(i, (i + 1) % ring) for i in range(ring)]
+    to_left = [((i + 1) % ring, i) for i in range(ring)]
+    edge_shape = shape((count, fields, REACH, layers, cells), f32)
+    face_scratch = [pltpu.VMEM((fields, planes, layers, cells), f32)]
+    face_cost = cost(10_000_000, 10 * windows.size)
+    if paired:
+        swap = [(0, 1), (1, 0)]
+        group_shape = shape((fields, 48, cells), bf16)
+        kept, to_next, to_last, near_group, later_group = pl.pallas_call(
+            paired_face_kernel,
+            out_shape=[shape(windows.shape, f32)] + [edge_shape] * 2 + [group_shape] * 2,
+            in_specs=[SCALAR, FAR],
+            out_specs=[WHOLE] * 5,
+            scratch_shapes=face_scratch
+            + [pltpu.VMEM((2, fields, 16, cells), f32), pltpu.SemaphoreType.DMA((count,))],
+            compiler_params=params(16),
+            cost_estimate=face_cost,
+            name="faces",
+        )(place, windows)
+        near_group = lax.ppermute(near_group, "analysis", swap)
+        from_left = lax.ppermute(to_next, "solver", to_right)
+        from_right = lax.ppermute(to_last, "solver", to_left)
+        later_group = lax.ppermute(later_group, "analysis", swap)
+    else:
+        kept, to_next, to_last, up, down = pl.pallas_call(
+            functools.partial(face_kernel, True),
+            out_shape=[shape(windows.shape, f32)]
+            + [edge_shape] * 2
+            + [shape(windows.shape, f32)] * 2,
+            in_specs=[SCALAR, FAR],
+            out_specs=[WHOLE] * 5,
+            scratch_shapes=face_scratch + [pltpu.SemaphoreType.DMA((count,))],
+            compiler_params=params(16),
+            cost_estimate=face_cost,
+            name="faces",
+        )(place, windows)
+        wall_terms = [
+            lax.ppermute(up, "analysis", [(i, i + 1) for i in range(walls - 1)]),
+            lax.ppermute(down, "analysis", [(i + 1, i) for i in range(walls - 1)]),
+        ]
+        from_left = lax.ppermute(to_next, "solver", to_right)
+        from_right = lax.ppermute(to_last, "solver", to_left)
+
+    early = 2
+    gram_flops = 2 * wide * wide * cells * tiles
+    inner, right, left, basis = pl.pallas_call(
+        functools.partial(inner_gram_kernel, early),
+        out_shape=[
+            shape(windows.shape, f32),
+            shape((wide, wide // 2), f32),
+            shape((wide // 2, wide // 2), f32),
+            shape(basis.shape, bf16),
+        ],
+        in_specs=[WHOLE, FAR],
+        out_specs=[WHOLE] * 4,
         scratch_shapes=[
             pltpu.VMEM((fields, planes, layers, cells), f32),
-            pltpu.SemaphoreType.DMA((count,)),
-        ],
-        compiler_params=params(16),
-        cost_estimate=cost(10_000_000, 10 * windows.size),
-        name="faces",
-    )(place, windows)
-    to_right = [(i, (i + 1) % ring) for i in range(ring)]
-    to_left = [((i + 1) % ring, i) for i in range(ring)]
-    upward = [(i, i + 1) for i in range(walls - 1)]
-    downward = [(i + 1, i) for i in range(walls - 1)]
-    if sides == 1:
-        wall_terms = [lax.ppermute(faces[2], "analysis", upward + downward)]
-    else:
-        wall_terms = [
-            lax.ppermute(faces[2], "analysis", upward),
-            lax.ppermute(faces[3], "analysis", downward),
-        ]
-    from_left = lax.ppermute(faces[0], "solver", to_right)
-    from_right = lax.ppermute(faces[1], "solver", to_left)
-
-    inner, gram, basis = pl.pallas_call(
-        inner_gram_kernel,
-        out_shape=[shape(windows.shape, f32), shape((modes, LANES), f32), shape(basis.shape, bf16)],
-        in_specs=[WHOLE, FAR],
-        out_specs=[WHOLE] * 3,
-        scratch_shapes=[
-            pltpu.VMEM((fields, planes, layers, cells), f32),
-            pltpu.VMEM((wide // LANES, wide, LANES), f32),
             pltpu.SemaphoreType.DMA((fields,)),
         ],
         compiler_params=params(40),
-        cost_estimate=cost(2 * wide * wide * cells * tiles, 2 * basis_bytes),
+        cost_estimate=cost(gram_flops // 2, 2 * basis_bytes),
         name="inner_gram",
     )(kept, basis)
+
+    def rest_of_gram(after):
+        return pl.pallas_call(
+            functools.partial(gram_kernel, early, fields),
+            out_shape=shape((modes, LANES), f32),
+            in_specs=[LOOSE] + [WHOLE] * 3,
+            out_specs=WHOLE,
+            scratch_shapes=[pltpu.VMEM((wide // LANES, wide, LANES), f32)],
+            compiler_params=params(24),
+            cost_estimate=cost(gram_flops // 2, basis_bytes),
+            name="gram",
+        )(after, right, left, basis)
+
+    join_cost = cost(1_000_000, 16 * windows.size)
+    if paired:
+        half_shape = (count, fields, planes * layers // 2, cells)
+
+        def join(own, after, group, *base):
+            return pl.pallas_call(
+                functools.partial(paired_join_kernel, own),
+                out_shape=[shape(windows.shape, f32), shape(half_shape, bf16)],
+                in_specs=[SCALAR, LOOSE] + [WHOLE] * 4 + [FAR] * len(base),
+                out_specs=[FAR, WHOLE],
+                scratch_shapes=[
+                    pltpu.VMEM((count, fields, planes // 2, layers, cells), f32),
+                    pltpu.SemaphoreType.DMA,
+                ],
+                input_output_aliases={6: 0} if base else {},
+                compiler_params=params(16),
+                cost_estimate=join_cost,
+                name="join_own" if own else "join_given",
+            )(place, after, inner, from_left, from_right, group, *base)
+
+        next_windows, given = join(False, place, near_group)
+        got = lax.ppermute(given, "analysis", swap)
+        gram = rest_of_gram(given)
+    else:
+        next_windows = pl.pallas_call(
+            functools.partial(join_kernel, 2),
+            out_shape=shape(windows.shape, f32),
+            in_specs=[WHOLE] * 5,
+            out_specs=WHOLE,
+            compiler_params=params(16),
+            cost_estimate=join_cost,
+            name="join",
+        )(inner, from_left, from_right, *wall_terms)
+        gram = rest_of_gram(place)
     *near, far = bits(ring)
     gram_far = lax.ppermute(gram, "solver", [(i, i ^ far) for i in range(ring)])
-    half_shape = (count, fields, planes * layers // 2, cells)
-    joined = pl.pallas_call(
-        functools.partial(join_kernel, sides, paired),
-        out_shape=[shape(windows.shape, f32)] + ([shape(half_shape, bf16)] * 2 if paired else []),
-        in_specs=[SCALAR] + [WHOLE] * (3 + sides),
-        out_specs=[WHOLE] * (3 if paired else 1),
-        compiler_params=params(16),
-        cost_estimate=cost(1_000_000, 16 * windows.size),
-        name="join",
-    )(place, inner, from_left, from_right, *wall_terms)
-    next_windows = joined[0]
-
-    sums_shape = shape((modes + 8, LANES), f32)
+    if paired:
+        next_windows, own = join(True, gram, later_group, next_windows)
+
+    sums_shape = shape((8, LANES), f32)
     snaps_shape = shape((tiles, 2 * 8, cells), bf16)
     scratch = [pltpu.VMEM((LANES, LANES), f32), pltpu.VMEM((1, wide, LANES), f32)]
     project_cost = cost(2 * wide * 16 * cells * tiles, basis_bytes)
     if paired:
-        own, given = joined[1], joined[2]
-        got = lax.ppermute(given, "analysis", [(0, 1), (1, 0)])
         sums, snaps = pl.pallas_call(
             functools.partial(project_kernel, True),
             out_shape=[sums_shape, snaps_shape],
-            in_specs=[SCALAR] + [WHOLE] * 5,
+            in_specs=[SCALAR] + [WHOLE] * 3,
             out_specs=[WHOLE] * 2,
             scratch_shapes=scratch,
             compiler_params=params(16),
             cost_estimate=project_cost,
             name="project",
-        )(place, gram, gram_far, own, got, basis)
+        )(place, own, got, basis)
     else:
         relaid = lax.all_to_all(
             next_windows.astype(bf16), "analysis", split_axis=2, concat_axis=3, tiled=True
@@ -481,13 +667,22 @@
         sums = pl.pallas_call(
             functools.partial(project_kernel, False),
             out_shape=sums_shape,
-            in_specs=[SCALAR] + [WHOLE] * 4,
+            in_specs=[SCALAR] + [WHOLE] * 2,
             out_specs=WHOLE,
             scratch_shapes=scratch,
             compiler_params=params(16),
             cost_estimate=project_cost,
             name="project",
-        )(place, gram, gram_far, snaps, basis)
+        )(place, snaps, basis)
+    sums = pl.pallas_call(
+        merge_kernel,
+        out_shape=shape((modes + 8, LANES), f32),
+        in_specs=[WHOLE] * 3,
+        out_specs=WHOLE,
+        compiler_params=params(16),
+        cost_estimate=cost(10_000, 8 * modes * LANES),
+        name="merge",
+    )(gram, gram_far, sums)
     for bit in bits(walls):
         sums = swap_added(sums, "analysis", bit)
     for bit in near:

time: 56.8 us -> 50.9 us (0.90)
  Pallas kernels: 26.1 us -> 22.2 us
  starting transfers between devices: 18.2 us -> 15.3 us
  waiting for transfers between devices: 10.5 us -> 11.3 us
    pallas_call x1, Pallas kernels: 5.51 us -> 1.77 us  [body(): pl.pallas_call(inverse_kernel, out_shape=shape((modes, modes), f32), in_s...]
    ppermute x5, waiting for transfers between devices: 8.23 us -> 11.3 us  [swap_added(): lax.ppermute(value, axis, [(i, i ^ bit) for i in range(count)])]
    ppermute x5, starting transfers between devices: 7.5 us -> 4.9 us  [swap_added(): lax.ppermute(value, axis, [(i, i ^ bit) for i in range(count)])]
    ppermute x1, waiting for transfers between devices: 2.22 us -> 0.01 us  [body(): gram_far = lax.ppermute(gram, 'solver', [(i, i ^ far) for i in range(ring)])]
    ppermute x1, starting transfers between devices: 2.59 us -> 0.86 us  [body(): gram_far = lax.ppermute(gram, 'solver', [(i, i ^ far) for i in range(ring)])]
    ppermute x4 -> x5, starting transfers between devices: 8.07 us -> 9.52 us  [the longest x1 5.06 us: body(): from_right = lax.ppermute(to_last, 'solver', to_left)]
    pallas_call x3 -> x6, Pallas kernels: 13.4 us -> 13.2 us  [the longest x1 6.83 us: body(): pl.pallas_call(functools.partial(inner_gram_kernel, early), out_shape=[sh...]
  transfers between devices with their start and end apart: 10 -> 11, of which waited for: 5 -> 5; matrix products, arithmetic and copies ran while one was open for 0% -> 0% of each run, Pallas kernels for 30% -> 33%
where the time goes in v5:
time: 50.9 us; the launch traced here: 50.7 us
  Pallas kernels  22.2 us (44%)
  starting transfers between devices  15.3 us (30%)
  waiting for transfers between devices  11.3 us (22%)
  local copies, waits for them, and re-layouts  1.08 us (2%)
  between operations  0.75 us (1%)
    ppermute x5, waiting for transfers between devices, swap_added(): lax.ppermute(value, axis, [(i, i ^ bit) for i in range(count)])  11.3 us
    pallas_call x1, Pallas kernels, body(): pl.pallas_call(functools.partial(inner_gram_kernel, early), out_shape=[sh...  6.83 us
    ppermute x1, starting transfers between devices, body(): from_right = lax.ppermute(to_last, 'solver', to_left)  5.06 us
    ppermute x5, starting transfers between devices, swap_added(): lax.ppermute(value, axis, [(i, i ^ bit) for i in range(count)])  4.9 us
    pallas_call x1, Pallas kernels, body(): pl.pallas_call(functools.partial(finish_kernel, rows_total), out_shape=[s...  4.18 us
    pallas_call x1, Pallas kernels, rest_of_gram(): pl.pallas_call(functools.partial(gram_kernel, early, fields), out_shape=s...  3.19 us
    pallas_call x1, Pallas kernels, body(): pl.pallas_call(functools.partial(project_kernel, True), out_shape=[sums_s...  3.09 us
    ppermute x1, starting transfers between devices, body(): got = lax.ppermute(given, 'analysis', swap)  1.94 us
  transfers between devices with their start and end apart: 11, of which 5 were waited for; matrix products, arithmetic and copies ran while one was open for 0% of the time, Pallas kernels for 33%

profile of v5, /device:TPU:0, one launch (start us, length us, event | category | flops | bytes accessed | tf_op | source)
XLA Modules:
  0.0 50.7 jit_solution(16758796606046680293)
XLA Ops:
  0.6 1.1 %copy-done = f32[2,5,8,4,512]{4,3,2,1,0:T(4,128)S(1)} copy-done((f32[2,5,8,4,512]{4,3,2,1,0:T(4,128)S(1)}, f32[2,5,8,4,512]{4,3,2,1,0:T(4,128)}, u32[]{:S(2)}) %copy-start) | copy-done | bytes 655384
  1.7 1.3 %faces.1 = (f32[2,5,8,4,512]{4,3,2,1,0:T(4,128)S(1)}, f32[2,5,4,4,512]{4,3,2,1,0:T(4,128)S(1)}, f32[2,5,4,4,512]{4,3,2,1,0:T(4,128)S(1)}, bf16[5,48,512]{2,1,0:T(8,128)(2,1)S(1)}, bf16[5,48,512]{2,1,0:T(8,128)(2,1)S(1)}) custom-call(s32[1]{0:T(128)} %bitcast.where_ref._, f32[2,5,8,4,512]{4,3,2,1,0:T(4,128)S(1)} %copy-done), custom_call_target="tpu_custom_call" | custom-call | flops 10000000 | bytes 1638400 | tf_op jit(solution)/shard_map/faces/pallas_call | solution.py:539
  3.1 0.5 collective-permute-start
  3.6 5.1 %collective-permute-start.1 = (f32[2,5,4,4,512]{4,3,2,1,0:T(4,128)S(1)}, f32[2,5,4,4,512]{4,3,2,1,0:T(4,128)S(1)}, u32[]{:S(2)}, u32[]{:S(2)}) collective-permute-start(f32[2,5,4,4,512]{4,3,2,1,0:T(4,128)S(1)} %get-tuple-element.25), channel_id=1, source_target_pairs={{2,0},{4,2},{6,4},{8,6},{10,8},{12,10},{14,12},{16,14},{18,16},{20... | collective-permute-start | bytes 983048 | tf_op jit(solution)/shard_map/ppermute | solution.py:552
  8.6 1.9 %collective-permute-start.2 = (bf16[5,48,512]{2,1,0:T(8,128)(2,1)S(1)}, bf16[5,48,512]{2,1,0:T(8,128)(2,1)S(1)}, u32[]{:S(2)}, u32[]{:S(2)}) collective-permute-start(bf16[5,48,512]{2,1,0:T(8,128)(2,1)S(1)} %get-tuple-element.26), channel_id=1, source_target_pairs={{0,1},{1,0},{2,3},{3,2},{4,5},{5,4},{6,7},{7,6},{8,9},{9,8},{10,11... | collective-permute-start | bytes 737288 | tf_op jit(solution)/shard_map/ppermute | solution.py:550
  10.5 0.2 collective-permute-start.3
  10.7 6.8 %inner_gram.1 = (f32[2,5,8,4,512]{4,3,2,1,0:T(4,128)S(1)}, f32[512,256]{1,0:T(8,128)S(1)}, f32[256,256]{1,0:T(8,128)S(1)}, bf16[64,20,8,512]{3,2,1,0:T(8,128)(2,1)S(1)}) custom-call(f32[2,5,8,4,512]{4,3,2,1,0:T(4,128)S(1)} %get-tuple-element.22.windows_ref, bf16[64,20,8,512]{3,2,1,0:T(8,128)(2,1)} %bitcast.3), custom_call_target="tpu_custom_call" | custom-call | flops 2684354560 | bytes 20971520 | tf_op jit(solution)/shard_map/inner_gram/pallas_call | solution.py:576
  17.5 0.9 %join_given.1 = (f32[2,5,8,4,512]{4,3,2,1,0:T(4,128)}, bf16[2,5,16,512]{3,2,1,0:T(8,128)(2,1)S(1)}) custom-call(s32[1]{0:T(128)} %bitcast.where_ref._, s32[1]{0:T(128)} %bitcast.where_ref._, f32[2,5,8,4,512]{4,3,2,1,0:T(4,128)S(1)} %get-tuple-element.23.part_ref, f32[2,5,4,4,512]{4,3,2,1,0:T(4,128)S(1)} %collective-permute-done.left_ref, ...), custom_call_target="tpu_custom_call" | custom-call | flops 1000000 | bytes 2621440 | tf_op jit(solution)/shard_map/join_given/pallas_call | solution.py:612
  18.5 1.9 %collective-permute-start.5 = (bf16[2,5,16,512]{3,2,1,0:T(8,128)(2,1)S(1)}, bf16[2,5,16,512]{3,2,1,0:T(8,128)(2,1)S(1)}, u32[]{:S(2)}, u32[]{:S(2)}) collective-permute-start(bf16[2,5,16,512]{3,2,1,0:T(8,128)(2,1)S(1)} %get-tuple-element.27._), channel_id=1, source_target_pairs={{0,1},{1,0},{2,3},{3,2},{4,5},{5,4},{6,7},{7,6},{8,9},{9,8},{10,11... | collective-permute-start | bytes 491528 | tf_op jit(solution)/shard_map/ppermute | solution.py:628
  20.4 3.2 %gram.1._.gram_ref = f32[64,128]{1,0:T(8,128)S(1)} custom-call(bf16[2,5,16,512]{3,2,1,0:T(8,128)(2,1)S(1)} %get-tuple-element.27._, f32[512,256]{1,0:T(8,128)S(1)} %get-tuple-element.28.right_ref, f32[256,256]{1,0:T(8,128)S(1)} %get-tuple-element.29.left_ref, bf16[64,20,8,512]{3,2,1,0:T(8,128)(2,1)S(1)} %get-tuple-element.30.basis_ref.rest_2_), custom_call_target="tpu_custom_call" | custom-call | flops 2684354560 | bytes 10485760 | tf_op jit(solution)/shard_map/gram/pallas_call | solution.py:596
  23.6 0.9 %collective-permute-start.4 = (f32[64,128]{1,0:T(8,128)S(1)}, f32[64,128]{1,0:T(8,128)S(1)}, u32[]{:S(2)}, u32[]{:S(2)}) collective-permute-start(f32[64,128]{1,0:T(8,128)S(1)} %gram.1._.gram_ref), channel_id=1, source_target_pairs={{0,16},{2,18},{4,20},{6,22},{8,24},{10,26},{12,28},{14,30},{16,0},... | collective-permute-start | bytes 98312 | tf_op jit(solution)/shard_map/ppermute | solution.py:642
  24.5 0.9 %join_own.1 = (f32[2,5,8,4,512]{4,3,2,1,0:T(4,128)}, bf16[2,5,16,512]{3,2,1,0:T(8,128)(2,1)S(1)}) custom-call(s32[1]{0:T(128)} %bitcast.where_ref._, f32[64,128]{1,0:T(8,128)S(1)} %gram.1._.gram_ref, f32[2,5,8,4,512]{4,3,2,1,0:T(4,128)S(1)} %get-tuple-element.23.part_ref, ...), custom_call_target="tpu_custom_call", output_to_operand_aliasing={{0}: (6, {})} | custom-call | flops 1000000 | bytes 2621440 | tf_op jit(solution)/shard_map/join_own/pallas_call | solution.py:612
  25.4 3.1 %project.1 = (f32[8,128]{1,0:T(8,128)S(1)}, bf16[20,16,512]{2,1,0:T(8,128)(2,1)S(1)}) custom-call(s32[1]{0:T(128)} %bitcast.where_ref._, bf16[2,5,16,512]{3,2,1,0:T(8,128)(2,1)S(1)} %get-tuple-element.34.rest_0_, bf16[2,5,16,512]{3,2,1,0:T(8,128)(2,1)S(1)} %collective-permute-done.5.rest_1_, bf16[64,20,8,512]{3,2,1,0:T(8,128)(2,1)S(1)} %get-tuple-element.30.basis_ref.rest_2_), custom_call_target="tpu_custom_call" | custom-call | flops 167772160 | bytes 10485760 | tf_op jit(solution)/shard_map/project/pallas_call | solution.py:651
  28.5 0.6 %collective-permute-start.6 = (f32[72,128]{1,0:T(8,128)S(1)}, f32[72,128]{1,0:T(8,128)S(1)}, u32[]{:S(2)}, u32[]{:S(2)}) collective-permute-start(f32[72,128]{1,0:T(8,128)S(1)} %merge.1), channel_id=1, source_target_pairs={{0,1},{1,0},{2,3},{3,2},{4,5},{5,4},{6,7},{7,6},{8,9},{9,8},{10,11... | collective-permute-start | bytes 110600 | tf_op jit(solution)/shard_map/ppermute | solution.py:508
  29.1 3.4 %collective-permute-done.6 = f32[72,128]{1,0:T(8,128)S(1)} collective-permute-done((f32[72,128]{1,0:T(8,128)S(1)}, f32[72,128]{1,0:T(8,128)S(1)}, u32[]{:S(2)}, u32[]{:S(2)}) %collective-permute-start.6) | collective-permute-done | bytes 36896 | tf_op jit(solution)/shard_map/ppermute | solution.py:508
  32.5 1.2 %collective-permute-done.7 = f32[72,128]{1,0:T(8,128)S(1)} collective-permute-done((f32[72,128]{1,0:T(8,128)S(1)}, f32[72,128]{1,0:T(8,128)S(1)}, u32[]{:S(2)}, u32[]{:S(2)}) %collective-permute-start.7) | collective-permute-done | bytes 36896 | tf_op jit(solution)/shard_map/ppermute | solution.py:508
  33.8 0.6 %collective-permute-start.8 = (f32[72,128]{1,0:T(8,128)S(1)}, f32[72,128]{1,0:T(8,128)S(1)}, u32[]{:S(2)}, u32[]{:S(2)}) collective-permute-start(f32[72,128]{1,0:T(8,128)S(1)} %add.16), channel_id=1, source_target_pairs={{0,4},{2,6},{4,0},{6,2},{8,12},{10,14},{12,8},{14,10},{16,20},{18,... | collective-permute-start | bytes 110600 | tf_op jit(solution)/shard_map/ppermute | solution.py:508
  34.4 3.4 %collective-permute-done.8 = f32[72,128]{1,0:T(8,128)S(1)} collective-permute-done((f32[72,128]{1,0:T(8,128)S(1)}, f32[72,128]{1,0:T(8,128)S(1)}, u32[]{:S(2)}, u32[]{:S(2)}) %collective-permute-start.8) | collective-permute-done | bytes 36896 | tf_op jit(solution)/shard_map/ppermute | solution.py:508
  37.7 1.6 %collective-permute-start.9 = (f32[72,128]{1,0:T(8,128)S(1)}, f32[72,128]{1,0:T(8,128)S(1)}, u32[]{:S(2)}, u32[]{:S(2)}) collective-permute-start(f32[72,128]{1,0:T(8,128)S(1)} %add.17), channel_id=1, source_target_pairs={{0,8},{2,10},{4,12},{6,14},{8,0},{10,2},{12,4},{14,6},{16,24},{18,... | collective-permute-start | bytes 110600 | tf_op jit(solution)/shard_map/ppermute | solution.py:508
  39.3 2.4 %collective-permute-done.9 = f32[72,128]{1,0:T(8,128)S(1)} collective-permute-done((f32[72,128]{1,0:T(8,128)S(1)}, f32[72,128]{1,0:T(8,128)S(1)}, u32[]{:S(2)}, u32[]{:S(2)}) %collective-permute-start.9) | collective-permute-done | bytes 36896 | tf_op jit(solution)/shard_map/ppermute | solution.py:508
  41.7 2.1 %collective-permute-start.10 = (f32[72,128]{1,0:T(8,128)S(1)}, f32[72,128]{1,0:T(8,128)S(1)}, u32[]{:S(2)}, u32[]{:S(2)}) collective-permute-start(f32[72,128]{1,0:T(8,128)S(1)} %add.18.sums_ref), channel_id=1, source_target_pairs={{0,16},{2,18},{4,20},{6,22},{8,24},{10,26},{12,28},{14,30},{16,0},... | collective-permute-start | bytes 110600 | tf_op jit(solution)/shard_map/ppermute | solution.py:508
  43.8 1.8 %inverse.1.inverse_ref = f32[64,64]{1,0:T(8,128)S(1)} custom-call(f32[72,128]{1,0:T(8,128)S(1)} %add.18.sums_ref), custom_call_target="tpu_custom_call" | custom-call | flops 20000000 | bytes 32768 | tf_op jit(solution)/shard_map/inverse/pallas_call | solution.py:690
  45.6 0.9 %collective-permute-done.10 = f32[72,128]{1,0:T(8,128)S(1)} collective-permute-done((f32[72,128]{1,0:T(8,128)S(1)}, f32[72,128]{1,0:T(8,128)S(1)}, u32[]{:S(2)}, u32[]{:S(2)}) %collective-permute-start.10) | collective-permute-done | bytes 36896 | tf_op jit(solution)/shard_map/ppermute | solution.py:508
  46.6 4.2 %finish.1 = (f32[2,20,8,512]{3,2,1,0:T(8,128)}, f32[2,64]{1,0:T(2,128)}, f32[2,2]{1,0:T(2,128)}) custom-call(f32[72,128]{1,0:T(8,128)S(1)} %add.19.projected_ref, f32[72,128]{1,0:T(8,128)S(1)} %add.18.sums_ref, f32[64,64]{1,0:T(8,128)S(1)} %inverse.1.inverse_ref, bf16[20,16,512]{2,1,0:T(8,128)(2,1)S(1)} %get-tuple-element.36.snaps_ref, ...), custom_call_target="tpu_custom_call" | custom-call | flops 335544320 | bytes 11796480 | tf_op jit(solution)/shard_map/finish/pallas_call | solution.py:703
  (14 shorter events, 0.1 us)
Async XLA Ops:
  0.6 1.1 %copy-start = (f32[2,5,8,4,512]{4,3,2,1,0:T(4,128)S(1)}, f32[2,5,8,4,512]{4,3,2,1,0:T(4,128)}, u32[]{:S(2)}) copy-start(f32[2,5,8,4,512]{4,3,2,1,0:T(4,128)} %source_ref.1) | copy-start | bytes 1966084
  3.1 14.4 %collective-permute-start = (f32[2,5,4,4,512]{4,3,2,1,0:T(4,128)S(1)}, f32[2,5,4,4,512]{4,3,2,1,0:T(4,128)S(1)}, u32[]{:S(2)}, u32[]{:S(2)}) collective-permute-start(f32[2,5,4,4,512]{4,3,2,1,0:T(4,128)S(1)} %get-tuple-element.24), channel_id=1, source_target_pairs={{0,2},{2,4},{4,6},{6,8},{8,10},{10,12},{12,14},{14,16},{16,18},{18... | collective-permute-start | bytes 983048 | tf_op jit(solution)/shard_map/ppermute | solution.py:551
  3.6 13.9 %collective-permute-start.1 = (f32[2,5,4,4,512]{4,3,2,1,0:T(4,128)S(1)}, f32[2,5,4,4,512]{4,3,2,1,0:T(4,128)S(1)}, u32[]{:S(2)}, u32[]{:S(2)}) collective-permute-start(f32[2,5,4,4,512]{4,3,2,1,0:T(4,128)S(1)} %get-tuple-element.25), channel_id=1, source_target_pairs={{2,0},{4,2},{6,4},{8,6},{10,8},{12,10},{14,12},{16,14},{18,16},{20... | collective-permute-start | bytes 983048 | tf_op jit(solution)/shard_map/ppermute | solution.py:552
  8.6 8.9 %collective-permute-start.2 = (bf16[5,48,512]{2,1,0:T(8,128)(2,1)S(1)}, bf16[5,48,512]{2,1,0:T(8,128)(2,1)S(1)}, u32[]{:S(2)}, u32[]{:S(2)}) collective-permute-start(bf16[5,48,512]{2,1,0:T(8,128)(2,1)S(1)} %get-tuple-element.26), channel_id=1, source_target_pairs={{0,1},{1,0},{2,3},{3,2},{4,5},{5,4},{6,7},{7,6},{8,9},{9,8},{10,11... | collective-permute-start | bytes 737288 | tf_op jit(solution)/shard_map/ppermute | solution.py:550
  10.5 13.9 %collective-permute-start.3 = (bf16[5,48,512]{2,1,0:T(8,128)(2,1)S(1)}, bf16[5,48,512]{2,1,0:T(8,128)(2,1)S(1)}, u32[]{:S(2)}, u32[]{:S(2)}) collective-permute-start(bf16[5,48,512]{2,1,0:T(8,128)(2,1)S(1)} %get-tuple-element.31), channel_id=1, source_target_pairs={{0,1},{1,0},{2,3},{3,2},{4,5},{5,4},{6,7},{7,6},{8,9},{9,8},{10,11... | collective-permute-start | bytes 737288 | tf_op jit(solution)/shard_map/ppermute | solution.py:553
  18.5 6.9 %collective-permute-start.5 = (bf16[2,5,16,512]{3,2,1,0:T(8,128)(2,1)S(1)}, bf16[2,5,16,512]{3,2,1,0:T(8,128)(2,1)S(1)}, u32[]{:S(2)}, u32[]{:S(2)}) collective-permute-start(bf16[2,5,16,512]{3,2,1,0:T(8,128)(2,1)S(1)} %get-tuple-element.27._), channel_id=1, source_target_pairs={{0,1},{1,0},{2,3},{3,2},{4,5},{5,4},{6,7},{7,6},{8,9},{9,8},{10,11... | collective-permute-start | bytes 491528 | tf_op jit(solution)/shard_map/ppermute | solution.py:628
  23.6 4.9 %collective-permute-start.4 = (f32[64,128]{1,0:T(8,128)S(1)}, f32[64,128]{1,0:T(8,128)S(1)}, u32[]{:S(2)}, u32[]{:S(2)}) collective-permute-start(f32[64,128]{1,0:T(8,128)S(1)} %gram.1._.gram_ref), channel_id=1, source_target_pairs={{0,16},{2,18},{4,20},{6,22},{8,24},{10,26},{12,28},{14,30},{16,0},... | collective-permute-start | bytes 98312 | tf_op jit(solution)/shard_map/ppermute | solution.py:642
  28.5 4.0 %collective-permute-start.6 = (f32[72,128]{1,0:T(8,128)S(1)}, f32[72,128]{1,0:T(8,128)S(1)}, u32[]{:S(2)}, u32[]{:S(2)}) collective-permute-start(f32[72,128]{1,0:T(8,128)S(1)} %merge.1), channel_id=1, source_target_pairs={{0,1},{1,0},{2,3},{3,2},{4,5},{5,4},{6,7},{7,6},{8,9},{9,8},{10,11... | collective-permute-start | bytes 110600 | tf_op jit(solution)/shard_map/ppermute | solution.py:508
  32.5 1.2 %collective-permute-start.7 = (f32[72,128]{1,0:T(8,128)S(1)}, f32[72,128]{1,0:T(8,128)S(1)}, u32[]{:S(2)}, u32[]{:S(2)}) collective-permute-start(f32[72,128]{1,0:T(8,128)S(1)} %add.15), channel_id=1, source_target_pairs={{0,2},{2,0},{4,6},{6,4},{8,10},{10,8},{12,14},{14,12},{16,18},{18,... | collective-permute-start | bytes 110600 | tf_op jit(solution)/shard_map/ppermute | solution.py:508
  33.8 4.0 %collective-permute-start.8 = (f32[72,128]{1,0:T(8,128)S(1)}, f32[72,128]{1,0:T(8,128)S(1)}, u32[]{:S(2)}, u32[]{:S(2)}) collective-permute-start(f32[72,128]{1,0:T(8,128)S(1)} %add.16), channel_id=1, source_target_pairs={{0,4},{2,6},{4,0},{6,2},{8,12},{10,14},{12,8},{14,10},{16,20},{18,... | collective-permute-start | bytes 110600 | tf_op jit(solution)/shard_map/ppermute | solution.py:508
  37.7 4.0 %collective-permute-start.9 = (f32[72,128]{1,0:T(8,128)S(1)}, f32[72,128]{1,0:T(8,128)S(1)}, u32[]{:S(2)}, u32[]{:S(2)}) collective-permute-start(f32[72,128]{1,0:T(8,128)S(1)} %add.17), channel_id=1, source_target_pairs={{0,8},{2,10},{4,12},{6,14},{8,0},{10,2},{12,4},{14,6},{16,24},{18,... | collective-permute-start | bytes 110600 | tf_op jit(solution)/shard_map/ppermute | solution.py:508
  41.7 4.9 %collective-permute-start.10 = (f32[72,128]{1,0:T(8,128)S(1)}, f32[72,128]{1,0:T(8,128)S(1)}, u32[]{:S(2)}, u32[]{:S(2)}) collective-permute-start(f32[72,128]{1,0:T(8,128)S(1)} %add.18.sums_ref), channel_id=1, source_target_pairs={{0,16},{2,18},{4,20},{6,22},{8,24},{10,26},{12,28},{14,30},{16,0},... | collective-permute-start | bytes 110600 | tf_op jit(solution)/shard_map/ppermute | solution.py:508

commit v6 on v5

--- a/solution.py
+++ b/solution.py
@@ -31,8 +31,8 @@
     return made
 
 
-def primitives(windows_ref, w, x):
-    density, mx, my, mz, energy = (windows_ref[w, f, x] for f in range(5))
+def primitives(fields):
+    density, mx, my, mz, energy = fields
     inverse = 1.0 / density
     ux, uy, uz = mx * inverse, my * inverse, mz * inverse
     pressure = PRESSURE_FACTOR * (energy - 0.5 * (mx * ux + my * uy + mz * uz))
@@ -74,7 +74,7 @@
     for w in range(windows):
         copies[w].wait()
         for x in range(planes):
-            parts = primitives(windows_ref, w, x)
+            parts = primitives([windows_ref[w, f, x] for f in range(5)])
             for f, value in enumerate(flux(parts, 0)):
                 scratch[f, x] = value
             for f, value in enumerate(flux(parts, 1)):
@@ -131,7 +131,7 @@
             upper = [[] for _ in range(5)]
             lower = [[] for _ in range(5)]
             for x in range(half):
-                parts = primitives(windows_ref, w, base + x)
+                parts = primitives([windows_ref[w, f, base + x] for f in range(5)])
                 for f, value in enumerate(flux(parts, 0)):
                     scratch[f, base + x] = value
                 for f, value in enumerate(flux(parts, 1)):
@@ -171,32 +171,40 @@
 
 def inner_part(windows_ref, part_ref, scratch):
     windows, _, planes, layers, cells = windows_ref.shape
-    tile = (layers, cells)
-    wall = [
-        row_weights(tile, [weight(j - i) for i in range(layers)]) for j in range(layers)
-    ]
-    for w in range(windows):
+    tile = (windows * layers, cells)
+    walls = {
+        k: row_weights(
+            tile, [weight(k) if 0 <= i + k < layers else 0.0 for i in range(layers)] * windows
+        )
+        for k in range(-REACH, REACH + 1)
+        if 0 < abs(k) < layers
+    }
+    for x in range(planes):
+        fields = [
+            jnp.concatenate([windows_ref[w, f, x] for w in range(windows)], axis=0)
+            for f in range(5)
+        ]
+        parts = primitives(fields)
+        for f, value in enumerate(flux(parts, 0)):
+            scratch[f, x] = value
+        flux_y, flux_z = flux(parts, 1), flux(parts, 2)
+        for f in range(5):
+            total = fields[f]
+            for k, line in walls.items():
+                total = total + line * pltpu.roll(flux_y[f], -k % tile[0], 0)
+            for k in range(1, REACH + 1):
+                total = total + weight(k) * (
+                    pltpu.roll(flux_z[f], cells - k, 1) - pltpu.roll(flux_z[f], k, 1)
+                )
+            scratch[5 + f, x] = total
+    for f in range(5):
         for x in range(planes):
-            parts = primitives(windows_ref, w, x)
-            for f, value in enumerate(flux(parts, 0)):
-                scratch[f, x] = value
-            flux_y, flux_z = flux(parts, 1), flux(parts, 2)
-            for f in range(5):
-                total = windows_ref[w, f, x]
-                for j in range(layers):
-                    total = total + wall[j] * flux_y[f][j : j + 1, :]
-                for k in range(1, REACH + 1):
-                    total = total + weight(k) * (
-                        pltpu.roll(flux_z[f], cells - k, 1) - pltpu.roll(flux_z[f], k, 1)
-                    )
-                part_ref[w, f, x] = total
-        for f in range(5):
-            for x in range(planes):
-                total = part_ref[w, f, x]
-                for k in range(-REACH, REACH + 1):
-                    if k and 0 <= x + k < planes:
-                        total = total + weight(k) * scratch[f, x + k]
-                part_ref[w, f, x] = total
+            total = scratch[5 + f, x]
+            for k in range(-REACH, REACH + 1):
+                if k and 0 <= x + k < planes:
+                    total = total + weight(k) * scratch[f, x + k]
+            for w in range(windows):
+                part_ref[w, f, x] = total[layers * w : layers * (w + 1)]
 
 
 def gram_blocks(basis_ref, chunks, per_chunk, right, left):
@@ -276,9 +284,8 @@
 
 
 def paired_join_kernel(
-    own, where_ref, _, part_ref, left_ref, right_ref, group_ref, *rest
+    own, where_ref, _, part_ref, left_ref, right_ref, group_ref, made, snaps_ref
 ):
-    next_ref, snaps_ref, made, sem = rest[-4:]
     windows, _, planes, layers, cells = part_ref.shape
     half = planes // 2
     first = where_ref[0] == 0
@@ -304,9 +311,6 @@
                 made[w, f, x] = total
                 done.append(total)
             snaps_ref[w, f] = jnp.concatenate(done, axis=0).astype(jnp.bfloat16)
-    copy = pltpu.make_async_copy(made, next_ref.at[:, :, pl.ds(base, half)], sem)
-    copy.start()
-    copy.wait()
 
 
 def same_layer(shape):
@@ -333,8 +337,20 @@
 
 def project_kernel(paired, where_ref, *rest):
     if paired:
-        own_ref, got_ref, basis_ref, sums_ref, snaps_ref, square, wide_sums = rest
+        (
+            own_ref, got_ref, next_own_ref, next_given_ref, basis_ref,
+            sums_ref, snaps_ref, next_ref, square, wide_sums, sems,
+        ) = rest
         first = where_ref[0] == 0
+        half = next_own_ref.shape[2]
+        copies = []
+        for i, (source, base) in enumerate(
+            ((next_own_ref, half * where_ref[0]), (next_given_ref, half * (1 - where_ref[0])))
+        ):
+            copies.append(
+                pltpu.make_async_copy(source, next_ref.at[:, :, pl.ds(base, half)], sems.at[i])
+            )
+            copies[i].start()
         for w in range(own_ref.shape[0]):
             for f in range(own_ref.shape[1]):
                 own = own_ref[w, f].astype(jnp.float32)
@@ -347,6 +363,7 @@
                     ).astype(jnp.bfloat16)
     else:
         snaps_ref, basis_ref, sums_ref, square, wide_sums = rest
+        copies = []
     modes, tiles = basis_ref.shape[:2]
     columns = snaps_ref.shape[1]
     total = jnp.zeros((modes * 8, columns), jnp.float32)
@@ -375,6 +392,8 @@
     sums_ref[...] = jnp.concatenate(
         [sums, jnp.zeros((6, sums.shape[1]), jnp.float32)], axis=0
     )
+    for copy in copies:
+        copy.wait()
 
 
 def merge_kernel(gram_ref, far_ref, sums_ref, merged_ref):
@@ -383,7 +402,7 @@
     merged_ref[modes:] = sums_ref[...]
 
 
-def inverse_kernel(sums_ref, inverse_ref, plain, scaled):
+def inverse_kernel(sums_ref, inverse_ref, spread_ref, plain, scaled):
     modes = inverse_ref.shape[0]
     rows = lax.broadcasted_iota(jnp.int32, (8, 2 * modes), 0)
     lanes = lax.broadcasted_iota(jnp.int32, (8, 2 * modes), 1)
@@ -416,24 +435,42 @@
                 columns[later] = [c - f * share for c, f in zip(columns[later], factors)]
             for tile in range(home, count):
                 tiles[tile] = tiles[tile] - factors[tile - home] * ready
-    inverse_ref[...] = lax.dot_general(
-        plain[:, modes:], scaled[:, modes:], (((0,), (0,)), ((), ())),
-        precision=HIGHEST, preferred_element_type=jnp.float32,
+    exact = functools.partial(
+        lax.dot_general, precision=HIGHEST, preferred_element_type=jnp.float32
     )
+    plainly = (((1,), (0,)), ((), ()))
+    inverse = exact(plain[:, modes:], scaled[:, modes:], (((0,), (0,)), ((), ())))
+    square = (modes, modes)
+    eye = lax.broadcasted_iota(jnp.int32, square, 0) == lax.broadcasted_iota(jnp.int32, square, 1)
+    off = eye.astype(jnp.float32) - exact(sums_ref[0:modes, 0:modes], inverse, plainly)
+    inverse = inverse + exact(inverse, off, plainly)
+    inverse_ref[...] = inverse
+    wide = spread_ref.shape[1]
+    spread = (
+        lax.broadcasted_iota(jnp.int32, (modes, wide), 1) // 8
+        == lax.broadcasted_iota(jnp.int32, (modes, wide), 0)
+    ).astype(jnp.float32)
+    spread_ref[...] = exact(inverse, spread, plainly)
 
 
 def finish_kernel(
-    rows_total, projected_ref, sums_ref, inverse_ref, snaps_ref, basis_ref,
+    rows_total, projected_ref, sums_ref, inverse_ref, spread_ref, snaps_ref, basis_ref,
     modes_ref, solved_ref, factor_ref, made, sems,
 ):
     modes, tiles, _, cells = basis_ref.shape
     wide = modes * 8
     exact = functools.partial(jnp.dot, precision=HIGHEST, preferred_element_type=jnp.float32)
     projected = projected_ref[modes : modes + 8, 0:modes]
-    gram, inverse = sums_ref[0:modes, 0:modes], inverse_ref[...]
-    solved = exact(projected, inverse)
-    solved = solved + exact(projected - exact(solved, gram), inverse)
-    left = projected - exact(solved, gram)
+    lines = exact(projected, spread_ref[...])
+    full = jnp.concatenate(
+        [jnp.broadcast_to(lines[0:1], (8, wide)), jnp.broadcast_to(lines[1:2], (8, wide))],
+        axis=0,
+    )
+    full = jnp.where(same_layer(full.shape), full, 0.0)
+    upper = full.astype(jnp.bfloat16)
+    fit = jnp.concatenate([upper, (full - upper.astype(jnp.float32)).astype(jnp.bfloat16)], axis=0)
+    solved = exact(projected, inverse_ref[...])
+    left = projected - exact(solved, sums_ref[0:modes, 0:modes])
 
     def inner(p, i, q, j):
         return jnp.sum(p[i : i + 1] * q[j : j + 1], axis=1, keepdims=True)
@@ -454,22 +491,6 @@
     factor_ref[0:1, 1:2] = below / scaling
     factor_ref[1:2, 0:1] = jnp.zeros_like(first)
     factor_ref[1:2, 1:2] = second / scaling
-    spread = (
-        lax.broadcasted_iota(jnp.int32, (modes, wide), 1) // 8
-        == lax.broadcasted_iota(jnp.int32, (modes, wide), 0)
-    ).astype(jnp.float32)
-    scaled = jnp.concatenate(
-        [solved[0:1] * w00, solved[1:2] * w11 + solved[0:1] * w01, solved[2:8]], axis=0
-    )
-    lines = exact(scaled, spread)
-    full = jnp.concatenate(
-        [jnp.broadcast_to(lines[0:1], (8, wide)), jnp.broadcast_to(lines[1:2], (8, wide))],
-        axis=0,
-    )
-    full = jnp.where(same_layer(full.shape), full, 0.0)
-    upper = full.astype(jnp.bfloat16)
-    fit = jnp.concatenate([upper, (full - upper.astype(jnp.float32)).astype(jnp.bfloat16)], axis=0)
-
     chunks = sems.shape[0]
     per_chunk = tiles // chunks
     copies = []
@@ -478,8 +499,9 @@
             fitted = jnp.dot(fit, modes_of(basis_ref, t), preferred_element_type=jnp.float32)
             fitted = fitted[0:16] + fitted[16:32]
             snaps = snaps_ref[t].astype(jnp.float32)
-            made[0, t] = snaps[0:8] * w00 - fitted[0:8]
-            made[1, t] = snaps[8:16] * w11 + snaps[0:8] * w01 - fitted[8:16]
+            left_over = snaps - fitted
+            made[0, t] = left_over[0:8] * w00
+            made[1, t] = left_over[8:16] * w11 + left_over[0:8] * w01
         span = pl.ds(c * per_chunk, per_chunk)
         copies.append(
             pltpu.make_async_copy(made.at[:, span], modes_ref.at[:, span], sems.at[c])
@@ -584,7 +606,7 @@
         in_specs=[WHOLE, FAR],
         out_specs=[WHOLE] * 4,
         scratch_shapes=[
-            pltpu.VMEM((fields, planes, layers, cells), f32),
+            pltpu.VMEM((2 * fields, planes, count * layers, cells), f32),
             pltpu.SemaphoreType.DMA((fields,)),
         ],
         compiler_params=params(40),
@@ -608,23 +630,20 @@
     if paired:
         half_shape = (count, fields, planes * layers // 2, cells)
 
-        def join(own, after, group, *base):
+        half_next = shape((count, fields, planes // 2, layers, cells), f32)
+
+        def join(own, after, group):
             return pl.pallas_call(
                 functools.partial(paired_join_kernel, own),
-                out_shape=[shape(windows.shape, f32), shape(half_shape, bf16)],
-                in_specs=[SCALAR, LOOSE] + [WHOLE] * 4 + [FAR] * len(base),
-                out_specs=[FAR, WHOLE],
-                scratch_shapes=[
-                    pltpu.VMEM((count, fields, planes // 2, layers, cells), f32),
-                    pltpu.SemaphoreType.DMA,
-                ],
-                input_output_aliases={6: 0} if base else {},
+                out_shape=[half_next, shape(half_shape, bf16)],
+                in_specs=[SCALAR, LOOSE] + [WHOLE] * 4,
+                out_specs=[WHOLE] * 2,
                 compiler_params=params(16),
                 cost_estimate=join_cost,
                 name="join_own" if own else "join_given",
-            )(place, after, inner, from_left, from_right, group, *base)
-
-        next_windows, given = join(False, place, near_group)
+            )(place, after, inner, from_left, from_right, group)
+
+        next_given, given = join(False, place, near_group)
         got = lax.ppermute(given, "analysis", swap)
         gram = rest_of_gram(given)
     else:
@@ -638,26 +657,27 @@
             name="join",
         )(inner, from_left, from_right, *wall_terms)
         gram = rest_of_gram(place)
-    *near, far = bits(ring)
-    gram_far = lax.ppermute(gram, "solver", [(i, i ^ far) for i in range(ring)])
+    ring_bits = bits(ring)
+    lone = ring_bits.pop(1 if len(ring_bits) > 1 else 0)
+    gram_far = lax.ppermute(gram, "solver", [(i, i ^ lone) for i in range(ring)])
     if paired:
-        next_windows, own = join(True, gram, later_group, next_windows)
+        next_own, own = join(True, gram, later_group)
 
     sums_shape = shape((8, LANES), f32)
     snaps_shape = shape((tiles, 2 * 8, cells), bf16)
     scratch = [pltpu.VMEM((LANES, LANES), f32), pltpu.VMEM((1, wide, LANES), f32)]
     project_cost = cost(2 * wide * 16 * cells * tiles, basis_bytes)
     if paired:
-        sums, snaps = pl.pallas_call(
+        sums, snaps, next_windows = pl.pallas_call(
             functools.partial(project_kernel, True),
-            out_shape=[sums_shape, snaps_shape],
-            in_specs=[SCALAR] + [WHOLE] * 3,
-            out_specs=[WHOLE] * 2,
-            scratch_shapes=scratch,
+            out_shape=[sums_shape, snaps_shape, shape(windows.shape, f32)],
+            in_specs=[SCALAR] + [WHOLE] * 5,
+            out_specs=[WHOLE, WHOLE, FAR],
+            scratch_shapes=scratch + [pltpu.SemaphoreType.DMA((2,))],
             compiler_params=params(16),
             cost_estimate=project_cost,
             name="project",
-        )(place, own, got, basis)
+        )(place, own, got, next_own, next_given, basis)
     else:
         relaid = lax.all_to_all(
             next_windows.astype(bf16), "analysis", split_axis=2, concat_axis=3, tiled=True
@@ -685,19 +705,19 @@
     )(gram, gram_far, sums)
     for bit in bits(walls):
         sums = swap_added(sums, "analysis", bit)
-    for bit in near:
+    for bit in ring_bits:
         sums = swap_added(sums, "solver", bit)
-    inverse = pl.pallas_call(
+    inverse, spread = pl.pallas_call(
         inverse_kernel,
-        out_shape=shape((modes, modes), f32),
+        out_shape=[shape((modes, modes), f32), shape((modes, wide), f32)],
         in_specs=[WHOLE],
-        out_specs=WHOLE,
+        out_specs=[WHOLE] * 2,
         scratch_shapes=[pltpu.VMEM((modes, 2 * modes), f32)] * 2,
         compiler_params=params(16),
         cost_estimate=cost(20_000_000, 8 * modes * modes),
         name="inverse",
     )(sums)
-    projected = swap_added(sums, "solver", far)
+    projected = swap_added(sums, "solver", lone)
 
     rows_total = ring * walls * tiles * 8 * cells
     new_modes, solved, factor = pl.pallas_call(
@@ -707,7 +727,7 @@
             shape((count, modes), f32),
             shape((count, count), f32),
         ],
-        in_specs=[WHOLE] * 5,
+        in_specs=[WHOLE] * 6,
         out_specs=[FAR, WHOLE, WHOLE],
         scratch_shapes=[
             pltpu.VMEM((count, tiles, 8, cells), f32),
@@ -716,7 +736,7 @@
         compiler_params=params(16),
         cost_estimate=cost(2 * wide * 32 * cells * tiles, basis_bytes + 8 * windows.size),
         name="finish",
-    )(projected, sums, inverse, snaps, basis)
+    )(projected, sums, inverse, spread, snaps, basis)
     new_modes = new_modes.reshape(count, fields, pod_planes, pod_layers, cells)
     return next_windows, solved, new_modes, factor
 

time: 50.9 us -> 47.4 us (0.931)
  Pallas kernels: 22.2 us -> 19.2 us
  waiting for transfers between devices: 11.3 us -> 9.92 us
  starting transfers between devices: 15.3 us -> 16.3 us
    ppermute x5, waiting for transfers between devices: 11.3 us -> 8.49 us  [swap_added(): lax.ppermute(value, axis, [(i, i ^ bit) for i in range(count)])]
    ppermute x5, starting transfers between devices: 4.9 us -> 7.13 us  [swap_added(): lax.ppermute(value, axis, [(i, i ^ bit) for i in range(count)])]
    pallas_call x1, Pallas kernels: 6.83 us -> 5.53 us  [body(): pl.pallas_call(functools.partial(inner_gram_kernel, early), out_shape=[sh...]
    pallas_call x1, Pallas kernels: 4.18 us -> 3.18 us  [body(): pl.pallas_call(functools.partial(finish_kernel, rows_total), out_shape=[s...]
    ppermute x1, waiting for transfers between devices: 0.01 us -> 0.92 us  [body(): got = lax.ppermute(given, 'analysis', swap)]
    pallas_call x3, Pallas kernels: 3.61 us -> 2.78 us  [the longest x1 2.37 us: body(): pl.pallas_call(inverse_kernel, out_shape=[shape((modes, modes), f32), sha...]
    ppermute x1, starting transfers between devices: 0.86 us -> 0.07 us  [body(): lax.ppermute(gram, 'solver', [(i, i ^ lone) for i in range(ring)])]
  transfers between devices with their start and end apart: 11 -> 11, of which waited for: 5 -> 7; matrix products, arithmetic and copies ran while one was open for 0% -> 0% of each run, Pallas kernels for 33% -> 31%
where the time goes in v6:
time: 47.4 us; the launch traced here: 47.3 us
  Pallas kernels  19.2 us (41%)
  starting transfers between devices  16.3 us (34%)
  waiting for transfers between devices  9.92 us (21%)
  local copies, waits for them, and re-layouts  1.08 us (2%)
  between operations  0.74 us (2%)
    ppermute x5, waiting for transfers between devices, swap_added(): lax.ppermute(value, axis, [(i, i ^ bit) for i in range(count)])  8.49 us
    ppermute x5, starting transfers between devices, swap_added(): lax.ppermute(value, axis, [(i, i ^ bit) for i in range(count)])  7.13 us
    pallas_call x1, Pallas kernels, body(): pl.pallas_call(functools.partial(inner_gram_kernel, early), out_shape=[sh...  5.53 us
    ppermute x1, starting transfers between devices, body(): from_right = lax.ppermute(to_last, 'solver', to_left)  5.06 us
    pallas_call x1, Pallas kernels, rest_of_gram(): pl.pallas_call(functools.partial(gram_kernel, early, fields), out_shape=s...  3.19 us
    pallas_call x1, Pallas kernels, body(): pl.pallas_call(functools.partial(finish_kernel, rows_total), out_shape=[s...  3.18 us
    pallas_call x1, Pallas kernels, body(): pl.pallas_call(functools.partial(project_kernel, True), out_shape=[sums_s...  3.12 us
    pallas_call x1, Pallas kernels, body(): pl.pallas_call(inverse_kernel, out_shape=[shape((modes, modes), f32), sha...  2.37 us
  transfers between devices with their start and end apart: 11, of which 7 were waited for; matrix products, arithmetic and copies ran while one was open for 0% of the time, Pallas kernels for 31%

profile of v6, /device:TPU:0, one launch (start us, length us, event | category | flops | bytes accessed | tf_op | source)
XLA Modules:
  0.0 47.3 jit_solution(12471769760325918222)
XLA Ops:
  0.6 1.1 %copy-done = f32[2,5,8,4,512]{4,3,2,1,0:T(4,128)S(1)} copy-done((f32[2,5,8,4,512]{4,3,2,1,0:T(4,128)S(1)}, f32[2,5,8,4,512]{4,3,2,1,0:T(4,128)}, u32[]{:S(2)}) %copy-start) | copy-done | bytes 655384
  1.7 1.3 %faces.1 = (f32[2,5,8,4,512]{4,3,2,1,0:T(4,128)S(1)}, f32[2,5,4,4,512]{4,3,2,1,0:T(4,128)S(1)}, f32[2,5,4,4,512]{4,3,2,1,0:T(4,128)S(1)}, bf16[5,48,512]{2,1,0:T(8,128)(2,1)S(1)}, bf16[5,48,512]{2,1,0:T(8,128)(2,1)S(1)}) custom-call(s32[1]{0:T(128)} %bitcast.where_ref._, f32[2,5,8,4,512]{4,3,2,1,0:T(4,128)S(1)} %copy-done), custom_call_target="tpu_custom_call" | custom-call | flops 10000000 | bytes 1638400 | tf_op jit(solution)/shard_map/faces/pallas_call | solution.py:561
  3.1 0.5 %collective-permute-start = (f32[2,5,4,4,512]{4,3,2,1,0:T(4,128)S(1)}, f32[2,5,4,4,512]{4,3,2,1,0:T(4,128)S(1)}, u32[]{:S(2)}, u32[]{:S(2)}) collective-permute-start(f32[2,5,4,4,512]{4,3,2,1,0:T(4,128)S(1)} %get-tuple-element.27), channel_id=1, source_target_pairs={{0,2},{2,4},{4,6},{6,8},{8,10},{10,12},{12,14},{14,16},{16,18},{18... | collective-permute-start | bytes 983048 | tf_op jit(solution)/shard_map/ppermute | solution.py:573
  3.6 5.1 %collective-permute-start.1 = (f32[2,5,4,4,512]{4,3,2,1,0:T(4,128)S(1)}, f32[2,5,4,4,512]{4,3,2,1,0:T(4,128)S(1)}, u32[]{:S(2)}, u32[]{:S(2)}) collective-permute-start(f32[2,5,4,4,512]{4,3,2,1,0:T(4,128)S(1)} %get-tuple-element.28), channel_id=1, source_target_pairs={{2,0},{4,2},{6,4},{8,6},{10,8},{12,10},{14,12},{16,14},{18,16},{20... | collective-permute-start | bytes 983048 | tf_op jit(solution)/shard_map/ppermute | solution.py:574
  8.6 1.9 %collective-permute-start.2 = (bf16[5,48,512]{2,1,0:T(8,128)(2,1)S(1)}, bf16[5,48,512]{2,1,0:T(8,128)(2,1)S(1)}, u32[]{:S(2)}, u32[]{:S(2)}) collective-permute-start(bf16[5,48,512]{2,1,0:T(8,128)(2,1)S(1)} %get-tuple-element.29), channel_id=1, source_target_pairs={{0,1},{1,0},{2,3},{3,2},{4,5},{5,4},{6,7},{7,6},{8,9},{9,8},{10,11... | collective-permute-start | bytes 737288 | tf_op jit(solution)/shard_map/ppermute | solution.py:572
  10.5 0.2 collective-permute-start.3
  10.7 5.5 %inner_gram.1 = (f32[2,5,8,4,512]{4,3,2,1,0:T(4,128)S(1)}, f32[512,256]{1,0:T(8,128)S(1)}, f32[256,256]{1,0:T(8,128)S(1)}, bf16[64,20,8,512]{3,2,1,0:T(8,128)(2,1)S(1)}) custom-call(f32[2,5,8,4,512]{4,3,2,1,0:T(4,128)S(1)} %get-tuple-element.25.windows_ref, bf16[64,20,8,512]{3,2,1,0:T(8,128)(2,1)} %bitcast.3), custom_call_target="tpu_custom_call" | custom-call | flops 2684354560 | bytes 20971520 | tf_op jit(solution)/shard_map/inner_gram/pallas_call | solution.py:598
  16.2 0.5 %collective-permute-done.2.group_ref = bf16[5,48,512]{2,1,0:T(8,128)(2,1)S(1)} collective-permute-done((bf16[5,48,512]{2,1,0:T(8,128)(2,1)S(1)}, bf16[5,48,512]{2,1,0:T(8,128)(2,1)S(1)}, u32[]{:S(2)}, u32[]{:S(2)}) %collective-permute-start.2) | collective-permute-done | bytes 245792 | tf_op jit(solution)/shard_map/ppermute | solution.py:572
  16.7 0.2 join_given.1
  16.9 1.6 %collective-permute-start.4 = (bf16[2,5,16,512]{3,2,1,0:T(8,128)(2,1)S(1)}, bf16[2,5,16,512]{3,2,1,0:T(8,128)(2,1)S(1)}, u32[]{:S(2)}, u32[]{:S(2)}) collective-permute-start(bf16[2,5,16,512]{3,2,1,0:T(8,128)(2,1)S(1)} %get-tuple-element.30._), channel_id=1, source_target_pairs={{0,1},{1,0},{2,3},{3,2},{4,5},{5,4},{6,7},{7,6},{8,9},{9,8},{10,11... | collective-permute-start | bytes 491528 | tf_op jit(solution)/shard_map/ppermute | solution.py:647
  18.5 3.2 %gram.1._.gram_ref = f32[64,128]{1,0:T(8,128)S(1)} custom-call(bf16[2,5,16,512]{3,2,1,0:T(8,128)(2,1)S(1)} %get-tuple-element.30._, f32[512,256]{1,0:T(8,128)S(1)} %get-tuple-element.31.right_ref, f32[256,256]{1,0:T(8,128)S(1)} %get-tuple-element.32.left_ref, bf16[64,20,8,512]{3,2,1,0:T(8,128)(2,1)S(1)} %get-tuple-element.33.basis_ref.rest_4_), custom_call_target="tpu_custom_call" | custom-call | flops 2684354560 | bytes 10485760 | tf_op jit(solution)/shard_map/gram/pallas_call | solution.py:618
  21.8 0.2 join_own.1
  22.0 0.9 %collective-permute-done.4.rest_1_ = bf16[2,5,16,512]{3,2,1,0:T(8,128)(2,1)S(1)} collective-permute-done((bf16[2,5,16,512]{3,2,1,0:T(8,128)(2,1)S(1)}, bf16[2,5,16,512]{3,2,1,0:T(8,128)(2,1)S(1)}, u32[]{:S(2)}, u32[]{:S(2)}) %collective-permute-start.4) | collective-permute-done | bytes 163872 | tf_op jit(solution)/shard_map/ppermute | solution.py:647
  22.9 3.1 %project.1 = (f32[8,128]{1,0:T(8,128)S(1)}, bf16[20,16,512]{2,1,0:T(8,128)(2,1)S(1)}, f32[2,5,8,4,512]{4,3,2,1,0:T(4,128)}) custom-call(s32[1]{0:T(128)} %bitcast.where_ref._, bf16[2,5,16,512]{3,2,1,0:T(8,128)(2,1)S(1)} %get-tuple-element.35.rest_0_, bf16[2,5,16,512]{3,2,1,0:T(8,128)(2,1)S(1)} %collective-permute-done.4.rest_1_, ...), custom_call_target="tpu_custom_call" | custom-call | flops 167772160 | bytes 10485760 | tf_op jit(solution)/shard_map/project/pallas_call | solution.py:671
  26.0 1.6 %collective-permute-start.6 = (f32[72,128]{1,0:T(8,128)S(1)}, f32[72,128]{1,0:T(8,128)S(1)}, u32[]{:S(2)}, u32[]{:S(2)}) collective-permute-start(f32[72,128]{1,0:T(8,128)S(1)} %merge.1), channel_id=1, source_target_pairs={{0,1},{1,0},{2,3},{3,2},{4,5},{5,4},{6,7},{7,6},{8,9},{9,8},{10,11... | collective-permute-start | bytes 110600 | tf_op jit(solution)/shard_map/ppermute | solution.py:530
  27.6 2.5 %collective-permute-done.6 = f32[72,128]{1,0:T(8,128)S(1)} collective-permute-done((f32[72,128]{1,0:T(8,128)S(1)}, f32[72,128]{1,0:T(8,128)S(1)}, u32[]{:S(2)}, u32[]{:S(2)}) %collective-permute-start.6) | collective-permute-done | bytes 36896 | tf_op jit(solution)/shard_map/ppermute | solution.py:530
  30.1 1.2 %collective-permute-done.7 = f32[72,128]{1,0:T(8,128)S(1)} collective-permute-done((f32[72,128]{1,0:T(8,128)S(1)}, f32[72,128]{1,0:T(8,128)S(1)}, u32[]{:S(2)}, u32[]{:S(2)}) %collective-permute-start.7) | collective-permute-done | bytes 36896 | tf_op jit(solution)/shard_map/ppermute | solution.py:530
  31.3 1.5 %collective-permute-start.8 = (f32[72,128]{1,0:T(8,128)S(1)}, f32[72,128]{1,0:T(8,128)S(1)}, u32[]{:S(2)}, u32[]{:S(2)}) collective-permute-start(f32[72,128]{1,0:T(8,128)S(1)} %add.16), channel_id=1, source_target_pairs={{0,8},{2,10},{4,12},{6,14},{8,0},{10,2},{12,4},{14,6},{16,24},{18,... | collective-permute-start | bytes 110600 | tf_op jit(solution)/shard_map/ppermute | solution.py:530
  32.8 2.4 %collective-permute-done.8 = f32[72,128]{1,0:T(8,128)S(1)} collective-permute-done((f32[72,128]{1,0:T(8,128)S(1)}, f32[72,128]{1,0:T(8,128)S(1)}, u32[]{:S(2)}, u32[]{:S(2)}) %collective-permute-start.8) | collective-permute-done | bytes 36896 | tf_op jit(solution)/shard_map/ppermute | solution.py:530
  35.3 2.5 %collective-permute-start.9 = (f32[72,128]{1,0:T(8,128)S(1)}, f32[72,128]{1,0:T(8,128)S(1)}, u32[]{:S(2)}, u32[]{:S(2)}) collective-permute-start(f32[72,128]{1,0:T(8,128)S(1)} %add.17), channel_id=1, source_target_pairs={{0,16},{2,18},{4,20},{6,22},{8,24},{10,26},{12,28},{14,30},{16,0},... | collective-permute-start | bytes 110600 | tf_op jit(solution)/shard_map/ppermute | solution.py:530
  37.8 2.3 %collective-permute-done.9 = f32[72,128]{1,0:T(8,128)S(1)} collective-permute-done((f32[72,128]{1,0:T(8,128)S(1)}, f32[72,128]{1,0:T(8,128)S(1)}, u32[]{:S(2)}, u32[]{:S(2)}) %collective-permute-start.9) | collective-permute-done | bytes 36896 | tf_op jit(solution)/shard_map/ppermute | solution.py:530
  40.1 1.5 %collective-permute-start.10 = (f32[72,128]{1,0:T(8,128)S(1)}, f32[72,128]{1,0:T(8,128)S(1)}, u32[]{:S(2)}, u32[]{:S(2)}) collective-permute-start(f32[72,128]{1,0:T(8,128)S(1)} %add.18.sums_ref), channel_id=1, source_target_pairs={{0,4},{2,6},{4,0},{6,2},{8,12},{10,14},{12,8},{14,10},{16,20},{18,... | collective-permute-start | bytes 110600 | tf_op jit(solution)/shard_map/ppermute | solution.py:530
  41.6 2.4 %inverse.1 = (f32[64,64]{1,0:T(8,128)S(1)}, f32[64,512]{1,0:T(8,128)S(1)}) custom-call(f32[72,128]{1,0:T(8,128)S(1)} %add.18.sums_ref), custom_call_target="tpu_custom_call" | custom-call | flops 20000000 | bytes 32768 | tf_op jit(solution)/shard_map/inverse/pallas_call | solution.py:710
  44.1 3.2 %finish.1 = (f32[2,20,8,512]{3,2,1,0:T(8,128)}, f32[2,64]{1,0:T(2,128)}, f32[2,2]{1,0:T(2,128)}) custom-call(f32[72,128]{1,0:T(8,128)S(1)} %add.19.projected_ref, f32[72,128]{1,0:T(8,128)S(1)} %add.18.sums_ref, f32[64,64]{1,0:T(8,128)S(1)} %get-tuple-element.40.inverse_ref, f32[64,512]{1,0:T(8,128)S(1)} %get-tuple-element.41.spread_ref, ...), custom_call_target="tpu_custom_call" | custom-call | flops 335544320 | bytes 11796480 | tf_op jit(solution)/shard_map/finish/pallas_call | solution.py:723
  (14 shorter events, 0.2 us)
Async XLA Ops:
  0.6 1.1 %copy-start = (f32[2,5,8,4,512]{4,3,2,1,0:T(4,128)S(1)}, f32[2,5,8,4,512]{4,3,2,1,0:T(4,128)}, u32[]{:S(2)}) copy-start(f32[2,5,8,4,512]{4,3,2,1,0:T(4,128)} %source_ref.1) | copy-start | bytes 1966084
  3.1 13.6 %collective-permute-start = (f32[2,5,4,4,512]{4,3,2,1,0:T(4,128)S(1)}, f32[2,5,4,4,512]{4,3,2,1,0:T(4,128)S(1)}, u32[]{:S(2)}, u32[]{:S(2)}) collective-permute-start(f32[2,5,4,4,512]{4,3,2,1,0:T(4,128)S(1)} %get-tuple-element.27), channel_id=1, source_target_pairs={{0,2},{2,4},{4,6},{6,8},{8,10},{10,12},{12,14},{14,16},{16,18},{18... | collective-permute-start | bytes 983048 | tf_op jit(solution)/shard_map/ppermute | solution.py:573
  3.6 13.1 %collective-permute-start.1 = (f32[2,5,4,4,512]{4,3,2,1,0:T(4,128)S(1)}, f32[2,5,4,4,512]{4,3,2,1,0:T(4,128)S(1)}, u32[]{:S(2)}, u32[]{:S(2)}) collective-permute-start(f32[2,5,4,4,512]{4,3,2,1,0:T(4,128)S(1)} %get-tuple-element.28), channel_id=1, source_target_pairs={{2,0},{4,2},{6,4},{8,6},{10,8},{12,10},{14,12},{16,14},{18,16},{20... | collective-permute-start | bytes 983048 | tf_op jit(solution)/shard_map/ppermute | solution.py:574
  8.6 8.1 %collective-permute-start.2 = (bf16[5,48,512]{2,1,0:T(8,128)(2,1)S(1)}, bf16[5,48,512]{2,1,0:T(8,128)(2,1)S(1)}, u32[]{:S(2)}, u32[]{:S(2)}) collective-permute-start(bf16[5,48,512]{2,1,0:T(8,128)(2,1)S(1)} %get-tuple-element.29), channel_id=1, source_target_pairs={{0,1},{1,0},{2,3},{3,2},{4,5},{5,4},{6,7},{7,6},{8,9},{9,8},{10,11... | collective-permute-start | bytes 737288 | tf_op jit(solution)/shard_map/ppermute | solution.py:572
  10.5 11.2 %collective-permute-start.3 = (bf16[5,48,512]{2,1,0:T(8,128)(2,1)S(1)}, bf16[5,48,512]{2,1,0:T(8,128)(2,1)S(1)}, u32[]{:S(2)}, u32[]{:S(2)}) collective-permute-start(bf16[5,48,512]{2,1,0:T(8,128)(2,1)S(1)} %get-tuple-element.34), channel_id=1, source_target_pairs={{0,1},{1,0},{2,3},{3,2},{4,5},{5,4},{6,7},{7,6},{8,9},{9,8},{10,11... | collective-permute-start | bytes 737288 | tf_op jit(solution)/shard_map/ppermute | solution.py:575
  16.9 6.0 %collective-permute-start.4 = (bf16[2,5,16,512]{3,2,1,0:T(8,128)(2,1)S(1)}, bf16[2,5,16,512]{3,2,1,0:T(8,128)(2,1)S(1)}, u32[]{:S(2)}, u32[]{:S(2)}) collective-permute-start(bf16[2,5,16,512]{3,2,1,0:T(8,128)(2,1)S(1)} %get-tuple-element.30._), channel_id=1, source_target_pairs={{0,1},{1,0},{2,3},{3,2},{4,5},{5,4},{6,7},{7,6},{8,9},{9,8},{10,11... | collective-permute-start | bytes 491528 | tf_op jit(solution)/shard_map/ppermute | solution.py:647
  21.7 4.4 %collective-permute-start.5 = (f32[64,128]{1,0:T(8,128)S(1)}, f32[64,128]{1,0:T(8,128)S(1)}, u32[]{:S(2)}, u32[]{:S(2)}) collective-permute-start(f32[64,128]{1,0:T(8,128)S(1)} %gram.1._.gram_ref), channel_id=1, source_target_pairs={{0,4},{2,6},{4,0},{6,2},{8,12},{10,14},{12,8},{14,10},{16,20},{18,... | collective-permute-start | bytes 98312 | tf_op jit(solution)/shard_map/ppermute | solution.py:662
  26.0 4.0 %collective-permute-start.6 = (f32[72,128]{1,0:T(8,128)S(1)}, f32[72,128]{1,0:T(8,128)S(1)}, u32[]{:S(2)}, u32[]{:S(2)}) collective-permute-start(f32[72,128]{1,0:T(8,128)S(1)} %merge.1), channel_id=1, source_target_pairs={{0,1},{1,0},{2,3},{3,2},{4,5},{5,4},{6,7},{7,6},{8,9},{9,8},{10,11... | collective-permute-start | bytes 110600 | tf_op jit(solution)/shard_map/ppermute | solution.py:530
  30.1 1.2 %collective-permute-start.7 = (f32[72,128]{1,0:T(8,128)S(1)}, f32[72,128]{1,0:T(8,128)S(1)}, u32[]{:S(2)}, u32[]{:S(2)}) collective-permute-start(f32[72,128]{1,0:T(8,128)S(1)} %add.15), channel_id=1, source_target_pairs={{0,2},{2,0},{4,6},{6,4},{8,10},{10,8},{12,14},{14,12},{16,18},{18,... | collective-permute-start | bytes 110600 | tf_op jit(solution)/shard_map/ppermute | solution.py:530
  31.3 4.0 %collective-permute-start.8 = (f32[72,128]{1,0:T(8,128)S(1)}, f32[72,128]{1,0:T(8,128)S(1)}, u32[]{:S(2)}, u32[]{:S(2)}) collective-permute-start(f32[72,128]{1,0:T(8,128)S(1)} %add.16), channel_id=1, source_target_pairs={{0,8},{2,10},{4,12},{6,14},{8,0},{10,2},{12,4},{14,6},{16,24},{18,... | collective-permute-start | bytes 110600 | tf_op jit(solution)/shard_map/ppermute | solution.py:530
  35.3 4.9 %collective-permute-start.9 = (f32[72,128]{1,0:T(8,128)S(1)}, f32[72,128]{1,0:T(8,128)S(1)}, u32[]{:S(2)}, u32[]{:S(2)}) collective-permute-start(f32[72,128]{1,0:T(8,128)S(1)} %add.17), channel_id=1, source_target_pairs={{0,16},{2,18},{4,20},{6,22},{8,24},{10,26},{12,28},{14,30},{16,0},... | collective-permute-start | bytes 110600 | tf_op jit(solution)/shard_map/ppermute | solution.py:530
  40.1 4.0 %collective-permute-start.10 = (f32[72,128]{1,0:T(8,128)S(1)}, f32[72,128]{1,0:T(8,128)S(1)}, u32[]{:S(2)}, u32[]{:S(2)}) collective-permute-start(f32[72,128]{1,0:T(8,128)S(1)} %add.18.sums_ref), channel_id=1, source_target_pairs={{0,4},{2,6},{4,0},{6,2},{8,12},{10,14},{12,8},{14,10},{16,20},{18,... | collective-permute-start | bytes 110600 | tf_op jit(solution)/shard_map/ppermute | solution.py:530

commit v7 on v6

--- a/solution.py
+++ b/solution.py
@@ -102,17 +102,8 @@
                 right_ref[w, f, i] = total
 
 
-def paired_face_kernel(
-    where_ref, source_ref, windows_ref, left_ref, right_ref, near_ref, later_ref,
-    scratch, lows, sems,
-):
+def wall_group(where_ref, windows_ref, group_ref, lows, base, keep_x):
     windows, _, planes, layers, cells = windows_ref.shape
-    copies = [
-        pltpu.make_async_copy(source_ref.at[w], windows_ref.at[w], sems.at[w])
-        for w in range(windows)
-    ]
-    for copy in copies:
-        copy.start()
     tile = (layers, cells)
     first = where_ref[0] == 0
     table = [
@@ -123,50 +114,62 @@
         )
         for j in range(layers)
     ]
+    for w in range(windows):
+        upper = [[] for _ in range(5)]
+        lower = [[] for _ in range(5)]
+        for x in range(planes // 2):
+            parts = primitives([windows_ref[w, f, base + x] for f in range(5)])
+            keep_x(w, base + x, parts)
+            for f, value in enumerate(flux(parts, 1)):
+                total = None
+                for j in range(layers):
+                    term = table[j] * value[j : j + 1, :]
+                    total = term if total is None else total + term
+                high = total.astype(jnp.bfloat16).astype(jnp.float32)
+                rest = total - high
+                upper[f].append(high)
+                lower[f].append(jnp.where(first, rest[0:2], rest[2:4]))
+        for f in range(5):
+            group_ref[f, 16 * w : 16 * w + 16] = jnp.concatenate(upper[f], axis=0).astype(
+                jnp.bfloat16
+            )
+            lows[f, 8 * w : 8 * w + 8] = jnp.concatenate(lower[f], axis=0)
+    for f in range(5):
+        group_ref[f, 32:48] = lows[f].astype(jnp.bfloat16)
+
+
+def near_kernel(where_ref, source_ref, group_ref, kept_ref, lows, sem):
+    copy = pltpu.make_async_copy(source_ref, kept_ref, sem)
+    copy.start()
+    base = source_ref.shape[2] // 2 * where_ref[0]
+    wall_group(where_ref, source_ref, group_ref, lows, base, lambda w, x, parts: None)
+    copy.wait()
+
+
+def later_kernel(where_ref, _, windows_ref, group_ref, left_ref, right_ref, scratch, lows):
+    windows, _, planes, layers, cells = windows_ref.shape
     half = planes // 2
+
+    def keep_x(w, x, parts):
+        for f, value in enumerate(flux(parts, 0)):
+            scratch[w, f, x] = value
+
+    base = half * (1 - where_ref[0])
+    wall_group(where_ref, windows_ref, group_ref, lows, base, keep_x)
     for w in range(windows):
-        copies[w].wait()
-        for group, group_ref in enumerate((near_ref, later_ref)):
-            base = half * (1 - where_ref[0] if group else where_ref[0])
-            upper = [[] for _ in range(5)]
-            lower = [[] for _ in range(5)]
-            for x in range(half):
-                parts = primitives([windows_ref[w, f, base + x] for f in range(5)])
-                for f, value in enumerate(flux(parts, 0)):
-                    scratch[f, base + x] = value
-                for f, value in enumerate(flux(parts, 1)):
-                    total = None
-                    for j in range(layers):
-                        term = table[j] * value[j : j + 1, :]
-                        total = term if total is None else total + term
-                    high = total.astype(jnp.bfloat16).astype(jnp.float32)
-                    rest = total - high
-                    upper[f].append(high)
-                    lower[f].append(jnp.where(first, rest[0:2], rest[2:4]))
-            for f in range(5):
-                group_ref[f, 16 * w : 16 * w + 16] = jnp.concatenate(upper[f], axis=0).astype(
-                    jnp.bfloat16
-                )
-                lows[group, f, 8 * w : 8 * w + 8] = jnp.concatenate(lower[f], axis=0)
+        for x in range(half):
+            plane = half * where_ref[0] + x
+            keep_x(w, plane, primitives([windows_ref[w, f, plane] for f in range(5)]))
         for f in range(5):
             for i in range(REACH):
-                total = None
-                for j in range(planes):
-                    c = weight(j - planes - i)
-                    if c:
-                        term = c * scratch[f, j]
-                        total = term if total is None else total + term
-                left_ref[w, f, i] = total
-                total = None
-                for j in range(planes):
-                    c = weight(j + REACH - i)
-                    if c:
-                        term = c * scratch[f, j]
-                        total = term if total is None else total + term
-                right_ref[w, f, i] = total
-    for group, group_ref in enumerate((near_ref, later_ref)):
-        for f in range(5):
-            group_ref[f, 32:48] = lows[group, f].astype(jnp.bfloat16)
+                for ref, offset in ((left_ref, -planes), (right_ref, REACH)):
+                    total = None
+                    for j in range(planes):
+                        c = weight(j + offset - i)
+                        if c:
+                            term = c * scratch[w, f, j]
+                            total = term if total is None else total + term
+                    ref[w, f, i] = total
 
 
 def inner_part(windows_ref, part_ref, scratch):
@@ -222,9 +225,7 @@
     return right, left
 
 
-def inner_gram_kernel(
-    early, windows_ref, basis_ref, part_ref, right_ref, left_ref, kept_ref, scratch, sems
-):
+def inner_kernel(windows_ref, basis_ref, part_ref, kept_ref, scratch, sems):
     chunks = sems.shape[0]
     per_chunk = kept_ref.shape[1] // chunks
     copies = []
@@ -235,11 +236,18 @@
         )
         copies[c].start()
     inner_part(windows_ref, part_ref, scratch)
-    right, left = jnp.zeros(right_ref.shape, jnp.float32), jnp.zeros(left_ref.shape, jnp.float32)
-    for c in range(chunks):
-        copies[c].wait()
-        if c < early:
-            right, left = gram_blocks(kept_ref, [c], per_chunk, right, left)
+    for copy in copies:
+        copy.wait()
+
+
+def early_gram_kernel(early, chunks, _, basis_ref, right_ref, left_ref):
+    right, left = gram_blocks(
+        basis_ref,
+        range(early),
+        basis_ref.shape[1] // chunks,
+        jnp.zeros(right_ref.shape, jnp.float32),
+        jnp.zeros(left_ref.shape, jnp.float32),
+    )
     right_ref[...] = right
     left_ref[...] = left
 
@@ -259,12 +267,13 @@
         total[tile, half:] = turned[:, span]
         total[tiles_left + tile] = right[:, span]
     rows = folded(total, modes)
-    lanes = gram_ref.shape[1]
     picks = (
-        lax.broadcasted_iota(jnp.int32, (wide, lanes), 0) // 8
-        == lax.broadcasted_iota(jnp.int32, (wide, lanes), 1)
+        lax.broadcasted_iota(jnp.int32, (wide, modes), 0) // 8
+        == lax.broadcasted_iota(jnp.int32, (wide, modes), 1)
     ).astype(jnp.float32)
-    gram_ref[...] = jnp.dot(rows, picks, precision=HIGHEST, preferred_element_type=jnp.float32)
+    gram = jnp.dot(rows, picks, precision=HIGHEST, preferred_element_type=jnp.float32)
+    gram_ref[:, 0:modes] = gram[0 : modes // 2]
+    gram_ref[:, modes:] = gram[modes // 2 :]
 
 
 def join_kernel(walls, part_ref, left_ref, right_ref, *rest):
@@ -397,9 +406,14 @@
 
 
 def merge_kernel(gram_ref, far_ref, sums_ref, merged_ref):
-    modes = gram_ref.shape[0]
-    merged_ref[0:modes] = gram_ref[...] + far_ref[...]
-    merged_ref[modes:] = sums_ref[...]
+    rows = gram_ref.shape[0]
+    merged_ref[0:rows] = gram_ref[...] + far_ref[...]
+    merged_ref[rows:] = sums_ref[...]
+
+
+def unpacked(sums_ref, modes):
+    half = modes // 2
+    return jnp.concatenate([sums_ref[0:half, 0:modes], sums_ref[0:half, modes:]], axis=0)
 
 
 def inverse_kernel(sums_ref, inverse_ref, spread_ref, plain, scaled):
@@ -407,9 +421,14 @@
     rows = lax.broadcasted_iota(jnp.int32, (8, 2 * modes), 0)
     lanes = lax.broadcasted_iota(jnp.int32, (8, 2 * modes), 1)
     tiles = []
+    gram = unpacked(sums_ref, modes)
     for tile in range(modes // 8):
         eye = (lanes == rows + (modes + 8 * tile)).astype(jnp.float32)
-        tiles.append(jnp.where(lanes < modes, sums_ref[8 * tile : 8 * tile + 8, :], eye))
+        start = 8 * tile % (modes // 2)
+        line = sums_ref[start : start + 8, :]
+        if 8 * tile >= modes // 2:
+            line = pltpu.roll(line, modes, 1)
+        tiles.append(jnp.where(lanes < modes, line, eye))
     count = modes // 8
     for home in range(count):
         columns = [
@@ -442,7 +461,7 @@
     inverse = exact(plain[:, modes:], scaled[:, modes:], (((0,), (0,)), ((), ())))
     square = (modes, modes)
     eye = lax.broadcasted_iota(jnp.int32, square, 0) == lax.broadcasted_iota(jnp.int32, square, 1)
-    off = eye.astype(jnp.float32) - exact(sums_ref[0:modes, 0:modes], inverse, plainly)
+    off = eye.astype(jnp.float32) - exact(gram, inverse, plainly)
     inverse = inverse + exact(inverse, off, plainly)
     inverse_ref[...] = inverse
     wide = spread_ref.shape[1]
@@ -460,7 +479,8 @@
     modes, tiles, _, cells = basis_ref.shape
     wide = modes * 8
     exact = functools.partial(jnp.dot, precision=HIGHEST, preferred_element_type=jnp.float32)
-    projected = projected_ref[modes : modes + 8, 0:modes]
+    base = modes // 2
+    projected = projected_ref[base : base + 8, 0:modes]
     lines = exact(projected, spread_ref[...])
     full = jnp.concatenate(
         [jnp.broadcast_to(lines[0:1], (8, wide)), jnp.broadcast_to(lines[1:2], (8, wide))],
@@ -470,13 +490,13 @@
     upper = full.astype(jnp.bfloat16)
     fit = jnp.concatenate([upper, (full - upper.astype(jnp.float32)).astype(jnp.bfloat16)], axis=0)
     solved = exact(projected, inverse_ref[...])
-    left = projected - exact(solved, sums_ref[0:modes, 0:modes])
+    left = projected - exact(solved, unpacked(sums_ref, modes))
 
     def inner(p, i, q, j):
         return jnp.sum(p[i : i + 1] * q[j : j + 1], axis=1, keepdims=True)
 
     def entry(i, j):
-        square = projected_ref[modes + i : modes + i + 1, modes + j : modes + j + 1]
+        square = projected_ref[base + i : base + i + 1, modes + j : modes + j + 1]
         return square - inner(projected, i, solved, j) - inner(solved, i, left, j)
 
     first = jnp.sqrt(entry(0, 0))
@@ -558,17 +578,27 @@
     if paired:
         swap = [(0, 1), (1, 0)]
         group_shape = shape((fields, 48, cells), bf16)
-        kept, to_next, to_last, near_group, later_group = pl.pallas_call(
-            paired_face_kernel,
-            out_shape=[shape(windows.shape, f32)] + [edge_shape] * 2 + [group_shape] * 2,
-            in_specs=[SCALAR, FAR],
-            out_specs=[WHOLE] * 5,
-            scratch_shapes=face_scratch
-            + [pltpu.VMEM((2, fields, 16, cells), f32), pltpu.SemaphoreType.DMA((count,))],
+        lows = pltpu.VMEM((fields, 16, cells), f32)
+        near_group, kept = pl.pallas_call(
+            near_kernel,
+            out_shape=[group_shape, shape(windows.shape, f32)],
+            in_specs=[SCALAR, WHOLE],
+            out_specs=[WHOLE] * 2,
+            scratch_shapes=[lows, pltpu.SemaphoreType.DMA],
             compiler_params=params(16),
             cost_estimate=face_cost,
-            name="faces",
+            name="near_faces",
         )(place, windows)
+        later_group, to_next, to_last = pl.pallas_call(
+            later_kernel,
+            out_shape=[group_shape] + [edge_shape] * 2,
+            in_specs=[SCALAR, LOOSE, WHOLE],
+            out_specs=[WHOLE] * 3,
+            scratch_shapes=[pltpu.VMEM((count, fields, planes, layers, cells), f32), lows],
+            compiler_params=params(16),
+            cost_estimate=face_cost,
+            name="later_faces",
+        )(place, near_group, kept)
         near_group = lax.ppermute(near_group, "analysis", swap)
         from_left = lax.ppermute(to_next, "solver", to_right)
         from_right = lax.ppermute(to_last, "solver", to_left)
@@ -595,29 +625,33 @@
 
     early = 2
     gram_flops = 2 * wide * wide * cells * tiles
-    inner, right, left, basis = pl.pallas_call(
-        functools.partial(inner_gram_kernel, early),
-        out_shape=[
-            shape(windows.shape, f32),
-            shape((wide, wide // 2), f32),
-            shape((wide // 2, wide // 2), f32),
-            shape(basis.shape, bf16),
-        ],
+    inner, basis = pl.pallas_call(
+        inner_kernel,
+        out_shape=[shape(windows.shape, f32), shape(basis.shape, bf16)],
         in_specs=[WHOLE, FAR],
-        out_specs=[WHOLE] * 4,
+        out_specs=[WHOLE] * 2,
         scratch_shapes=[
             pltpu.VMEM((2 * fields, planes, count * layers, cells), f32),
             pltpu.SemaphoreType.DMA((fields,)),
         ],
         compiler_params=params(40),
-        cost_estimate=cost(gram_flops // 2, 2 * basis_bytes),
-        name="inner_gram",
+        cost_estimate=cost(1_000_000, windows.size),
+        name="inner",
     )(kept, basis)
+    right, left = pl.pallas_call(
+        functools.partial(early_gram_kernel, early, fields),
+        out_shape=[shape((wide, wide // 2), f32), shape((wide // 2, wide // 2), f32)],
+        in_specs=[LOOSE, WHOLE],
+        out_specs=[WHOLE] * 2,
+        compiler_params=params(24),
+        cost_estimate=cost(gram_flops // 2, basis_bytes),
+        name="early_gram",
+    )(near_group if paired else place, basis)
 
     def rest_of_gram(after):
         return pl.pallas_call(
             functools.partial(gram_kernel, early, fields),
-            out_shape=shape((modes, LANES), f32),
+            out_shape=shape((modes // 2, 2 * modes), f32),
             in_specs=[LOOSE] + [WHOLE] * 3,
             out_specs=WHOLE,
             scratch_shapes=[pltpu.VMEM((wide // LANES, wide, LANES), f32)],
@@ -696,7 +730,7 @@
         )(place, snaps, basis)
     sums = pl.pallas_call(
         merge_kernel,
-        out_shape=shape((modes + 8, LANES), f32),
+        out_shape=shape((modes // 2 + 8, LANES), f32),
         in_specs=[WHOLE] * 3,
         out_specs=WHOLE,
         compiler_params=params(16),

time: 47.4 us -> 48.3 us (1.019)
  Pallas kernels: 19.2 us -> 21.1 us
  starting transfers between devices: 16.3 us -> 15.3 us
    pallas_call x3 -> x5, Pallas kernels: 6.89 us -> 8.69 us  [the longest x1 5.48 us: body(): pl.pallas_call(inner_kernel, out_shape=[shape(windows.shape, f32), shape(...]
    ppermute x5, starting transfers between devices: 7.13 us -> 5.7 us  [swap_added(): lax.ppermute(value, axis, [(i, i ^ bit) for i in range(count)])]
    ppermute x1, starting transfers between devices: 1.87 us -> 3 us  [body(): near_group = lax.ppermute(near_group, 'analysis', swap)]
    ppermute x5, waiting for transfers between devices: 8.49 us -> 9.4 us  [swap_added(): lax.ppermute(value, axis, [(i, i ^ bit) for i in range(count)])]
    ppermute x1, starting transfers between devices: 5.06 us -> 4.43 us  [body(): from_right = lax.ppermute(to_last, 'solver', to_left)]
    ppermute x1, starting transfers between devices: 1.56 us -> 2.07 us  [body(): got = lax.ppermute(given, 'analysis', swap)]
    ppermute x1, waiting for transfers between devices: 0.92 us -> 0.41 us  [body(): got = lax.ppermute(given, 'analysis', swap)]
    ppermute x1, waiting for transfers between devices: 0.5 us -> 0.01 us  [body(): near_group = lax.ppermute(near_group, 'analysis', swap)]
  transfers between devices with their start and end apart: 11 -> 11, of which waited for: 7 -> 5; matrix products, arithmetic and copies ran while one was open for 0% -> 0% of each run, Pallas kernels for 31% -> 36%
where the time goes in v7:
time: 48.3 us; the launch traced here: 48.1 us
  Pallas kernels  21.1 us (44%)
  starting transfers between devices  15.3 us (32%)
  waiting for transfers between devices  9.82 us (20%)
  local copies, waits for them, and re-layouts  1.08 us (2%)
  between operations  0.79 us (2%)
    ppermute x5, waiting for transfers between devices, swap_added(): lax.ppermute(value, axis, [(i, i ^ bit) for i in range(count)])  9.4 us
    ppermute x5, starting transfers between devices, swap_added(): lax.ppermute(value, axis, [(i, i ^ bit) for i in range(count)])  5.7 us
    pallas_call x1, Pallas kernels, body(): pl.pallas_call(inner_kernel, out_shape=[shape(windows.shape, f32), shape(...  5.48 us
    ppermute x1, starting transfers between devices, body(): from_right = lax.ppermute(to_last, 'solver', to_left)  4.43 us
    pallas_call x1, Pallas kernels, rest_of_gram(): pl.pallas_call(functools.partial(gram_kernel, early, fields), out_shape=s...  3.25 us
    pallas_call x1, Pallas kernels, body(): pl.pallas_call(functools.partial(finish_kernel, rows_total), out_shape=[s...  3.18 us
    pallas_call x1, Pallas kernels, body(): pl.pallas_call(functools.partial(project_kernel, True), out_shape=[sums_s...  3.12 us
    ppermute x1, starting transfers between devices, body(): near_group = lax.ppermute(near_group, 'analysis', swap)  3 us
  transfers between devices with their start and end apart: 11, of which 5 were waited for; matrix products, arithmetic and copies ran while one was open for 0% of the time, Pallas kernels for 36%

profile of v7, /device:TPU:0, one launch (start us, length us, event | category | flops | bytes accessed | tf_op | source)
XLA Modules:
  0.0 48.1 jit_solution(7208442486549525384)
XLA Ops:
  0.6 1.1 %copy-done = f32[2,5,8,4,512]{4,3,2,1,0:T(4,128)S(1)} copy-done((f32[2,5,8,4,512]{4,3,2,1,0:T(4,128)S(1)}, f32[2,5,8,4,512]{4,3,2,1,0:T(4,128)}, u32[]{:S(2)}) %copy-start) | copy-done | bytes 655384
  1.7 0.7 %near_faces.1 = (bf16[5,48,512]{2,1,0:T(8,128)(2,1)S(1)}, f32[2,5,8,4,512]{4,3,2,1,0:T(4,128)S(1)}) custom-call(s32[1]{0:T(128)} %bitcast.where_ref._, f32[2,5,8,4,512]{4,3,2,1,0:T(4,128)S(1)} %copy-done), custom_call_target="tpu_custom_call" | custom-call | flops 10000000 | bytes 1638400 | tf_op jit(solution)/shard_map/near_faces/pallas_call | solution.py:582
  2.4 3.0 %collective-permute-start.2 = (bf16[5,48,512]{2,1,0:T(8,128)(2,1)S(1)}, bf16[5,48,512]{2,1,0:T(8,128)(2,1)S(1)}, u32[]{:S(2)}, u32[]{:S(2)}) collective-permute-start(bf16[5,48,512]{2,1,0:T(8,128)(2,1)S(1)} %get-tuple-element.27._), channel_id=1, source_target_pairs={{0,1},{1,0},{2,3},{3,2},{4,5},{5,4},{6,7},{7,6},{8,9},{9,8},{10,11... | collective-permute-start | bytes 737288 | tf_op jit(solution)/shard_map/ppermute | solution.py:602
  5.5 0.7 %later_faces.1 = (bf16[5,48,512]{2,1,0:T(8,128)(2,1)S(1)}, f32[2,5,4,4,512]{4,3,2,1,0:T(4,128)S(1)}, f32[2,5,4,4,512]{4,3,2,1,0:T(4,128)S(1)}) custom-call(s32[1]{0:T(128)} %bitcast.where_ref._, bf16[5,48,512]{2,1,0:T(8,128)(2,1)S(1)} %get-tuple-element.27._, f32[2,5,8,4,512]{4,3,2,1,0:T(4,128)S(1)} %get-tuple-element.25.windows_ref), custom_call_target="tpu_custom_call" | custom-call | flops 10000000 | bytes 1638400 | tf_op jit(solution)/shard_map/later_faces/pallas_call | solution.py:592
  6.1 0.1 collective-permute-start
  6.2 4.4 %collective-permute-start.1 = (f32[2,5,4,4,512]{4,3,2,1,0:T(4,128)S(1)}, f32[2,5,4,4,512]{4,3,2,1,0:T(4,128)S(1)}, u32[]{:S(2)}, u32[]{:S(2)}) collective-permute-start(f32[2,5,4,4,512]{4,3,2,1,0:T(4,128)S(1)} %get-tuple-element.29), channel_id=1, source_target_pairs={{2,0},{4,2},{6,4},{8,6},{10,8},{12,10},{14,12},{16,14},{18,16},{20... | collective-permute-start | bytes 983048 | tf_op jit(solution)/shard_map/ppermute | solution.py:604
  10.6 5.5 %inner.1 = (f32[2,5,8,4,512]{4,3,2,1,0:T(4,128)S(1)}, bf16[64,20,8,512]{3,2,1,0:T(8,128)(2,1)S(1)}) custom-call(f32[2,5,8,4,512]{4,3,2,1,0:T(4,128)S(1)} %get-tuple-element.25.windows_ref, bf16[64,20,8,512]{3,2,1,0:T(8,128)(2,1)} %bitcast.3), custom_call_target="tpu_custom_call" | custom-call | flops 1000000 | bytes 163840 | tf_op jit(solution)/shard_map/inner/pallas_call | solution.py:628
  16.1 1.8 %early_gram.1 = (f32[512,256]{1,0:T(8,128)S(1)}, f32[256,256]{1,0:T(8,128)S(1)}) custom-call(bf16[5,48,512]{2,1,0:T(8,128)(2,1)S(1)} %collective-permute-done.2.group_ref._, bf16[64,20,8,512]{3,2,1,0:T(8,128)(2,1)S(1)} %get-tuple-element.31.basis_ref.rest_4_), custom_call_target="tpu_custom_call" | custom-call | flops 2684354560 | bytes 10485760 | tf_op jit(solution)/shard_map/early_gram/pallas_call | solution.py:641
  18.0 0.2 join_given.1
  18.2 2.1 %collective-permute-start.4 = (bf16[2,5,16,512]{3,2,1,0:T(8,128)(2,1)S(1)}, bf16[2,5,16,512]{3,2,1,0:T(8,128)(2,1)S(1)}, u32[]{:S(2)}, u32[]{:S(2)}) collective-permute-start(bf16[2,5,16,512]{3,2,1,0:T(8,128)(2,1)S(1)} %get-tuple-element.30._), channel_id=1, source_target_pairs={{0,1},{1,0},{2,3},{3,2},{4,5},{5,4},{6,7},{7,6},{8,9},{9,8},{10,11... | collective-permute-start | bytes 491528 | tf_op jit(solution)/shard_map/ppermute | solution.py:681
  20.3 3.3 %gram.1._.gram_ref = f32[32,128]{1,0:T(8,128)S(1)} custom-call(bf16[2,5,16,512]{3,2,1,0:T(8,128)(2,1)S(1)} %get-tuple-element.30._, f32[512,256]{1,0:T(8,128)S(1)} %get-tuple-element.32.right_ref, f32[256,256]{1,0:T(8,128)S(1)} %get-tuple-element.33.left_ref, bf16[64,20,8,512]{3,2,1,0:T(8,128)(2,1)S(1)} %get-tuple-element.31.basis_ref.rest_4_), custom_call_target="tpu_custom_call" | custom-call | flops 2684354560 | bytes 10485760 | tf_op jit(solution)/shard_map/gram/pallas_call | solution.py:652
  23.6 0.2 join_own.1
  23.8 0.4 collective-permute-done.4.rest_1_
  24.2 3.1 %project.1 = (f32[8,128]{1,0:T(8,128)S(1)}, bf16[20,16,512]{2,1,0:T(8,128)(2,1)S(1)}, f32[2,5,8,4,512]{4,3,2,1,0:T(4,128)}) custom-call(s32[1]{0:T(128)} %bitcast.where_ref._, bf16[2,5,16,512]{3,2,1,0:T(8,128)(2,1)S(1)} %get-tuple-element.35.rest_0_, bf16[2,5,16,512]{3,2,1,0:T(8,128)(2,1)S(1)} %collective-permute-done.4.rest_1_, ...), custom_call_target="tpu_custom_call" | custom-call | flops 167772160 | bytes 10485760 | tf_op jit(solution)/shard_map/project/pallas_call | solution.py:705
  27.3 1.5 %collective-permute-start.6 = (f32[40,128]{1,0:T(8,128)S(1)}, f32[40,128]{1,0:T(8,128)S(1)}, u32[]{:S(2)}, u32[]{:S(2)}) collective-permute-start(f32[40,128]{1,0:T(8,128)S(1)} %merge.1), channel_id=1, source_target_pairs={{0,1},{1,0},{2,3},{3,2},{4,5},{5,4},{6,7},{7,6},{8,9},{9,8},{10,11... | collective-permute-start | bytes 61448 | tf_op jit(solution)/shard_map/ppermute | solution.py:550
  28.8 2.4 %collective-permute-done.6 = f32[40,128]{1,0:T(8,128)S(1)} collective-permute-done((f32[40,128]{1,0:T(8,128)S(1)}, f32[40,128]{1,0:T(8,128)S(1)}, u32[]{:S(2)}, u32[]{:S(2)}) %collective-permute-start.6) | collective-permute-done | bytes 20512 | tf_op jit(solution)/shard_map/ppermute | solution.py:550
  31.2 1.2 %collective-permute-done.7 = f32[40,128]{1,0:T(8,128)S(1)} collective-permute-done((f32[40,128]{1,0:T(8,128)S(1)}, f32[40,128]{1,0:T(8,128)S(1)}, u32[]{:S(2)}, u32[]{:S(2)}) %collective-permute-start.7) | collective-permute-done | bytes 20512 | tf_op jit(solution)/shard_map/ppermute | solution.py:550
  32.4 0.8 %collective-permute-start.8 = (f32[40,128]{1,0:T(8,128)S(1)}, f32[40,128]{1,0:T(8,128)S(1)}, u32[]{:S(2)}, u32[]{:S(2)}) collective-permute-start(f32[40,128]{1,0:T(8,128)S(1)} %add.16), channel_id=1, source_target_pairs={{0,8},{2,10},{4,12},{6,14},{8,0},{10,2},{12,4},{14,6},{16,24},{18,... | collective-permute-start | bytes 61448 | tf_op jit(solution)/shard_map/ppermute | solution.py:550
  33.2 3.0 %collective-permute-done.8 = f32[40,128]{1,0:T(8,128)S(1)} collective-permute-done((f32[40,128]{1,0:T(8,128)S(1)}, f32[40,128]{1,0:T(8,128)S(1)}, u32[]{:S(2)}, u32[]{:S(2)}) %collective-permute-start.8) | collective-permute-done | bytes 20512 | tf_op jit(solution)/shard_map/ppermute | solution.py:550
  36.2 1.8 %collective-permute-start.9 = (f32[40,128]{1,0:T(8,128)S(1)}, f32[40,128]{1,0:T(8,128)S(1)}, u32[]{:S(2)}, u32[]{:S(2)}) collective-permute-start(f32[40,128]{1,0:T(8,128)S(1)} %add.17), channel_id=1, source_target_pairs={{0,16},{2,18},{4,20},{6,22},{8,24},{10,26},{12,28},{14,30},{16,0},... | collective-permute-start | bytes 61448 | tf_op jit(solution)/shard_map/ppermute | solution.py:550
  38.0 2.9 %collective-permute-done.9 = f32[40,128]{1,0:T(8,128)S(1)} collective-permute-done((f32[40,128]{1,0:T(8,128)S(1)}, f32[40,128]{1,0:T(8,128)S(1)}, u32[]{:S(2)}, u32[]{:S(2)}) %collective-permute-start.9) | collective-permute-done | bytes 20512 | tf_op jit(solution)/shard_map/ppermute | solution.py:550
  40.9 1.6 %collective-permute-start.10 = (f32[40,128]{1,0:T(8,128)S(1)}, f32[40,128]{1,0:T(8,128)S(1)}, u32[]{:S(2)}, u32[]{:S(2)}) collective-permute-start(f32[40,128]{1,0:T(8,128)S(1)} %add.18.sums_ref), channel_id=1, source_target_pairs={{0,4},{2,6},{4,0},{6,2},{8,12},{10,14},{12,8},{14,10},{16,20},{18,... | collective-permute-start | bytes 61448 | tf_op jit(solution)/shard_map/ppermute | solution.py:550
  42.5 2.4 %inverse.1 = (f32[64,64]{1,0:T(8,128)S(1)}, f32[64,512]{1,0:T(8,128)S(1)}) custom-call(f32[40,128]{1,0:T(8,128)S(1)} %add.18.sums_ref), custom_call_target="tpu_custom_call" | custom-call | flops 20000000 | bytes 32768 | tf_op jit(solution)/shard_map/inverse/pallas_call | solution.py:744
  44.9 3.2 %finish.1 = (f32[2,20,8,512]{3,2,1,0:T(8,128)}, f32[2,64]{1,0:T(2,128)}, f32[2,2]{1,0:T(2,128)}) custom-call(f32[40,128]{1,0:T(8,128)S(1)} %add.19.projected_ref, f32[40,128]{1,0:T(8,128)S(1)} %add.18.sums_ref, f32[64,64]{1,0:T(8,128)S(1)} %get-tuple-element.40.inverse_ref, f32[64,512]{1,0:T(8,128)S(1)} %get-tuple-element.41.spread_ref, ...), custom_call_target="tpu_custom_call" | custom-call | flops 335544320 | bytes 11796480 | tf_op jit(solution)/shard_map/finish/pallas_call | solution.py:757
  (16 shorter events, 0.1 us)
Async XLA Ops:
  0.6 1.1 %copy-start = (f32[2,5,8,4,512]{4,3,2,1,0:T(4,128)S(1)}, f32[2,5,8,4,512]{4,3,2,1,0:T(4,128)}, u32[]{:S(2)}) copy-start(f32[2,5,8,4,512]{4,3,2,1,0:T(4,128)} %source_ref.1) | copy-start | bytes 1966084
  2.4 13.7 %collective-permute-start.2 = (bf16[5,48,512]{2,1,0:T(8,128)(2,1)S(1)}, bf16[5,48,512]{2,1,0:T(8,128)(2,1)S(1)}, u32[]{:S(2)}, u32[]{:S(2)}) collective-permute-start(bf16[5,48,512]{2,1,0:T(8,128)(2,1)S(1)} %get-tuple-element.27._), channel_id=1, source_target_pairs={{0,1},{1,0},{2,3},{3,2},{4,5},{5,4},{6,7},{7,6},{8,9},{9,8},{10,11... | collective-permute-start | bytes 737288 | tf_op jit(solution)/shard_map/ppermute | solution.py:602
  6.1 11.9 %collective-permute-start = (f32[2,5,4,4,512]{4,3,2,1,0:T(4,128)S(1)}, f32[2,5,4,4,512]{4,3,2,1,0:T(4,128)S(1)}, u32[]{:S(2)}, u32[]{:S(2)}) collective-permute-start(f32[2,5,4,4,512]{4,3,2,1,0:T(4,128)S(1)} %get-tuple-element.28), channel_id=1, source_target_pairs={{0,2},{2,4},{4,6},{6,8},{8,10},{10,12},{12,14},{14,16},{16,18},{18... | collective-permute-start | bytes 983048 | tf_op jit(solution)/shard_map/ppermute | solution.py:603
  6.2 11.8 %collective-permute-start.1 = (f32[2,5,4,4,512]{4,3,2,1,0:T(4,128)S(1)}, f32[2,5,4,4,512]{4,3,2,1,0:T(4,128)S(1)}, u32[]{:S(2)}, u32[]{:S(2)}) collective-permute-start(f32[2,5,4,4,512]{4,3,2,1,0:T(4,128)S(1)} %get-tuple-element.29), channel_id=1, source_target_pairs={{2,0},{4,2},{6,4},{8,6},{10,8},{12,10},{14,12},{16,14},{18,16},{20... | collective-permute-start | bytes 983048 | tf_op jit(solution)/shard_map/ppermute | solution.py:604
  10.6 12.9 %collective-permute-start.3 = (bf16[5,48,512]{2,1,0:T(8,128)(2,1)S(1)}, bf16[5,48,512]{2,1,0:T(8,128)(2,1)S(1)}, u32[]{:S(2)}, u32[]{:S(2)}) collective-permute-start(bf16[5,48,512]{2,1,0:T(8,128)(2,1)S(1)} %get-tuple-element.34), channel_id=1, source_target_pairs={{0,1},{1,0},{2,3},{3,2},{4,5},{5,4},{6,7},{7,6},{8,9},{9,8},{10,11... | collective-permute-start | bytes 737288 | tf_op jit(solution)/shard_map/ppermute | solution.py:605
  18.2 6.0 %collective-permute-start.4 = (bf16[2,5,16,512]{3,2,1,0:T(8,128)(2,1)S(1)}, bf16[2,5,16,512]{3,2,1,0:T(8,128)(2,1)S(1)}, u32[]{:S(2)}, u32[]{:S(2)}) collective-permute-start(bf16[2,5,16,512]{3,2,1,0:T(8,128)(2,1)S(1)} %get-tuple-element.30._), channel_id=1, source_target_pairs={{0,1},{1,0},{2,3},{3,2},{4,5},{5,4},{6,7},{7,6},{8,9},{9,8},{10,11... | collective-permute-start | bytes 491528 | tf_op jit(solution)/shard_map/ppermute | solution.py:681
  23.5 3.8 %collective-permute-start.5 = (f32[32,128]{1,0:T(8,128)S(1)}, f32[32,128]{1,0:T(8,128)S(1)}, u32[]{:S(2)}, u32[]{:S(2)}) collective-permute-start(f32[32,128]{1,0:T(8,128)S(1)} %gram.1._.gram_ref), channel_id=1, source_target_pairs={{0,4},{2,6},{4,0},{6,2},{8,12},{10,14},{12,8},{14,10},{16,20},{18,... | collective-permute-start | bytes 49160 | tf_op jit(solution)/shard_map/ppermute | solution.py:696
  27.3 3.8 %collective-permute-start.6 = (f32[40,128]{1,0:T(8,128)S(1)}, f32[40,128]{1,0:T(8,128)S(1)}, u32[]{:S(2)}, u32[]{:S(2)}) collective-permute-start(f32[40,128]{1,0:T(8,128)S(1)} %merge.1), channel_id=1, source_target_pairs={{0,1},{1,0},{2,3},{3,2},{4,5},{5,4},{6,7},{7,6},{8,9},{9,8},{10,11... | collective-permute-start | bytes 61448 | tf_op jit(solution)/shard_map/ppermute | solution.py:550
  31.2 1.2 %collective-permute-start.7 = (f32[40,128]{1,0:T(8,128)S(1)}, f32[40,128]{1,0:T(8,128)S(1)}, u32[]{:S(2)}, u32[]{:S(2)}) collective-permute-start(f32[40,128]{1,0:T(8,128)S(1)} %add.15), channel_id=1, source_target_pairs={{0,2},{2,0},{4,6},{6,4},{8,10},{10,8},{12,14},{14,12},{16,18},{18,... | collective-permute-start | bytes 61448 | tf_op jit(solution)/shard_map/ppermute | solution.py:550
  32.4 3.8 %collective-permute-start.8 = (f32[40,128]{1,0:T(8,128)S(1)}, f32[40,128]{1,0:T(8,128)S(1)}, u32[]{:S(2)}, u32[]{:S(2)}) collective-permute-start(f32[40,128]{1,0:T(8,128)S(1)} %add.16), channel_id=1, source_target_pairs={{0,8},{2,10},{4,12},{6,14},{8,0},{10,2},{12,4},{14,6},{16,24},{18,... | collective-permute-start | bytes 61448 | tf_op jit(solution)/shard_map/ppermute | solution.py:550
  36.2 4.7 %collective-permute-start.9 = (f32[40,128]{1,0:T(8,128)S(1)}, f32[40,128]{1,0:T(8,128)S(1)}, u32[]{:S(2)}, u32[]{:S(2)}) collective-permute-start(f32[40,128]{1,0:T(8,128)S(1)} %add.17), channel_id=1, source_target_pairs={{0,16},{2,18},{4,20},{6,22},{8,24},{10,26},{12,28},{14,30},{16,0},... | collective-permute-start | bytes 61448 | tf_op jit(solution)/shard_map/ppermute | solution.py:550
  40.9 4.0 %collective-permute-start.10 = (f32[40,128]{1,0:T(8,128)S(1)}, f32[40,128]{1,0:T(8,128)S(1)}, u32[]{:S(2)}, u32[]{:S(2)}) collective-permute-start(f32[40,128]{1,0:T(8,128)S(1)} %add.18.sums_ref), channel_id=1, source_target_pairs={{0,4},{2,6},{4,0},{6,2},{8,12},{10,14},{12,8},{14,10},{16,20},{18,... | collective-permute-start | bytes 61448 | tf_op jit(solution)/shard_map/ppermute | solution.py:550

commit v8 on v7

--- a/solution.py
+++ b/solution.py
@@ -225,7 +225,9 @@
     return right, left
 
 
-def inner_kernel(windows_ref, basis_ref, part_ref, kept_ref, scratch, sems):
+def inner_gram_kernel(
+    early, windows_ref, basis_ref, part_ref, right_ref, left_ref, kept_ref, scratch, sems
+):
     chunks = sems.shape[0]
     per_chunk = kept_ref.shape[1] // chunks
     copies = []
@@ -236,18 +238,11 @@
         )
         copies[c].start()
     inner_part(windows_ref, part_ref, scratch)
-    for copy in copies:
-        copy.wait()
-
-
-def early_gram_kernel(early, chunks, _, basis_ref, right_ref, left_ref):
-    right, left = gram_blocks(
-        basis_ref,
-        range(early),
-        basis_ref.shape[1] // chunks,
-        jnp.zeros(right_ref.shape, jnp.float32),
-        jnp.zeros(left_ref.shape, jnp.float32),
-    )
+    right, left = jnp.zeros(right_ref.shape, jnp.float32), jnp.zeros(left_ref.shape, jnp.float32)
+    for c in range(chunks):
+        copies[c].wait()
+        if c < early:
+            right, left = gram_blocks(kept_ref, [c], per_chunk, right, left)
     right_ref[...] = right
     left_ref[...] = left
 
@@ -292,30 +287,52 @@
                 next_ref[w, f, x] = total
 
 
-def paired_join_kernel(
-    own, where_ref, _, part_ref, left_ref, right_ref, group_ref, made, snaps_ref
-):
-    windows, _, planes, layers, cells = part_ref.shape
-    half = planes // 2
-    first = where_ref[0] == 0
-    base = half * (where_ref[0] if own else 1 - where_ref[0])
-    ahead = base == 0
-    zero = jnp.zeros((2, cells), jnp.float32)
+def wall_terms_of(first, group_ref, w, f):
+    upper = group_ref[f, 16 * w : 16 * w + 16].astype(jnp.float32)
+    lower = group_ref[f, 32:48].astype(jnp.float32)[8 * w : 8 * w + 8]
+    zero = jnp.zeros((2, upper.shape[1]), jnp.float32)
+    made = []
+    for x in range(4):
+        rest = lower[2 * x : 2 * x + 2]
+        rest = jnp.where(
+            first, jnp.concatenate([zero, rest], axis=0), jnp.concatenate([rest, zero], axis=0)
+        )
+        made.append(upper[4 * x : 4 * x + 4] + rest)
+    return made
+
+
+def wall_join_kernel(where_ref, part_ref, group_ref, given_ref):
+    windows, _, planes = part_ref.shape[:3]
+    base = planes // 2 * (1 - where_ref[0])
     for w in range(windows):
         for f in range(5):
-            upper = group_ref[f, 16 * w : 16 * w + 16].astype(jnp.float32)
-            lower = group_ref[f, 32:48].astype(jnp.float32)[8 * w : 8 * w + 8]
+            for x, term in enumerate(wall_terms_of(where_ref[0] == 0, group_ref, w, f)):
+                given_ref[w, f, x] = part_ref[w, f, base + x] + term
+
+
+def edge_join_kernel(where_ref, part_ref, left_ref, right_ref, made, snaps_ref):
+    windows, _, half = part_ref.shape[:3]
+    ahead = where_ref[0] == 1
+    for w in range(windows):
+        for f in range(5):
             done = []
             for x in range(half):
-                rest_now = lower[2 * x : 2 * x + 2]
-                total = part_ref[w, f, base + x] + (
-                    upper[layers * x : layers * x + layers]
-                    + jnp.where(
-                        first,
-                        jnp.concatenate([zero, rest_now], axis=0),
-                        jnp.concatenate([rest_now, zero], axis=0),
-                    )
-                )
+                total = part_ref[w, f, x] + jnp.where(ahead, left_ref[w, f, x], right_ref[w, f, x])
+                made[w, f, x] = total
+                done.append(total)
+            snaps_ref[w, f] = jnp.concatenate(done, axis=0).astype(jnp.bfloat16)
+
+
+def own_join_kernel(where_ref, _, part_ref, left_ref, right_ref, group_ref, made, snaps_ref):
+    windows, _, planes = part_ref.shape[:3]
+    half = planes // 2
+    ahead = where_ref[0] == 0
+    base = half * where_ref[0]
+    for w in range(windows):
+        for f in range(5):
+            done = []
+            for x, term in enumerate(wall_terms_of(ahead, group_ref, w, f)):
+                total = part_ref[w, f, base + x] + term
                 total = total + jnp.where(ahead, left_ref[w, f, x], right_ref[w, f, x])
                 made[w, f, x] = total
                 done.append(total)
@@ -623,30 +640,26 @@
         from_left = lax.ppermute(to_next, "solver", to_right)
         from_right = lax.ppermute(to_last, "solver", to_left)
 
-    early = 2
+    early = 3
     gram_flops = 2 * wide * wide * cells * tiles
-    inner, basis = pl.pallas_call(
-        inner_kernel,
-        out_shape=[shape(windows.shape, f32), shape(basis.shape, bf16)],
+    inner, right, left, basis = pl.pallas_call(
+        functools.partial(inner_gram_kernel, early),
+        out_shape=[
+            shape(windows.shape, f32),
+            shape((wide, wide // 2), f32),
+            shape((wide // 2, wide // 2), f32),
+            shape(basis.shape, bf16),
+        ],
         in_specs=[WHOLE, FAR],
-        out_specs=[WHOLE] * 2,
+        out_specs=[WHOLE] * 4,
         scratch_shapes=[
             pltpu.VMEM((2 * fields, planes, count * layers, cells), f32),
             pltpu.SemaphoreType.DMA((fields,)),
         ],
         compiler_params=params(40),
         cost_estimate=cost(1_000_000, windows.size),
-        name="inner",
+        name="inner_gram",
     )(kept, basis)
-    right, left = pl.pallas_call(
-        functools.partial(early_gram_kernel, early, fields),
-        out_shape=[shape((wide, wide // 2), f32), shape((wide // 2, wide // 2), f32)],
-        in_specs=[LOOSE, WHOLE],
-        out_specs=[WHOLE] * 2,
-        compiler_params=params(24),
-        cost_estimate=cost(gram_flops // 2, basis_bytes),
-        name="early_gram",
-    )(near_group if paired else place, basis)
 
     def rest_of_gram(after):
         return pl.pallas_call(
@@ -666,18 +679,24 @@
 
         half_next = shape((count, fields, planes // 2, layers, cells), f32)
 
-        def join(own, after, group):
-            return pl.pallas_call(
-                functools.partial(paired_join_kernel, own),
-                out_shape=[half_next, shape(half_shape, bf16)],
-                in_specs=[SCALAR, LOOSE] + [WHOLE] * 4,
-                out_specs=[WHOLE] * 2,
-                compiler_params=params(16),
-                cost_estimate=join_cost,
-                name="join_own" if own else "join_given",
-            )(place, after, inner, from_left, from_right, group)
-
-        next_given, given = join(False, place, near_group)
+        inner_given = pl.pallas_call(
+            wall_join_kernel,
+            out_shape=half_next,
+            in_specs=[SCALAR] + [WHOLE] * 2,
+            out_specs=WHOLE,
+            compiler_params=params(16),
+            cost_estimate=cost(gram_flops, 2 * basis_bytes),
+            name="wall_join",
+        )(place, inner, near_group)
+        next_given, given = pl.pallas_call(
+            edge_join_kernel,
+            out_shape=[half_next, shape(half_shape, bf16)],
+            in_specs=[SCALAR] + [WHOLE] * 3,
+            out_specs=[WHOLE] * 2,
+            compiler_params=params(16),
+            cost_estimate=join_cost,
+            name="edge_join",
+        )(place, inner_given, from_left, from_right)
         got = lax.ppermute(given, "analysis", swap)
         gram = rest_of_gram(given)
     else:
@@ -695,7 +714,15 @@
     lone = ring_bits.pop(1 if len(ring_bits) > 1 else 0)
     gram_far = lax.ppermute(gram, "solver", [(i, i ^ lone) for i in range(ring)])
     if paired:
-        next_own, own = join(True, gram, later_group)
+        next_own, own = pl.pallas_call(
+            own_join_kernel,
+            out_shape=[half_next, shape(half_shape, bf16)],
+            in_specs=[SCALAR, LOOSE] + [WHOLE] * 4,
+            out_specs=[WHOLE] * 2,
+            compiler_params=params(16),
+            cost_estimate=join_cost,
+            name="own_join",
+        )(place, gram, inner, from_left, from_right, later_group)
 
     sums_shape = shape((8, LANES), f32)
     snaps_shape = shape((tiles, 2 * 8, cells), bf16)

time: 48.3 us -> 48.6 us (level)
  waiting for transfers between devices: 9.82 us -> 13.2 us
  starting transfers between devices: 15.3 us -> 13.5 us
  Pallas kernels: 21.1 us -> 19.9 us
    ppermute x5, starting transfers between devices: 5.7 us -> 3.91 us  [swap_added(): lax.ppermute(value, axis, [(i, i ^ bit) for i in range(count)])]
    ppermute x5, waiting for transfers between devices: 9.4 us -> 11.2 us  [swap_added(): lax.ppermute(value, axis, [(i, i ^ bit) for i in range(count)])]
    ppermute x1, waiting for transfers between devices: 0.41 us -> 1.99 us  [body(): got = lax.ppermute(given, 'analysis', swap)]
    pallas_call x1, Pallas kernels: 3.25 us -> 2.44 us  [rest_of_gram(): pl.pallas_call(functools.partial(gram_kernel, early, fields), out_shape=s...]
  transfers between devices with their start and end apart: 11 -> 11, of which waited for: 5 -> 6; matrix products, arithmetic and copies ran while one was open for 0% -> 0% of each run, Pallas kernels for 36% -> 33%
where the time goes in v8:
time: 48.6 us; the launch traced here: 48.5 us
  Pallas kernels  19.9 us (41%)
  starting transfers between devices  13.5 us (28%)
  waiting for transfers between devices  13.2 us (27%)
  local copies, waits for them, and re-layouts  1.08 us (2%)
  between operations  0.77 us (2%)
    ppermute x5, waiting for transfers between devices, swap_added(): lax.ppermute(value, axis, [(i, i ^ bit) for i in range(count)])  11.2 us
    pallas_call x1, Pallas kernels, body(): pl.pallas_call(functools.partial(inner_gram_kernel, early), out_shape=[sh...  6.93 us
    ppermute x1, starting transfers between devices, body(): from_right = lax.ppermute(to_last, 'solver', to_left)  4.43 us
    ppermute x5, starting transfers between devices, swap_added(): lax.ppermute(value, axis, [(i, i ^ bit) for i in range(count)])  3.91 us
    pallas_call x1, Pallas kernels, body(): pl.pallas_call(functools.partial(finish_kernel, rows_total), out_shape=[s...  3.18 us
    pallas_call x1, Pallas kernels, body(): pl.pallas_call(functools.partial(project_kernel, True), out_shape=[sums_s...  3.12 us
    ppermute x1, starting transfers between devices, body(): near_group = lax.ppermute(near_group, 'analysis', swap)  3 us
    pallas_call x1, Pallas kernels, rest_of_gram(): pl.pallas_call(functools.partial(gram_kernel, early, fields), out_shape=s...  2.44 us
  transfers between devices with their start and end apart: 11, of which 6 were waited for; matrix products, arithmetic and copies ran while one was open for 0% of the time, Pallas kernels for 33%

profile of v8, /device:TPU:0, one launch (start us, length us, event | category | flops | bytes accessed | tf_op | source)
XLA Modules:
  0.0 48.5 jit_solution(11822742222554665298)
XLA Ops:
  0.6 1.1 %copy-done = f32[2,5,8,4,512]{4,3,2,1,0:T(4,128)S(1)} copy-done((f32[2,5,8,4,512]{4,3,2,1,0:T(4,128)S(1)}, f32[2,5,8,4,512]{4,3,2,1,0:T(4,128)}, u32[]{:S(2)}) %copy-start) | copy-done | bytes 655384
  1.7 0.7 %near_faces.1 = (bf16[5,48,512]{2,1,0:T(8,128)(2,1)S(1)}, f32[2,5,8,4,512]{4,3,2,1,0:T(4,128)S(1)}) custom-call(s32[1]{0:T(128)} %bitcast.where_ref, f32[2,5,8,4,512]{4,3,2,1,0:T(4,128)S(1)} %copy-done), custom_call_target="tpu_custom_call" | custom-call | flops 10000000 | bytes 1638400 | tf_op jit(solution)/shard_map/near_faces/pallas_call | solution.py:599
  2.4 3.0 %collective-permute-start = (bf16[5,48,512]{2,1,0:T(8,128)(2,1)S(1)}, bf16[5,48,512]{2,1,0:T(8,128)(2,1)S(1)}, u32[]{:S(2)}, u32[]{:S(2)}) collective-permute-start(bf16[5,48,512]{2,1,0:T(8,128)(2,1)S(1)} %get-tuple-element.27._), channel_id=1, source_target_pairs={{0,1},{1,0},{2,3},{3,2},{4,5},{5,4},{6,7},{7,6},{8,9},{9,8},{10,11... | collective-permute-start | bytes 737288 | tf_op jit(solution)/shard_map/ppermute | solution.py:619
  5.5 0.7 %later_faces.1 = (bf16[5,48,512]{2,1,0:T(8,128)(2,1)S(1)}, f32[2,5,4,4,512]{4,3,2,1,0:T(4,128)S(1)}, f32[2,5,4,4,512]{4,3,2,1,0:T(4,128)S(1)}) custom-call(s32[1]{0:T(128)} %bitcast.where_ref, bf16[5,48,512]{2,1,0:T(8,128)(2,1)S(1)} %get-tuple-element.27._, f32[2,5,8,4,512]{4,3,2,1,0:T(4,128)S(1)} %get-tuple-element.25.windows_ref), custom_call_target="tpu_custom_call" | custom-call | flops 10000000 | bytes 1638400 | tf_op jit(solution)/shard_map/later_faces/pallas_call | solution.py:609
  6.1 0.1 collective-permute-start.3
  6.3 4.4 %collective-permute-start.2 = (f32[2,5,4,4,512]{4,3,2,1,0:T(4,128)S(1)}, f32[2,5,4,4,512]{4,3,2,1,0:T(4,128)S(1)}, u32[]{:S(2)}, u32[]{:S(2)}) collective-permute-start(f32[2,5,4,4,512]{4,3,2,1,0:T(4,128)S(1)} %get-tuple-element.29), channel_id=1, source_target_pairs={{2,0},{4,2},{6,4},{8,6},{10,8},{12,10},{14,12},{16,14},{18,16},{20... | collective-permute-start | bytes 983048 | tf_op jit(solution)/shard_map/ppermute | solution.py:621
  10.7 6.9 %inner_gram.1 = (f32[2,5,8,4,512]{4,3,2,1,0:T(4,128)S(1)}, f32[512,256]{1,0:T(8,128)S(1)}, f32[256,256]{1,0:T(8,128)S(1)}, bf16[64,20,8,512]{3,2,1,0:T(8,128)(2,1)S(1)}) custom-call(f32[2,5,8,4,512]{4,3,2,1,0:T(4,128)S(1)} %get-tuple-element.25.windows_ref, bf16[64,20,8,512]{3,2,1,0:T(8,128)(2,1)} %bitcast.3), custom_call_target="tpu_custom_call" | custom-call | flops 1000000 | bytes 163840 | tf_op jit(solution)/shard_map/inner_gram/pallas_call | solution.py:645
  17.6 0.2 wall_join.1.part_ref
  17.8 0.1 edge_join.1
  17.9 2.0 %collective-permute-start.4 = (bf16[2,5,16,512]{3,2,1,0:T(8,128)(2,1)S(1)}, bf16[2,5,16,512]{3,2,1,0:T(8,128)(2,1)S(1)}, u32[]{:S(2)}, u32[]{:S(2)}) collective-permute-start(bf16[2,5,16,512]{3,2,1,0:T(8,128)(2,1)S(1)} %get-tuple-element.30._), channel_id=1, source_target_pairs={{0,1},{1,0},{2,3},{3,2},{4,5},{5,4},{6,7},{7,6},{8,9},{9,8},{10,11... | collective-permute-start | bytes 491528 | tf_op jit(solution)/shard_map/ppermute | solution.py:700
  19.9 2.4 %gram.1._.gram_ref = f32[32,128]{1,0:T(8,128)S(1)} custom-call(bf16[2,5,16,512]{3,2,1,0:T(8,128)(2,1)S(1)} %get-tuple-element.30._, f32[512,256]{1,0:T(8,128)S(1)} %get-tuple-element.31.right_ref, f32[256,256]{1,0:T(8,128)S(1)} %get-tuple-element.32.left_ref, bf16[64,20,8,512]{3,2,1,0:T(8,128)(2,1)S(1)} %get-tuple-element.33.basis_ref.rest_4_), custom_call_target="tpu_custom_call" | custom-call | flops 2684354560 | bytes 10485760 | tf_op jit(solution)/shard_map/gram/pallas_call | solution.py:665
  22.4 0.2 own_join.1
  22.6 2.0 %collective-permute-done.4.rest_1_ = bf16[2,5,16,512]{3,2,1,0:T(8,128)(2,1)S(1)} collective-permute-done((bf16[2,5,16,512]{3,2,1,0:T(8,128)(2,1)S(1)}, bf16[2,5,16,512]{3,2,1,0:T(8,128)(2,1)S(1)}, u32[]{:S(2)}, u32[]{:S(2)}) %collective-permute-start.4) | collective-permute-done | bytes 163872 | tf_op jit(solution)/shard_map/ppermute | solution.py:700
  24.6 3.1 %project.1 = (f32[8,128]{1,0:T(8,128)S(1)}, bf16[20,16,512]{2,1,0:T(8,128)(2,1)S(1)}, f32[2,5,8,4,512]{4,3,2,1,0:T(4,128)}) custom-call(s32[1]{0:T(128)} %bitcast.where_ref, bf16[2,5,16,512]{3,2,1,0:T(8,128)(2,1)S(1)} %get-tuple-element.35.rest_0_, bf16[2,5,16,512]{3,2,1,0:T(8,128)(2,1)S(1)} %collective-permute-done.4.rest_1_, ...), custom_call_target="tpu_custom_call" | custom-call | flops 167772160 | bytes 10485760 | tf_op jit(solution)/shard_map/project/pallas_call | solution.py:732
  27.8 1.6 %collective-permute-start.6 = (f32[40,128]{1,0:T(8,128)S(1)}, f32[40,128]{1,0:T(8,128)S(1)}, u32[]{:S(2)}, u32[]{:S(2)}) collective-permute-start(f32[40,128]{1,0:T(8,128)S(1)} %merge.1), channel_id=1, source_target_pairs={{0,1},{1,0},{2,3},{3,2},{4,5},{5,4},{6,7},{7,6},{8,9},{9,8},{10,11... | collective-permute-start | bytes 61448 | tf_op jit(solution)/shard_map/ppermute | solution.py:567
  29.3 2.3 %collective-permute-done.6 = f32[40,128]{1,0:T(8,128)S(1)} collective-permute-done((f32[40,128]{1,0:T(8,128)S(1)}, f32[40,128]{1,0:T(8,128)S(1)}, u32[]{:S(2)}, u32[]{:S(2)}) %collective-permute-start.6) | collective-permute-done | bytes 20512 | tf_op jit(solution)/shard_map/ppermute | solution.py:567
  31.6 1.2 %collective-permute-done.7 = f32[40,128]{1,0:T(8,128)S(1)} collective-permute-done((f32[40,128]{1,0:T(8,128)S(1)}, f32[40,128]{1,0:T(8,128)S(1)}, u32[]{:S(2)}, u32[]{:S(2)}) %collective-permute-start.7) | collective-permute-done | bytes 20512 | tf_op jit(solution)/shard_map/ppermute | solution.py:567
  32.8 0.7 %collective-permute-start.8 = (f32[40,128]{1,0:T(8,128)S(1)}, f32[40,128]{1,0:T(8,128)S(1)}, u32[]{:S(2)}, u32[]{:S(2)}) collective-permute-start(f32[40,128]{1,0:T(8,128)S(1)} %add.16), channel_id=1, source_target_pairs={{0,8},{2,10},{4,12},{6,14},{8,0},{10,2},{12,4},{14,6},{16,24},{18,... | collective-permute-start | bytes 61448 | tf_op jit(solution)/shard_map/ppermute | solution.py:567
  33.5 3.1 %collective-permute-done.8 = f32[40,128]{1,0:T(8,128)S(1)} collective-permute-done((f32[40,128]{1,0:T(8,128)S(1)}, f32[40,128]{1,0:T(8,128)S(1)}, u32[]{:S(2)}, u32[]{:S(2)}) %collective-permute-start.8) | collective-permute-done | bytes 20512 | tf_op jit(solution)/shard_map/ppermute | solution.py:567
  36.6 1.7 %collective-permute-start.9 = (f32[40,128]{1,0:T(8,128)S(1)}, f32[40,128]{1,0:T(8,128)S(1)}, u32[]{:S(2)}, u32[]{:S(2)}) collective-permute-start(f32[40,128]{1,0:T(8,128)S(1)} %add.17), channel_id=1, source_target_pairs={{0,16},{2,18},{4,20},{6,22},{8,24},{10,26},{12,28},{14,30},{16,0},... | collective-permute-start | bytes 61448 | tf_op jit(solution)/shard_map/ppermute | solution.py:567
  38.3 3.2 %collective-permute-done.9 = f32[40,128]{1,0:T(8,128)S(1)} collective-permute-done((f32[40,128]{1,0:T(8,128)S(1)}, f32[40,128]{1,0:T(8,128)S(1)}, u32[]{:S(2)}, u32[]{:S(2)}) %collective-permute-start.9) | collective-permute-done | bytes 20512 | tf_op jit(solution)/shard_map/ppermute | solution.py:567
  41.5 2.4 %inverse.1 = (f32[64,64]{1,0:T(8,128)S(1)}, f32[64,512]{1,0:T(8,128)S(1)}) custom-call(f32[40,128]{1,0:T(8,128)S(1)} %add.18.sums_ref), custom_call_target="tpu_custom_call" | custom-call | flops 20000000 | bytes 32768 | tf_op jit(solution)/shard_map/inverse/pallas_call | solution.py:771
  43.9 1.3 %collective-permute-done.10 = f32[40,128]{1,0:T(8,128)S(1)} collective-permute-done((f32[40,128]{1,0:T(8,128)S(1)}, f32[40,128]{1,0:T(8,128)S(1)}, u32[]{:S(2)}, u32[]{:S(2)}) %collective-permute-start.10) | collective-permute-done | bytes 20512 | tf_op jit(solution)/shard_map/ppermute | solution.py:567
  45.3 3.2 %finish.1 = (f32[2,20,8,512]{3,2,1,0:T(8,128)}, f32[2,64]{1,0:T(2,128)}, f32[2,2]{1,0:T(2,128)}) custom-call(f32[40,128]{1,0:T(8,128)S(1)} %add.19.projected_ref, f32[40,128]{1,0:T(8,128)S(1)} %add.18.sums_ref, f32[64,64]{1,0:T(8,128)S(1)} %get-tuple-element.40.inverse_ref, f32[64,512]{1,0:T(8,128)S(1)} %get-tuple-element.41.spread_ref, ...), custom_call_target="tpu_custom_call" | custom-call | flops 335544320 | bytes 11796480 | tf_op jit(solution)/shard_map/finish/pallas_call | solution.py:784
  (16 shorter events, 0.1 us)
Async XLA Ops:
  0.6 1.1 %copy-start = (f32[2,5,8,4,512]{4,3,2,1,0:T(4,128)S(1)}, f32[2,5,8,4,512]{4,3,2,1,0:T(4,128)}, u32[]{:S(2)}) copy-start(f32[2,5,8,4,512]{4,3,2,1,0:T(4,128)} %source_ref.1) | copy-start | bytes 1966084
  2.4 15.2 %collective-permute-start = (bf16[5,48,512]{2,1,0:T(8,128)(2,1)S(1)}, bf16[5,48,512]{2,1,0:T(8,128)(2,1)S(1)}, u32[]{:S(2)}, u32[]{:S(2)}) collective-permute-start(bf16[5,48,512]{2,1,0:T(8,128)(2,1)S(1)} %get-tuple-element.27._), channel_id=1, source_target_pairs={{0,1},{1,0},{2,3},{3,2},{4,5},{5,4},{6,7},{7,6},{8,9},{9,8},{10,11... | collective-permute-start | bytes 737288 | tf_op jit(solution)/shard_map/ppermute | solution.py:619
  6.1 16.3 %collective-permute-start.3 = (bf16[5,48,512]{2,1,0:T(8,128)(2,1)S(1)}, bf16[5,48,512]{2,1,0:T(8,128)(2,1)S(1)}, u32[]{:S(2)}, u32[]{:S(2)}) collective-permute-start(bf16[5,48,512]{2,1,0:T(8,128)(2,1)S(1)} %get-tuple-element.34), channel_id=1, source_target_pairs={{0,1},{1,0},{2,3},{3,2},{4,5},{5,4},{6,7},{7,6},{8,9},{9,8},{10,11... | collective-permute-start | bytes 737288 | tf_op jit(solution)/shard_map/ppermute | solution.py:622
  6.2 11.6 %collective-permute-start.1 = (f32[2,5,4,4,512]{4,3,2,1,0:T(4,128)S(1)}, f32[2,5,4,4,512]{4,3,2,1,0:T(4,128)S(1)}, u32[]{:S(2)}, u32[]{:S(2)}) collective-permute-start(f32[2,5,4,4,512]{4,3,2,1,0:T(4,128)S(1)} %get-tuple-element.28), channel_id=1, source_target_pairs={{0,2},{2,4},{4,6},{6,8},{8,10},{10,12},{12,14},{14,16},{16,18},{18... | collective-permute-start | bytes 983048 | tf_op jit(solution)/shard_map/ppermute | solution.py:620
  6.3 11.6 %collective-permute-start.2 = (f32[2,5,4,4,512]{4,3,2,1,0:T(4,128)S(1)}, f32[2,5,4,4,512]{4,3,2,1,0:T(4,128)S(1)}, u32[]{:S(2)}, u32[]{:S(2)}) collective-permute-start(f32[2,5,4,4,512]{4,3,2,1,0:T(4,128)S(1)} %get-tuple-element.29), channel_id=1, source_target_pairs={{2,0},{4,2},{6,4},{8,6},{10,8},{12,10},{14,12},{16,14},{18,16},{20... | collective-permute-start | bytes 983048 | tf_op jit(solution)/shard_map/ppermute | solution.py:621
  17.9 6.7 %collective-permute-start.4 = (bf16[2,5,16,512]{3,2,1,0:T(8,128)(2,1)S(1)}, bf16[2,5,16,512]{3,2,1,0:T(8,128)(2,1)S(1)}, u32[]{:S(2)}, u32[]{:S(2)}) collective-permute-start(bf16[2,5,16,512]{3,2,1,0:T(8,128)(2,1)S(1)} %get-tuple-element.30._), channel_id=1, source_target_pairs={{0,1},{1,0},{2,3},{3,2},{4,5},{5,4},{6,7},{7,6},{8,9},{9,8},{10,11... | collective-permute-start | bytes 491528 | tf_op jit(solution)/shard_map/ppermute | solution.py:700
  22.4 5.4 %collective-permute-start.5 = (f32[32,128]{1,0:T(8,128)S(1)}, f32[32,128]{1,0:T(8,128)S(1)}, u32[]{:S(2)}, u32[]{:S(2)}) collective-permute-start(f32[32,128]{1,0:T(8,128)S(1)} %gram.1._.gram_ref), channel_id=1, source_target_pairs={{0,4},{2,6},{4,0},{6,2},{8,12},{10,14},{12,8},{14,10},{16,20},{18,... | collective-permute-start | bytes 49160 | tf_op jit(solution)/shard_map/ppermute | solution.py:715
  27.8 3.8 %collective-permute-start.6 = (f32[40,128]{1,0:T(8,128)S(1)}, f32[40,128]{1,0:T(8,128)S(1)}, u32[]{:S(2)}, u32[]{:S(2)}) collective-permute-start(f32[40,128]{1,0:T(8,128)S(1)} %merge.1), channel_id=1, source_target_pairs={{0,1},{1,0},{2,3},{3,2},{4,5},{5,4},{6,7},{7,6},{8,9},{9,8},{10,11... | collective-permute-start | bytes 61448 | tf_op jit(solution)/shard_map/ppermute | solution.py:567
  31.6 1.2 %collective-permute-start.7 = (f32[40,128]{1,0:T(8,128)S(1)}, f32[40,128]{1,0:T(8,128)S(1)}, u32[]{:S(2)}, u32[]{:S(2)}) collective-permute-start(f32[40,128]{1,0:T(8,128)S(1)} %add.15), channel_id=1, source_target_pairs={{0,2},{2,0},{4,6},{6,4},{8,10},{10,8},{12,14},{14,12},{16,18},{18,... | collective-permute-start | bytes 61448 | tf_op jit(solution)/shard_map/ppermute | solution.py:567
  32.8 3.8 %collective-permute-start.8 = (f32[40,128]{1,0:T(8,128)S(1)}, f32[40,128]{1,0:T(8,128)S(1)}, u32[]{:S(2)}, u32[]{:S(2)}) collective-permute-start(f32[40,128]{1,0:T(8,128)S(1)} %add.16), channel_id=1, source_target_pairs={{0,8},{2,10},{4,12},{6,14},{8,0},{10,2},{12,4},{14,6},{16,24},{18,... | collective-permute-start | bytes 61448 | tf_op jit(solution)/shard_map/ppermute | solution.py:567
  36.6 4.9 %collective-permute-start.9 = (f32[40,128]{1,0:T(8,128)S(1)}, f32[40,128]{1,0:T(8,128)S(1)}, u32[]{:S(2)}, u32[]{:S(2)}) collective-permute-start(f32[40,128]{1,0:T(8,128)S(1)} %add.17), channel_id=1, source_target_pairs={{0,16},{2,18},{4,20},{6,22},{8,24},{10,26},{12,28},{14,30},{16,0},... | collective-permute-start | bytes 61448 | tf_op jit(solution)/shard_map/ppermute | solution.py:567
  41.5 3.8 %collective-permute-start.10 = (f32[40,128]{1,0:T(8,128)S(1)}, f32[40,128]{1,0:T(8,128)S(1)}, u32[]{:S(2)}, u32[]{:S(2)}) collective-permute-start(f32[40,128]{1,0:T(8,128)S(1)} %add.18.sums_ref), channel_id=1, source_target_pairs={{0,4},{2,6},{4,0},{6,2},{8,12},{10,14},{12,8},{14,10},{16,20},{18,... | collective-permute-start | bytes 61448 | tf_op jit(solution)/shard_map/ppermute | solution.py:567

commit v9 on v8

--- a/solution.py
+++ b/solution.py
@@ -640,7 +640,7 @@
         from_left = lax.ppermute(to_next, "solver", to_right)
         from_right = lax.ppermute(to_last, "solver", to_left)
 
-    early = 3
+    early = 2
     gram_flops = 2 * wide * wide * cells * tiles
     inner, right, left, basis = pl.pallas_call(
         functools.partial(inner_gram_kernel, early),
@@ -685,7 +685,7 @@
             in_specs=[SCALAR] + [WHOLE] * 2,
             out_specs=WHOLE,
             compiler_params=params(16),
-            cost_estimate=cost(gram_flops, 2 * basis_bytes),
+            cost_estimate=cost(gram_flops // 2, basis_bytes),
             name="wall_join",
         )(place, inner, near_group)
         next_given, given = pl.pallas_call(

time: 48.6 us -> 47 us (0.967)
  waiting for transfers between devices: 13.2 us -> 12 us
  Pallas kernels: 19.9 us -> 19.3 us
    pallas_call x1, Pallas kernels: 6.93 us -> 5.53 us  [body(): pl.pallas_call(functools.partial(inner_gram_kernel, early), out_shape=[sh...]
    ppermute x1, waiting for transfers between devices: 1.99 us -> 1.17 us  [body(): got = lax.ppermute(given, 'analysis', swap)]
    pallas_call x1, Pallas kernels: 2.44 us -> 3.25 us  [rest_of_gram(): pl.pallas_call(functools.partial(gram_kernel, early, fields), out_shape=s...]
where the time goes in v9:
time: 47 us; the launch traced here: 46.8 us
  Pallas kernels  19.3 us (41%)
  starting transfers between devices  13.6 us (29%)
  waiting for transfers between devices  12 us (26%)
  local copies, waits for them, and re-layouts  1.08 us (2%)
  between operations  0.77 us (2%)
    ppermute x5, waiting for transfers between devices, swap_added(): lax.ppermute(value, axis, [(i, i ^ bit) for i in range(count)])  10.8 us
    pallas_call x1, Pallas kernels, body(): pl.pallas_call(functools.partial(inner_gram_kernel, early), out_shape=[sh...  5.53 us
    ppermute x1, starting transfers between devices, body(): from_right = lax.ppermute(to_last, 'solver', to_left)  4.43 us
    ppermute x5, starting transfers between devices, swap_added(): lax.ppermute(value, axis, [(i, i ^ bit) for i in range(count)])  4.05 us
    pallas_call x1, Pallas kernels, rest_of_gram(): pl.pallas_call(functools.partial(gram_kernel, early, fields), out_shape=s...  3.25 us
    pallas_call x1, Pallas kernels, body(): pl.pallas_call(functools.partial(finish_kernel, rows_total), out_shape=[s...  3.18 us
    pallas_call x1, Pallas kernels, body(): pl.pallas_call(functools.partial(project_kernel, True), out_shape=[sums_s...  3.12 us
    ppermute x1, starting transfers between devices, body(): near_group = lax.ppermute(near_group, 'analysis', swap)  3 us
  transfers between devices with their start and end apart: 11, of which 6 were waited for; matrix products, arithmetic and copies ran while one was open for 0% of the time, Pallas kernels for 33%

profile of v9, /device:TPU:0, one launch (start us, length us, event | category | flops | bytes accessed | tf_op | source)
XLA Modules:
  0.0 46.8 jit_solution(12069543222678008712)
XLA Ops:
  0.6 1.1 %copy-done = f32[2,5,8,4,512]{4,3,2,1,0:T(4,128)S(1)} copy-done((f32[2,5,8,4,512]{4,3,2,1,0:T(4,128)S(1)}, f32[2,5,8,4,512]{4,3,2,1,0:T(4,128)}, u32[]{:S(2)}) %copy-start) | copy-done | bytes 655384
  1.7 0.7 %near_faces.1 = (bf16[5,48,512]{2,1,0:T(8,128)(2,1)S(1)}, f32[2,5,8,4,512]{4,3,2,1,0:T(4,128)S(1)}) custom-call(s32[1]{0:T(128)} %bitcast.where_ref, f32[2,5,8,4,512]{4,3,2,1,0:T(4,128)S(1)} %copy-done), custom_call_target="tpu_custom_call" | custom-call | flops 10000000 | bytes 1638400 | tf_op jit(solution)/shard_map/near_faces/pallas_call | solution.py:599
  2.4 3.0 %collective-permute-start = (bf16[5,48,512]{2,1,0:T(8,128)(2,1)S(1)}, bf16[5,48,512]{2,1,0:T(8,128)(2,1)S(1)}, u32[]{:S(2)}, u32[]{:S(2)}) collective-permute-start(bf16[5,48,512]{2,1,0:T(8,128)(2,1)S(1)} %get-tuple-element.27._), channel_id=1, source_target_pairs={{0,1},{1,0},{2,3},{3,2},{4,5},{5,4},{6,7},{7,6},{8,9},{9,8},{10,11... | collective-permute-start | bytes 737288 | tf_op jit(solution)/shard_map/ppermute | solution.py:619
  5.5 0.7 %later_faces.1 = (bf16[5,48,512]{2,1,0:T(8,128)(2,1)S(1)}, f32[2,5,4,4,512]{4,3,2,1,0:T(4,128)S(1)}, f32[2,5,4,4,512]{4,3,2,1,0:T(4,128)S(1)}) custom-call(s32[1]{0:T(128)} %bitcast.where_ref, bf16[5,48,512]{2,1,0:T(8,128)(2,1)S(1)} %get-tuple-element.27._, f32[2,5,8,4,512]{4,3,2,1,0:T(4,128)S(1)} %get-tuple-element.25.windows_ref), custom_call_target="tpu_custom_call" | custom-call | flops 10000000 | bytes 1638400 | tf_op jit(solution)/shard_map/later_faces/pallas_call | solution.py:609
  6.2 4.4 %collective-permute-start.2 = (f32[2,5,4,4,512]{4,3,2,1,0:T(4,128)S(1)}, f32[2,5,4,4,512]{4,3,2,1,0:T(4,128)S(1)}, u32[]{:S(2)}, u32[]{:S(2)}) collective-permute-start(f32[2,5,4,4,512]{4,3,2,1,0:T(4,128)S(1)} %get-tuple-element.29), channel_id=1, source_target_pairs={{2,0},{4,2},{6,4},{8,6},{10,8},{12,10},{14,12},{16,14},{18,16},{20... | collective-permute-start | bytes 983048 | tf_op jit(solution)/shard_map/ppermute | solution.py:621
  10.6 5.5 %inner_gram.1 = (f32[2,5,8,4,512]{4,3,2,1,0:T(4,128)S(1)}, f32[512,256]{1,0:T(8,128)S(1)}, f32[256,256]{1,0:T(8,128)S(1)}, bf16[64,20,8,512]{3,2,1,0:T(8,128)(2,1)S(1)}) custom-call(f32[2,5,8,4,512]{4,3,2,1,0:T(4,128)S(1)} %get-tuple-element.25.windows_ref, bf16[64,20,8,512]{3,2,1,0:T(8,128)(2,1)} %bitcast.3), custom_call_target="tpu_custom_call" | custom-call | flops 1000000 | bytes 163840 | tf_op jit(solution)/shard_map/inner_gram/pallas_call | solution.py:645
  16.2 0.2 wall_join.1.part_ref
  16.4 0.1 edge_join.1
  16.4 2.1 %collective-permute-start.4 = (bf16[2,5,16,512]{3,2,1,0:T(8,128)(2,1)S(1)}, bf16[2,5,16,512]{3,2,1,0:T(8,128)(2,1)S(1)}, u32[]{:S(2)}, u32[]{:S(2)}) collective-permute-start(bf16[2,5,16,512]{3,2,1,0:T(8,128)(2,1)S(1)} %get-tuple-element.30._), channel_id=1, source_target_pairs={{0,1},{1,0},{2,3},{3,2},{4,5},{5,4},{6,7},{7,6},{8,9},{9,8},{10,11... | collective-permute-start | bytes 491528 | tf_op jit(solution)/shard_map/ppermute | solution.py:700
  18.5 3.3 %gram.1._.gram_ref = f32[32,128]{1,0:T(8,128)S(1)} custom-call(bf16[2,5,16,512]{3,2,1,0:T(8,128)(2,1)S(1)} %get-tuple-element.30._, f32[512,256]{1,0:T(8,128)S(1)} %get-tuple-element.31.right_ref, f32[256,256]{1,0:T(8,128)S(1)} %get-tuple-element.32.left_ref, bf16[64,20,8,512]{3,2,1,0:T(8,128)(2,1)S(1)} %get-tuple-element.33.basis_ref.rest_4_), custom_call_target="tpu_custom_call" | custom-call | flops 2684354560 | bytes 10485760 | tf_op jit(solution)/shard_map/gram/pallas_call | solution.py:665
  21.8 0.2 own_join.1
  22.0 1.2 %collective-permute-done.4.rest_1_ = bf16[2,5,16,512]{3,2,1,0:T(8,128)(2,1)S(1)} collective-permute-done((bf16[2,5,16,512]{3,2,1,0:T(8,128)(2,1)S(1)}, bf16[2,5,16,512]{3,2,1,0:T(8,128)(2,1)S(1)}, u32[]{:S(2)}, u32[]{:S(2)}) %collective-permute-start.4) | collective-permute-done | bytes 163872 | tf_op jit(solution)/shard_map/ppermute | solution.py:700
  23.2 3.1 %project.1 = (f32[8,128]{1,0:T(8,128)S(1)}, bf16[20,16,512]{2,1,0:T(8,128)(2,1)S(1)}, f32[2,5,8,4,512]{4,3,2,1,0:T(4,128)}) custom-call(s32[1]{0:T(128)} %bitcast.where_ref, bf16[2,5,16,512]{3,2,1,0:T(8,128)(2,1)S(1)} %get-tuple-element.35.rest_0_, bf16[2,5,16,512]{3,2,1,0:T(8,128)(2,1)S(1)} %collective-permute-done.4.rest_1_, ...), custom_call_target="tpu_custom_call" | custom-call | flops 167772160 | bytes 10485760 | tf_op jit(solution)/shard_map/project/pallas_call | solution.py:732
  26.3 1.7 %collective-permute-start.6 = (f32[40,128]{1,0:T(8,128)S(1)}, f32[40,128]{1,0:T(8,128)S(1)}, u32[]{:S(2)}, u32[]{:S(2)}) collective-permute-start(f32[40,128]{1,0:T(8,128)S(1)} %merge.1), channel_id=1, source_target_pairs={{0,1},{1,0},{2,3},{3,2},{4,5},{5,4},{6,7},{7,6},{8,9},{9,8},{10,11... | collective-permute-start | bytes 61448 | tf_op jit(solution)/shard_map/ppermute | solution.py:567
  28.0 2.2 %collective-permute-done.6 = f32[40,128]{1,0:T(8,128)S(1)} collective-permute-done((f32[40,128]{1,0:T(8,128)S(1)}, f32[40,128]{1,0:T(8,128)S(1)}, u32[]{:S(2)}, u32[]{:S(2)}) %collective-permute-start.6) | collective-permute-done | bytes 20512 | tf_op jit(solution)/shard_map/ppermute | solution.py:567
  30.2 1.2 %collective-permute-done.7 = f32[40,128]{1,0:T(8,128)S(1)} collective-permute-done((f32[40,128]{1,0:T(8,128)S(1)}, f32[40,128]{1,0:T(8,128)S(1)}, u32[]{:S(2)}, u32[]{:S(2)}) %collective-permute-start.7) | collective-permute-done | bytes 20512 | tf_op jit(solution)/shard_map/ppermute | solution.py:567
  31.4 0.3 collective-permute-start.8
  31.6 3.5 %collective-permute-done.8 = f32[40,128]{1,0:T(8,128)S(1)} collective-permute-done((f32[40,128]{1,0:T(8,128)S(1)}, f32[40,128]{1,0:T(8,128)S(1)}, u32[]{:S(2)}, u32[]{:S(2)}) %collective-permute-start.8) | collective-permute-done | bytes 20512 | tf_op jit(solution)/shard_map/ppermute | solution.py:567
  35.2 1.3 %collective-permute-start.9 = (f32[40,128]{1,0:T(8,128)S(1)}, f32[40,128]{1,0:T(8,128)S(1)}, u32[]{:S(2)}, u32[]{:S(2)}) collective-permute-start(f32[40,128]{1,0:T(8,128)S(1)} %add.17), channel_id=1, source_target_pairs={{0,16},{2,18},{4,20},{6,22},{8,24},{10,26},{12,28},{14,30},{16,0},... | collective-permute-start | bytes 61448 | tf_op jit(solution)/shard_map/ppermute | solution.py:567
  36.4 3.4 %collective-permute-done.9 = f32[40,128]{1,0:T(8,128)S(1)} collective-permute-done((f32[40,128]{1,0:T(8,128)S(1)}, f32[40,128]{1,0:T(8,128)S(1)}, u32[]{:S(2)}, u32[]{:S(2)}) %collective-permute-start.9) | collective-permute-done | bytes 20512 | tf_op jit(solution)/shard_map/ppermute | solution.py:567
  39.9 0.9 %collective-permute-start.10 = (f32[40,128]{1,0:T(8,128)S(1)}, f32[40,128]{1,0:T(8,128)S(1)}, u32[]{:S(2)}, u32[]{:S(2)}) collective-permute-start(f32[40,128]{1,0:T(8,128)S(1)} %add.18.sums_ref), channel_id=1, source_target_pairs={{0,4},{2,6},{4,0},{6,2},{8,12},{10,14},{12,8},{14,10},{16,20},{18,... | collective-permute-start | bytes 61448 | tf_op jit(solution)/shard_map/ppermute | solution.py:567
  40.7 2.4 %inverse.1 = (f32[64,64]{1,0:T(8,128)S(1)}, f32[64,512]{1,0:T(8,128)S(1)}) custom-call(f32[40,128]{1,0:T(8,128)S(1)} %add.18.sums_ref), custom_call_target="tpu_custom_call" | custom-call | flops 20000000 | bytes 32768 | tf_op jit(solution)/shard_map/inverse/pallas_call | solution.py:771
  43.1 0.5 %collective-permute-done.10 = f32[40,128]{1,0:T(8,128)S(1)} collective-permute-done((f32[40,128]{1,0:T(8,128)S(1)}, f32[40,128]{1,0:T(8,128)S(1)}, u32[]{:S(2)}, u32[]{:S(2)}) %collective-permute-start.10) | collective-permute-done | bytes 20512 | tf_op jit(solution)/shard_map/ppermute | solution.py:567
  43.6 3.2 %finish.1 = (f32[2,20,8,512]{3,2,1,0:T(8,128)}, f32[2,64]{1,0:T(2,128)}, f32[2,2]{1,0:T(2,128)}) custom-call(f32[40,128]{1,0:T(8,128)S(1)} %add.19.projected_ref, f32[40,128]{1,0:T(8,128)S(1)} %add.18.sums_ref, f32[64,64]{1,0:T(8,128)S(1)} %get-tuple-element.40.inverse_ref, f32[64,512]{1,0:T(8,128)S(1)} %get-tuple-element.41.spread_ref, ...), custom_call_target="tpu_custom_call" | custom-call | flops 335544320 | bytes 11796480 | tf_op jit(solution)/shard_map/finish/pallas_call | solution.py:784
  (16 shorter events, 0.1 us)
Async XLA Ops:
  0.6 1.1 %copy-start = (f32[2,5,8,4,512]{4,3,2,1,0:T(4,128)S(1)}, f32[2,5,8,4,512]{4,3,2,1,0:T(4,128)}, u32[]{:S(2)}) copy-start(f32[2,5,8,4,512]{4,3,2,1,0:T(4,128)} %source_ref.1) | copy-start | bytes 1966084
  2.4 13.7 %collective-permute-start = (bf16[5,48,512]{2,1,0:T(8,128)(2,1)S(1)}, bf16[5,48,512]{2,1,0:T(8,128)(2,1)S(1)}, u32[]{:S(2)}, u32[]{:S(2)}) collective-permute-start(bf16[5,48,512]{2,1,0:T(8,128)(2,1)S(1)} %get-tuple-element.27._), channel_id=1, source_target_pairs={{0,1},{1,0},{2,3},{3,2},{4,5},{5,4},{6,7},{7,6},{8,9},{9,8},{10,11... | collective-permute-start | bytes 737288 | tf_op jit(solution)/shard_map/ppermute | solution.py:619
  6.1 10.2 %collective-permute-start.1 = (f32[2,5,4,4,512]{4,3,2,1,0:T(4,128)S(1)}, f32[2,5,4,4,512]{4,3,2,1,0:T(4,128)S(1)}, u32[]{:S(2)}, u32[]{:S(2)}) collective-permute-start(f32[2,5,4,4,512]{4,3,2,1,0:T(4,128)S(1)} %get-tuple-element.28), channel_id=1, source_target_pairs={{0,2},{2,4},{4,6},{6,8},{8,10},{10,12},{12,14},{14,16},{16,18},{18... | collective-permute-start | bytes 983048 | tf_op jit(solution)/shard_map/ppermute | solution.py:620
  6.2 10.2 %collective-permute-start.2 = (f32[2,5,4,4,512]{4,3,2,1,0:T(4,128)S(1)}, f32[2,5,4,4,512]{4,3,2,1,0:T(4,128)S(1)}, u32[]{:S(2)}, u32[]{:S(2)}) collective-permute-start(f32[2,5,4,4,512]{4,3,2,1,0:T(4,128)S(1)} %get-tuple-element.29), channel_id=1, source_target_pairs={{2,0},{4,2},{6,4},{8,6},{10,8},{12,10},{14,12},{16,14},{18,16},{20... | collective-permute-start | bytes 983048 | tf_op jit(solution)/shard_map/ppermute | solution.py:621
  10.6 11.2 %collective-permute-start.3 = (bf16[5,48,512]{2,1,0:T(8,128)(2,1)S(1)}, bf16[5,48,512]{2,1,0:T(8,128)(2,1)S(1)}, u32[]{:S(2)}, u32[]{:S(2)}) collective-permute-start(bf16[5,48,512]{2,1,0:T(8,128)(2,1)S(1)} %get-tuple-element.34), channel_id=1, source_target_pairs={{0,1},{1,0},{2,3},{3,2},{4,5},{5,4},{6,7},{7,6},{8,9},{9,8},{10,11... | collective-permute-start | bytes 737288 | tf_op jit(solution)/shard_map/ppermute | solution.py:622
  16.4 6.7 %collective-permute-start.4 = (bf16[2,5,16,512]{3,2,1,0:T(8,128)(2,1)S(1)}, bf16[2,5,16,512]{3,2,1,0:T(8,128)(2,1)S(1)}, u32[]{:S(2)}, u32[]{:S(2)}) collective-permute-start(bf16[2,5,16,512]{3,2,1,0:T(8,128)(2,1)S(1)} %get-tuple-element.30._), channel_id=1, source_target_pairs={{0,1},{1,0},{2,3},{3,2},{4,5},{5,4},{6,7},{7,6},{8,9},{9,8},{10,11... | collective-permute-start | bytes 491528 | tf_op jit(solution)/shard_map/ppermute | solution.py:700
  21.8 4.5 %collective-permute-start.5 = (f32[32,128]{1,0:T(8,128)S(1)}, f32[32,128]{1,0:T(8,128)S(1)}, u32[]{:S(2)}, u32[]{:S(2)}) collective-permute-start(f32[32,128]{1,0:T(8,128)S(1)} %gram.1._.gram_ref), channel_id=1, source_target_pairs={{0,4},{2,6},{4,0},{6,2},{8,12},{10,14},{12,8},{14,10},{16,20},{18,... | collective-permute-start | bytes 49160 | tf_op jit(solution)/shard_map/ppermute | solution.py:715
  26.3 3.8 %collective-permute-start.6 = (f32[40,128]{1,0:T(8,128)S(1)}, f32[40,128]{1,0:T(8,128)S(1)}, u32[]{:S(2)}, u32[]{:S(2)}) collective-permute-start(f32[40,128]{1,0:T(8,128)S(1)} %merge.1), channel_id=1, source_target_pairs={{0,1},{1,0},{2,3},{3,2},{4,5},{5,4},{6,7},{7,6},{8,9},{9,8},{10,11... | collective-permute-start | bytes 61448 | tf_op jit(solution)/shard_map/ppermute | solution.py:567
  30.2 1.2 %collective-permute-start.7 = (f32[40,128]{1,0:T(8,128)S(1)}, f32[40,128]{1,0:T(8,128)S(1)}, u32[]{:S(2)}, u32[]{:S(2)}) collective-permute-start(f32[40,128]{1,0:T(8,128)S(1)} %add.15), channel_id=1, source_target_pairs={{0,2},{2,0},{4,6},{6,4},{8,10},{10,8},{12,14},{14,12},{16,18},{18,... | collective-permute-start | bytes 61448 | tf_op jit(solution)/shard_map/ppermute | solution.py:567
  31.4 3.8 %collective-permute-start.8 = (f32[40,128]{1,0:T(8,128)S(1)}, f32[40,128]{1,0:T(8,128)S(1)}, u32[]{:S(2)}, u32[]{:S(2)}) collective-permute-start(f32[40,128]{1,0:T(8,128)S(1)} %add.16), channel_id=1, source_target_pairs={{0,8},{2,10},{4,12},{6,14},{8,0},{10,2},{12,4},{14,6},{16,24},{18,... | collective-permute-start | bytes 61448 | tf_op jit(solution)/shard_map/ppermute | solution.py:567
  35.2 4.7 %collective-permute-start.9 = (f32[40,128]{1,0:T(8,128)S(1)}, f32[40,128]{1,0:T(8,128)S(1)}, u32[]{:S(2)}, u32[]{:S(2)}) collective-permute-start(f32[40,128]{1,0:T(8,128)S(1)} %add.17), channel_id=1, source_target_pairs={{0,16},{2,18},{4,20},{6,22},{8,24},{10,26},{12,28},{14,30},{16,0},... | collective-permute-start | bytes 61448 | tf_op jit(solution)/shard_map/ppermute | solution.py:567
  39.9 3.8 %collective-permute-start.10 = (f32[40,128]{1,0:T(8,128)S(1)}, f32[40,128]{1,0:T(8,128)S(1)}, u32[]{:S(2)}, u32[]{:S(2)}) collective-permute-start(f32[40,128]{1,0:T(8,128)S(1)} %add.18.sums_ref), channel_id=1, source_target_pairs={{0,4},{2,6},{4,0},{6,2},{8,12},{10,14},{12,8},{14,10},{16,20},{18,... | collective-permute-start | bytes 61448 | tf_op jit(solution)/shard_map/ppermute | solution.py:567

commit v10 on v9

--- a/solution.py
+++ b/solution.py
@@ -146,7 +146,7 @@
     copy.wait()
 
 
-def later_kernel(where_ref, _, windows_ref, group_ref, left_ref, right_ref, scratch, lows):
+def later_kernel(where_ref, _, windows_ref, group_ref, first_ref, second_ref, scratch, lows):
     windows, _, planes, layers, cells = windows_ref.shape
     half = planes // 2
 
@@ -162,14 +162,18 @@
             keep_x(w, plane, primitives([windows_ref[w, f, plane] for f in range(5)]))
         for f in range(5):
             for i in range(REACH):
-                for ref, offset in ((left_ref, -planes), (right_ref, REACH)):
+                sides = []
+                for offset in (-planes, REACH):
                     total = None
                     for j in range(planes):
                         c = weight(j + offset - i)
                         if c:
                             term = c * scratch[w, f, j]
                             total = term if total is None else total + term
-                    ref[w, f, i] = total
+                    sides.append(total)
+                to_next, to_last = sides
+                first_ref[w, f, i] = jnp.where(where_ref[0] == 0, to_last, to_next)
+                second_ref[w, f, i] = jnp.where(where_ref[0] == 0, to_next, to_last)
 
 
 def inner_part(windows_ref, part_ref, scratch):
@@ -310,30 +314,26 @@
                 given_ref[w, f, x] = part_ref[w, f, base + x] + term
 
 
-def edge_join_kernel(where_ref, part_ref, left_ref, right_ref, made, snaps_ref):
+def edge_join_kernel(part_ref, edge_ref, made, snaps_ref):
     windows, _, half = part_ref.shape[:3]
-    ahead = where_ref[0] == 1
     for w in range(windows):
         for f in range(5):
             done = []
             for x in range(half):
-                total = part_ref[w, f, x] + jnp.where(ahead, left_ref[w, f, x], right_ref[w, f, x])
+                total = part_ref[w, f, x] + edge_ref[w, f, x]
                 made[w, f, x] = total
                 done.append(total)
             snaps_ref[w, f] = jnp.concatenate(done, axis=0).astype(jnp.bfloat16)
 
 
-def own_join_kernel(where_ref, _, part_ref, left_ref, right_ref, group_ref, made, snaps_ref):
+def own_join_kernel(where_ref, _, part_ref, edge_ref, group_ref, made, snaps_ref):
     windows, _, planes = part_ref.shape[:3]
-    half = planes // 2
-    ahead = where_ref[0] == 0
-    base = half * where_ref[0]
+    base = planes // 2 * where_ref[0]
     for w in range(windows):
         for f in range(5):
             done = []
-            for x, term in enumerate(wall_terms_of(ahead, group_ref, w, f)):
-                total = part_ref[w, f, base + x] + term
-                total = total + jnp.where(ahead, left_ref[w, f, x], right_ref[w, f, x])
+            for x, term in enumerate(wall_terms_of(where_ref[0] == 0, group_ref, w, f)):
+                total = part_ref[w, f, base + x] + term + edge_ref[w, f, x]
                 made[w, f, x] = total
                 done.append(total)
             snaps_ref[w, f] = jnp.concatenate(done, axis=0).astype(jnp.bfloat16)
@@ -606,7 +606,7 @@
             cost_estimate=face_cost,
             name="near_faces",
         )(place, windows)
-        later_group, to_next, to_last = pl.pallas_call(
+        later_group, first_edge, second_edge = pl.pallas_call(
             later_kernel,
             out_shape=[group_shape] + [edge_shape] * 2,
             in_specs=[SCALAR, LOOSE, WHOLE],
@@ -617,8 +617,11 @@
             name="later_faces",
         )(place, near_group, kept)
         near_group = lax.ppermute(near_group, "analysis", swap)
-        from_left = lax.ppermute(to_next, "solver", to_right)
-        from_right = lax.ppermute(to_last, "solver", to_left)
+        down = [(2 * ((i + 1) % ring), 2 * i) for i in range(ring)]
+        up = [(2 * i, 2 * ((i + 1) % ring)) for i in range(ring)]
+        odd = lambda pairs: [(a + 1, b + 1) for a, b in pairs]
+        first_edge = lax.ppermute(first_edge, ("solver", "analysis"), down + odd(up))
+        second_edge = lax.ppermute(second_edge, ("solver", "analysis"), up + odd(down))
         later_group = lax.ppermute(later_group, "analysis", swap)
     else:
         kept, to_next, to_last, up, down = pl.pallas_call(
@@ -691,12 +694,12 @@
         next_given, given = pl.pallas_call(
             edge_join_kernel,
             out_shape=[half_next, shape(half_shape, bf16)],
-            in_specs=[SCALAR] + [WHOLE] * 3,
+            in_specs=[WHOLE] * 2,
             out_specs=[WHOLE] * 2,
             compiler_params=params(16),
             cost_estimate=join_cost,
             name="edge_join",
-        )(place, inner_given, from_left, from_right)
+        )(inner_given, first_edge)
         got = lax.ppermute(given, "analysis", swap)
         gram = rest_of_gram(given)
     else:
@@ -717,12 +720,12 @@
         next_own, own = pl.pallas_call(
             own_join_kernel,
             out_shape=[half_next, shape(half_shape, bf16)],
-            in_specs=[SCALAR, LOOSE] + [WHOLE] * 4,
+            in_specs=[SCALAR, LOOSE] + [WHOLE] * 3,
             out_specs=[WHOLE] * 2,
             compiler_params=params(16),
             cost_estimate=join_cost,
             name="own_join",
-        )(place, gram, inner, from_left, from_right, later_group)
+        )(place, gram, inner, second_edge, later_group)
 
     sums_shape = shape((8, LANES), f32)
     snaps_shape = shape((tiles, 2 * 8, cells), bf16)

time: 47 us -> 46.5 us (0.989)
  waiting for transfers between devices: 12 us -> 9.9 us
  starting transfers between devices: 13.6 us -> 15.2 us
    ppermute x5, starting transfers between devices: 4.05 us -> 5.67 us  [swap_added(): lax.ppermute(value, axis, [(i, i ^ bit) for i in range(count)])]
    ppermute x5, waiting for transfers between devices: 10.8 us -> 9.19 us  [swap_added(): lax.ppermute(value, axis, [(i, i ^ bit) for i in range(count)])]
    ppermute x2, starting transfers between devices: 4.49 us -> 3.77 us  [the longest x1 3.77 us: body(): lax.ppermute(first_edge, ('solver', 'analysis'), down + odd(up))]
    ppermute x1, starting transfers between devices: 2.07 us -> 2.77 us  [body(): got = lax.ppermute(given, 'analysis', swap)]
    ppermute x1, waiting for transfers between devices: 1.17 us -> 0.69 us  [body(): got = lax.ppermute(given, 'analysis', swap)]
  transfers between devices with their start and end apart: 11 -> 11, of which waited for: 6 -> 5; matrix products, arithmetic and copies ran while one was open for 0% -> 0% of each run, Pallas kernels for 33% -> 33%
where the time goes in v10:
time: 46.5 us; the launch traced here: 46.3 us
  Pallas kernels  19.3 us (42%)
  starting transfers between devices  15.2 us (33%)
  waiting for transfers between devices  9.9 us (21%)
  local copies, waits for them, and re-layouts  1.08 us (2%)
  between operations  0.77 us (2%)
    ppermute x5, waiting for transfers between devices, swap_added(): lax.ppermute(value, axis, [(i, i ^ bit) for i in range(count)])  9.19 us
    ppermute x5, starting transfers between devices, swap_added(): lax.ppermute(value, axis, [(i, i ^ bit) for i in range(count)])  5.67 us
    pallas_call x1, Pallas kernels, body(): pl.pallas_call(functools.partial(inner_gram_kernel, early), out_shape=[sh...  5.53 us
    ppermute x1, starting transfers between devices, body(): lax.ppermute(first_edge, ('solver', 'analysis'), down + odd(up))  3.77 us
    pallas_call x1, Pallas kernels, rest_of_gram(): pl.pallas_call(functools.partial(gram_kernel, early, fields), out_shape=s...  3.25 us
    pallas_call x1, Pallas kernels, body(): pl.pallas_call(functools.partial(finish_kernel, rows_total), out_shape=[s...  3.18 us
    pallas_call x1, Pallas kernels, body(): pl.pallas_call(functools.partial(project_kernel, True), out_shape=[sums_s...  3.12 us
    ppermute x1, starting transfers between devices, body(): near_group = lax.ppermute(near_group, 'analysis', swap)  3 us
  transfers between devices with their start and end apart: 11, of which 5 were waited for; matrix products, arithmetic and copies ran while one was open for 0% of the time, Pallas kernels for 33%

profile of v10, /device:TPU:0, one launch (start us, length us, event | category | flops | bytes accessed | tf_op | source)
XLA Modules:
  0.0 46.3 jit_solution(2631497455882726398)
XLA Ops:
  0.6 1.1 %copy-done = f32[2,5,8,4,512]{4,3,2,1,0:T(4,128)S(1)} copy-done((f32[2,5,8,4,512]{4,3,2,1,0:T(4,128)S(1)}, f32[2,5,8,4,512]{4,3,2,1,0:T(4,128)}, u32[]{:S(2)}) %copy-start) | copy-done | bytes 655384
  1.7 0.7 %near_faces.1 = (bf16[5,48,512]{2,1,0:T(8,128)(2,1)S(1)}, f32[2,5,8,4,512]{4,3,2,1,0:T(4,128)S(1)}) custom-call(s32[1]{0:T(128)} %bitcast.where_ref, f32[2,5,8,4,512]{4,3,2,1,0:T(4,128)S(1)} %copy-done), custom_call_target="tpu_custom_call" | custom-call | flops 10000000 | bytes 1638400 | tf_op jit(solution)/shard_map/near_faces/pallas_call | solution.py:599
  2.4 3.0 %collective-permute-start = (bf16[5,48,512]{2,1,0:T(8,128)(2,1)S(1)}, bf16[5,48,512]{2,1,0:T(8,128)(2,1)S(1)}, u32[]{:S(2)}, u32[]{:S(2)}) collective-permute-start(bf16[5,48,512]{2,1,0:T(8,128)(2,1)S(1)} %get-tuple-element.27._), channel_id=1, source_target_pairs={{0,1},{1,0},{2,3},{3,2},{4,5},{5,4},{6,7},{7,6},{8,9},{9,8},{10,11... | collective-permute-start | bytes 737288 | tf_op jit(solution)/shard_map/ppermute | solution.py:619
  5.5 0.7 %later_faces.1 = (bf16[5,48,512]{2,1,0:T(8,128)(2,1)S(1)}, f32[2,5,4,4,512]{4,3,2,1,0:T(4,128)S(1)}, f32[2,5,4,4,512]{4,3,2,1,0:T(4,128)S(1)}) custom-call(s32[1]{0:T(128)} %bitcast.where_ref, bf16[5,48,512]{2,1,0:T(8,128)(2,1)S(1)} %get-tuple-element.27._, f32[2,5,8,4,512]{4,3,2,1,0:T(4,128)S(1)} %get-tuple-element.25.windows_ref), custom_call_target="tpu_custom_call" | custom-call | flops 10000000 | bytes 1638400 | tf_op jit(solution)/shard_map/later_faces/pallas_call | solution.py:609
  6.1 3.8 %collective-permute-start.1 = (f32[2,5,4,4,512]{4,3,2,1,0:T(4,128)S(1)}, f32[2,5,4,4,512]{4,3,2,1,0:T(4,128)S(1)}, u32[]{:S(2)}, u32[]{:S(2)}) collective-permute-start(f32[2,5,4,4,512]{4,3,2,1,0:T(4,128)S(1)} %get-tuple-element.28), channel_id=1, source_target_pairs={{2,0},{4,2},{6,4},{8,6},{10,8},{12,10},{14,12},{16,14},{18,16},{20... | collective-permute-start | bytes 983048 | tf_op jit(solution)/shard_map/ppermute | solution.py:623
  9.9 5.5 %inner_gram.1 = (f32[2,5,8,4,512]{4,3,2,1,0:T(4,128)S(1)}, f32[512,256]{1,0:T(8,128)S(1)}, f32[256,256]{1,0:T(8,128)S(1)}, bf16[64,20,8,512]{3,2,1,0:T(8,128)(2,1)S(1)}) custom-call(f32[2,5,8,4,512]{4,3,2,1,0:T(4,128)S(1)} %get-tuple-element.25.windows_ref, bf16[64,20,8,512]{3,2,1,0:T(8,128)(2,1)} %bitcast.3), custom_call_target="tpu_custom_call" | custom-call | flops 1000000 | bytes 163840 | tf_op jit(solution)/shard_map/inner_gram/pallas_call | solution.py:648
  15.5 0.2 wall_join.1.part_ref
  15.7 2.8 %collective-permute-start.4 = (bf16[2,5,16,512]{3,2,1,0:T(8,128)(2,1)S(1)}, bf16[2,5,16,512]{3,2,1,0:T(8,128)(2,1)S(1)}, u32[]{:S(2)}, u32[]{:S(2)}) collective-permute-start(bf16[2,5,16,512]{3,2,1,0:T(8,128)(2,1)S(1)} %get-tuple-element.29._), channel_id=1, source_target_pairs={{0,1},{1,0},{2,3},{3,2},{4,5},{5,4},{6,7},{7,6},{8,9},{9,8},{10,11... | collective-permute-start | bytes 491528 | tf_op jit(solution)/shard_map/ppermute | solution.py:703
  18.5 3.2 %gram.1._.gram_ref = f32[32,128]{1,0:T(8,128)S(1)} custom-call(bf16[2,5,16,512]{3,2,1,0:T(8,128)(2,1)S(1)} %get-tuple-element.29._, f32[512,256]{1,0:T(8,128)S(1)} %get-tuple-element.30.right_ref, f32[256,256]{1,0:T(8,128)S(1)} %get-tuple-element.31.left_ref, bf16[64,20,8,512]{3,2,1,0:T(8,128)(2,1)S(1)} %get-tuple-element.32.basis_ref.rest_4_), custom_call_target="tpu_custom_call" | custom-call | flops 2684354560 | bytes 10485760 | tf_op jit(solution)/shard_map/gram/pallas_call | solution.py:668
  21.7 0.0 collective-permute-start.5
  21.8 0.2 own_join.1
  22.0 0.7 %collective-permute-done.4.rest_1_ = bf16[2,5,16,512]{3,2,1,0:T(8,128)(2,1)S(1)} collective-permute-done((bf16[2,5,16,512]{3,2,1,0:T(8,128)(2,1)S(1)}, bf16[2,5,16,512]{3,2,1,0:T(8,128)(2,1)S(1)}, u32[]{:S(2)}, u32[]{:S(2)}) %collective-permute-start.4) | collective-permute-done | bytes 163872 | tf_op jit(solution)/shard_map/ppermute | solution.py:703
  22.6 3.1 %project.1 = (f32[8,128]{1,0:T(8,128)S(1)}, bf16[20,16,512]{2,1,0:T(8,128)(2,1)S(1)}, f32[2,5,8,4,512]{4,3,2,1,0:T(4,128)}) custom-call(s32[1]{0:T(128)} %bitcast.where_ref, bf16[2,5,16,512]{3,2,1,0:T(8,128)(2,1)S(1)} %get-tuple-element.35.rest_0_, bf16[2,5,16,512]{3,2,1,0:T(8,128)(2,1)S(1)} %collective-permute-done.4.rest_1_, ...), custom_call_target="tpu_custom_call" | custom-call | flops 167772160 | bytes 10485760 | tf_op jit(solution)/shard_map/project/pallas_call | solution.py:735
  25.8 1.8 %collective-permute-start.6 = (f32[40,128]{1,0:T(8,128)S(1)}, f32[40,128]{1,0:T(8,128)S(1)}, u32[]{:S(2)}, u32[]{:S(2)}) collective-permute-start(f32[40,128]{1,0:T(8,128)S(1)} %merge.1), channel_id=1, source_target_pairs={{0,1},{1,0},{2,3},{3,2},{4,5},{5,4},{6,7},{7,6},{8,9},{9,8},{10,11... | collective-permute-start | bytes 61448 | tf_op jit(solution)/shard_map/ppermute | solution.py:567
  27.6 2.0 %collective-permute-done.6 = f32[40,128]{1,0:T(8,128)S(1)} collective-permute-done((f32[40,128]{1,0:T(8,128)S(1)}, f32[40,128]{1,0:T(8,128)S(1)}, u32[]{:S(2)}, u32[]{:S(2)}) %collective-permute-start.6) | collective-permute-done | bytes 20512 | tf_op jit(solution)/shard_map/ppermute | solution.py:567
  29.7 1.2 %collective-permute-done.7 = f32[40,128]{1,0:T(8,128)S(1)} collective-permute-done((f32[40,128]{1,0:T(8,128)S(1)}, f32[40,128]{1,0:T(8,128)S(1)}, u32[]{:S(2)}, u32[]{:S(2)}) %collective-permute-start.7) | collective-permute-done | bytes 20512 | tf_op jit(solution)/shard_map/ppermute | solution.py:567
  30.8 0.8 %collective-permute-start.8 = (f32[40,128]{1,0:T(8,128)S(1)}, f32[40,128]{1,0:T(8,128)S(1)}, u32[]{:S(2)}, u32[]{:S(2)}) collective-permute-start(f32[40,128]{1,0:T(8,128)S(1)} %add.16), channel_id=1, source_target_pairs={{0,8},{2,10},{4,12},{6,14},{8,0},{10,2},{12,4},{14,6},{16,24},{18,... | collective-permute-start | bytes 61448 | tf_op jit(solution)/shard_map/ppermute | solution.py:567
  31.6 3.0 %collective-permute-done.8 = f32[40,128]{1,0:T(8,128)S(1)} collective-permute-done((f32[40,128]{1,0:T(8,128)S(1)}, f32[40,128]{1,0:T(8,128)S(1)}, u32[]{:S(2)}, u32[]{:S(2)}) %collective-permute-start.8) | collective-permute-done | bytes 20512 | tf_op jit(solution)/shard_map/ppermute | solution.py:567
  34.6 1.8 %collective-permute-start.9 = (f32[40,128]{1,0:T(8,128)S(1)}, f32[40,128]{1,0:T(8,128)S(1)}, u32[]{:S(2)}, u32[]{:S(2)}) collective-permute-start(f32[40,128]{1,0:T(8,128)S(1)} %add.17), channel_id=1, source_target_pairs={{0,16},{2,18},{4,20},{6,22},{8,24},{10,26},{12,28},{14,30},{16,0},... | collective-permute-start | bytes 61448 | tf_op jit(solution)/shard_map/ppermute | solution.py:567
  36.4 2.9 %collective-permute-done.9 = f32[40,128]{1,0:T(8,128)S(1)} collective-permute-done((f32[40,128]{1,0:T(8,128)S(1)}, f32[40,128]{1,0:T(8,128)S(1)}, u32[]{:S(2)}, u32[]{:S(2)}) %collective-permute-start.9) | collective-permute-done | bytes 20512 | tf_op jit(solution)/shard_map/ppermute | solution.py:567
  39.3 1.3 %collective-permute-start.10 = (f32[40,128]{1,0:T(8,128)S(1)}, f32[40,128]{1,0:T(8,128)S(1)}, u32[]{:S(2)}, u32[]{:S(2)}) collective-permute-start(f32[40,128]{1,0:T(8,128)S(1)} %add.18.sums_ref), channel_id=1, source_target_pairs={{0,4},{2,6},{4,0},{6,2},{8,12},{10,14},{12,8},{14,10},{16,20},{18,... | collective-permute-start | bytes 61448 | tf_op jit(solution)/shard_map/ppermute | solution.py:567
  40.6 2.4 %inverse.1 = (f32[64,64]{1,0:T(8,128)S(1)}, f32[64,512]{1,0:T(8,128)S(1)}) custom-call(f32[40,128]{1,0:T(8,128)S(1)} %add.18.sums_ref), custom_call_target="tpu_custom_call" | custom-call | flops 20000000 | bytes 32768 | tf_op jit(solution)/shard_map/inverse/pallas_call | solution.py:774
  43.1 0.0 collective-permute-done.10
  43.1 3.2 %finish.1 = (f32[2,20,8,512]{3,2,1,0:T(8,128)}, f32[2,64]{1,0:T(2,128)}, f32[2,2]{1,0:T(2,128)}) custom-call(f32[40,128]{1,0:T(8,128)S(1)} %add.19.projected_ref, f32[40,128]{1,0:T(8,128)S(1)} %add.18.sums_ref, f32[64,64]{1,0:T(8,128)S(1)} %get-tuple-element.40.inverse_ref, f32[64,512]{1,0:T(8,128)S(1)} %get-tuple-element.41.spread_ref, ...), custom_call_target="tpu_custom_call" | custom-call | flops 335544320 | bytes 11796480 | tf_op jit(solution)/shard_map/finish/pallas_call | solution.py:787
  (16 shorter events, 0.1 us)
Async XLA Ops:
  0.6 1.1 %copy-start = (f32[2,5,8,4,512]{4,3,2,1,0:T(4,128)S(1)}, f32[2,5,8,4,512]{4,3,2,1,0:T(4,128)}, u32[]{:S(2)}) copy-start(f32[2,5,8,4,512]{4,3,2,1,0:T(4,128)} %source_ref.1) | copy-start | bytes 1966084
  2.4 13.0 %collective-permute-start = (bf16[5,48,512]{2,1,0:T(8,128)(2,1)S(1)}, bf16[5,48,512]{2,1,0:T(8,128)(2,1)S(1)}, u32[]{:S(2)}, u32[]{:S(2)}) collective-permute-start(bf16[5,48,512]{2,1,0:T(8,128)(2,1)S(1)} %get-tuple-element.27._), channel_id=1, source_target_pairs={{0,1},{1,0},{2,3},{3,2},{4,5},{5,4},{6,7},{7,6},{8,9},{9,8},{10,11... | collective-permute-start | bytes 737288 | tf_op jit(solution)/shard_map/ppermute | solution.py:619
  6.1 9.5 %collective-permute-start.1 = (f32[2,5,4,4,512]{4,3,2,1,0:T(4,128)S(1)}, f32[2,5,4,4,512]{4,3,2,1,0:T(4,128)S(1)}, u32[]{:S(2)}, u32[]{:S(2)}) collective-permute-start(f32[2,5,4,4,512]{4,3,2,1,0:T(4,128)S(1)} %get-tuple-element.28), channel_id=1, source_target_pairs={{2,0},{4,2},{6,4},{8,6},{10,8},{12,10},{14,12},{16,14},{18,16},{20... | collective-permute-start | bytes 983048 | tf_op jit(solution)/shard_map/ppermute | solution.py:623
  9.9 11.8 %collective-permute-start.3 = (bf16[5,48,512]{2,1,0:T(8,128)(2,1)S(1)}, bf16[5,48,512]{2,1,0:T(8,128)(2,1)S(1)}, u32[]{:S(2)}, u32[]{:S(2)}) collective-permute-start(bf16[5,48,512]{2,1,0:T(8,128)(2,1)S(1)} %get-tuple-element.34), channel_id=1, source_target_pairs={{0,1},{1,0},{2,3},{3,2},{4,5},{5,4},{6,7},{7,6},{8,9},{9,8},{10,11... | collective-permute-start | bytes 737288 | tf_op jit(solution)/shard_map/ppermute | solution.py:625
  9.9 11.8 %collective-permute-start.2 = (f32[2,5,4,4,512]{4,3,2,1,0:T(4,128)S(1)}, f32[2,5,4,4,512]{4,3,2,1,0:T(4,128)S(1)}, u32[]{:S(2)}, u32[]{:S(2)}) collective-permute-start(f32[2,5,4,4,512]{4,3,2,1,0:T(4,128)S(1)} %get-tuple-element.33), channel_id=1, source_target_pairs={{0,2},{2,4},{4,6},{6,8},{8,10},{10,12},{12,14},{14,16},{16,18},{18... | collective-permute-start | bytes 983048 | tf_op jit(solution)/shard_map/ppermute | solution.py:624
  15.7 7.0 %collective-permute-start.4 = (bf16[2,5,16,512]{3,2,1,0:T(8,128)(2,1)S(1)}, bf16[2,5,16,512]{3,2,1,0:T(8,128)(2,1)S(1)}, u32[]{:S(2)}, u32[]{:S(2)}) collective-permute-start(bf16[2,5,16,512]{3,2,1,0:T(8,128)(2,1)S(1)} %get-tuple-element.29._), channel_id=1, source_target_pairs={{0,1},{1,0},{2,3},{3,2},{4,5},{5,4},{6,7},{7,6},{8,9},{9,8},{10,11... | collective-permute-start | bytes 491528 | tf_op jit(solution)/shard_map/ppermute | solution.py:703
  21.7 4.1 %collective-permute-start.5 = (f32[32,128]{1,0:T(8,128)S(1)}, f32[32,128]{1,0:T(8,128)S(1)}, u32[]{:S(2)}, u32[]{:S(2)}) collective-permute-start(f32[32,128]{1,0:T(8,128)S(1)} %gram.1._.gram_ref), channel_id=1, source_target_pairs={{0,4},{2,6},{4,0},{6,2},{8,12},{10,14},{12,8},{14,10},{16,20},{18,... | collective-permute-start | bytes 49160 | tf_op jit(solution)/shard_map/ppermute | solution.py:718
  25.8 3.8 %collective-permute-start.6 = (f32[40,128]{1,0:T(8,128)S(1)}, f32[40,128]{1,0:T(8,128)S(1)}, u32[]{:S(2)}, u32[]{:S(2)}) collective-permute-start(f32[40,128]{1,0:T(8,128)S(1)} %merge.1), channel_id=1, source_target_pairs={{0,1},{1,0},{2,3},{3,2},{4,5},{5,4},{6,7},{7,6},{8,9},{9,8},{10,11... | collective-permute-start | bytes 61448 | tf_op jit(solution)/shard_map/ppermute | solution.py:567
  29.7 1.2 %collective-permute-start.7 = (f32[40,128]{1,0:T(8,128)S(1)}, f32[40,128]{1,0:T(8,128)S(1)}, u32[]{:S(2)}, u32[]{:S(2)}) collective-permute-start(f32[40,128]{1,0:T(8,128)S(1)} %add.15), channel_id=1, source_target_pairs={{0,2},{2,0},{4,6},{6,4},{8,10},{10,8},{12,14},{14,12},{16,18},{18,... | collective-permute-start | bytes 61448 | tf_op jit(solution)/shard_map/ppermute | solution.py:567
  30.8 3.8 %collective-permute-start.8 = (f32[40,128]{1,0:T(8,128)S(1)}, f32[40,128]{1,0:T(8,128)S(1)}, u32[]{:S(2)}, u32[]{:S(2)}) collective-permute-start(f32[40,128]{1,0:T(8,128)S(1)} %add.16), channel_id=1, source_target_pairs={{0,8},{2,10},{4,12},{6,14},{8,0},{10,2},{12,4},{14,6},{16,24},{18,... | collective-permute-start | bytes 61448 | tf_op jit(solution)/shard_map/ppermute | solution.py:567
  34.6 4.7 %collective-permute-start.9 = (f32[40,128]{1,0:T(8,128)S(1)}, f32[40,128]{1,0:T(8,128)S(1)}, u32[]{:S(2)}, u32[]{:S(2)}) collective-permute-start(f32[40,128]{1,0:T(8,128)S(1)} %add.17), channel_id=1, source_target_pairs={{0,16},{2,18},{4,20},{6,22},{8,24},{10,26},{12,28},{14,30},{16,0},... | collective-permute-start | bytes 61448 | tf_op jit(solution)/shard_map/ppermute | solution.py:567
  39.3 3.8 %collective-permute-start.10 = (f32[40,128]{1,0:T(8,128)S(1)}, f32[40,128]{1,0:T(8,128)S(1)}, u32[]{:S(2)}, u32[]{:S(2)}) collective-permute-start(f32[40,128]{1,0:T(8,128)S(1)} %add.18.sums_ref), channel_id=1, source_target_pairs={{0,4},{2,6},{4,0},{6,2},{8,12},{10,14},{12,8},{14,10},{16,20},{18,... | collective-permute-start | bytes 61448 | tf_op jit(solution)/shard_map/ppermute | solution.py:567

commit v11 on v10

--- a/solution.py
+++ b/solution.py
@@ -643,7 +643,7 @@
         from_left = lax.ppermute(to_next, "solver", to_right)
         from_right = lax.ppermute(to_last, "solver", to_left)
 
-    early = 2
+    early = 3
     gram_flops = 2 * wide * wide * cells * tiles
     inner, right, left, basis = pl.pallas_call(
         functools.partial(inner_gram_kernel, early),

time: 46.5 us -> 47.8 us (1.028)
  waiting for transfers between devices: 9.9 us -> 13.3 us
  starting transfers between devices: 15.2 us -> 12.6 us
  Pallas kernels: 19.3 us -> 19.9 us
    ppermute x5, starting transfers between devices: 5.67 us -> 3.02 us  [swap_added(): lax.ppermute(value, axis, [(i, i ^ bit) for i in range(count)])]
    ppermute x5, waiting for transfers between devices: 9.19 us -> 11.8 us  [swap_added(): lax.ppermute(value, axis, [(i, i ^ bit) for i in range(count)])]
    pallas_call x1, Pallas kernels: 5.53 us -> 6.93 us  [body(): pl.pallas_call(functools.partial(inner_gram_kernel, early), out_shape=[sh...]
    ppermute x1, waiting for transfers between devices: 0.69 us -> 1.51 us  [body(): got = lax.ppermute(given, 'analysis', swap)]
    pallas_call x1, Pallas kernels: 3.25 us -> 2.44 us  [rest_of_gram(): pl.pallas_call(functools.partial(gram_kernel, early, fields), out_shape=s...]
  transfers between devices with their start and end apart: 11 -> 11, of which waited for: 5 -> 6; matrix products, arithmetic and copies ran while one was open for 0% -> 0% of each run, Pallas kernels for 33% -> 34%
where the time goes in v11:
time: 47.8 us; the launch traced here: 47.7 us
  Pallas kernels  19.9 us (42%)
  waiting for transfers between devices  13.3 us (28%)
  starting transfers between devices  12.6 us (26%)
  local copies, waits for them, and re-layouts  1.08 us (2%)
  between operations  0.77 us (2%)
    ppermute x5, waiting for transfers between devices, swap_added(): lax.ppermute(value, axis, [(i, i ^ bit) for i in range(count)])  11.8 us
    pallas_call x1, Pallas kernels, body(): pl.pallas_call(functools.partial(inner_gram_kernel, early), out_shape=[sh...  6.93 us
    ppermute x1, starting transfers between devices, body(): lax.ppermute(first_edge, ('solver', 'analysis'), down + odd(up))  3.77 us
    pallas_call x1, Pallas kernels, body(): pl.pallas_call(functools.partial(finish_kernel, rows_total), out_shape=[s...  3.18 us
    pallas_call x1, Pallas kernels, body(): pl.pallas_call(functools.partial(project_kernel, True), out_shape=[sums_s...  3.12 us
    ppermute x5, starting transfers between devices, swap_added(): lax.ppermute(value, axis, [(i, i ^ bit) for i in range(count)])  3.02 us
    ppermute x1, starting transfers between devices, body(): near_group = lax.ppermute(near_group, 'analysis', swap)  3 us
    ppermute x1, starting transfers between devices, body(): got = lax.ppermute(given, 'analysis', swap)  2.77 us
  transfers between devices with their start and end apart: 11, of which 6 were waited for; matrix products, arithmetic and copies ran while one was open for 0% of the time, Pallas kernels for 34%

profile of v11, /device:TPU:0, one launch (start us, length us, event | category | flops | bytes accessed | tf_op | source)
XLA Modules:
  0.0 47.7 jit_solution(1764795021952038382)
XLA Ops:
  0.6 1.1 %copy-done = f32[2,5,8,4,512]{4,3,2,1,0:T(4,128)S(1)} copy-done((f32[2,5,8,4,512]{4,3,2,1,0:T(4,128)S(1)}, f32[2,5,8,4,512]{4,3,2,1,0:T(4,128)}, u32[]{:S(2)}) %copy-start) | copy-done | bytes 655384
  1.7 0.7 %near_faces.1 = (bf16[5,48,512]{2,1,0:T(8,128)(2,1)S(1)}, f32[2,5,8,4,512]{4,3,2,1,0:T(4,128)S(1)}) custom-call(s32[1]{0:T(128)} %bitcast.where_ref, f32[2,5,8,4,512]{4,3,2,1,0:T(4,128)S(1)} %copy-done), custom_call_target="tpu_custom_call" | custom-call | flops 10000000 | bytes 1638400 | tf_op jit(solution)/shard_map/near_faces/pallas_call | solution.py:599
  2.4 3.0 %collective-permute-start = (bf16[5,48,512]{2,1,0:T(8,128)(2,1)S(1)}, bf16[5,48,512]{2,1,0:T(8,128)(2,1)S(1)}, u32[]{:S(2)}, u32[]{:S(2)}) collective-permute-start(bf16[5,48,512]{2,1,0:T(8,128)(2,1)S(1)} %get-tuple-element.27._), channel_id=1, source_target_pairs={{0,1},{1,0},{2,3},{3,2},{4,5},{5,4},{6,7},{7,6},{8,9},{9,8},{10,11... | collective-permute-start | bytes 737288 | tf_op jit(solution)/shard_map/ppermute | solution.py:619
  5.5 0.7 %later_faces.1 = (bf16[5,48,512]{2,1,0:T(8,128)(2,1)S(1)}, f32[2,5,4,4,512]{4,3,2,1,0:T(4,128)S(1)}, f32[2,5,4,4,512]{4,3,2,1,0:T(4,128)S(1)}) custom-call(s32[1]{0:T(128)} %bitcast.where_ref, bf16[5,48,512]{2,1,0:T(8,128)(2,1)S(1)} %get-tuple-element.27._, f32[2,5,8,4,512]{4,3,2,1,0:T(4,128)S(1)} %get-tuple-element.25.windows_ref), custom_call_target="tpu_custom_call" | custom-call | flops 10000000 | bytes 1638400 | tf_op jit(solution)/shard_map/later_faces/pallas_call | solution.py:609
  6.1 3.8 %collective-permute-start.1 = (f32[2,5,4,4,512]{4,3,2,1,0:T(4,128)S(1)}, f32[2,5,4,4,512]{4,3,2,1,0:T(4,128)S(1)}, u32[]{:S(2)}, u32[]{:S(2)}) collective-permute-start(f32[2,5,4,4,512]{4,3,2,1,0:T(4,128)S(1)} %get-tuple-element.28), channel_id=1, source_target_pairs={{2,0},{4,2},{6,4},{8,6},{10,8},{12,10},{14,12},{16,14},{18,16},{20... | collective-permute-start | bytes 983048 | tf_op jit(solution)/shard_map/ppermute | solution.py:623
  9.9 6.9 %inner_gram.1 = (f32[2,5,8,4,512]{4,3,2,1,0:T(4,128)S(1)}, f32[512,256]{1,0:T(8,128)S(1)}, f32[256,256]{1,0:T(8,128)S(1)}, bf16[64,20,8,512]{3,2,1,0:T(8,128)(2,1)S(1)}) custom-call(f32[2,5,8,4,512]{4,3,2,1,0:T(4,128)S(1)} %get-tuple-element.25.windows_ref, bf16[64,20,8,512]{3,2,1,0:T(8,128)(2,1)} %bitcast.3), custom_call_target="tpu_custom_call" | custom-call | flops 1000000 | bytes 163840 | tf_op jit(solution)/shard_map/inner_gram/pallas_call | solution.py:648
  16.8 0.0 collective-permute-done.group_ref
  16.9 0.2 wall_join.1.part_ref
  17.1 2.8 %collective-permute-start.4 = (bf16[2,5,16,512]{3,2,1,0:T(8,128)(2,1)S(1)}, bf16[2,5,16,512]{3,2,1,0:T(8,128)(2,1)S(1)}, u32[]{:S(2)}, u32[]{:S(2)}) collective-permute-start(bf16[2,5,16,512]{3,2,1,0:T(8,128)(2,1)S(1)} %get-tuple-element.29._), channel_id=1, source_target_pairs={{0,1},{1,0},{2,3},{3,2},{4,5},{5,4},{6,7},{7,6},{8,9},{9,8},{10,11... | collective-permute-start | bytes 491528 | tf_op jit(solution)/shard_map/ppermute | solution.py:703
  19.9 2.4 %gram.1._.gram_ref = f32[32,128]{1,0:T(8,128)S(1)} custom-call(bf16[2,5,16,512]{3,2,1,0:T(8,128)(2,1)S(1)} %get-tuple-element.29._, f32[512,256]{1,0:T(8,128)S(1)} %get-tuple-element.30.right_ref, f32[256,256]{1,0:T(8,128)S(1)} %get-tuple-element.31.left_ref, bf16[64,20,8,512]{3,2,1,0:T(8,128)(2,1)S(1)} %get-tuple-element.32.basis_ref.rest_4_), custom_call_target="tpu_custom_call" | custom-call | flops 2684354560 | bytes 10485760 | tf_op jit(solution)/shard_map/gram/pallas_call | solution.py:668
  22.3 0.0 collective-permute-start.5
  22.3 0.2 own_join.1
  22.5 1.5 %collective-permute-done.4.rest_1_ = bf16[2,5,16,512]{3,2,1,0:T(8,128)(2,1)S(1)} collective-permute-done((bf16[2,5,16,512]{3,2,1,0:T(8,128)(2,1)S(1)}, bf16[2,5,16,512]{3,2,1,0:T(8,128)(2,1)S(1)}, u32[]{:S(2)}, u32[]{:S(2)}) %collective-permute-start.4) | collective-permute-done | bytes 163872 | tf_op jit(solution)/shard_map/ppermute | solution.py:703
  24.0 3.1 %project.1 = (f32[8,128]{1,0:T(8,128)S(1)}, bf16[20,16,512]{2,1,0:T(8,128)(2,1)S(1)}, f32[2,5,8,4,512]{4,3,2,1,0:T(4,128)}) custom-call(s32[1]{0:T(128)} %bitcast.where_ref, bf16[2,5,16,512]{3,2,1,0:T(8,128)(2,1)S(1)} %get-tuple-element.35.rest_0_, bf16[2,5,16,512]{3,2,1,0:T(8,128)(2,1)S(1)} %collective-permute-done.4.rest_1_, ...), custom_call_target="tpu_custom_call" | custom-call | flops 167772160 | bytes 10485760 | tf_op jit(solution)/shard_map/project/pallas_call | solution.py:735
  27.2 1.8 %collective-permute-start.6 = (f32[40,128]{1,0:T(8,128)S(1)}, f32[40,128]{1,0:T(8,128)S(1)}, u32[]{:S(2)}, u32[]{:S(2)}) collective-permute-start(f32[40,128]{1,0:T(8,128)S(1)} %merge.1), channel_id=1, source_target_pairs={{0,1},{1,0},{2,3},{3,2},{4,5},{5,4},{6,7},{7,6},{8,9},{9,8},{10,11... | collective-permute-start | bytes 61448 | tf_op jit(solution)/shard_map/ppermute | solution.py:567
  29.0 2.0 %collective-permute-done.6 = f32[40,128]{1,0:T(8,128)S(1)} collective-permute-done((f32[40,128]{1,0:T(8,128)S(1)}, f32[40,128]{1,0:T(8,128)S(1)}, u32[]{:S(2)}, u32[]{:S(2)}) %collective-permute-start.6) | collective-permute-done | bytes 20512 | tf_op jit(solution)/shard_map/ppermute | solution.py:567
  31.1 1.2 %collective-permute-done.7 = f32[40,128]{1,0:T(8,128)S(1)} collective-permute-done((f32[40,128]{1,0:T(8,128)S(1)}, f32[40,128]{1,0:T(8,128)S(1)}, u32[]{:S(2)}, u32[]{:S(2)}) %collective-permute-start.7) | collective-permute-done | bytes 20512 | tf_op jit(solution)/shard_map/ppermute | solution.py:567
  32.3 3.8 %collective-permute-done.8 = f32[40,128]{1,0:T(8,128)S(1)} collective-permute-done((f32[40,128]{1,0:T(8,128)S(1)}, f32[40,128]{1,0:T(8,128)S(1)}, u32[]{:S(2)}, u32[]{:S(2)}) %collective-permute-start.8) | collective-permute-done | bytes 20512 | tf_op jit(solution)/shard_map/ppermute | solution.py:567
  36.0 0.7 %collective-permute-start.9 = (f32[40,128]{1,0:T(8,128)S(1)}, f32[40,128]{1,0:T(8,128)S(1)}, u32[]{:S(2)}, u32[]{:S(2)}) collective-permute-start(f32[40,128]{1,0:T(8,128)S(1)} %add.17), channel_id=1, source_target_pairs={{0,16},{2,18},{4,20},{6,22},{8,24},{10,26},{12,28},{14,30},{16,0},... | collective-permute-start | bytes 61448 | tf_op jit(solution)/shard_map/ppermute | solution.py:567
  36.7 4.0 %collective-permute-done.9 = f32[40,128]{1,0:T(8,128)S(1)} collective-permute-done((f32[40,128]{1,0:T(8,128)S(1)}, f32[40,128]{1,0:T(8,128)S(1)}, u32[]{:S(2)}, u32[]{:S(2)}) %collective-permute-start.9) | collective-permute-done | bytes 20512 | tf_op jit(solution)/shard_map/ppermute | solution.py:567
  40.7 0.5 %collective-permute-start.10 = (f32[40,128]{1,0:T(8,128)S(1)}, f32[40,128]{1,0:T(8,128)S(1)}, u32[]{:S(2)}, u32[]{:S(2)}) collective-permute-start(f32[40,128]{1,0:T(8,128)S(1)} %add.18.sums_ref), channel_id=1, source_target_pairs={{0,4},{2,6},{4,0},{6,2},{8,12},{10,14},{12,8},{14,10},{16,20},{18,... | collective-permute-start | bytes 61448 | tf_op jit(solution)/shard_map/ppermute | solution.py:567
  41.2 2.4 %inverse.1 = (f32[64,64]{1,0:T(8,128)S(1)}, f32[64,512]{1,0:T(8,128)S(1)}) custom-call(f32[40,128]{1,0:T(8,128)S(1)} %add.18.sums_ref), custom_call_target="tpu_custom_call" | custom-call | flops 20000000 | bytes 32768 | tf_op jit(solution)/shard_map/inverse/pallas_call | solution.py:774
  43.7 0.9 %collective-permute-done.10 = f32[40,128]{1,0:T(8,128)S(1)} collective-permute-done((f32[40,128]{1,0:T(8,128)S(1)}, f32[40,128]{1,0:T(8,128)S(1)}, u32[]{:S(2)}, u32[]{:S(2)}) %collective-permute-start.10) | collective-permute-done | bytes 20512 | tf_op jit(solution)/shard_map/ppermute | solution.py:567
  44.5 3.2 %finish.1 = (f32[2,20,8,512]{3,2,1,0:T(8,128)}, f32[2,64]{1,0:T(2,128)}, f32[2,2]{1,0:T(2,128)}) custom-call(f32[40,128]{1,0:T(8,128)S(1)} %add.19.projected_ref, f32[40,128]{1,0:T(8,128)S(1)} %add.18.sums_ref, f32[64,64]{1,0:T(8,128)S(1)} %get-tuple-element.40.inverse_ref, f32[64,512]{1,0:T(8,128)S(1)} %get-tuple-element.41.spread_ref, ...), custom_call_target="tpu_custom_call" | custom-call | flops 335544320 | bytes 11796480 | tf_op jit(solution)/shard_map/finish/pallas_call | solution.py:787
  (16 shorter events, 0.1 us)
Async XLA Ops:
  0.6 1.1 %copy-start = (f32[2,5,8,4,512]{4,3,2,1,0:T(4,128)S(1)}, f32[2,5,8,4,512]{4,3,2,1,0:T(4,128)}, u32[]{:S(2)}) copy-start(f32[2,5,8,4,512]{4,3,2,1,0:T(4,128)} %source_ref.1) | copy-start | bytes 1966084
  2.4 14.4 %collective-permute-start = (bf16[5,48,512]{2,1,0:T(8,128)(2,1)S(1)}, bf16[5,48,512]{2,1,0:T(8,128)(2,1)S(1)}, u32[]{:S(2)}, u32[]{:S(2)}) collective-permute-start(bf16[5,48,512]{2,1,0:T(8,128)(2,1)S(1)} %get-tuple-element.27._), channel_id=1, source_target_pairs={{0,1},{1,0},{2,3},{3,2},{4,5},{5,4},{6,7},{7,6},{8,9},{9,8},{10,11... | collective-permute-start | bytes 737288 | tf_op jit(solution)/shard_map/ppermute | solution.py:619
  6.1 10.9 %collective-permute-start.1 = (f32[2,5,4,4,512]{4,3,2,1,0:T(4,128)S(1)}, f32[2,5,4,4,512]{4,3,2,1,0:T(4,128)S(1)}, u32[]{:S(2)}, u32[]{:S(2)}) collective-permute-start(f32[2,5,4,4,512]{4,3,2,1,0:T(4,128)S(1)} %get-tuple-element.28), channel_id=1, source_target_pairs={{2,0},{4,2},{6,4},{8,6},{10,8},{12,10},{14,12},{16,14},{18,16},{20... | collective-permute-start | bytes 983048 | tf_op jit(solution)/shard_map/ppermute | solution.py:623
  9.9 12.4 %collective-permute-start.3 = (bf16[5,48,512]{2,1,0:T(8,128)(2,1)S(1)}, bf16[5,48,512]{2,1,0:T(8,128)(2,1)S(1)}, u32[]{:S(2)}, u32[]{:S(2)}) collective-permute-start(bf16[5,48,512]{2,1,0:T(8,128)(2,1)S(1)} %get-tuple-element.34), channel_id=1, source_target_pairs={{0,1},{1,0},{2,3},{3,2},{4,5},{5,4},{6,7},{7,6},{8,9},{9,8},{10,11... | collective-permute-start | bytes 737288 | tf_op jit(solution)/shard_map/ppermute | solution.py:625
  9.9 12.4 %collective-permute-start.2 = (f32[2,5,4,4,512]{4,3,2,1,0:T(4,128)S(1)}, f32[2,5,4,4,512]{4,3,2,1,0:T(4,128)S(1)}, u32[]{:S(2)}, u32[]{:S(2)}) collective-permute-start(f32[2,5,4,4,512]{4,3,2,1,0:T(4,128)S(1)} %get-tuple-element.33), channel_id=1, source_target_pairs={{0,2},{2,4},{4,6},{6,8},{8,10},{10,12},{12,14},{14,16},{16,18},{18... | collective-permute-start | bytes 983048 | tf_op jit(solution)/shard_map/ppermute | solution.py:624
  17.1 7.0 %collective-permute-start.4 = (bf16[2,5,16,512]{3,2,1,0:T(8,128)(2,1)S(1)}, bf16[2,5,16,512]{3,2,1,0:T(8,128)(2,1)S(1)}, u32[]{:S(2)}, u32[]{:S(2)}) collective-permute-start(bf16[2,5,16,512]{3,2,1,0:T(8,128)(2,1)S(1)} %get-tuple-element.29._), channel_id=1, source_target_pairs={{0,1},{1,0},{2,3},{3,2},{4,5},{5,4},{6,7},{7,6},{8,9},{9,8},{10,11... | collective-permute-start | bytes 491528 | tf_op jit(solution)/shard_map/ppermute | solution.py:703
  22.3 4.9 %collective-permute-start.5 = (f32[32,128]{1,0:T(8,128)S(1)}, f32[32,128]{1,0:T(8,128)S(1)}, u32[]{:S(2)}, u32[]{:S(2)}) collective-permute-start(f32[32,128]{1,0:T(8,128)S(1)} %gram.1._.gram_ref), channel_id=1, source_target_pairs={{0,4},{2,6},{4,0},{6,2},{8,12},{10,14},{12,8},{14,10},{16,20},{18,... | collective-permute-start | bytes 49160 | tf_op jit(solution)/shard_map/ppermute | solution.py:718
  27.2 3.8 %collective-permute-start.6 = (f32[40,128]{1,0:T(8,128)S(1)}, f32[40,128]{1,0:T(8,128)S(1)}, u32[]{:S(2)}, u32[]{:S(2)}) collective-permute-start(f32[40,128]{1,0:T(8,128)S(1)} %merge.1), channel_id=1, source_target_pairs={{0,1},{1,0},{2,3},{3,2},{4,5},{5,4},{6,7},{7,6},{8,9},{9,8},{10,11... | collective-permute-start | bytes 61448 | tf_op jit(solution)/shard_map/ppermute | solution.py:567
  31.0 1.2 %collective-permute-start.7 = (f32[40,128]{1,0:T(8,128)S(1)}, f32[40,128]{1,0:T(8,128)S(1)}, u32[]{:S(2)}, u32[]{:S(2)}) collective-permute-start(f32[40,128]{1,0:T(8,128)S(1)} %add.15), channel_id=1, source_target_pairs={{0,2},{2,0},{4,6},{6,4},{8,10},{10,8},{12,14},{14,12},{16,18},{18,... | collective-permute-start | bytes 61448 | tf_op jit(solution)/shard_map/ppermute | solution.py:567
  32.2 3.8 %collective-permute-start.8 = (f32[40,128]{1,0:T(8,128)S(1)}, f32[40,128]{1,0:T(8,128)S(1)}, u32[]{:S(2)}, u32[]{:S(2)}) collective-permute-start(f32[40,128]{1,0:T(8,128)S(1)} %add.16), channel_id=1, source_target_pairs={{0,8},{2,10},{4,12},{6,14},{8,0},{10,2},{12,4},{14,6},{16,24},{18,... | collective-permute-start | bytes 61448 | tf_op jit(solution)/shard_map/ppermute | solution.py:567
  36.0 4.7 %collective-permute-start.9 = (f32[40,128]{1,0:T(8,128)S(1)}, f32[40,128]{1,0:T(8,128)S(1)}, u32[]{:S(2)}, u32[]{:S(2)}) collective-permute-start(f32[40,128]{1,0:T(8,128)S(1)} %add.17), channel_id=1, source_target_pairs={{0,16},{2,18},{4,20},{6,22},{8,24},{10,26},{12,28},{14,30},{16,0},... | collective-permute-start | bytes 61448 | tf_op jit(solution)/shard_map/ppermute | solution.py:567
  40.7 3.8 %collective-permute-start.10 = (f32[40,128]{1,0:T(8,128)S(1)}, f32[40,128]{1,0:T(8,128)S(1)}, u32[]{:S(2)}, u32[]{:S(2)}) collective-permute-start(f32[40,128]{1,0:T(8,128)S(1)} %add.18.sums_ref), channel_id=1, source_target_pairs={{0,4},{2,6},{4,0},{6,2},{8,12},{10,14},{12,8},{14,10},{16,20},{18,... | collective-permute-start | bytes 61448 | tf_op jit(solution)/shard_map/ppermute | solution.py:567

commit v12 on v10

--- a/solution.py
+++ b/solution.py
@@ -392,14 +392,16 @@
         copies = []
     modes, tiles = basis_ref.shape[:2]
     columns = snaps_ref.shape[1]
-    total = jnp.zeros((modes * 8, columns), jnp.float32)
-    small = jnp.zeros((columns, columns), jnp.float32)
-    for t in range(tiles):
-        snaps = snaps_ref[t]
+    total = jnp.zeros((modes * 8 + columns, columns), jnp.float32)
+    for start in range(0, tiles, 4):
+        span = range(start, min(start + 4, tiles))
+        snaps = jnp.concatenate([snaps_ref[t] for t in span], axis=1)
+        rows = jnp.concatenate([modes_of(basis_ref, t) for t in span], axis=1)
         total = total + lax.dot_general(
-            modes_of(basis_ref, t), snaps, NT, preferred_element_type=jnp.float32
-        )
-        small = small + lax.dot_general(snaps, snaps, NT, preferred_element_type=jnp.float32)
+            jnp.concatenate([rows, snaps], axis=0), snaps, NT, preferred_element_type=jnp.float32
+        )
+    small = total[modes * 8 :]
+    total = total[: modes * 8]
     wide_sums[0, :, 0:columns] = total
     square[...] = jnp.zeros_like(square)
     square[0:modes, :] = folded(wide_sums, modes)
@@ -485,8 +487,18 @@
     spread = (
         lax.broadcasted_iota(jnp.int32, (modes, wide), 1) // 8
         == lax.broadcasted_iota(jnp.int32, (modes, wide), 0)
-    ).astype(jnp.float32)
-    spread_ref[...] = exact(inverse, spread, plainly)
+    ).astype(jnp.bfloat16)
+    parts = []
+    rest = inverse
+    for _ in range(3):
+        parts.append(rest.astype(jnp.bfloat16))
+        rest = rest - parts[-1].astype(jnp.float32)
+    wide_parts = jnp.dot(
+        jnp.concatenate(parts, axis=0), spread, preferred_element_type=jnp.float32
+    )
+    spread_ref[...] = (
+        wide_parts[0:modes] + wide_parts[modes : 2 * modes] + wide_parts[2 * modes :]
+    )
 
 
 def finish_kernel(

time: 46.5 us -> 46.4 us (level)
  transfers between devices with their start and end apart: 11 -> 11, of which waited for: 5 -> 6; matrix products, arithmetic and copies ran while one was open for 0% -> 0% of each run, Pallas kernels for 33% -> 33%
where the time goes in v12:
time: 46.4 us; the launch traced here: 46.2 us
  Pallas kernels  19.2 us (41%)
  starting transfers between devices  15.2 us (33%)
  waiting for transfers between devices  9.95 us (21%)
  local copies, waits for them, and re-layouts  1.08 us (2%)
  between operations  0.77 us (2%)
    ppermute x5, waiting for transfers between devices, swap_added(): lax.ppermute(value, axis, [(i, i ^ bit) for i in range(count)])  9.24 us
    ppermute x5, starting transfers between devices, swap_added(): lax.ppermute(value, axis, [(i, i ^ bit) for i in range(count)])  5.66 us
    pallas_call x1, Pallas kernels, body(): pl.pallas_call(functools.partial(inner_gram_kernel, early), out_shape=[sh...  5.53 us
    ppermute x1, starting transfers between devices, body(): lax.ppermute(first_edge, ('solver', 'analysis'), down + odd(up))  3.77 us
    pallas_call x1, Pallas kernels, rest_of_gram(): pl.pallas_call(functools.partial(gram_kernel, early, fields), out_shape=s...  3.25 us
    pallas_call x1, Pallas kernels, body(): pl.pallas_call(functools.partial(finish_kernel, rows_total), out_shape=[s...  3.18 us
    pallas_call x1, Pallas kernels, body(): pl.pallas_call(functools.partial(project_kernel, True), out_shape=[sums_s...  3.04 us
    ppermute x1, starting transfers between devices, body(): near_group = lax.ppermute(near_group, 'analysis', swap)  3 us
  transfers between devices with their start and end apart: 11, of which 6 were waited for; matrix products, arithmetic and copies ran while one was open for 0% of the time, Pallas kernels for 33%

profile of v12, /device:TPU:0, one launch (start us, length us, event | category | flops | bytes accessed | tf_op | source)
XLA Modules:
  0.0 46.2 jit_solution(13014538873439607309)
XLA Ops:
  0.6 1.1 %copy-done = f32[2,5,8,4,512]{4,3,2,1,0:T(4,128)S(1)} copy-done((f32[2,5,8,4,512]{4,3,2,1,0:T(4,128)S(1)}, f32[2,5,8,4,512]{4,3,2,1,0:T(4,128)}, u32[]{:S(2)}) %copy-start) | copy-done | bytes 655384
  1.7 0.7 %near_faces.1 = (bf16[5,48,512]{2,1,0:T(8,128)(2,1)S(1)}, f32[2,5,8,4,512]{4,3,2,1,0:T(4,128)S(1)}) custom-call(s32[1]{0:T(128)} %bitcast.where_ref, f32[2,5,8,4,512]{4,3,2,1,0:T(4,128)S(1)} %copy-done), custom_call_target="tpu_custom_call" | custom-call | flops 10000000 | bytes 1638400 | tf_op jit(solution)/shard_map/near_faces/pallas_call | solution.py:611
  2.4 3.0 %collective-permute-start = (bf16[5,48,512]{2,1,0:T(8,128)(2,1)S(1)}, bf16[5,48,512]{2,1,0:T(8,128)(2,1)S(1)}, u32[]{:S(2)}, u32[]{:S(2)}) collective-permute-start(bf16[5,48,512]{2,1,0:T(8,128)(2,1)S(1)} %get-tuple-element.27._), channel_id=1, source_target_pairs={{0,1},{1,0},{2,3},{3,2},{4,5},{5,4},{6,7},{7,6},{8,9},{9,8},{10,11... | collective-permute-start | bytes 737288 | tf_op jit(solution)/shard_map/ppermute | solution.py:631
  5.5 0.7 %later_faces.1 = (bf16[5,48,512]{2,1,0:T(8,128)(2,1)S(1)}, f32[2,5,4,4,512]{4,3,2,1,0:T(4,128)S(1)}, f32[2,5,4,4,512]{4,3,2,1,0:T(4,128)S(1)}) custom-call(s32[1]{0:T(128)} %bitcast.where_ref, bf16[5,48,512]{2,1,0:T(8,128)(2,1)S(1)} %get-tuple-element.27._, f32[2,5,8,4,512]{4,3,2,1,0:T(4,128)S(1)} %get-tuple-element.25.windows_ref), custom_call_target="tpu_custom_call" | custom-call | flops 10000000 | bytes 1638400 | tf_op jit(solution)/shard_map/later_faces/pallas_call | solution.py:621
  6.1 3.8 %collective-permute-start.1 = (f32[2,5,4,4,512]{4,3,2,1,0:T(4,128)S(1)}, f32[2,5,4,4,512]{4,3,2,1,0:T(4,128)S(1)}, u32[]{:S(2)}, u32[]{:S(2)}) collective-permute-start(f32[2,5,4,4,512]{4,3,2,1,0:T(4,128)S(1)} %get-tuple-element.28), channel_id=1, source_target_pairs={{2,0},{4,2},{6,4},{8,6},{10,8},{12,10},{14,12},{16,14},{18,16},{20... | collective-permute-start | bytes 983048 | tf_op jit(solution)/shard_map/ppermute | solution.py:635
  9.9 5.5 %inner_gram.1 = (f32[2,5,8,4,512]{4,3,2,1,0:T(4,128)S(1)}, f32[512,256]{1,0:T(8,128)S(1)}, f32[256,256]{1,0:T(8,128)S(1)}, bf16[64,20,8,512]{3,2,1,0:T(8,128)(2,1)S(1)}) custom-call(f32[2,5,8,4,512]{4,3,2,1,0:T(4,128)S(1)} %get-tuple-element.25.windows_ref, bf16[64,20,8,512]{3,2,1,0:T(8,128)(2,1)} %bitcast.3), custom_call_target="tpu_custom_call" | custom-call | flops 1000000 | bytes 163840 | tf_op jit(solution)/shard_map/inner_gram/pallas_call | solution.py:660
  15.5 0.2 wall_join.1.part_ref
  15.7 2.8 %collective-permute-start.4 = (bf16[2,5,16,512]{3,2,1,0:T(8,128)(2,1)S(1)}, bf16[2,5,16,512]{3,2,1,0:T(8,128)(2,1)S(1)}, u32[]{:S(2)}, u32[]{:S(2)}) collective-permute-start(bf16[2,5,16,512]{3,2,1,0:T(8,128)(2,1)S(1)} %get-tuple-element.29._), channel_id=1, source_target_pairs={{0,1},{1,0},{2,3},{3,2},{4,5},{5,4},{6,7},{7,6},{8,9},{9,8},{10,11... | collective-permute-start | bytes 491528 | tf_op jit(solution)/shard_map/ppermute | solution.py:715
  18.5 3.2 %gram.1._.gram_ref = f32[32,128]{1,0:T(8,128)S(1)} custom-call(bf16[2,5,16,512]{3,2,1,0:T(8,128)(2,1)S(1)} %get-tuple-element.29._, f32[512,256]{1,0:T(8,128)S(1)} %get-tuple-element.30.right_ref, f32[256,256]{1,0:T(8,128)S(1)} %get-tuple-element.31.left_ref, bf16[64,20,8,512]{3,2,1,0:T(8,128)(2,1)S(1)} %get-tuple-element.32.basis_ref.rest_4_), custom_call_target="tpu_custom_call" | custom-call | flops 2684354560 | bytes 10485760 | tf_op jit(solution)/shard_map/gram/pallas_call | solution.py:680
  21.7 0.0 collective-permute-start.5
  21.8 0.2 own_join.1
  22.0 0.7 %collective-permute-done.4.rest_1_ = bf16[2,5,16,512]{3,2,1,0:T(8,128)(2,1)S(1)} collective-permute-done((bf16[2,5,16,512]{3,2,1,0:T(8,128)(2,1)S(1)}, bf16[2,5,16,512]{3,2,1,0:T(8,128)(2,1)S(1)}, u32[]{:S(2)}, u32[]{:S(2)}) %collective-permute-start.4) | collective-permute-done | bytes 163872 | tf_op jit(solution)/shard_map/ppermute | solution.py:715
  22.6 3.0 %project.1 = (f32[8,128]{1,0:T(8,128)S(1)}, bf16[20,16,512]{2,1,0:T(8,128)(2,1)S(1)}, f32[2,5,8,4,512]{4,3,2,1,0:T(4,128)}) custom-call(s32[1]{0:T(128)} %bitcast.where_ref, bf16[2,5,16,512]{3,2,1,0:T(8,128)(2,1)S(1)} %get-tuple-element.35.rest_0_, bf16[2,5,16,512]{3,2,1,0:T(8,128)(2,1)S(1)} %collective-permute-done.4.rest_1_, ...), custom_call_target="tpu_custom_call" | custom-call | flops 167772160 | bytes 10485760 | tf_op jit(solution)/shard_map/project/pallas_call | solution.py:747
  25.7 1.8 %collective-permute-start.6 = (f32[40,128]{1,0:T(8,128)S(1)}, f32[40,128]{1,0:T(8,128)S(1)}, u32[]{:S(2)}, u32[]{:S(2)}) collective-permute-start(f32[40,128]{1,0:T(8,128)S(1)} %merge.1), channel_id=1, source_target_pairs={{0,1},{1,0},{2,3},{3,2},{4,5},{5,4},{6,7},{7,6},{8,9},{9,8},{10,11... | collective-permute-start | bytes 61448 | tf_op jit(solution)/shard_map/ppermute | solution.py:579
  27.5 2.0 %collective-permute-done.6 = f32[40,128]{1,0:T(8,128)S(1)} collective-permute-done((f32[40,128]{1,0:T(8,128)S(1)}, f32[40,128]{1,0:T(8,128)S(1)}, u32[]{:S(2)}, u32[]{:S(2)}) %collective-permute-start.6) | collective-permute-done | bytes 20512 | tf_op jit(solution)/shard_map/ppermute | solution.py:579
  29.6 1.2 %collective-permute-done.7 = f32[40,128]{1,0:T(8,128)S(1)} collective-permute-done((f32[40,128]{1,0:T(8,128)S(1)}, f32[40,128]{1,0:T(8,128)S(1)}, u32[]{:S(2)}, u32[]{:S(2)}) %collective-permute-start.7) | collective-permute-done | bytes 20512 | tf_op jit(solution)/shard_map/ppermute | solution.py:579
  30.8 0.8 %collective-permute-start.8 = (f32[40,128]{1,0:T(8,128)S(1)}, f32[40,128]{1,0:T(8,128)S(1)}, u32[]{:S(2)}, u32[]{:S(2)}) collective-permute-start(f32[40,128]{1,0:T(8,128)S(1)} %add.16), channel_id=1, source_target_pairs={{0,8},{2,10},{4,12},{6,14},{8,0},{10,2},{12,4},{14,6},{16,24},{18,... | collective-permute-start | bytes 61448 | tf_op jit(solution)/shard_map/ppermute | solution.py:579
  31.5 3.0 %collective-permute-done.8 = f32[40,128]{1,0:T(8,128)S(1)} collective-permute-done((f32[40,128]{1,0:T(8,128)S(1)}, f32[40,128]{1,0:T(8,128)S(1)}, u32[]{:S(2)}, u32[]{:S(2)}) %collective-permute-start.8) | collective-permute-done | bytes 20512 | tf_op jit(solution)/shard_map/ppermute | solution.py:579
  34.6 1.8 %collective-permute-start.9 = (f32[40,128]{1,0:T(8,128)S(1)}, f32[40,128]{1,0:T(8,128)S(1)}, u32[]{:S(2)}, u32[]{:S(2)}) collective-permute-start(f32[40,128]{1,0:T(8,128)S(1)} %add.17), channel_id=1, source_target_pairs={{0,16},{2,18},{4,20},{6,22},{8,24},{10,26},{12,28},{14,30},{16,0},... | collective-permute-start | bytes 61448 | tf_op jit(solution)/shard_map/ppermute | solution.py:579
  36.3 2.9 %collective-permute-done.9 = f32[40,128]{1,0:T(8,128)S(1)} collective-permute-done((f32[40,128]{1,0:T(8,128)S(1)}, f32[40,128]{1,0:T(8,128)S(1)}, u32[]{:S(2)}, u32[]{:S(2)}) %collective-permute-start.9) | collective-permute-done | bytes 20512 | tf_op jit(solution)/shard_map/ppermute | solution.py:579
  39.3 1.3 %collective-permute-start.10 = (f32[40,128]{1,0:T(8,128)S(1)}, f32[40,128]{1,0:T(8,128)S(1)}, u32[]{:S(2)}, u32[]{:S(2)}) collective-permute-start(f32[40,128]{1,0:T(8,128)S(1)} %add.18.sums_ref), channel_id=1, source_target_pairs={{0,4},{2,6},{4,0},{6,2},{8,12},{10,14},{12,8},{14,10},{16,20},{18,... | collective-permute-start | bytes 61448 | tf_op jit(solution)/shard_map/ppermute | solution.py:579
  40.6 2.4 %inverse.1 = (f32[64,64]{1,0:T(8,128)S(1)}, f32[64,512]{1,0:T(8,128)S(1)}) custom-call(f32[40,128]{1,0:T(8,128)S(1)} %add.18.sums_ref), custom_call_target="tpu_custom_call" | custom-call | flops 20000000 | bytes 32768 | tf_op jit(solution)/shard_map/inverse/pallas_call | solution.py:786
  43.0 0.1 collective-permute-done.10
  43.0 3.2 %finish.1 = (f32[2,20,8,512]{3,2,1,0:T(8,128)}, f32[2,64]{1,0:T(2,128)}, f32[2,2]{1,0:T(2,128)}) custom-call(f32[40,128]{1,0:T(8,128)S(1)} %add.19.projected_ref, f32[40,128]{1,0:T(8,128)S(1)} %add.18.sums_ref, f32[64,64]{1,0:T(8,128)S(1)} %get-tuple-element.40.inverse_ref, f32[64,512]{1,0:T(8,128)S(1)} %get-tuple-element.41.spread_ref, ...), custom_call_target="tpu_custom_call" | custom-call | flops 335544320 | bytes 11796480 | tf_op jit(solution)/shard_map/finish/pallas_call | solution.py:799
  (16 shorter events, 0.1 us)
Async XLA Ops:
  0.6 1.1 %copy-start = (f32[2,5,8,4,512]{4,3,2,1,0:T(4,128)S(1)}, f32[2,5,8,4,512]{4,3,2,1,0:T(4,128)}, u32[]{:S(2)}) copy-start(f32[2,5,8,4,512]{4,3,2,1,0:T(4,128)} %source_ref.1) | copy-start | bytes 1966084
  2.4 13.0 %collective-permute-start = (bf16[5,48,512]{2,1,0:T(8,128)(2,1)S(1)}, bf16[5,48,512]{2,1,0:T(8,128)(2,1)S(1)}, u32[]{:S(2)}, u32[]{:S(2)}) collective-permute-start(bf16[5,48,512]{2,1,0:T(8,128)(2,1)S(1)} %get-tuple-element.27._), channel_id=1, source_target_pairs={{0,1},{1,0},{2,3},{3,2},{4,5},{5,4},{6,7},{7,6},{8,9},{9,8},{10,11... | collective-permute-start | bytes 737288 | tf_op jit(solution)/shard_map/ppermute | solution.py:631
  6.1 9.5 %collective-permute-start.1 = (f32[2,5,4,4,512]{4,3,2,1,0:T(4,128)S(1)}, f32[2,5,4,4,512]{4,3,2,1,0:T(4,128)S(1)}, u32[]{:S(2)}, u32[]{:S(2)}) collective-permute-start(f32[2,5,4,4,512]{4,3,2,1,0:T(4,128)S(1)} %get-tuple-element.28), channel_id=1, source_target_pairs={{2,0},{4,2},{6,4},{8,6},{10,8},{12,10},{14,12},{16,14},{18,16},{20... | collective-permute-start | bytes 983048 | tf_op jit(solution)/shard_map/ppermute | solution.py:635
  9.9 11.8 %collective-permute-start.3 = (bf16[5,48,512]{2,1,0:T(8,128)(2,1)S(1)}, bf16[5,48,512]{2,1,0:T(8,128)(2,1)S(1)}, u32[]{:S(2)}, u32[]{:S(2)}) collective-permute-start(bf16[5,48,512]{2,1,0:T(8,128)(2,1)S(1)} %get-tuple-element.34), channel_id=1, source_target_pairs={{0,1},{1,0},{2,3},{3,2},{4,5},{5,4},{6,7},{7,6},{8,9},{9,8},{10,11... | collective-permute-start | bytes 737288 | tf_op jit(solution)/shard_map/ppermute | solution.py:637
  9.9 11.8 %collective-permute-start.2 = (f32[2,5,4,4,512]{4,3,2,1,0:T(4,128)S(1)}, f32[2,5,4,4,512]{4,3,2,1,0:T(4,128)S(1)}, u32[]{:S(2)}, u32[]{:S(2)}) collective-permute-start(f32[2,5,4,4,512]{4,3,2,1,0:T(4,128)S(1)} %get-tuple-element.33), channel_id=1, source_target_pairs={{0,2},{2,4},{4,6},{6,8},{8,10},{10,12},{12,14},{14,16},{16,18},{18... | collective-permute-start | bytes 983048 | tf_op jit(solution)/shard_map/ppermute | solution.py:636
  15.7 7.0 %collective-permute-start.4 = (bf16[2,5,16,512]{3,2,1,0:T(8,128)(2,1)S(1)}, bf16[2,5,16,512]{3,2,1,0:T(8,128)(2,1)S(1)}, u32[]{:S(2)}, u32[]{:S(2)}) collective-permute-start(bf16[2,5,16,512]{3,2,1,0:T(8,128)(2,1)S(1)} %get-tuple-element.29._), channel_id=1, source_target_pairs={{0,1},{1,0},{2,3},{3,2},{4,5},{5,4},{6,7},{7,6},{8,9},{9,8},{10,11... | collective-permute-start | bytes 491528 | tf_op jit(solution)/shard_map/ppermute | solution.py:715
  21.7 4.0 %collective-permute-start.5 = (f32[32,128]{1,0:T(8,128)S(1)}, f32[32,128]{1,0:T(8,128)S(1)}, u32[]{:S(2)}, u32[]{:S(2)}) collective-permute-start(f32[32,128]{1,0:T(8,128)S(1)} %gram.1._.gram_ref), channel_id=1, source_target_pairs={{0,4},{2,6},{4,0},{6,2},{8,12},{10,14},{12,8},{14,10},{16,20},{18,... | collective-permute-start | bytes 49160 | tf_op jit(solution)/shard_map/ppermute | solution.py:730
  25.7 3.8 %collective-permute-start.6 = (f32[40,128]{1,0:T(8,128)S(1)}, f32[40,128]{1,0:T(8,128)S(1)}, u32[]{:S(2)}, u32[]{:S(2)}) collective-permute-start(f32[40,128]{1,0:T(8,128)S(1)} %merge.1), channel_id=1, source_target_pairs={{0,1},{1,0},{2,3},{3,2},{4,5},{5,4},{6,7},{7,6},{8,9},{9,8},{10,11... | collective-permute-start | bytes 61448 | tf_op jit(solution)/shard_map/ppermute | solution.py:579
  29.6 1.2 %collective-permute-start.7 = (f32[40,128]{1,0:T(8,128)S(1)}, f32[40,128]{1,0:T(8,128)S(1)}, u32[]{:S(2)}, u32[]{:S(2)}) collective-permute-start(f32[40,128]{1,0:T(8,128)S(1)} %add.15), channel_id=1, source_target_pairs={{0,2},{2,0},{4,6},{6,4},{8,10},{10,8},{12,14},{14,12},{16,18},{18,... | collective-permute-start | bytes 61448 | tf_op jit(solution)/shard_map/ppermute | solution.py:579
  30.8 3.8 %collective-permute-start.8 = (f32[40,128]{1,0:T(8,128)S(1)}, f32[40,128]{1,0:T(8,128)S(1)}, u32[]{:S(2)}, u32[]{:S(2)}) collective-permute-start(f32[40,128]{1,0:T(8,128)S(1)} %add.16), channel_id=1, source_target_pairs={{0,8},{2,10},{4,12},{6,14},{8,0},{10,2},{12,4},{14,6},{16,24},{18,... | collective-permute-start | bytes 61448 | tf_op jit(solution)/shard_map/ppermute | solution.py:579
  34.6 4.7 %collective-permute-start.9 = (f32[40,128]{1,0:T(8,128)S(1)}, f32[40,128]{1,0:T(8,128)S(1)}, u32[]{:S(2)}, u32[]{:S(2)}) collective-permute-start(f32[40,128]{1,0:T(8,128)S(1)} %add.17), channel_id=1, source_target_pairs={{0,16},{2,18},{4,20},{6,22},{8,24},{10,26},{12,28},{14,30},{16,0},... | collective-permute-start | bytes 61448 | tf_op jit(solution)/shard_map/ppermute | solution.py:579
  39.3 3.8 %collective-permute-start.10 = (f32[40,128]{1,0:T(8,128)S(1)}, f32[40,128]{1,0:T(8,128)S(1)}, u32[]{:S(2)}, u32[]{:S(2)}) collective-permute-start(f32[40,128]{1,0:T(8,128)S(1)} %add.18.sums_ref), channel_id=1, source_target_pairs={{0,4},{2,6},{4,0},{6,2},{8,12},{10,14},{12,8},{14,10},{16,20},{18,... | collective-permute-start | bytes 61448 | tf_op jit(solution)/shard_map/ppermute | solution.py:579

commit v13 on v12

--- a/solution.py
+++ b/solution.py
@@ -326,14 +326,21 @@
             snaps_ref[w, f] = jnp.concatenate(done, axis=0).astype(jnp.bfloat16)
 
 
-def own_join_kernel(where_ref, _, part_ref, edge_ref, group_ref, made, snaps_ref):
+def own_edge_kernel(where_ref, _, part_ref, edge_ref, own_ref):
     windows, _, planes = part_ref.shape[:3]
     base = planes // 2 * where_ref[0]
     for w in range(windows):
         for f in range(5):
+            for x in range(planes // 2):
+                own_ref[w, f, x] = part_ref[w, f, base + x] + edge_ref[w, f, x]
+
+
+def own_join_kernel(where_ref, _, part_ref, group_ref, made, snaps_ref):
+    for w in range(part_ref.shape[0]):
+        for f in range(5):
             done = []
             for x, term in enumerate(wall_terms_of(where_ref[0] == 0, group_ref, w, f)):
-                total = part_ref[w, f, base + x] + term + edge_ref[w, f, x]
+                total = part_ref[w, f, x] + term
                 made[w, f, x] = total
                 done.append(total)
             snaps_ref[w, f] = jnp.concatenate(done, axis=0).astype(jnp.bfloat16)
@@ -713,7 +720,16 @@
             name="edge_join",
         )(inner_given, first_edge)
         got = lax.ppermute(given, "analysis", swap)
-        gram = rest_of_gram(given)
+        inner_own = pl.pallas_call(
+            own_edge_kernel,
+            out_shape=half_next,
+            in_specs=[SCALAR, LOOSE] + [WHOLE] * 2,
+            out_specs=WHOLE,
+            compiler_params=params(16),
+            cost_estimate=join_cost,
+            name="own_edge",
+        )(place, given, inner, second_edge)
+        gram = rest_of_gram(inner_own)
     else:
         next_windows = pl.pallas_call(
             functools.partial(join_kernel, 2),
@@ -732,12 +748,12 @@
         next_own, own = pl.pallas_call(
             own_join_kernel,
             out_shape=[half_next, shape(half_shape, bf16)],
-            in_specs=[SCALAR, LOOSE] + [WHOLE] * 3,
+            in_specs=[SCALAR, LOOSE] + [WHOLE] * 2,
             out_specs=[WHOLE] * 2,
             compiler_params=params(16),
             cost_estimate=join_cost,
             name="own_join",
-        )(place, gram, inner, second_edge, later_group)
+        )(place, gram, inner_own, later_group)
 
     sums_shape = shape((8, LANES), f32)
     snaps_shape = shape((tiles, 2 * 8, cells), bf16)

time: 46.4 us -> 47 us (1.013)
  waiting for transfers between devices: 9.95 us -> 13.2 us
  starting transfers between devices: 15.2 us -> 12.5 us
    ppermute x5, waiting for transfers between devices: 9.24 us -> 11.4 us  [swap_added(): lax.ppermute(value, axis, [(i, i ^ bit) for i in range(count)])]
    ppermute x5, starting transfers between devices: 5.66 us -> 3.62 us  [swap_added(): lax.ppermute(value, axis, [(i, i ^ bit) for i in range(count)])]
    ppermute x1, starting transfers between devices: 2.77 us -> 1.35 us  [body(): got = lax.ppermute(given, 'analysis', swap)]
    ppermute x1, waiting for transfers between devices: 0.01 us -> 1.32 us  [body(): lax.ppermute(second_edge, ('solver', 'analysis'), up + odd(down))]
    ppermute x1, starting transfers between devices: 0.01 us -> 0.74 us  [body(): later_group = lax.ppermute(later_group, 'analysis', swap)]
    ppermute x1, waiting for transfers between devices: 0.69 us -> 0.01 us  [body(): got = lax.ppermute(given, 'analysis', swap)]
where the time goes in v13:
time: 47 us; the launch traced here: 46.8 us
  Pallas kernels  19.2 us (41%)
  waiting for transfers between devices  13.2 us (28%)
  starting transfers between devices  12.5 us (27%)
  local copies, waits for them, and re-layouts  1.08 us (2%)
  between operations  0.77 us (2%)
    ppermute x5, waiting for transfers between devices, swap_added(): lax.ppermute(value, axis, [(i, i ^ bit) for i in range(count)])  11.4 us
    pallas_call x1, Pallas kernels, body(): pl.pallas_call(functools.partial(inner_gram_kernel, early), out_shape=[sh...  5.53 us
    ppermute x1, starting transfers between devices, body(): lax.ppermute(first_edge, ('solver', 'analysis'), down + odd(up))  3.77 us
    ppermute x5, starting transfers between devices, swap_added(): lax.ppermute(value, axis, [(i, i ^ bit) for i in range(count)])  3.62 us
    pallas_call x1, Pallas kernels, rest_of_gram(): pl.pallas_call(functools.partial(gram_kernel, early, fields), out_shape=s...  3.25 us
    pallas_call x1, Pallas kernels, body(): pl.pallas_call(functools.partial(finish_kernel, rows_total), out_shape=[s...  3.18 us
    pallas_call x1, Pallas kernels, body(): pl.pallas_call(functools.partial(project_kernel, True), out_shape=[sums_s...  3.05 us
    ppermute x1, starting transfers between devices, body(): near_group = lax.ppermute(near_group, 'analysis', swap)  3 us
  transfers between devices with their start and end apart: 11, of which 6 were waited for; matrix products, arithmetic and copies ran while one was open for 0% of the time, Pallas kernels for 33%

profile of v13, /device:TPU:0, one launch (start us, length us, event | category | flops | bytes accessed | tf_op | source)
XLA Modules:
  0.0 46.8 jit_solution(8387375861680571141)
XLA Ops:
  0.6 1.1 %copy-done = f32[2,5,8,4,512]{4,3,2,1,0:T(4,128)S(1)} copy-done((f32[2,5,8,4,512]{4,3,2,1,0:T(4,128)S(1)}, f32[2,5,8,4,512]{4,3,2,1,0:T(4,128)}, u32[]{:S(2)}) %copy-start) | copy-done | bytes 655384
  1.7 0.7 %near_faces.1 = (bf16[5,48,512]{2,1,0:T(8,128)(2,1)S(1)}, f32[2,5,8,4,512]{4,3,2,1,0:T(4,128)S(1)}) custom-call(s32[1]{0:T(128)} %bitcast.where_ref, f32[2,5,8,4,512]{4,3,2,1,0:T(4,128)S(1)} %copy-done), custom_call_target="tpu_custom_call" | custom-call | flops 10000000 | bytes 1638400 | tf_op jit(solution)/shard_map/near_faces/pallas_call | solution.py:618
  2.4 3.0 %collective-permute-start = (bf16[5,48,512]{2,1,0:T(8,128)(2,1)S(1)}, bf16[5,48,512]{2,1,0:T(8,128)(2,1)S(1)}, u32[]{:S(2)}, u32[]{:S(2)}) collective-permute-start(bf16[5,48,512]{2,1,0:T(8,128)(2,1)S(1)} %get-tuple-element.27._), channel_id=1, source_target_pairs={{0,1},{1,0},{2,3},{3,2},{4,5},{5,4},{6,7},{7,6},{8,9},{9,8},{10,11... | collective-permute-start | bytes 737288 | tf_op jit(solution)/shard_map/ppermute | solution.py:638
  5.5 0.7 %later_faces.1 = (bf16[5,48,512]{2,1,0:T(8,128)(2,1)S(1)}, f32[2,5,4,4,512]{4,3,2,1,0:T(4,128)S(1)}, f32[2,5,4,4,512]{4,3,2,1,0:T(4,128)S(1)}) custom-call(s32[1]{0:T(128)} %bitcast.where_ref, bf16[5,48,512]{2,1,0:T(8,128)(2,1)S(1)} %get-tuple-element.27._, f32[2,5,8,4,512]{4,3,2,1,0:T(4,128)S(1)} %get-tuple-element.25.windows_ref), custom_call_target="tpu_custom_call" | custom-call | flops 10000000 | bytes 1638400 | tf_op jit(solution)/shard_map/later_faces/pallas_call | solution.py:628
  6.1 3.8 %collective-permute-start.1 = (f32[2,5,4,4,512]{4,3,2,1,0:T(4,128)S(1)}, f32[2,5,4,4,512]{4,3,2,1,0:T(4,128)S(1)}, u32[]{:S(2)}, u32[]{:S(2)}) collective-permute-start(f32[2,5,4,4,512]{4,3,2,1,0:T(4,128)S(1)} %get-tuple-element.28), channel_id=1, source_target_pairs={{2,0},{4,2},{6,4},{8,6},{10,8},{12,10},{14,12},{16,14},{18,16},{20... | collective-permute-start | bytes 983048 | tf_op jit(solution)/shard_map/ppermute | solution.py:642
  9.9 0.7 %collective-permute-start.3 = (bf16[5,48,512]{2,1,0:T(8,128)(2,1)S(1)}, bf16[5,48,512]{2,1,0:T(8,128)(2,1)S(1)}, u32[]{:S(2)}, u32[]{:S(2)}) collective-permute-start(bf16[5,48,512]{2,1,0:T(8,128)(2,1)S(1)} %get-tuple-element.34), channel_id=1, source_target_pairs={{0,1},{1,0},{2,3},{3,2},{4,5},{5,4},{6,7},{7,6},{8,9},{9,8},{10,11... | collective-permute-start | bytes 737288 | tf_op jit(solution)/shard_map/ppermute | solution.py:644
  10.6 5.5 %inner_gram.1 = (f32[2,5,8,4,512]{4,3,2,1,0:T(4,128)S(1)}, f32[512,256]{1,0:T(8,128)S(1)}, f32[256,256]{1,0:T(8,128)S(1)}, bf16[64,20,8,512]{3,2,1,0:T(8,128)(2,1)S(1)}) custom-call(f32[2,5,8,4,512]{4,3,2,1,0:T(4,128)S(1)} %get-tuple-element.25.windows_ref, bf16[64,20,8,512]{3,2,1,0:T(8,128)(2,1)} %bitcast.3), custom_call_target="tpu_custom_call" | custom-call | flops 1000000 | bytes 163840 | tf_op jit(solution)/shard_map/inner_gram/pallas_call | solution.py:667
  16.2 0.2 wall_join.1.part_ref
  16.4 1.3 %collective-permute-start.4 = (bf16[2,5,16,512]{3,2,1,0:T(8,128)(2,1)S(1)}, bf16[2,5,16,512]{3,2,1,0:T(8,128)(2,1)S(1)}, u32[]{:S(2)}, u32[]{:S(2)}) collective-permute-start(bf16[2,5,16,512]{3,2,1,0:T(8,128)(2,1)S(1)} %get-tuple-element.29._), channel_id=1, source_target_pairs={{0,1},{1,0},{2,3},{3,2},{4,5},{5,4},{6,7},{7,6},{8,9},{9,8},{10,11... | collective-permute-start | bytes 491528 | tf_op jit(solution)/shard_map/ppermute | solution.py:722
  17.8 1.3 %collective-permute-done.2.edge_ref = f32[2,5,4,4,512]{4,3,2,1,0:T(4,128)S(1)} collective-permute-done((f32[2,5,4,4,512]{4,3,2,1,0:T(4,128)S(1)}, f32[2,5,4,4,512]{4,3,2,1,0:T(4,128)S(1)}, u32[]{:S(2)}, u32[]{:S(2)}) %collective-permute-start.2) | collective-permute-done | bytes 327712 | tf_op jit(solution)/shard_map/ppermute | solution.py:643
  19.1 3.3 %gram.1._.gram_ref = f32[32,128]{1,0:T(8,128)S(1)} custom-call(f32[2,5,4,4,512]{4,3,2,1,0:T(4,128)S(1)} %own_edge.1._.part_ref, f32[512,256]{1,0:T(8,128)S(1)} %get-tuple-element.31.right_ref, f32[256,256]{1,0:T(8,128)S(1)} %get-tuple-element.32.left_ref, bf16[64,20,8,512]{3,2,1,0:T(8,128)(2,1)S(1)} %get-tuple-element.33.basis_ref.rest_4_), custom_call_target="tpu_custom_call" | custom-call | flops 2684354560 | bytes 10485760 | tf_op jit(solution)/shard_map/gram/pallas_call | solution.py:687
  22.4 0.2 own_join.1
  22.6 3.0 %project.1 = (f32[8,128]{1,0:T(8,128)S(1)}, bf16[20,16,512]{2,1,0:T(8,128)(2,1)S(1)}, f32[2,5,8,4,512]{4,3,2,1,0:T(4,128)}) custom-call(s32[1]{0:T(128)} %bitcast.where_ref, bf16[2,5,16,512]{3,2,1,0:T(8,128)(2,1)S(1)} %get-tuple-element.35.rest_0_, bf16[2,5,16,512]{3,2,1,0:T(8,128)(2,1)S(1)} %collective-permute-done.4.rest_1_, ...), custom_call_target="tpu_custom_call" | custom-call | flops 167772160 | bytes 10485760 | tf_op jit(solution)/shard_map/project/pallas_call | solution.py:763
  25.7 0.5 collective-permute-done.5.far_ref
  26.1 0.1 collective-permute-start.6
  26.2 3.7 %collective-permute-done.6 = f32[40,128]{1,0:T(8,128)S(1)} collective-permute-done((f32[40,128]{1,0:T(8,128)S(1)}, f32[40,128]{1,0:T(8,128)S(1)}, u32[]{:S(2)}, u32[]{:S(2)}) %collective-permute-start.6) | collective-permute-done | bytes 20512 | tf_op jit(solution)/shard_map/ppermute | solution.py:586
  29.9 1.2 %collective-permute-done.7 = f32[40,128]{1,0:T(8,128)S(1)} collective-permute-done((f32[40,128]{1,0:T(8,128)S(1)}, f32[40,128]{1,0:T(8,128)S(1)}, u32[]{:S(2)}, u32[]{:S(2)}) %collective-permute-start.7) | collective-permute-done | bytes 20512 | tf_op jit(solution)/shard_map/ppermute | solution.py:586
  31.1 0.5 %collective-permute-start.8 = (f32[40,128]{1,0:T(8,128)S(1)}, f32[40,128]{1,0:T(8,128)S(1)}, u32[]{:S(2)}, u32[]{:S(2)}) collective-permute-start(f32[40,128]{1,0:T(8,128)S(1)} %add.16), channel_id=1, source_target_pairs={{0,8},{2,10},{4,12},{6,14},{8,0},{10,2},{12,4},{14,6},{16,24},{18,... | collective-permute-start | bytes 61448 | tf_op jit(solution)/shard_map/ppermute | solution.py:586
  31.7 3.2 %collective-permute-done.8 = f32[40,128]{1,0:T(8,128)S(1)} collective-permute-done((f32[40,128]{1,0:T(8,128)S(1)}, f32[40,128]{1,0:T(8,128)S(1)}, u32[]{:S(2)}, u32[]{:S(2)}) %collective-permute-start.8) | collective-permute-done | bytes 20512 | tf_op jit(solution)/shard_map/ppermute | solution.py:586
  34.9 1.6 %collective-permute-start.9 = (f32[40,128]{1,0:T(8,128)S(1)}, f32[40,128]{1,0:T(8,128)S(1)}, u32[]{:S(2)}, u32[]{:S(2)}) collective-permute-start(f32[40,128]{1,0:T(8,128)S(1)} %add.17), channel_id=1, source_target_pairs={{0,16},{2,18},{4,20},{6,22},{8,24},{10,26},{12,28},{14,30},{16,0},... | collective-permute-start | bytes 61448 | tf_op jit(solution)/shard_map/ppermute | solution.py:586
  36.5 3.3 %collective-permute-done.9 = f32[40,128]{1,0:T(8,128)S(1)} collective-permute-done((f32[40,128]{1,0:T(8,128)S(1)}, f32[40,128]{1,0:T(8,128)S(1)}, u32[]{:S(2)}, u32[]{:S(2)}) %collective-permute-start.9) | collective-permute-done | bytes 20512 | tf_op jit(solution)/shard_map/ppermute | solution.py:586
  39.8 1.4 %collective-permute-start.10 = (f32[40,128]{1,0:T(8,128)S(1)}, f32[40,128]{1,0:T(8,128)S(1)}, u32[]{:S(2)}, u32[]{:S(2)}) collective-permute-start(f32[40,128]{1,0:T(8,128)S(1)} %add.18.sums_ref), channel_id=1, source_target_pairs={{0,4},{2,6},{4,0},{6,2},{8,12},{10,14},{12,8},{14,10},{16,20},{18,... | collective-permute-start | bytes 61448 | tf_op jit(solution)/shard_map/ppermute | solution.py:586
  41.2 2.4 %inverse.1 = (f32[64,64]{1,0:T(8,128)S(1)}, f32[64,512]{1,0:T(8,128)S(1)}) custom-call(f32[40,128]{1,0:T(8,128)S(1)} %add.18.sums_ref), custom_call_target="tpu_custom_call" | custom-call | flops 20000000 | bytes 32768 | tf_op jit(solution)/shard_map/inverse/pallas_call | solution.py:802
  43.6 3.2 %finish.1 = (f32[2,20,8,512]{3,2,1,0:T(8,128)}, f32[2,64]{1,0:T(2,128)}, f32[2,2]{1,0:T(2,128)}) custom-call(f32[40,128]{1,0:T(8,128)S(1)} %add.19.projected_ref, f32[40,128]{1,0:T(8,128)S(1)} %add.18.sums_ref, f32[64,64]{1,0:T(8,128)S(1)} %get-tuple-element.40.inverse_ref, f32[64,512]{1,0:T(8,128)S(1)} %get-tuple-element.41.spread_ref, ...), custom_call_target="tpu_custom_call" | custom-call | flops 335544320 | bytes 11796480 | tf_op jit(solution)/shard_map/finish/pallas_call | solution.py:815
  (17 shorter events, 0.1 us)
Async XLA Ops:
  0.6 1.1 %copy-start = (f32[2,5,8,4,512]{4,3,2,1,0:T(4,128)S(1)}, f32[2,5,8,4,512]{4,3,2,1,0:T(4,128)}, u32[]{:S(2)}) copy-start(f32[2,5,8,4,512]{4,3,2,1,0:T(4,128)} %source_ref.1) | copy-start | bytes 1966084
  2.4 13.7 %collective-permute-start = (bf16[5,48,512]{2,1,0:T(8,128)(2,1)S(1)}, bf16[5,48,512]{2,1,0:T(8,128)(2,1)S(1)}, u32[]{:S(2)}, u32[]{:S(2)}) collective-permute-start(bf16[5,48,512]{2,1,0:T(8,128)(2,1)S(1)} %get-tuple-element.27._), channel_id=1, source_target_pairs={{0,1},{1,0},{2,3},{3,2},{4,5},{5,4},{6,7},{7,6},{8,9},{9,8},{10,11... | collective-permute-start | bytes 737288 | tf_op jit(solution)/shard_map/ppermute | solution.py:638
  6.1 10.2 %collective-permute-start.1 = (f32[2,5,4,4,512]{4,3,2,1,0:T(4,128)S(1)}, f32[2,5,4,4,512]{4,3,2,1,0:T(4,128)S(1)}, u32[]{:S(2)}, u32[]{:S(2)}) collective-permute-start(f32[2,5,4,4,512]{4,3,2,1,0:T(4,128)S(1)} %get-tuple-element.28), channel_id=1, source_target_pairs={{2,0},{4,2},{6,4},{8,6},{10,8},{12,10},{14,12},{16,14},{18,16},{20... | collective-permute-start | bytes 983048 | tf_op jit(solution)/shard_map/ppermute | solution.py:642
  9.9 9.2 %collective-permute-start.2 = (f32[2,5,4,4,512]{4,3,2,1,0:T(4,128)S(1)}, f32[2,5,4,4,512]{4,3,2,1,0:T(4,128)S(1)}, u32[]{:S(2)}, u32[]{:S(2)}) collective-permute-start(f32[2,5,4,4,512]{4,3,2,1,0:T(4,128)S(1)} %get-tuple-element.30), channel_id=1, source_target_pairs={{0,2},{2,4},{4,6},{6,8},{8,10},{10,12},{12,14},{14,16},{16,18},{18... | collective-permute-start | bytes 983048 | tf_op jit(solution)/shard_map/ppermute | solution.py:643
  9.9 12.5 %collective-permute-start.3 = (bf16[5,48,512]{2,1,0:T(8,128)(2,1)S(1)}, bf16[5,48,512]{2,1,0:T(8,128)(2,1)S(1)}, u32[]{:S(2)}, u32[]{:S(2)}) collective-permute-start(bf16[5,48,512]{2,1,0:T(8,128)(2,1)S(1)} %get-tuple-element.34), channel_id=1, source_target_pairs={{0,1},{1,0},{2,3},{3,2},{4,5},{5,4},{6,7},{7,6},{8,9},{9,8},{10,11... | collective-permute-start | bytes 737288 | tf_op jit(solution)/shard_map/ppermute | solution.py:644
  16.4 6.2 %collective-permute-start.4 = (bf16[2,5,16,512]{3,2,1,0:T(8,128)(2,1)S(1)}, bf16[2,5,16,512]{3,2,1,0:T(8,128)(2,1)S(1)}, u32[]{:S(2)}, u32[]{:S(2)}) collective-permute-start(bf16[2,5,16,512]{3,2,1,0:T(8,128)(2,1)S(1)} %get-tuple-element.29._), channel_id=1, source_target_pairs={{0,1},{1,0},{2,3},{3,2},{4,5},{5,4},{6,7},{7,6},{8,9},{9,8},{10,11... | collective-permute-start | bytes 491528 | tf_op jit(solution)/shard_map/ppermute | solution.py:722
  22.4 3.7 %collective-permute-start.5 = (f32[32,128]{1,0:T(8,128)S(1)}, f32[32,128]{1,0:T(8,128)S(1)}, u32[]{:S(2)}, u32[]{:S(2)}) collective-permute-start(f32[32,128]{1,0:T(8,128)S(1)} %gram.1._.gram_ref), channel_id=1, source_target_pairs={{0,4},{2,6},{4,0},{6,2},{8,12},{10,14},{12,8},{14,10},{16,20},{18,... | collective-permute-start | bytes 49160 | tf_op jit(solution)/shard_map/ppermute | solution.py:746
  26.1 3.8 %collective-permute-start.6 = (f32[40,128]{1,0:T(8,128)S(1)}, f32[40,128]{1,0:T(8,128)S(1)}, u32[]{:S(2)}, u32[]{:S(2)}) collective-permute-start(f32[40,128]{1,0:T(8,128)S(1)} %merge.1), channel_id=1, source_target_pairs={{0,1},{1,0},{2,3},{3,2},{4,5},{5,4},{6,7},{7,6},{8,9},{9,8},{10,11... | collective-permute-start | bytes 61448 | tf_op jit(solution)/shard_map/ppermute | solution.py:586
  29.9 1.2 %collective-permute-start.7 = (f32[40,128]{1,0:T(8,128)S(1)}, f32[40,128]{1,0:T(8,128)S(1)}, u32[]{:S(2)}, u32[]{:S(2)}) collective-permute-start(f32[40,128]{1,0:T(8,128)S(1)} %add.15), channel_id=1, source_target_pairs={{0,2},{2,0},{4,6},{6,4},{8,10},{10,8},{12,14},{14,12},{16,18},{18,... | collective-permute-start | bytes 61448 | tf_op jit(solution)/shard_map/ppermute | solution.py:586
  31.1 3.8 %collective-permute-start.8 = (f32[40,128]{1,0:T(8,128)S(1)}, f32[40,128]{1,0:T(8,128)S(1)}, u32[]{:S(2)}, u32[]{:S(2)}) collective-permute-start(f32[40,128]{1,0:T(8,128)S(1)} %add.16), channel_id=1, source_target_pairs={{0,8},{2,10},{4,12},{6,14},{8,0},{10,2},{12,4},{14,6},{16,24},{18,... | collective-permute-start | bytes 61448 | tf_op jit(solution)/shard_map/ppermute | solution.py:586
  34.9 4.9 %collective-permute-start.9 = (f32[40,128]{1,0:T(8,128)S(1)}, f32[40,128]{1,0:T(8,128)S(1)}, u32[]{:S(2)}, u32[]{:S(2)}) collective-permute-start(f32[40,128]{1,0:T(8,128)S(1)} %add.17), channel_id=1, source_target_pairs={{0,16},{2,18},{4,20},{6,22},{8,24},{10,26},{12,28},{14,30},{16,0},... | collective-permute-start | bytes 61448 | tf_op jit(solution)/shard_map/ppermute | solution.py:586
  39.8 3.8 %collective-permute-start.10 = (f32[40,128]{1,0:T(8,128)S(1)}, f32[40,128]{1,0:T(8,128)S(1)}, u32[]{:S(2)}, u32[]{:S(2)}) collective-permute-start(f32[40,128]{1,0:T(8,128)S(1)} %add.18.sums_ref), channel_id=1, source_target_pairs={{0,4},{2,6},{4,0},{6,2},{8,12},{10,14},{12,8},{14,10},{16,20},{18,... | collective-permute-start | bytes 61448 | tf_op jit(solution)/shard_map/ppermute | solution.py:586

commit v14 on v12

--- a/solution.py
+++ b/solution.py
@@ -146,7 +146,10 @@
     copy.wait()
 
 
-def later_kernel(where_ref, _, windows_ref, group_ref, first_ref, second_ref, scratch, lows):
+def later_kernel(
+    where_ref, _, windows_ref, group_ref, first_ref, second_ref, scratch, lows,
+    edge_lows,
+):
     windows, _, planes, layers, cells = windows_ref.shape
     half = planes // 2
 
@@ -161,19 +164,30 @@
             plane = half * where_ref[0] + x
             keep_x(w, plane, primitives([windows_ref[w, f, plane] for f in range(5)]))
         for f in range(5):
-            for i in range(REACH):
-                sides = []
-                for offset in (-planes, REACH):
+            last, after = [], []
+            for made, offset in ((after, -planes), (last, REACH)):
+                for i in range(REACH):
                     total = None
                     for j in range(planes):
                         c = weight(j + offset - i)
                         if c:
                             term = c * scratch[w, f, j]
                             total = term if total is None else total + term
-                    sides.append(total)
-                to_next, to_last = sides
-                first_ref[w, f, i] = jnp.where(where_ref[0] == 0, to_last, to_next)
-                second_ref[w, f, i] = jnp.where(where_ref[0] == 0, to_next, to_last)
+                    made.append(total)
+            zeroth = where_ref[0] == 0
+            for k, (ref, high) in enumerate(((first_ref, zeroth), (second_ref, where_ref[0] == 1))):
+                both = [
+                    jnp.where(high, x, y) for x, y in zip(last, after)
+                ]
+                upper = [x.astype(jnp.bfloat16).astype(jnp.float32) for x in both]
+                rest = [x - y for x, y in zip(both, upper)]
+                ref[f, 16 * w : 16 * w + 16] = jnp.concatenate(upper, axis=0).astype(jnp.bfloat16)
+                edge_lows[k, f, 8 * w : 8 * w + 8] = jnp.concatenate(
+                    [jnp.where(high, rest[2], rest[0]), jnp.where(high, rest[3], rest[1])], axis=0
+                )
+    for k, ref in enumerate((first_ref, second_ref)):
+        for f in range(5):
+            ref[f, 32:48] = edge_lows[k, f].astype(jnp.bfloat16)
 
 
 def inner_part(windows_ref, part_ref, scratch):
@@ -314,13 +328,24 @@
                 given_ref[w, f, x] = part_ref[w, f, base + x] + term
 
 
-def edge_join_kernel(part_ref, edge_ref, made, snaps_ref):
-    windows, _, half = part_ref.shape[:3]
+def edge_terms_of(high, edge_ref, w, f):
+    upper = edge_ref[f, 16 * w : 16 * w + 16].astype(jnp.float32)
+    lower = edge_ref[f, 32:48].astype(jnp.float32)[8 * w : 8 * w + 8]
+    made = []
+    for x in range(4):
+        rest = lower[4 * (x % 2) : 4 * (x % 2) + 4]
+        rest = jnp.where(high, rest, 0.0) if x > 1 else jnp.where(high, 0.0, rest)
+        made.append(upper[4 * x : 4 * x + 4] + rest)
+    return made
+
+
+def edge_join_kernel(where_ref, part_ref, edge_ref, made, snaps_ref):
+    windows = part_ref.shape[0]
     for w in range(windows):
         for f in range(5):
             done = []
-            for x in range(half):
-                total = part_ref[w, f, x] + edge_ref[w, f, x]
+            for x, term in enumerate(edge_terms_of(where_ref[0] == 0, edge_ref, w, f)):
+                total = part_ref[w, f, x] + term
                 made[w, f, x] = total
                 done.append(total)
             snaps_ref[w, f] = jnp.concatenate(done, axis=0).astype(jnp.bfloat16)
@@ -332,8 +357,9 @@
     for w in range(windows):
         for f in range(5):
             done = []
+            edges = edge_terms_of(where_ref[0] == 1, edge_ref, w, f)
             for x, term in enumerate(wall_terms_of(where_ref[0] == 0, group_ref, w, f)):
-                total = part_ref[w, f, base + x] + term + edge_ref[w, f, x]
+                total = part_ref[w, f, base + x] + term + edges[x]
                 made[w, f, x] = total
                 done.append(total)
             snaps_ref[w, f] = jnp.concatenate(done, axis=0).astype(jnp.bfloat16)
@@ -620,10 +646,14 @@
         )(place, windows)
         later_group, first_edge, second_edge = pl.pallas_call(
             later_kernel,
-            out_shape=[group_shape] + [edge_shape] * 2,
+            out_shape=[group_shape] * 3,
             in_specs=[SCALAR, LOOSE, WHOLE],
             out_specs=[WHOLE] * 3,
-            scratch_shapes=[pltpu.VMEM((count, fields, planes, layers, cells), f32), lows],
+            scratch_shapes=[
+                pltpu.VMEM((count, fields, planes, layers, cells), f32),
+                lows,
+                pltpu.VMEM((2, fields, 16, cells), f32),
+            ],
             compiler_params=params(16),
             cost_estimate=face_cost,
             name="later_faces",
@@ -706,12 +736,12 @@
         next_given, given = pl.pallas_call(
             edge_join_kernel,
             out_shape=[half_next, shape(half_shape, bf16)],
-            in_specs=[WHOLE] * 2,
+            in_specs=[SCALAR] + [WHOLE] * 2,
             out_specs=[WHOLE] * 2,
             compiler_params=params(16),
             cost_estimate=join_cost,
             name="edge_join",
-        )(inner_given, first_edge)
+        )(place, inner_given, first_edge)
         got = lax.ppermute(given, "analysis", swap)
         gram = rest_of_gram(given)
     else:

time: 46.4 us -> 46 us (level)
  starting transfers between devices: 15.2 us -> 13.8 us
  waiting for transfers between devices: 9.95 us -> 10.7 us
    ppermute x1, starting transfers between devices: 2.77 us -> 1.35 us  [body(): got = lax.ppermute(given, 'analysis', swap)]
    ppermute x5, waiting for transfers between devices: 9.24 us -> 10.2 us  [swap_added(): lax.ppermute(value, axis, [(i, i ^ bit) for i in range(count)])]
    ppermute x5, starting transfers between devices: 5.66 us -> 4.9 us  [swap_added(): lax.ppermute(value, axis, [(i, i ^ bit) for i in range(count)])]
    ppermute x1, starting transfers between devices: 0.01 us -> 0.74 us  [body(): later_group = lax.ppermute(later_group, 'analysis', swap)]
  transfers between devices with their start and end apart: 11 -> 11, of which waited for: 6 -> 6; matrix products, arithmetic and copies ran while one was open for 0% -> 0% of each run, Pallas kernels for 33% -> 34%
where the time goes in v14:
time: 46 us; the launch traced here: 45.9 us
  Pallas kernels  19.5 us (42%)
  starting transfers between devices  13.8 us (30%)
  waiting for transfers between devices  10.7 us (23%)
  local copies, waits for them, and re-layouts  1.08 us (2%)
  between operations  0.77 us (2%)
    ppermute x5, waiting for transfers between devices, swap_added(): lax.ppermute(value, axis, [(i, i ^ bit) for i in range(count)])  10.2 us
    pallas_call x1, Pallas kernels, body(): pl.pallas_call(functools.partial(inner_gram_kernel, early), out_shape=[sh...  5.53 us
    ppermute x5, starting transfers between devices, swap_added(): lax.ppermute(value, axis, [(i, i ^ bit) for i in range(count)])  4.9 us
    ppermute x1, starting transfers between devices, body(): lax.ppermute(first_edge, ('solver', 'analysis'), down + odd(up))  3.77 us
    pallas_call x1, Pallas kernels, rest_of_gram(): pl.pallas_call(functools.partial(gram_kernel, early, fields), out_shape=s...  3.25 us
    pallas_call x1, Pallas kernels, body(): pl.pallas_call(functools.partial(finish_kernel, rows_total), out_shape=[s...  3.18 us
    pallas_call x1, Pallas kernels, body(): pl.pallas_call(functools.partial(project_kernel, True), out_shape=[sums_s...  3.04 us
    ppermute x1, starting transfers between devices, body(): near_group = lax.ppermute(near_group, 'analysis', swap)  3 us
  transfers between devices with their start and end apart: 11, of which 6 were waited for; matrix products, arithmetic and copies ran while one was open for 0% of the time, Pallas kernels for 34%

profile of v14, /device:TPU:0, one launch (start us, length us, event | category | flops | bytes accessed | tf_op | source)
XLA Modules:
  0.0 45.9 jit_solution(6112846951990978703)
XLA Ops:
  0.6 1.1 %copy-done = f32[2,5,8,4,512]{4,3,2,1,0:T(4,128)S(1)} copy-done((f32[2,5,8,4,512]{4,3,2,1,0:T(4,128)S(1)}, f32[2,5,8,4,512]{4,3,2,1,0:T(4,128)}, u32[]{:S(2)}) %copy-start) | copy-done | bytes 655384
  1.7 0.7 %near_faces.1 = (bf16[5,48,512]{2,1,0:T(8,128)(2,1)S(1)}, f32[2,5,8,4,512]{4,3,2,1,0:T(4,128)S(1)}) custom-call(s32[1]{0:T(128)} %bitcast.where_ref, f32[2,5,8,4,512]{4,3,2,1,0:T(4,128)S(1)} %copy-done), custom_call_target="tpu_custom_call" | custom-call | flops 10000000 | bytes 1638400 | tf_op jit(solution)/shard_map/near_faces/pallas_call | solution.py:637
  2.4 3.0 %collective-permute-start = (bf16[5,48,512]{2,1,0:T(8,128)(2,1)S(1)}, bf16[5,48,512]{2,1,0:T(8,128)(2,1)S(1)}, u32[]{:S(2)}, u32[]{:S(2)}) collective-permute-start(bf16[5,48,512]{2,1,0:T(8,128)(2,1)S(1)} %get-tuple-element.27._), channel_id=1, source_target_pairs={{0,1},{1,0},{2,3},{3,2},{4,5},{5,4},{6,7},{7,6},{8,9},{9,8},{10,11... | collective-permute-start | bytes 737288 | tf_op jit(solution)/shard_map/ppermute | solution.py:661
  5.5 0.9 %later_faces.1 = (bf16[5,48,512]{2,1,0:T(8,128)(2,1)S(1)}, bf16[5,48,512]{2,1,0:T(8,128)(2,1)S(1)}, bf16[5,48,512]{2,1,0:T(8,128)(2,1)S(1)}) custom-call(s32[1]{0:T(128)} %bitcast.where_ref, bf16[5,48,512]{2,1,0:T(8,128)(2,1)S(1)} %get-tuple-element.27._, f32[2,5,8,4,512]{4,3,2,1,0:T(4,128)S(1)} %get-tuple-element.25.windows_ref), custom_call_target="tpu_custom_call" | custom-call | flops 10000000 | bytes 1638400 | tf_op jit(solution)/shard_map/later_faces/pallas_call | solution.py:647
  6.4 3.8 %collective-permute-start.1 = (bf16[5,48,512]{2,1,0:T(8,128)(2,1)S(1)}, bf16[5,48,512]{2,1,0:T(8,128)(2,1)S(1)}, u32[]{:S(2)}, u32[]{:S(2)}) collective-permute-start(bf16[5,48,512]{2,1,0:T(8,128)(2,1)S(1)} %get-tuple-element.28), channel_id=1, source_target_pairs={{2,0},{4,2},{6,4},{8,6},{10,8},{12,10},{14,12},{16,14},{18,16},{20... | collective-permute-start | bytes 737288 | tf_op jit(solution)/shard_map/ppermute | solution.py:665
  10.1 0.7 %collective-permute-start.3 = (bf16[5,48,512]{2,1,0:T(8,128)(2,1)S(1)}, bf16[5,48,512]{2,1,0:T(8,128)(2,1)S(1)}, u32[]{:S(2)}, u32[]{:S(2)}) collective-permute-start(bf16[5,48,512]{2,1,0:T(8,128)(2,1)S(1)} %get-tuple-element.34), channel_id=1, source_target_pairs={{0,1},{1,0},{2,3},{3,2},{4,5},{5,4},{6,7},{7,6},{8,9},{9,8},{10,11... | collective-permute-start | bytes 737288 | tf_op jit(solution)/shard_map/ppermute | solution.py:667
  10.9 5.5 %inner_gram.1 = (f32[2,5,8,4,512]{4,3,2,1,0:T(4,128)S(1)}, f32[512,256]{1,0:T(8,128)S(1)}, f32[256,256]{1,0:T(8,128)S(1)}, bf16[64,20,8,512]{3,2,1,0:T(8,128)(2,1)S(1)}) custom-call(f32[2,5,8,4,512]{4,3,2,1,0:T(4,128)S(1)} %get-tuple-element.25.windows_ref, bf16[64,20,8,512]{3,2,1,0:T(8,128)(2,1)} %bitcast.3), custom_call_target="tpu_custom_call" | custom-call | flops 1000000 | bytes 163840 | tf_op jit(solution)/shard_map/inner_gram/pallas_call | solution.py:690
  16.4 0.2 wall_join.1.part_ref
  16.7 1.4 %collective-permute-start.4 = (bf16[2,5,16,512]{3,2,1,0:T(8,128)(2,1)S(1)}, bf16[2,5,16,512]{3,2,1,0:T(8,128)(2,1)S(1)}, u32[]{:S(2)}, u32[]{:S(2)}) collective-permute-start(bf16[2,5,16,512]{3,2,1,0:T(8,128)(2,1)S(1)} %get-tuple-element.29._), channel_id=1, source_target_pairs={{0,1},{1,0},{2,3},{3,2},{4,5},{5,4},{6,7},{7,6},{8,9},{9,8},{10,11... | collective-permute-start | bytes 491528 | tf_op jit(solution)/shard_map/ppermute | solution.py:745
  18.1 3.2 %gram.1._.gram_ref = f32[32,128]{1,0:T(8,128)S(1)} custom-call(bf16[2,5,16,512]{3,2,1,0:T(8,128)(2,1)S(1)} %get-tuple-element.29._, f32[512,256]{1,0:T(8,128)S(1)} %get-tuple-element.30.right_ref, f32[256,256]{1,0:T(8,128)S(1)} %get-tuple-element.31.left_ref, bf16[64,20,8,512]{3,2,1,0:T(8,128)(2,1)S(1)} %get-tuple-element.32.basis_ref.rest_4_), custom_call_target="tpu_custom_call" | custom-call | flops 2684354560 | bytes 10485760 | tf_op jit(solution)/shard_map/gram/pallas_call | solution.py:710
  21.4 0.2 own_join.1
  21.6 0.5 %collective-permute-done.4.rest_1_ = bf16[2,5,16,512]{3,2,1,0:T(8,128)(2,1)S(1)} collective-permute-done((bf16[2,5,16,512]{3,2,1,0:T(8,128)(2,1)S(1)}, bf16[2,5,16,512]{3,2,1,0:T(8,128)(2,1)S(1)}, u32[]{:S(2)}, u32[]{:S(2)}) %collective-permute-start.4) | collective-permute-done | bytes 163872 | tf_op jit(solution)/shard_map/ppermute | solution.py:745
  22.1 3.0 %project.1 = (f32[8,128]{1,0:T(8,128)S(1)}, bf16[20,16,512]{2,1,0:T(8,128)(2,1)S(1)}, f32[2,5,8,4,512]{4,3,2,1,0:T(4,128)}) custom-call(s32[1]{0:T(128)} %bitcast.where_ref, bf16[2,5,16,512]{3,2,1,0:T(8,128)(2,1)S(1)} %get-tuple-element.35.rest_0_, bf16[2,5,16,512]{3,2,1,0:T(8,128)(2,1)S(1)} %collective-permute-done.4.rest_1_, ...), custom_call_target="tpu_custom_call" | custom-call | flops 167772160 | bytes 10485760 | tf_op jit(solution)/shard_map/project/pallas_call | solution.py:777
  25.2 1.4 %collective-permute-start.6 = (f32[40,128]{1,0:T(8,128)S(1)}, f32[40,128]{1,0:T(8,128)S(1)}, u32[]{:S(2)}, u32[]{:S(2)}) collective-permute-start(f32[40,128]{1,0:T(8,128)S(1)} %merge.1), channel_id=1, source_target_pairs={{0,1},{1,0},{2,3},{3,2},{4,5},{5,4},{6,7},{7,6},{8,9},{9,8},{10,11... | collective-permute-start | bytes 61448 | tf_op jit(solution)/shard_map/ppermute | solution.py:605
  26.5 2.5 %collective-permute-done.6 = f32[40,128]{1,0:T(8,128)S(1)} collective-permute-done((f32[40,128]{1,0:T(8,128)S(1)}, f32[40,128]{1,0:T(8,128)S(1)}, u32[]{:S(2)}, u32[]{:S(2)}) %collective-permute-start.6) | collective-permute-done | bytes 20512 | tf_op jit(solution)/shard_map/ppermute | solution.py:605
  29.0 1.2 %collective-permute-done.7 = f32[40,128]{1,0:T(8,128)S(1)} collective-permute-done((f32[40,128]{1,0:T(8,128)S(1)}, f32[40,128]{1,0:T(8,128)S(1)}, u32[]{:S(2)}, u32[]{:S(2)}) %collective-permute-start.7) | collective-permute-done | bytes 20512 | tf_op jit(solution)/shard_map/ppermute | solution.py:605
  30.2 0.6 %collective-permute-start.8 = (f32[40,128]{1,0:T(8,128)S(1)}, f32[40,128]{1,0:T(8,128)S(1)}, u32[]{:S(2)}, u32[]{:S(2)}) collective-permute-start(f32[40,128]{1,0:T(8,128)S(1)} %add.16), channel_id=1, source_target_pairs={{0,8},{2,10},{4,12},{6,14},{8,0},{10,2},{12,4},{14,6},{16,24},{18,... | collective-permute-start | bytes 61448 | tf_op jit(solution)/shard_map/ppermute | solution.py:605
  30.8 3.2 %collective-permute-done.8 = f32[40,128]{1,0:T(8,128)S(1)} collective-permute-done((f32[40,128]{1,0:T(8,128)S(1)}, f32[40,128]{1,0:T(8,128)S(1)}, u32[]{:S(2)}, u32[]{:S(2)}) %collective-permute-start.8) | collective-permute-done | bytes 20512 | tf_op jit(solution)/shard_map/ppermute | solution.py:605
  34.0 1.6 %collective-permute-start.9 = (f32[40,128]{1,0:T(8,128)S(1)}, f32[40,128]{1,0:T(8,128)S(1)}, u32[]{:S(2)}, u32[]{:S(2)}) collective-permute-start(f32[40,128]{1,0:T(8,128)S(1)} %add.17), channel_id=1, source_target_pairs={{0,16},{2,18},{4,20},{6,22},{8,24},{10,26},{12,28},{14,30},{16,0},... | collective-permute-start | bytes 61448 | tf_op jit(solution)/shard_map/ppermute | solution.py:605
  35.6 3.3 %collective-permute-done.9 = f32[40,128]{1,0:T(8,128)S(1)} collective-permute-done((f32[40,128]{1,0:T(8,128)S(1)}, f32[40,128]{1,0:T(8,128)S(1)}, u32[]{:S(2)}, u32[]{:S(2)}) %collective-permute-start.9) | collective-permute-done | bytes 20512 | tf_op jit(solution)/shard_map/ppermute | solution.py:605
  38.9 1.3 %collective-permute-start.10 = (f32[40,128]{1,0:T(8,128)S(1)}, f32[40,128]{1,0:T(8,128)S(1)}, u32[]{:S(2)}, u32[]{:S(2)}) collective-permute-start(f32[40,128]{1,0:T(8,128)S(1)} %add.18.sums_ref), channel_id=1, source_target_pairs={{0,4},{2,6},{4,0},{6,2},{8,12},{10,14},{12,8},{14,10},{16,20},{18,... | collective-permute-start | bytes 61448 | tf_op jit(solution)/shard_map/ppermute | solution.py:605
  40.2 2.4 %inverse.1 = (f32[64,64]{1,0:T(8,128)S(1)}, f32[64,512]{1,0:T(8,128)S(1)}) custom-call(f32[40,128]{1,0:T(8,128)S(1)} %add.18.sums_ref), custom_call_target="tpu_custom_call" | custom-call | flops 20000000 | bytes 32768 | tf_op jit(solution)/shard_map/inverse/pallas_call | solution.py:816
  42.6 0.1 collective-permute-done.10
  42.7 3.2 %finish.1 = (f32[2,20,8,512]{3,2,1,0:T(8,128)}, f32[2,64]{1,0:T(2,128)}, f32[2,2]{1,0:T(2,128)}) custom-call(f32[40,128]{1,0:T(8,128)S(1)} %add.19.projected_ref, f32[40,128]{1,0:T(8,128)S(1)} %add.18.sums_ref, f32[64,64]{1,0:T(8,128)S(1)} %get-tuple-element.40.inverse_ref, f32[64,512]{1,0:T(8,128)S(1)} %get-tuple-element.41.spread_ref, ...), custom_call_target="tpu_custom_call" | custom-call | flops 335544320 | bytes 11796480 | tf_op jit(solution)/shard_map/finish/pallas_call | solution.py:829
  (16 shorter events, 0.2 us)
Async XLA Ops:
  0.6 1.1 %copy-start = (f32[2,5,8,4,512]{4,3,2,1,0:T(4,128)S(1)}, f32[2,5,8,4,512]{4,3,2,1,0:T(4,128)}, u32[]{:S(2)}) copy-start(f32[2,5,8,4,512]{4,3,2,1,0:T(4,128)} %source_ref.1) | copy-start | bytes 1966084
  2.4 14.0 %collective-permute-start = (bf16[5,48,512]{2,1,0:T(8,128)(2,1)S(1)}, bf16[5,48,512]{2,1,0:T(8,128)(2,1)S(1)}, u32[]{:S(2)}, u32[]{:S(2)}) collective-permute-start(bf16[5,48,512]{2,1,0:T(8,128)(2,1)S(1)} %get-tuple-element.27._), channel_id=1, source_target_pairs={{0,1},{1,0},{2,3},{3,2},{4,5},{5,4},{6,7},{7,6},{8,9},{9,8},{10,11... | collective-permute-start | bytes 737288 | tf_op jit(solution)/shard_map/ppermute | solution.py:661
  6.4 10.2 %collective-permute-start.1 = (bf16[5,48,512]{2,1,0:T(8,128)(2,1)S(1)}, bf16[5,48,512]{2,1,0:T(8,128)(2,1)S(1)}, u32[]{:S(2)}, u32[]{:S(2)}) collective-permute-start(bf16[5,48,512]{2,1,0:T(8,128)(2,1)S(1)} %get-tuple-element.28), channel_id=1, source_target_pairs={{2,0},{4,2},{6,4},{8,6},{10,8},{12,10},{14,12},{16,14},{18,16},{20... | collective-permute-start | bytes 737288 | tf_op jit(solution)/shard_map/ppermute | solution.py:665
  10.1 11.2 %collective-permute-start.2 = (bf16[5,48,512]{2,1,0:T(8,128)(2,1)S(1)}, bf16[5,48,512]{2,1,0:T(8,128)(2,1)S(1)}, u32[]{:S(2)}, u32[]{:S(2)}) collective-permute-start(bf16[5,48,512]{2,1,0:T(8,128)(2,1)S(1)} %get-tuple-element.33), channel_id=1, source_target_pairs={{0,2},{2,4},{4,6},{6,8},{8,10},{10,12},{12,14},{14,16},{16,18},{18... | collective-permute-start | bytes 737288 | tf_op jit(solution)/shard_map/ppermute | solution.py:666
  10.1 11.2 %collective-permute-start.3 = (bf16[5,48,512]{2,1,0:T(8,128)(2,1)S(1)}, bf16[5,48,512]{2,1,0:T(8,128)(2,1)S(1)}, u32[]{:S(2)}, u32[]{:S(2)}) collective-permute-start(bf16[5,48,512]{2,1,0:T(8,128)(2,1)S(1)} %get-tuple-element.34), channel_id=1, source_target_pairs={{0,1},{1,0},{2,3},{3,2},{4,5},{5,4},{6,7},{7,6},{8,9},{9,8},{10,11... | collective-permute-start | bytes 737288 | tf_op jit(solution)/shard_map/ppermute | solution.py:667
  16.7 5.4 %collective-permute-start.4 = (bf16[2,5,16,512]{3,2,1,0:T(8,128)(2,1)S(1)}, bf16[2,5,16,512]{3,2,1,0:T(8,128)(2,1)S(1)}, u32[]{:S(2)}, u32[]{:S(2)}) collective-permute-start(bf16[2,5,16,512]{3,2,1,0:T(8,128)(2,1)S(1)} %get-tuple-element.29._), channel_id=1, source_target_pairs={{0,1},{1,0},{2,3},{3,2},{4,5},{5,4},{6,7},{7,6},{8,9},{9,8},{10,11... | collective-permute-start | bytes 491528 | tf_op jit(solution)/shard_map/ppermute | solution.py:745
  21.3 3.8 %collective-permute-start.5 = (f32[32,128]{1,0:T(8,128)S(1)}, f32[32,128]{1,0:T(8,128)S(1)}, u32[]{:S(2)}, u32[]{:S(2)}) collective-permute-start(f32[32,128]{1,0:T(8,128)S(1)} %gram.1._.gram_ref), channel_id=1, source_target_pairs={{0,4},{2,6},{4,0},{6,2},{8,12},{10,14},{12,8},{14,10},{16,20},{18,... | collective-permute-start | bytes 49160 | tf_op jit(solution)/shard_map/ppermute | solution.py:760
  25.2 3.8 %collective-permute-start.6 = (f32[40,128]{1,0:T(8,128)S(1)}, f32[40,128]{1,0:T(8,128)S(1)}, u32[]{:S(2)}, u32[]{:S(2)}) collective-permute-start(f32[40,128]{1,0:T(8,128)S(1)} %merge.1), channel_id=1, source_target_pairs={{0,1},{1,0},{2,3},{3,2},{4,5},{5,4},{6,7},{7,6},{8,9},{9,8},{10,11... | collective-permute-start | bytes 61448 | tf_op jit(solution)/shard_map/ppermute | solution.py:605
  29.0 1.2 %collective-permute-start.7 = (f32[40,128]{1,0:T(8,128)S(1)}, f32[40,128]{1,0:T(8,128)S(1)}, u32[]{:S(2)}, u32[]{:S(2)}) collective-permute-start(f32[40,128]{1,0:T(8,128)S(1)} %add.15), channel_id=1, source_target_pairs={{0,2},{2,0},{4,6},{6,4},{8,10},{10,8},{12,14},{14,12},{16,18},{18,... | collective-permute-start | bytes 61448 | tf_op jit(solution)/shard_map/ppermute | solution.py:605
  30.2 3.8 %collective-permute-start.8 = (f32[40,128]{1,0:T(8,128)S(1)}, f32[40,128]{1,0:T(8,128)S(1)}, u32[]{:S(2)}, u32[]{:S(2)}) collective-permute-start(f32[40,128]{1,0:T(8,128)S(1)} %add.16), channel_id=1, source_target_pairs={{0,8},{2,10},{4,12},{6,14},{8,0},{10,2},{12,4},{14,6},{16,24},{18,... | collective-permute-start | bytes 61448 | tf_op jit(solution)/shard_map/ppermute | solution.py:605
  34.0 4.9 %collective-permute-start.9 = (f32[40,128]{1,0:T(8,128)S(1)}, f32[40,128]{1,0:T(8,128)S(1)}, u32[]{:S(2)}, u32[]{:S(2)}) collective-permute-start(f32[40,128]{1,0:T(8,128)S(1)} %add.17), channel_id=1, source_target_pairs={{0,16},{2,18},{4,20},{6,22},{8,24},{10,26},{12,28},{14,30},{16,0},... | collective-permute-start | bytes 61448 | tf_op jit(solution)/shard_map/ppermute | solution.py:605
  38.9 3.8 %collective-permute-start.10 = (f32[40,128]{1,0:T(8,128)S(1)}, f32[40,128]{1,0:T(8,128)S(1)}, u32[]{:S(2)}, u32[]{:S(2)}) collective-permute-start(f32[40,128]{1,0:T(8,128)S(1)} %add.18.sums_ref), channel_id=1, source_target_pairs={{0,4},{2,6},{4,0},{6,2},{8,12},{10,14},{12,8},{14,10},{16,20},{18,... | collective-permute-start | bytes 61448 | tf_op jit(solution)/shard_map/ppermute | solution.py:605

commit v15 on v14

--- a/solution.py
+++ b/solution.py
@@ -837,7 +837,7 @@
         out_specs=[FAR, WHOLE, WHOLE],
         scratch_shapes=[
             pltpu.VMEM((count, tiles, 8, cells), f32),
-            pltpu.SemaphoreType.DMA((fields,)),
+            pltpu.SemaphoreType.DMA((2 * fields,)),
         ],
         compiler_params=params(16),
         cost_estimate=cost(2 * wide * 32 * cells * tiles, basis_bytes + 8 * windows.size),

time: 46 us -> 46 us (level)
  no operation moved by 1% of the time
where the time goes in v15:
time: 46 us; the launch traced here: 45.9 us
  Pallas kernels  19.5 us (42%)
  starting transfers between devices  13.8 us (30%)
  waiting for transfers between devices  10.7 us (23%)
  local copies, waits for them, and re-layouts  1.08 us (2%)
  between operations  0.77 us (2%)
    ppermute x5, waiting for transfers between devices, swap_added(): lax.ppermute(value, axis, [(i, i ^ bit) for i in range(count)])  10.2 us
    pallas_call x1, Pallas kernels, body(): pl.pallas_call(functools.partial(inner_gram_kernel, early), out_shape=[sh...  5.53 us
    ppermute x5, starting transfers between devices, swap_added(): lax.ppermute(value, axis, [(i, i ^ bit) for i in range(count)])  4.9 us
    ppermute x1, starting transfers between devices, body(): lax.ppermute(first_edge, ('solver', 'analysis'), down + odd(up))  3.77 us
    pallas_call x1, Pallas kernels, rest_of_gram(): pl.pallas_call(functools.partial(gram_kernel, early, fields), out_shape=s...  3.25 us
    pallas_call x1, Pallas kernels, body(): pl.pallas_call(functools.partial(finish_kernel, rows_total), out_shape=[s...  3.15 us
    pallas_call x1, Pallas kernels, body(): pl.pallas_call(functools.partial(project_kernel, True), out_shape=[sums_s...  3.04 us
    ppermute x1, starting transfers between devices, body(): near_group = lax.ppermute(near_group, 'analysis', swap)  3 us
  transfers between devices with their start and end apart: 11, of which 6 were waited for; matrix products, arithmetic and copies ran while one was open for 0% of the time, Pallas kernels for 34%

profile of v15, /device:TPU:0, one launch (start us, length us, event | category | flops | bytes accessed | tf_op | source)
XLA Modules:
  0.0 45.9 jit_solution(12597537403395212648)
XLA Ops:
  0.6 1.1 %copy-done = f32[2,5,8,4,512]{4,3,2,1,0:T(4,128)S(1)} copy-done((f32[2,5,8,4,512]{4,3,2,1,0:T(4,128)S(1)}, f32[2,5,8,4,512]{4,3,2,1,0:T(4,128)}, u32[]{:S(2)}) %copy-start) | copy-done | bytes 655384
  1.7 0.7 %near_faces.1 = (bf16[5,48,512]{2,1,0:T(8,128)(2,1)S(1)}, f32[2,5,8,4,512]{4,3,2,1,0:T(4,128)S(1)}) custom-call(s32[1]{0:T(128)} %bitcast.where_ref, f32[2,5,8,4,512]{4,3,2,1,0:T(4,128)S(1)} %copy-done), custom_call_target="tpu_custom_call" | custom-call | flops 10000000 | bytes 1638400 | tf_op jit(solution)/shard_map/near_faces/pallas_call | solution.py:637
  2.4 3.0 %collective-permute-start = (bf16[5,48,512]{2,1,0:T(8,128)(2,1)S(1)}, bf16[5,48,512]{2,1,0:T(8,128)(2,1)S(1)}, u32[]{:S(2)}, u32[]{:S(2)}) collective-permute-start(bf16[5,48,512]{2,1,0:T(8,128)(2,1)S(1)} %get-tuple-element.27._), channel_id=1, source_target_pairs={{0,1},{1,0},{2,3},{3,2},{4,5},{5,4},{6,7},{7,6},{8,9},{9,8},{10,11... | collective-permute-start | bytes 737288 | tf_op jit(solution)/shard_map/ppermute | solution.py:661
  5.5 0.9 %later_faces.1 = (bf16[5,48,512]{2,1,0:T(8,128)(2,1)S(1)}, bf16[5,48,512]{2,1,0:T(8,128)(2,1)S(1)}, bf16[5,48,512]{2,1,0:T(8,128)(2,1)S(1)}) custom-call(s32[1]{0:T(128)} %bitcast.where_ref, bf16[5,48,512]{2,1,0:T(8,128)(2,1)S(1)} %get-tuple-element.27._, f32[2,5,8,4,512]{4,3,2,1,0:T(4,128)S(1)} %get-tuple-element.25.windows_ref), custom_call_target="tpu_custom_call" | custom-call | flops 10000000 | bytes 1638400 | tf_op jit(solution)/shard_map/later_faces/pallas_call | solution.py:647
  6.4 3.8 %collective-permute-start.1 = (bf16[5,48,512]{2,1,0:T(8,128)(2,1)S(1)}, bf16[5,48,512]{2,1,0:T(8,128)(2,1)S(1)}, u32[]{:S(2)}, u32[]{:S(2)}) collective-permute-start(bf16[5,48,512]{2,1,0:T(8,128)(2,1)S(1)} %get-tuple-element.28), channel_id=1, source_target_pairs={{2,0},{4,2},{6,4},{8,6},{10,8},{12,10},{14,12},{16,14},{18,16},{20... | collective-permute-start | bytes 737288 | tf_op jit(solution)/shard_map/ppermute | solution.py:665
  10.1 0.7 %collective-permute-start.3 = (bf16[5,48,512]{2,1,0:T(8,128)(2,1)S(1)}, bf16[5,48,512]{2,1,0:T(8,128)(2,1)S(1)}, u32[]{:S(2)}, u32[]{:S(2)}) collective-permute-start(bf16[5,48,512]{2,1,0:T(8,128)(2,1)S(1)} %get-tuple-element.34), channel_id=1, source_target_pairs={{0,1},{1,0},{2,3},{3,2},{4,5},{5,4},{6,7},{7,6},{8,9},{9,8},{10,11... | collective-permute-start | bytes 737288 | tf_op jit(solution)/shard_map/ppermute | solution.py:667
  10.9 5.5 %inner_gram.1 = (f32[2,5,8,4,512]{4,3,2,1,0:T(4,128)S(1)}, f32[512,256]{1,0:T(8,128)S(1)}, f32[256,256]{1,0:T(8,128)S(1)}, bf16[64,20,8,512]{3,2,1,0:T(8,128)(2,1)S(1)}) custom-call(f32[2,5,8,4,512]{4,3,2,1,0:T(4,128)S(1)} %get-tuple-element.25.windows_ref, bf16[64,20,8,512]{3,2,1,0:T(8,128)(2,1)} %bitcast.3), custom_call_target="tpu_custom_call" | custom-call | flops 1000000 | bytes 163840 | tf_op jit(solution)/shard_map/inner_gram/pallas_call | solution.py:690
  16.4 0.2 wall_join.1.part_ref
  16.7 1.4 %collective-permute-start.4 = (bf16[2,5,16,512]{3,2,1,0:T(8,128)(2,1)S(1)}, bf16[2,5,16,512]{3,2,1,0:T(8,128)(2,1)S(1)}, u32[]{:S(2)}, u32[]{:S(2)}) collective-permute-start(bf16[2,5,16,512]{3,2,1,0:T(8,128)(2,1)S(1)} %get-tuple-element.29._), channel_id=1, source_target_pairs={{0,1},{1,0},{2,3},{3,2},{4,5},{5,4},{6,7},{7,6},{8,9},{9,8},{10,11... | collective-permute-start | bytes 491528 | tf_op jit(solution)/shard_map/ppermute | solution.py:745
  18.1 3.2 %gram.1._.gram_ref = f32[32,128]{1,0:T(8,128)S(1)} custom-call(bf16[2,5,16,512]{3,2,1,0:T(8,128)(2,1)S(1)} %get-tuple-element.29._, f32[512,256]{1,0:T(8,128)S(1)} %get-tuple-element.30.right_ref, f32[256,256]{1,0:T(8,128)S(1)} %get-tuple-element.31.left_ref, bf16[64,20,8,512]{3,2,1,0:T(8,128)(2,1)S(1)} %get-tuple-element.32.basis_ref.rest_4_), custom_call_target="tpu_custom_call" | custom-call | flops 2684354560 | bytes 10485760 | tf_op jit(solution)/shard_map/gram/pallas_call | solution.py:710
  21.4 0.2 own_join.1
  21.6 0.5 %collective-permute-done.4.rest_1_ = bf16[2,5,16,512]{3,2,1,0:T(8,128)(2,1)S(1)} collective-permute-done((bf16[2,5,16,512]{3,2,1,0:T(8,128)(2,1)S(1)}, bf16[2,5,16,512]{3,2,1,0:T(8,128)(2,1)S(1)}, u32[]{:S(2)}, u32[]{:S(2)}) %collective-permute-start.4) | collective-permute-done | bytes 163872 | tf_op jit(solution)/shard_map/ppermute | solution.py:745
  22.1 3.0 %project.1 = (f32[8,128]{1,0:T(8,128)S(1)}, bf16[20,16,512]{2,1,0:T(8,128)(2,1)S(1)}, f32[2,5,8,4,512]{4,3,2,1,0:T(4,128)}) custom-call(s32[1]{0:T(128)} %bitcast.where_ref, bf16[2,5,16,512]{3,2,1,0:T(8,128)(2,1)S(1)} %get-tuple-element.35.rest_0_, bf16[2,5,16,512]{3,2,1,0:T(8,128)(2,1)S(1)} %collective-permute-done.4.rest_1_, ...), custom_call_target="tpu_custom_call" | custom-call | flops 167772160 | bytes 10485760 | tf_op jit(solution)/shard_map/project/pallas_call | solution.py:777
  25.2 1.4 %collective-permute-start.6 = (f32[40,128]{1,0:T(8,128)S(1)}, f32[40,128]{1,0:T(8,128)S(1)}, u32[]{:S(2)}, u32[]{:S(2)}) collective-permute-start(f32[40,128]{1,0:T(8,128)S(1)} %merge.1), channel_id=1, source_target_pairs={{0,1},{1,0},{2,3},{3,2},{4,5},{5,4},{6,7},{7,6},{8,9},{9,8},{10,11... | collective-permute-start | bytes 61448 | tf_op jit(solution)/shard_map/ppermute | solution.py:605
  26.5 2.5 %collective-permute-done.6 = f32[40,128]{1,0:T(8,128)S(1)} collective-permute-done((f32[40,128]{1,0:T(8,128)S(1)}, f32[40,128]{1,0:T(8,128)S(1)}, u32[]{:S(2)}, u32[]{:S(2)}) %collective-permute-start.6) | collective-permute-done | bytes 20512 | tf_op jit(solution)/shard_map/ppermute | solution.py:605
  29.0 1.2 %collective-permute-done.7 = f32[40,128]{1,0:T(8,128)S(1)} collective-permute-done((f32[40,128]{1,0:T(8,128)S(1)}, f32[40,128]{1,0:T(8,128)S(1)}, u32[]{:S(2)}, u32[]{:S(2)}) %collective-permute-start.7) | collective-permute-done | bytes 20512 | tf_op jit(solution)/shard_map/ppermute | solution.py:605
  30.2 0.6 %collective-permute-start.8 = (f32[40,128]{1,0:T(8,128)S(1)}, f32[40,128]{1,0:T(8,128)S(1)}, u32[]{:S(2)}, u32[]{:S(2)}) collective-permute-start(f32[40,128]{1,0:T(8,128)S(1)} %add.16), channel_id=1, source_target_pairs={{0,8},{2,10},{4,12},{6,14},{8,0},{10,2},{12,4},{14,6},{16,24},{18,... | collective-permute-start | bytes 61448 | tf_op jit(solution)/shard_map/ppermute | solution.py:605
  30.8 3.2 %collective-permute-done.8 = f32[40,128]{1,0:T(8,128)S(1)} collective-permute-done((f32[40,128]{1,0:T(8,128)S(1)}, f32[40,128]{1,0:T(8,128)S(1)}, u32[]{:S(2)}, u32[]{:S(2)}) %collective-permute-start.8) | collective-permute-done | bytes 20512 | tf_op jit(solution)/shard_map/ppermute | solution.py:605
  34.0 1.6 %collective-permute-start.9 = (f32[40,128]{1,0:T(8,128)S(1)}, f32[40,128]{1,0:T(8,128)S(1)}, u32[]{:S(2)}, u32[]{:S(2)}) collective-permute-start(f32[40,128]{1,0:T(8,128)S(1)} %add.17), channel_id=1, source_target_pairs={{0,16},{2,18},{4,20},{6,22},{8,24},{10,26},{12,28},{14,30},{16,0},... | collective-permute-start | bytes 61448 | tf_op jit(solution)/shard_map/ppermute | solution.py:605
  35.6 3.3 %collective-permute-done.9 = f32[40,128]{1,0:T(8,128)S(1)} collective-permute-done((f32[40,128]{1,0:T(8,128)S(1)}, f32[40,128]{1,0:T(8,128)S(1)}, u32[]{:S(2)}, u32[]{:S(2)}) %collective-permute-start.9) | collective-permute-done | bytes 20512 | tf_op jit(solution)/shard_map/ppermute | solution.py:605
  38.9 1.3 %collective-permute-start.10 = (f32[40,128]{1,0:T(8,128)S(1)}, f32[40,128]{1,0:T(8,128)S(1)}, u32[]{:S(2)}, u32[]{:S(2)}) collective-permute-start(f32[40,128]{1,0:T(8,128)S(1)} %add.18.sums_ref), channel_id=1, source_target_pairs={{0,4},{2,6},{4,0},{6,2},{8,12},{10,14},{12,8},{14,10},{16,20},{18,... | collective-permute-start | bytes 61448 | tf_op jit(solution)/shard_map/ppermute | solution.py:605
  40.2 2.4 %inverse.1 = (f32[64,64]{1,0:T(8,128)S(1)}, f32[64,512]{1,0:T(8,128)S(1)}) custom-call(f32[40,128]{1,0:T(8,128)S(1)} %add.18.sums_ref), custom_call_target="tpu_custom_call" | custom-call | flops 20000000 | bytes 32768 | tf_op jit(solution)/shard_map/inverse/pallas_call | solution.py:816
  42.6 0.1 collective-permute-done.10
  42.7 3.2 %finish.1 = (f32[2,20,8,512]{3,2,1,0:T(8,128)}, f32[2,64]{1,0:T(2,128)}, f32[2,2]{1,0:T(2,128)}) custom-call(f32[40,128]{1,0:T(8,128)S(1)} %add.19.projected_ref, f32[40,128]{1,0:T(8,128)S(1)} %add.18.sums_ref, f32[64,64]{1,0:T(8,128)S(1)} %get-tuple-element.40.inverse_ref, f32[64,512]{1,0:T(8,128)S(1)} %get-tuple-element.41.spread_ref, ...), custom_call_target="tpu_custom_call" | custom-call | flops 335544320 | bytes 11796480 | tf_op jit(solution)/shard_map/finish/pallas_call | solution.py:829
  (16 shorter events, 0.2 us)
Async XLA Ops:
  0.6 1.1 %copy-start = (f32[2,5,8,4,512]{4,3,2,1,0:T(4,128)S(1)}, f32[2,5,8,4,512]{4,3,2,1,0:T(4,128)}, u32[]{:S(2)}) copy-start(f32[2,5,8,4,512]{4,3,2,1,0:T(4,128)} %source_ref.1) | copy-start | bytes 1966084
  2.4 14.0 %collective-permute-start = (bf16[5,48,512]{2,1,0:T(8,128)(2,1)S(1)}, bf16[5,48,512]{2,1,0:T(8,128)(2,1)S(1)}, u32[]{:S(2)}, u32[]{:S(2)}) collective-permute-start(bf16[5,48,512]{2,1,0:T(8,128)(2,1)S(1)} %get-tuple-element.27._), channel_id=1, source_target_pairs={{0,1},{1,0},{2,3},{3,2},{4,5},{5,4},{6,7},{7,6},{8,9},{9,8},{10,11... | collective-permute-start | bytes 737288 | tf_op jit(solution)/shard_map/ppermute | solution.py:661
  6.4 10.2 %collective-permute-start.1 = (bf16[5,48,512]{2,1,0:T(8,128)(2,1)S(1)}, bf16[5,48,512]{2,1,0:T(8,128)(2,1)S(1)}, u32[]{:S(2)}, u32[]{:S(2)}) collective-permute-start(bf16[5,48,512]{2,1,0:T(8,128)(2,1)S(1)} %get-tuple-element.28), channel_id=1, source_target_pairs={{2,0},{4,2},{6,4},{8,6},{10,8},{12,10},{14,12},{16,14},{18,16},{20... | collective-permute-start | bytes 737288 | tf_op jit(solution)/shard_map/ppermute | solution.py:665
  10.1 11.2 %collective-permute-start.2 = (bf16[5,48,512]{2,1,0:T(8,128)(2,1)S(1)}, bf16[5,48,512]{2,1,0:T(8,128)(2,1)S(1)}, u32[]{:S(2)}, u32[]{:S(2)}) collective-permute-start(bf16[5,48,512]{2,1,0:T(8,128)(2,1)S(1)} %get-tuple-element.33), channel_id=1, source_target_pairs={{0,2},{2,4},{4,6},{6,8},{8,10},{10,12},{12,14},{14,16},{16,18},{18... | collective-permute-start | bytes 737288 | tf_op jit(solution)/shard_map/ppermute | solution.py:666
  10.1 11.2 %collective-permute-start.3 = (bf16[5,48,512]{2,1,0:T(8,128)(2,1)S(1)}, bf16[5,48,512]{2,1,0:T(8,128)(2,1)S(1)}, u32[]{:S(2)}, u32[]{:S(2)}) collective-permute-start(bf16[5,48,512]{2,1,0:T(8,128)(2,1)S(1)} %get-tuple-element.34), channel_id=1, source_target_pairs={{0,1},{1,0},{2,3},{3,2},{4,5},{5,4},{6,7},{7,6},{8,9},{9,8},{10,11... | collective-permute-start | bytes 737288 | tf_op jit(solution)/shard_map/ppermute | solution.py:667
  16.7 5.4 %collective-permute-start.4 = (bf16[2,5,16,512]{3,2,1,0:T(8,128)(2,1)S(1)}, bf16[2,5,16,512]{3,2,1,0:T(8,128)(2,1)S(1)}, u32[]{:S(2)}, u32[]{:S(2)}) collective-permute-start(bf16[2,5,16,512]{3,2,1,0:T(8,128)(2,1)S(1)} %get-tuple-element.29._), channel_id=1, source_target_pairs={{0,1},{1,0},{2,3},{3,2},{4,5},{5,4},{6,7},{7,6},{8,9},{9,8},{10,11... | collective-permute-start | bytes 491528 | tf_op jit(solution)/shard_map/ppermute | solution.py:745
  21.3 3.8 %collective-permute-start.5 = (f32[32,128]{1,0:T(8,128)S(1)}, f32[32,128]{1,0:T(8,128)S(1)}, u32[]{:S(2)}, u32[]{:S(2)}) collective-permute-start(f32[32,128]{1,0:T(8,128)S(1)} %gram.1._.gram_ref), channel_id=1, source_target_pairs={{0,4},{2,6},{4,0},{6,2},{8,12},{10,14},{12,8},{14,10},{16,20},{18,... | collective-permute-start | bytes 49160 | tf_op jit(solution)/shard_map/ppermute | solution.py:760
  25.2 3.8 %collective-permute-start.6 = (f32[40,128]{1,0:T(8,128)S(1)}, f32[40,128]{1,0:T(8,128)S(1)}, u32[]{:S(2)}, u32[]{:S(2)}) collective-permute-start(f32[40,128]{1,0:T(8,128)S(1)} %merge.1), channel_id=1, source_target_pairs={{0,1},{1,0},{2,3},{3,2},{4,5},{5,4},{6,7},{7,6},{8,9},{9,8},{10,11... | collective-permute-start | bytes 61448 | tf_op jit(solution)/shard_map/ppermute | solution.py:605
  29.0 1.2 %collective-permute-start.7 = (f32[40,128]{1,0:T(8,128)S(1)}, f32[40,128]{1,0:T(8,128)S(1)}, u32[]{:S(2)}, u32[]{:S(2)}) collective-permute-start(f32[40,128]{1,0:T(8,128)S(1)} %add.15), channel_id=1, source_target_pairs={{0,2},{2,0},{4,6},{6,4},{8,10},{10,8},{12,14},{14,12},{16,18},{18,... | collective-permute-start | bytes 61448 | tf_op jit(solution)/shard_map/ppermute | solution.py:605
  30.2 3.8 %collective-permute-start.8 = (f32[40,128]{1,0:T(8,128)S(1)}, f32[40,128]{1,0:T(8,128)S(1)}, u32[]{:S(2)}, u32[]{:S(2)}) collective-permute-start(f32[40,128]{1,0:T(8,128)S(1)} %add.16), channel_id=1, source_target_pairs={{0,8},{2,10},{4,12},{6,14},{8,0},{10,2},{12,4},{14,6},{16,24},{18,... | collective-permute-start | bytes 61448 | tf_op jit(solution)/shard_map/ppermute | solution.py:605
  34.0 4.9 %collective-permute-start.9 = (f32[40,128]{1,0:T(8,128)S(1)}, f32[40,128]{1,0:T(8,128)S(1)}, u32[]{:S(2)}, u32[]{:S(2)}) collective-permute-start(f32[40,128]{1,0:T(8,128)S(1)} %add.17), channel_id=1, source_target_pairs={{0,16},{2,18},{4,20},{6,22},{8,24},{10,26},{12,28},{14,30},{16,0},... | collective-permute-start | bytes 61448 | tf_op jit(solution)/shard_map/ppermute | solution.py:605
  38.9 3.8 %collective-permute-start.10 = (f32[40,128]{1,0:T(8,128)S(1)}, f32[40,128]{1,0:T(8,128)S(1)}, u32[]{:S(2)}, u32[]{:S(2)}) collective-permute-start(f32[40,128]{1,0:T(8,128)S(1)} %add.18.sums_ref), channel_id=1, source_target_pairs={{0,4},{2,6},{4,0},{6,2},{8,12},{10,14},{12,8},{14,10},{16,20},{18,... | collective-permute-start | bytes 61448 | tf_op jit(solution)/shard_map/ppermute | solution.py:605
